TPU v7x, 32 devices: a whole 2x2x4 slice. The times are simulated.
32 devices in a mesh: row: 8 (over y, x, core), col: 4 (over z).
Axes of the slice: x: 2, y: 2, z: 4, core: 2. Of those that a mesh axis runs over, the one named last changes fastest.
Arguments:
- front_matrix: float32 [3072, 16384], P('row', 'col'), may hold values from -6 to 6
- child_rows: float32 [512, 16384], P('row', 'col'), may hold values from -6 to 6
- child_owner: int32 [512, 1], P('row'), may hold values from 0 to 7; in each aligned block of 64 rows (0 to 63, 64 to 127, ...) at most 16 rows name the same one
- child_offset: int32 [512, 1], P('row'), may hold values from 0 to 383
Outputs:
- upper_rows: float32 [512, 16384], P(None, 'col')
- reduced_front: float32 [3072, 16384], P('row', 'col')
- basis_scaled: float32 [3072, 512], P('row')
Inputs may be any that keep to these rules, and one draw needn't show every extreme that they name: `child_owner`: within the rows of one device (aligned blocks of 64 rows) no value occurs more than 16 times, and some value occurs exactly 16 times.
All inputs are finite; a program needn't handle non-finite values.
Results may differ from a plain program's by a relative error of at most 0.0001.
Values sent between devices are 32-bit elements; how exact they have to be, the bound alone decides.
No kernel may reach another device: no remote copies, remote signals or barrier semaphores. Data moves between devices by JAX's collectives and lax.ppermute only.
A program may use at most 128 MiB of HBM per device.

v0:
```python
import math

import jax
import jax.numpy as jnp
from jax import lax
from jax.sharding import PartitionSpec as P

PB = 128
PANELS = 4


def spread(block, axis, owner):
    block = jnp.where(lax.axis_index(axis) == owner, block, jnp.zeros_like(block))
    return lax.psum(block, axis)


def product(left_op, right_op):
    return jnp.dot(
        left_op, right_op, precision=lax.Precision.HIGHEST, preferred_element_type=jnp.float32
    )


def factor_panel(panel_cols):
    gram_part = product(panel_cols.T, panel_cols)
    gram_total = lax.psum(gram_part, "row")
    lower_factor = jnp.linalg.cholesky(gram_total)
    basis = lax.linalg.triangular_solve(
        lower_factor, panel_cols, left_side=False, lower=True, transpose_a=True
    )
    return spread(basis, "col", 0)


def on_device(front_matrix, child_rows, child_owner, child_offset):
    row_count = lax.axis_size("row")
    local_rows = front_matrix.shape[0]
    local_cols = front_matrix.shape[1]
    child_count = child_rows.shape[0]
    capacity = 2 * child_count // row_count
    slot_total = row_count * capacity
    owner_rows = child_owner[:, 0]
    onehot = (owner_rows[:, None] == jnp.arange(row_count, dtype=jnp.int32)[None, :]).astype(
        jnp.int32
    )
    rank_in = jnp.sum(onehot * (jnp.cumsum(onehot, axis=0) - 1), axis=1)
    position = owner_rows * capacity + rank_in
    sender = jnp.zeros((slot_total, local_cols), jnp.float32).at[position].set(child_rows)
    offsets = jnp.full((slot_total,), local_rows, jnp.int32).at[position].set(child_offset[:, 0])
    received, placed = (
        lax.all_to_all(
            sender.reshape(row_count, capacity, local_cols),
            "row",
            split_axis=0,
            concat_axis=0,
            tiled=True,
        ),
        lax.all_to_all(
            offsets.reshape(row_count, capacity), "row", split_axis=0, concat_axis=0, tiled=True
        ),
    )
    current = front_matrix.at[placed.reshape(slot_total)].add(
        received.reshape(slot_total, local_cols), mode="drop"
    )
    top_list = []
    basis_list = []
    for panel_index in range(PANELS):
        basis = factor_panel(current[:, panel_index * PB : (panel_index + 1) * PB])
        split_at = min((panel_index + 2) * PB, local_cols)
        near_part = current[:, :split_at]
        near_top = lax.psum(product(basis.T, near_part), "row")
        near_part = near_part - product(basis, near_top)
        far_part = current[:, split_at:]
        far_top = lax.psum(product(basis.T, far_part), "row")
        far_part = far_part - product(basis, far_top)
        top_rows = jnp.concatenate([near_top, far_top], axis=1)
        current = jnp.concatenate([near_part, far_part], axis=1)
        top_list.append(top_rows)
        basis_list.append(basis)
    total_rows = local_rows * row_count
    scaled = jnp.concatenate(basis_list, axis=1) * math.sqrt(total_rows)
    return (jnp.concatenate(top_list, axis=0), current, scaled)


def solution(mesh):
    placed = (P("row", "col"), P("row", "col"), P("row", None), P("row", None))
    return jax.shard_map(
        on_device,
        mesh=mesh,
        in_specs=placed,
        out_specs=(P(None, "col"), P("row", "col"), P("row", None)),
        check_vma=False,
    )
```

profile of v0, /device:TPU:21, one launch (start us, length us, event | category | flops | bytes accessed | tf_op | source)
XLA Modules:
  0.0 816.2 jit_solution(10974969824685472685)
XLA Ops:
  29.3 21.6 %all-to-all-done.1 = f32[8,16,4096]{2,1,0:T(8,128)S(1)} async-done(((f32[8,16,4096]{2,1,0:T(8,128)}), f32[8,16,4096]{2,1,0:T(8,128)S(1)}, u32[]{:S(2)}, u32[]{:S(2)}) %all-to-all-start.1) | async-done | bytes 2097184 | tf_op jit(solution)/shard_map/all_to_all | solution.py:49
  50.9 8.7 %scatter_fusion = f32[384,4096]{1,0:T(8,128)} fusion(f32[384,4096]{1,0:T(8,128)} %copy.68, s32[128]{0:T(128)S(1)} %fusion.40, f32[128,4096]{1,0:T(8,128)S(1)} %bitcast.94), kind=kCustom, calls=%fused_computation.2 | custom fusion | flops 524288 | bytes 6291968 | tf_op jit(solution)/shard_map/scatter-add | solution.py:60
  62.3 52.5 %all-reduce.17.cloned.1.call-done = f32[128,128]{0,1:T(8,128)} async-done(((f32[128,128]{0,1:T(8,128)}), f32[128,128]{0,1:T(8,128)}) %all-reduce.17.cloned.1.call-update) | async-done | bytes 65552 | tf_op jit(solution)/shard_map/psum | solution.py:25
  116.6 11.7 %cholesky.74 = f32[128,128]{1,0:T(8,128)S(1)} custom-call(f32[128,128]{1,0:T(8,128)S(1)} %fusion.37), custom_call_target="Cholesky" | custom-call | tf_op jit(solution)/shard_map/jit(cholesky)/cholesky | solution.py:26
  129.7 9.8 %custom-call.8 = f32[1,128,128]{1,2,0:T(8,128)S(1)} custom-call(f32[1,128,128]{2,1,0:T(8,128)S(1)} %fusion.26), custom_call_target="InvertDiagBlocksLowerTriangular" | custom-call | tf_op jit(solution)/shard_map/triangular_solve/custom-call.0 | solution.py:27
  142.8 32.4 %all-reduce.19.cloned.1.call-done = f32[384,128]{0,1:T(8,128)} async-done(((f32[384,128]{0,1:T(8,128)}), f32[384,128]{0,1:T(8,128)}) %all-reduce.19.cloned.1.call-update) | async-done | bytes 196624 | tf_op jit(solution)/shard_map/psum | solution.py:14
  185.0 47.0 %all-reduce.21.cloned.1.call-done = f32[128,256]{1,0:T(8,128)} async-done(((f32[128,256]{1,0:T(8,128)}), f32[128,256]{1,0:T(8,128)}) %all-reduce.21.cloned.1.call-update) | async-done | bytes 131088 | tf_op jit(solution)/shard_map/psum | solution.py:69
  235.0 62.3 %all-reduce.39.cloned.1.call-done = (f32[128,128]{0,1:T(8,128)}, f32[128,3840]{1,0:T(8,128)}) async-done(((f32[128,128]{0,1:T(8,128)}, f32[128,3840]{1,0:T(8,128)}), (f32[128,128]{0,1:T(8,128)}, f32[128,3840]{1,0:T(8,128)})) %all-reduce.39.cloned.1.call-update) | async-done | bytes 2031632 | tf_op jit(solution)/shard_map/psum | solution.py:25
  299.1 11.7 %cholesky.85 = f32[128,128]{1,0:T(8,128)S(1)} custom-call(f32[128,128]{1,0:T(8,128)S(1)} %fusion.35), custom_call_target="Cholesky" | custom-call | tf_op jit(solution)/shard_map/jit(cholesky)/cholesky | solution.py:26
  312.1 9.8 %custom-call.9 = f32[1,128,128]{1,2,0:T(8,128)S(1)} custom-call(f32[1,128,128]{2,1,0:T(8,128)S(1)} %fusion.27), custom_call_target="InvertDiagBlocksLowerTriangular" | custom-call | tf_op jit(solution)/shard_map/triangular_solve/custom-call.0 | solution.py:27
  323.3 8.1 convolution_subtract_fusion.3
  334.0 22.2 %all-reduce.23.cloned.1.call-done = f32[384,128]{0,1:T(8,128)} async-done(((f32[384,128]{0,1:T(8,128)}), f32[384,128]{0,1:T(8,128)}) %all-reduce.23.cloned.1.call-update) | async-done | bytes 196624 | tf_op jit(solution)/shard_map/psum | solution.py:14
  366.1 47.6 %all-reduce.25.cloned.1.call-done = f32[128,384]{1,0:T(8,128)} async-done(((f32[128,384]{1,0:T(8,128)}), f32[128,384]{1,0:T(8,128)}) %all-reduce.25.cloned.1.call-update) | async-done | bytes 196624 | tf_op jit(solution)/shard_map/psum | solution.py:69
  416.9 61.1 %all-reduce.37.cloned.1.call-done = (f32[128,3712]{1,0:T(8,128)}, f32[128,128]{0,1:T(8,128)}) async-done(((f32[128,3712]{1,0:T(8,128)}, f32[128,128]{0,1:T(8,128)}), (f32[128,3712]{1,0:T(8,128)}, f32[128,128]{0,1:T(8,128)})) %all-reduce.37.cloned.1.call-update) | async-done | bytes 1966096 | tf_op jit(solution)/shard_map/psum | solution.py:72
  479.9 11.7 %cholesky.96 = f32[128,128]{1,0:T(8,128)S(1)} custom-call(f32[128,128]{1,0:T(8,128)S(1)} %fusion.33), custom_call_target="Cholesky" | custom-call | tf_op jit(solution)/shard_map/jit(cholesky)/cholesky | solution.py:26
  492.9 9.8 %custom-call.10 = f32[1,128,128]{1,2,0:T(8,128)S(1)} custom-call(f32[1,128,128]{2,1,0:T(8,128)S(1)} %fusion.28), custom_call_target="InvertDiagBlocksLowerTriangular" | custom-call | tf_op jit(solution)/shard_map/triangular_solve/custom-call.0 | solution.py:27
  503.9 8.1 convolution_subtract_fusion.2
  514.6 23.0 %all-reduce.27.cloned.1.call-done = f32[384,128]{0,1:T(8,128)} async-done(((f32[384,128]{0,1:T(8,128)}), f32[384,128]{0,1:T(8,128)}) %all-reduce.27.cloned.1.call-update) | async-done | bytes 196624 | tf_op jit(solution)/shard_map/psum | solution.py:14
  547.5 47.6 %all-reduce.29.cloned.1.call-done = f32[128,512]{1,0:T(8,128)} async-done(((f32[128,512]{1,0:T(8,128)}), f32[128,512]{1,0:T(8,128)}) %all-reduce.29.cloned.1.call-update) | async-done | bytes 262160 | tf_op jit(solution)/shard_map/psum | solution.py:69
  598.1 61.1 %all-reduce.35.cloned.1.call-done = (f32[128,128]{0,1:T(8,128)}, f32[128,3584]{1,0:T(8,128)}) async-done(((f32[128,128]{0,1:T(8,128)}, f32[128,3584]{1,0:T(8,128)}), (f32[128,128]{0,1:T(8,128)}, f32[128,3584]{1,0:T(8,128)})) %all-reduce.35.cloned.1.call-update) | async-done | bytes 1900560 | tf_op jit(solution)/shard_map/psum | solution.py:25
  661.0 11.7 %cholesky.107 = f32[128,128]{1,0:T(8,128)S(1)} custom-call(f32[128,128]{1,0:T(8,128)S(1)} %fusion.31), custom_call_target="Cholesky" | custom-call | tf_op jit(solution)/shard_map/jit(cholesky)/cholesky | solution.py:26
  674.0 9.8 %custom-call.11 = f32[1,128,128]{1,2,0:T(8,128)S(1)} custom-call(f32[1,128,128]{2,1,0:T(8,128)S(1)} %fusion.29), custom_call_target="InvertDiagBlocksLowerTriangular" | custom-call | tf_op jit(solution)/shard_map/triangular_solve/custom-call.0 | solution.py:27
  695.6 23.0 %all-reduce.31.cloned.1.call-done = f32[384,128]{0,1:T(8,128)} async-done(((f32[384,128]{0,1:T(8,128)}), f32[384,128]{0,1:T(8,128)}) %all-reduce.31.cloned.1.call-update) | async-done | bytes 196624 | tf_op jit(solution)/shard_map/psum | solution.py:14
  728.7 61.1 %all-reduce.33.cloned.1.call-done = (f32[128,3456]{1,0:T(8,128)}, f32[128,640]{1,0:T(8,128)}) async-done(((f32[128,3456]{1,0:T(8,128)}, f32[128,640]{1,0:T(8,128)}), (f32[128,3456]{1,0:T(8,128)}, f32[128,640]{1,0:T(8,128)})) %all-reduce.33.cloned.1.call-update) | async-done | bytes 2097168 | tf_op jit(solution)/shard_map/psum | solution.py:72
  (123 shorter events, 127.7 us)
Async XLA Ops:
  7.2 6.2 copy-start.15
  15.3 7.8 all-to-all-start
  23.1 27.7 %all-to-all-start.1 = ((f32[8,16,4096]{2,1,0:T(8,128)}), f32[8,16,4096]{2,1,0:T(8,128)S(1)}, u32[]{:S(2)}, u32[]{:S(2)}) async-start(f32[8,16,4096]{2,1,0:T(8,128)} %bitcast.95), calls=%async_computation.1 | async-start | bytes 4194304 | tf_op jit(solution)/shard_map/all_to_all | solution.py:49
  28.0 86.8 %all-reduce.17.cloned.1.call-start = ((), (), s32[]{:S(2)}) async-start(), calls=%async_computation.2 | async-start | bytes 131072 | tf_op jit(solution)/shard_map/psum | solution.py:25
  61.7 113.5 %all-reduce.19.cloned.1.call-start = ((), (), s32[]{:S(2)}) async-start(), calls=%async_computation.3 | async-start | bytes 393216 | tf_op jit(solution)/shard_map/psum | solution.py:14
  141.5 90.6 %all-reduce.21.cloned.1.call-start = ((), (), s32[]{:S(2)}) async-start(), calls=%async_computation.4 | async-start | bytes 262144 | tf_op jit(solution)/shard_map/psum | solution.py:69
  175.2 56.9 %copy-start.9 = (f32[384,128]{0,1:T(8,128)S(1)}, f32[384,128]{0,1:T(8,128)}, u32[]{:S(2)}) copy-start(f32[384,128]{0,1:T(8,128)} %all-reduce.19.cloned.1.call-done) | copy-start | bytes 589828
  177.4 119.9 %all-reduce.39.cloned.1.call-start = ((), (), s32[]{:S(2)}) async-start(), calls=%async_computation.13 | async-start | bytes 4063232 | tf_op jit(solution)/shard_map/psum | solution.py:25
  234.6 121.6 %all-reduce.23.cloned.1.call-start = ((), (), s32[]{:S(2)}) async-start(), calls=%async_computation.5 | async-start | bytes 393216 | tf_op jit(solution)/shard_map/psum | solution.py:14
  323.0 90.7 %all-reduce.25.cloned.1.call-start = ((), (), s32[]{:S(2)}) async-start(), calls=%async_computation.6 | async-start | bytes 393216 | tf_op jit(solution)/shard_map/psum | solution.py:69
  356.2 57.5 %copy-start.7 = (f32[384,128]{0,1:T(8,128)S(1)}, f32[384,128]{0,1:T(8,128)}, u32[]{:S(2)}) copy-start(f32[384,128]{0,1:T(8,128)} %all-reduce.23.cloned.1.call-done) | copy-start | bytes 589828
  358.5 119.6 %all-reduce.37.cloned.1.call-start = ((), (), s32[]{:S(2)}) async-start(), calls=%async_computation.12 | async-start | bytes 3932160 | tf_op jit(solution)/shard_map/psum | solution.py:72
  416.5 121.1 %all-reduce.27.cloned.1.call-start = ((), (), s32[]{:S(2)}) async-start(), calls=%async_computation.7 | async-start | bytes 393216 | tf_op jit(solution)/shard_map/psum | solution.py:14
  503.8 91.3 %all-reduce.29.cloned.1.call-start = ((), (), s32[]{:S(2)}) async-start(), calls=%async_computation.8 | async-start | bytes 524288 | tf_op jit(solution)/shard_map/psum | solution.py:69
  537.6 57.5 %copy-start.10 = (f32[384,128]{0,1:T(8,128)S(1)}, f32[384,128]{0,1:T(8,128)}, u32[]{:S(2)}) copy-start(f32[384,128]{0,1:T(8,128)} %all-reduce.27.cloned.1.call-done) | copy-start | bytes 589828
  539.9 119.2 %all-reduce.35.cloned.1.call-start = ((), (), s32[]{:S(2)}) async-start(), calls=%async_computation.11 | async-start | bytes 3801088 | tf_op jit(solution)/shard_map/psum | solution.py:25
  598.0 120.6 %all-reduce.31.cloned.1.call-start = ((), (), s32[]{:S(2)}) async-start(), calls=%async_computation.9 | async-start | bytes 393216 | tf_op jit(solution)/shard_map/psum | solution.py:14
  684.9 104.8 %all-reduce.33.cloned.1.call-start = ((), (), s32[]{:S(2)}) async-start(), calls=%async_computation.10 | async-start | bytes 4194304 | tf_op jit(solution)/shard_map/psum | solution.py:72
  718.6 7.2 copy-start.8
  789.8 8.0 copy-start.11
  798.8 5.4 copy-start.6
  798.9 5.4 copy-start.12
  798.9 5.4 copy-start.13
  798.9 5.5 copy-start.14
  (6 other events, 20.4 us)
Sparse Core Ops, SparseCore 0:
  61.8 52.9 all-reduce.16
  141.6 33.4 all-reduce.18
  178.8 53.2 all-reduce.20
  236.3 60.9 all-reduce.38
  323.1 33.0 all-reduce.22
  360.0 53.6 all-reduce.24
  418.0 59.9 all-reduce.36
  503.9 33.5 all-reduce.26
  541.2 53.8 all-reduce.28
  599.3 59.8 all-reduce.34
  685.1 33.5 all-reduce.30
  727.6 62.1 all-reduce.32
where the time goes:
time: 825 us; the launch traced here: 816 us
  waiting for transfers between devices  563 us (68%)
  other arithmetic  114 us (14%)
  matrix products  86.5 us (10%)
  local copies, waits for them, and re-layouts  26.8 us (3%)
  between operations  14.8 us (2%)
  starting transfers between devices  11.5 us (1%)
    psum x3, waiting for transfers between devices, factor_panel(): gram_total = lax.psum(gram_part, 'row')  176 us
    psum x3, waiting for transfers between devices, on_device(): near_top = lax.psum(product(basis.T, near_part), 'row')  142 us
    psum x2, waiting for transfers between devices, on_device(): far_top = lax.psum(product(basis.T, far_part), 'row')  122 us
    psum x4, waiting for transfers between devices, spread(): return lax.psum(block, axis)  101 us
    dot_general x20, matrix products, product(): jnp.dot(left_op, right_op, precision=lax.Precision.HIGHEST, preferred_ele...  81.3 us
    another operation x12, other arithmetic, factor_panel(): lower_factor = jnp.linalg.cholesky(gram_total)  49.6 us
    another operation x8, other arithmetic, factor_panel(): lax.linalg.triangular_solve(lower_factor, panel_cols, left_side=False, lo...  41.9 us
    all_to_all x1, waiting for transfers between devices, on_device(): lax.all_to_all(sender.reshape(row_count, capacity, local_cols), 'row', sp...  21.6 us
  transfers between devices with their start and end apart: 14, of which 13 were waited for; matrix products, arithmetic and copies ran while one was open for 7% of the time, Pallas kernels for 0%

commit v1 on v0

v1 whole, which is shorter than its diff:
```python
import functools
import math

import jax
import jax.numpy as jnp
import numpy as np
from jax import lax
from jax.experimental import pallas as pl
from jax.experimental.pallas import tpu as pltpu
from jax.sharding import PartitionSpec as P

PB = 128
PANELS = 4
LEAD = PB * PANELS
GROUP = 256
VMEM_BYTES = 48 * 1024 * 1024
HIGHEST = lax.Precision.HIGHEST
F32 = jnp.float32
BF16 = jnp.bfloat16
SMEM = pltpu.SMEM
VMEM = pltpu.VMEM


def params():
    return pltpu.CompilerParams(vmem_limit_bytes=VMEM_BYTES)


def mask_orders(count):
    others = [1 << b for b in range(1, count.bit_length() - 1)]
    half = len(others) // 2
    return ([1] + others, [1] + others[half:] + others[:half])


def swap(value, step, count):
    orders = mask_orders(count)
    pairs = [(d, d ^ orders[d & 1][step]) for d in range(count)]
    return lax.ppermute(value, "row", pairs)


def upper_side(step, count):
    orders = mask_orders(count)
    me = lax.axis_index("row")
    mask = jnp.where(me & 1 == 0, orders[0][step], orders[1][step])
    return ((me & mask) != 0).astype(jnp.int32)


def shard_table(count):
    orders = mask_orders(count)
    steps = len(orders[0])
    return np.array(
        [
            sum(((d & orders[d & 1][t]) != 0) << (steps - 1 - t) for t in range(steps))
            for d in range(count)
        ]
    )


def piece_table(count):
    orders = mask_orders(count)
    steps = len(orders[0])
    shard = shard_table(count)

    def pieces(device, done):
        if done == 0:
            return [device]
        mask = orders[device & 1][steps - done]
        return pieces(device, done - 1) + pieces(device ^ mask, done - 1)

    return np.array([[shard[p] for p in pieces(d, steps)] for d in range(count)], np.int32)


def halve(value, other, axis, step, count):
    side = upper_side(step, count)
    size = value.shape[axis] // 2

    def take(which):
        mine = lax.dynamic_slice_in_dim(value, which * size, size, axis)
        if other is None:
            return mine
        return mine + lax.dynamic_slice_in_dim(other, which * size, size, axis)

    return take(side), take(1 - side)


def scatter_sum(keep, send, axis, count):
    steps = count.bit_length() - 1
    for step in range(steps):
        got = swap(send, step, count)
        if step == steps - 1:
            return keep + got
        keep, send = halve(keep, got, axis, step + 1, count)


def total_rows(value, count):
    keep, send = halve(value, None, 0, 0, count)
    mine = scatter_sum(keep, send, 0, count)
    for step in reversed(range(count.bit_length() - 1)):
        got = swap(mine, step, count)
        side = upper_side(step, count)
        mine = jnp.where(
            side == 0,
            jnp.concatenate([mine, got], axis=0),
            jnp.concatenate([got, mine], axis=0),
        )
    return mine


def spread(value, count):
    me = lax.axis_index("col")
    stride = count
    while stride > 1:
        half = stride // 2
        pairs = [(c, c + half) for c in range(0, count, stride)]
        got = lax.ppermute(value, "col", pairs)
        value = jnp.where(me % stride == half, got, value)
        stride = half
    return value


def parts3(x):
    hi = x.astype(BF16)
    rest = x - hi.astype(F32)
    mid = rest.astype(BF16)
    return hi, mid, (rest - mid.astype(F32)).astype(BF16)


def parts2(x):
    hi = x.astype(BF16)
    return hi, (x - hi.astype(F32)).astype(BF16)


def pack_kernel(row_count, capacity, sentinel, owner_ref, offset_ref, child_ref, out_ref, tag_ref, tally):
    out_ref[...] = jnp.zeros_like(out_ref)
    tag_ref[...] = jnp.full(tag_ref.shape, sentinel, F32)
    for d in range(row_count):
        tally[d] = 0

    def body(i, carry):
        owner = owner_ref[i]
        rank = tally[owner]
        tally[owner] = rank + 1
        slot = owner * capacity + rank
        out_ref[pl.ds(slot, 1), :] = child_ref[pl.ds(i, 1), :]
        tag_ref[pl.ds(slot, 1), :] = jnp.full((1, tag_ref.shape[1]), offset_ref[i].astype(F32))
        return carry

    lax.fori_loop(0, child_ref.shape[0], body, 0)


def pack(child_rows, owner, offset, row_count, capacity, sentinel):
    slots = row_count * capacity
    return pl.pallas_call(
        functools.partial(pack_kernel, row_count, capacity, float(sentinel)),
        out_shape=(
            jax.ShapeDtypeStruct((slots, child_rows.shape[1]), F32),
            jax.ShapeDtypeStruct((slots, PB), F32),
        ),
        in_specs=[
            pl.BlockSpec(memory_space=SMEM),
            pl.BlockSpec(memory_space=SMEM),
            pl.BlockSpec(memory_space=VMEM),
        ],
        out_specs=(pl.BlockSpec(memory_space=VMEM), pl.BlockSpec(memory_space=VMEM)),
        scratch_shapes=[pltpu.SMEM((row_count,), jnp.int32)],
        compiler_params=params(),
        name="pack_children",
    )(owner, offset, child_rows)


def assemble_kernel(front_ref, child_ref, tag_ref, out_ref):
    rows = front_ref.shape[0]
    slots = child_ref.shape[0]
    place = jnp.transpose(tag_ref[...])[0:1, :]
    at = lax.broadcasted_iota(jnp.int32, (rows, slots), 0).astype(F32)
    onehot = jnp.where(at == place, 1.0, 0.0).astype(BF16)
    added = jnp.zeros(front_ref.shape, F32)
    for part in reversed(parts3(child_ref[...])):
        added = added + jnp.dot(onehot, part, preferred_element_type=F32)
    out_ref[...] = front_ref[...] + added


def assemble(front, child, tags, columns, block):
    rows = front.shape[0]
    slots = child.shape[0]
    return pl.pallas_call(
        assemble_kernel,
        grid=(columns // block,),
        out_shape=jax.ShapeDtypeStruct((rows, columns), F32),
        in_specs=[
            pl.BlockSpec((rows, block), lambda i: (0, i)),
            pl.BlockSpec((slots, block), lambda i: (0, i)),
            pl.BlockSpec((slots, PB), lambda i: (0, 0)),
        ],
        out_specs=pl.BlockSpec((rows, block), lambda i: (0, i)),
        compiler_params=params(),
        name="assemble_front",
    )(front, child, tags)


def lead_product_kernel(half_ref, lead_ref, front_ref, out_ref):
    del half_ref
    lead_hi, lead_lo = parts2(jnp.transpose(lead_ref[...]))
    hi, lo = parts2(front_ref[...])
    left = jnp.concatenate([lead_hi, lead_hi, lead_lo], axis=1)
    right = jnp.concatenate([hi, lo, hi], axis=0)
    out_ref[...] = jnp.dot(left, right, preferred_element_type=F32)


def lead_product(half, lead, front, block):
    rows, columns = front.shape
    width = lead.shape[1]
    steps = columns // 2 // block
    return pl.pallas_call(
        lead_product_kernel,
        grid_spec=pltpu.PrefetchScalarGridSpec(
            num_scalar_prefetch=1,
            grid=(steps,),
            in_specs=[
                pl.BlockSpec((rows, width), lambda i, h: (0, 0)),
                pl.BlockSpec((rows, block), lambda i, h: (0, h[0] * steps + i)),
            ],
            out_specs=pl.BlockSpec((width, block), lambda i, h: (0, i)),
        ),
        out_shape=jax.ShapeDtypeStruct((width, columns // 2), F32),
        compiler_params=params(),
        name="lead_product",
    )(half, lead, front)


def dot_high(a, b, dims):
    return lax.dot_general(a, b, (dims, ((), ())), precision=HIGHEST, preferred_element_type=F32)


def invert_factor(block):
    lane = lax.broadcasted_iota(jnp.int32, (8, PB), 1)
    sub = lax.broadcasted_iota(jnp.int32, (8, PB), 0)
    tiles = [block[8 * t : 8 * t + 8, :] for t in range(PB // 8)]
    for j in range(PB):
        home, inner = divmod(j, 8)
        tile = tiles[home]
        row = tile[inner : inner + 1, :]
        inverse = 1.0 / row[:, j : j + 1]
        row = jnp.where(lane[0:1, :] == j, 1.0, row) * inverse
        here = lane == j
        for t in range(home, PB // 8):
            factor = tiles[t][:, j : j + 1]
            cleared = jnp.where(here, 0.0, tiles[t])
            updated = cleared - factor * row
            if t == home:
                updated = jnp.where(sub > inner, updated, tiles[t])
            tiles[t] = updated
    done = []
    for t in range(PB // 8):
        diagonal = lane == sub + 8 * t
        pivot = jnp.sum(jnp.where(diagonal, tiles[t], 0.0), axis=1, keepdims=True)
        scale = lax.rsqrt(pivot)
        scale = scale * (1.5 - 0.5 * pivot * scale * scale)
        unit = jnp.where(diagonal, 1.0, jnp.where(lane < sub + 8 * t, tiles[t], 0.0))
        done.append(unit * scale)
    return jnp.concatenate(done, axis=0)


def eliminate_kernel(k, in_ref, out_ref):
    lo, hi = k * PB, (k + 1) * PB
    inverse = invert_factor(in_ref[lo:hi, lo:hi])
    pieces = []
    for j in range(PANELS):
        if j == k:
            pieces.append(inverse)
        else:
            pieces.append(dot_high(inverse, in_ref[lo:hi, j * PB : (j + 1) * PB], ((1,), (0,))))
    row = jnp.concatenate(pieces, axis=1)
    if k > 0:
        out_ref[:lo, :] = in_ref[:lo, :]
    out_ref[lo:hi, :] = row
    if k < PANELS - 1:
        column = dot_high(in_ref[hi:, lo:hi], inverse, ((1,), (1,)))
        change = dot_high(column, row, ((1,), (0,)))
        out_ref[hi:, :] = in_ref[hi:, :] - change
        out_ref[hi:, lo:hi] = -change[:, lo:hi]


def eliminate(matrix, k):
    return pl.pallas_call(
        functools.partial(eliminate_kernel, k),
        out_shape=jax.ShapeDtypeStruct(matrix.shape, F32),
        in_specs=[pl.BlockSpec(memory_space=VMEM)],
        out_specs=pl.BlockSpec(memory_space=VMEM),
        compiler_params=params(),
        name="eliminate_panel",
    )(matrix)


def project_kernel(has_upper, places_ref, inverse_ref, basis_ref, sums_ref, front_ref, *rest):
    del places_ref
    rest = rest[1:] if has_upper else rest
    upper_ref, out_ref, inverse3, basis3 = rest

    @pl.when(pl.program_id(0) == 0)
    def _():
        for source, held in ((inverse_ref, inverse3), (basis_ref, basis3)):
            hi, lo = parts2(source[...])
            held[...] = jnp.concatenate([hi, hi, lo], axis=1)

    hi, lo = parts2(sums_ref[...])
    upper = jnp.dot(
        inverse3[...], jnp.concatenate([hi, lo, hi], axis=0), preferred_element_type=F32
    )
    upper_ref[...] = upper
    hi, lo = parts2(upper)
    out_ref[...] = front_ref[...] - jnp.dot(
        basis3[...], jnp.concatenate([hi, lo, hi], axis=0), preferred_element_type=F32
    )


def project(places, inverse, basis, sums, front, upper):
    rows, columns = front.shape
    piece = sums.shape[1]
    count = sums.shape[0] // LEAD
    has_upper = upper is not None
    in_specs = [
        pl.BlockSpec((LEAD, LEAD), lambda i, p: (0, 0)),
        pl.BlockSpec((rows, LEAD), lambda i, p: (0, 0)),
        pl.BlockSpec((LEAD, piece), lambda i, p: (i, 0)),
        pl.BlockSpec((rows, piece), lambda i, p: (0, p[i])),
    ]
    operands = [places, inverse, basis, sums, front]
    aliases = {4: 1}
    if has_upper:
        in_specs.append(pl.BlockSpec(memory_space=pl.ANY))
        operands.append(upper)
        aliases[5] = 0
    return pl.pallas_call(
        functools.partial(project_kernel, has_upper),
        grid_spec=pltpu.PrefetchScalarGridSpec(
            num_scalar_prefetch=1,
            grid=(count,),
            in_specs=in_specs,
            out_specs=(
                pl.BlockSpec((LEAD, piece), lambda i, p: (0, p[i])),
                pl.BlockSpec((rows, piece), lambda i, p: (0, p[i])),
            ),
            scratch_shapes=[
                pltpu.VMEM((LEAD, 3 * LEAD), BF16),
                pltpu.VMEM((rows, 3 * LEAD), BF16),
            ],
        ),
        out_shape=(
            jax.ShapeDtypeStruct((LEAD, columns), F32),
            jax.ShapeDtypeStruct((rows, columns), F32),
        ),
        input_output_aliases=aliases,
        compiler_params=params(),
        name="project_columns",
    )(*operands)


def exchange(value, row_count):
    slots, width = value.shape
    shaped = value.reshape(row_count, slots // row_count, width)
    return lax.all_to_all(shaped, "row", split_axis=0, concat_axis=0, tiled=True).reshape(
        slots, width
    )


def on_device(front_matrix, child_rows, child_owner, child_offset):
    row_count = lax.axis_size("row")
    col_count = lax.axis_size("col")
    local_rows, local_cols = front_matrix.shape
    child_count = child_rows.shape[0]
    capacity = 2 * child_count // row_count
    me = lax.axis_index("row")

    packed, tags = pack(
        child_rows, child_owner[:, 0], child_offset[:, 0], row_count, capacity, local_rows
    )
    lead_child = exchange(jnp.concatenate([packed[:, :LEAD], tags], axis=1), row_count)
    tags = lead_child[:, LEAD:]
    all_child = exchange(packed, row_count)
    own_lead = assemble(front_matrix, lead_child, tags, LEAD, LEAD)
    panels = [spread(own_lead[:, k * PB : (k + 1) * PB], col_count) for k in range(PANELS)]
    lead = jnp.concatenate(panels, axis=1)

    gram = total_rows(dot_high(lead, lead, ((0,), (0,))), row_count)
    for k in range(PANELS):
        gram = eliminate(gram, k)
    block_row = np.arange(LEAD) // PB
    inverse = jnp.where(block_row[:, None] >= block_row[None, :], gram, 0.0)
    basis = dot_high(lead, inverse, ((1,), (1,)))

    front = assemble(front_matrix, all_child, tags, local_cols, 512)
    side = upper_side(0, row_count)
    shards = []
    for g in range(LEAD // GROUP):
        group = jnp.concatenate(panels[g * GROUP // PB : (g + 1) * GROUP // PB], axis=1)
        send = lead_product((1 - side)[None], group, front, 512)
        keep = lead_product(side[None], group, front, 512)
        shards.append(scatter_sum(keep, send, 1, row_count))
    shard = jnp.concatenate(shards, axis=0)

    width = shard.shape[1]
    piece = min(256, width)
    chunks = width // piece
    places = jnp.asarray(piece_table(row_count))[me] * chunks
    steps = row_count.bit_length() - 1
    held = []
    for c in range(chunks):
        buf = shard[:, c * piece : (c + 1) * piece]
        for step in reversed(range(steps)):
            got = swap(buf, step, row_count)
            if step == 0:
                held.append((buf, got))
            else:
                buf = jnp.concatenate([buf, got], axis=0)
    upper = None
    for c in range(chunks):
        near = places + c
        for sums, at in zip(held[c], (near[: row_count // 2], near[row_count // 2 :])):
            upper, front = project(at, inverse, basis, sums, front, upper)
    return upper, front, basis * math.sqrt(local_rows * row_count)


def solution(mesh):
    placed = (P("row", "col"), P("row", "col"), P("row", None), P("row", None))
    return jax.shard_map(
        on_device,
        mesh=mesh,
        in_specs=placed,
        out_specs=(P(None, "col"), P("row", "col"), P("row", None)),
        check_vma=False,
    )
```

time: 825 us -> 286 us (0.35)
  waiting for transfers between devices: 563 us -> 82.6 us
  Pallas kernels: 0 us -> 113 us
  other arithmetic: 114 us -> 25 us
  matrix products: 86.5 us -> 4.25 us
  starting transfers between devices: 11.5 us -> 39.9 us
  local copies, waits for them, and re-layouts: 26.8 us -> 3.63 us
  between operations: 14.8 us -> 1.13 us
  blocking collectives: 0 us -> 10.2 us
    psum x12 -> x0, waiting for transfers between devices: 541 us -> none  [the longest x3 176 us: factor_panel(): gram_total = lax.psum(gram_part, 'row')]
    pallas_call x0 -> x15, Pallas kernels: none -> 113 us  [the longest x4 46.9 us: eliminate(): pl.pallas_call(functools.partial(eliminate_kernel, k), out_shape=jax.Shap...]
    another operation x21 -> x0, other arithmetic: 91.5 us -> none  [the longest x12 49.6 us: factor_panel(): lower_factor = jnp.linalg.cholesky(gram_total)]
    ppermute x0 -> x26, waiting for transfers between devices: none -> 82.6 us  [the longest x18 62.1 us: swap(): return lax.ppermute(value, 'row', pairs)]
    dot_general x20 -> x2, matrix products: 81.3 us -> 4.25 us  [dot_high(): lax.dot_general(a, b, (dims, ((), ())), precision=HIGHEST, preferred_elem...]
    ppermute x0 -> x26, starting transfers between devices: none -> 34.6 us  [the longest x18 23.6 us: swap(): return lax.ppermute(value, 'row', pairs)]
    all_to_all x2 -> x1, waiting for transfers between devices: 21.6 us -> 0.01 us  [exchange(): lax.all_to_all(shaped, 'row', split_axis=0, concat_axis=0, tiled=True)]
    unnamed x36 -> x40, local copies, waits for them, and re-layouts: 17.5 us -> 2.61 us
  transfers between devices with their start and end apart: 14 -> 27, of which waited for: 13 -> 14; matrix products, arithmetic and copies ran while one was open for 7% -> 10% of each run, Pallas kernels for 0% -> 37%
where the time goes in v1:
time: 286 us; the launch traced here: 280 us
  Pallas kernels  113 us (40%)
  waiting for transfers between devices  82.6 us (29%)
  starting transfers between devices  39.9 us (14%)
  other arithmetic  25 us (9%)
  blocking collectives  10.2 us (4%)
  matrix products  4.25 us (1%)
  local copies, waits for them, and re-layouts  3.63 us (1%)
    ppermute x18, waiting for transfers between devices, swap(): return lax.ppermute(value, 'row', pairs)  62.1 us
    pallas_call x4, Pallas kernels, eliminate(): pl.pallas_call(functools.partial(eliminate_kernel, k), out_shape=jax.Shap...  46.9 us
    pallas_call x4, Pallas kernels, project(): pl.pallas_call(functools.partial(project_kernel, has_upper), grid_spec=pl...  35.7 us
    ppermute x18, starting transfers between devices, swap(): return lax.ppermute(value, 'row', pairs)  23.6 us
    ppermute x8, waiting for transfers between devices, spread(): got = lax.ppermute(value, 'col', pairs)  20.5 us
    pallas_call x4, Pallas kernels, lead_product(): pl.pallas_call(lead_product_kernel, grid_spec=pltpu.PrefetchScalarGridSpe...  18.6 us
    ppermute x8, starting transfers between devices, spread(): got = lax.ppermute(value, 'col', pairs)  11 us
    add x6, other arithmetic, take(): return mine + lax.dynamic_slice_in_dim(other, which * size, size, axis)  10.8 us
  transfers between devices with their start and end apart: 27, of which 14 were waited for; matrix products, arithmetic and copies ran while one was open for 10% of the time, Pallas kernels for 37%

profile of v1, /device:TPU:21, one launch (start us, length us, event | category | flops | bytes accessed | tf_op | source)
XLA Modules:
  0.0 280.3 jit_solution(11853199431939752225)
XLA Ops:
  4.7 10.2 %all_to_all.10 = f32[8,16,640]{2,1,0:T(8,128)S(1)} all-to-all(f32[8,16,640]{2,1,0:T(8,128)S(1)} %bitcast.22), channel_id=1, replica_groups=mesh['row'=8,'col'=4] {'row'}, dimensions={0} | all-to-all | bytes 655360 | tf_op jit(solution)/shard_map/all_to_all | solution.py:361
  14.9 5.3 %all-to-all-start.1 = ((f32[8,16,4096]{2,1,0:T(8,128)}), f32[8,16,4096]{2,1,0:T(8,128)S(1)}, u32[]{:S(2)}, u32[]{:S(2)}) async-start(f32[8,16,4096]{2,1,0:T(8,128)} %bitcast.17), calls=%async_computation.1 | async-start | bytes 4194304 | tf_op jit(solution)/shard_map/all_to_all | solution.py:361
  23.2 7.7 %collective-permute-done = f32[384,128]{1,0:T(8,128)} collective-permute-done((f32[384,128]{1,0:T(8,128)S(1)}, f32[384,128]{1,0:T(8,128)}, u32[]{:S(2)}, u32[]{:S(2)}) %collective-permute-start) | collective-permute-done | bytes 196640 | tf_op jit(solution)/shard_map/ppermute | solution.py:114
  40.9 4.3 %collective-permute-done.4 = f32[384,128]{1,0:T(8,128)} collective-permute-done((f32[384,128]{1,0:T(8,128)}, f32[384,128]{1,0:T(8,128)}, u32[]{:S(2)}, u32[]{:S(2)}) %collective-permute-start.4) | collective-permute-done | bytes 196640 | tf_op jit(solution)/shard_map/ppermute | solution.py:114
  45.2 4.2 %collective-permute-done.6 = f32[384,128]{1,0:T(8,128)} collective-permute-done((f32[384,128]{1,0:T(8,128)S(1)}, f32[384,128]{1,0:T(8,128)}, u32[]{:S(2)}, u32[]{:S(2)}) %collective-permute-start.6) | collective-permute-done | bytes 196640 | tf_op jit(solution)/shard_map/ppermute | solution.py:114
  56.5 9.1 %assemble_front.3.front_ref = f32[384,4096]{1,0:T(8,128)} custom-call(f32[384,4096]{1,0:T(8,128)} %front_ref.3, f32[128,4096]{1,0:T(8,128)S(1)} %bitcast.16, f32[128,128]{1,0:T(8,128)S(1)} %slice.64.tag_ref), custom_call_target="tpu_custom_call" | custom-call | tf_op jit(solution)/shard_map/assemble_front/pallas_call | solution.py:185
  65.7 5.2 %lead_product.5 = f32[256,2048]{1,0:T(8,128)} custom-call(s32[1]{0:T(128)} %bitcast.8.half_ref, f32[384,256]{1,0:T(8,128)S(1)} %pad_maximum_fusion.8.lead_ref, f32[384,4096]{1,0:T(8,128)} %assemble_front.3.front_ref), custom_call_target="tpu_custom_call" | custom-call | tf_op jit(solution)/shard_map/lead_product/pallas_call | solution.py:213
  70.8 6.7 %collective-permute-start.14 = (f32[256,2048]{1,0:T(8,128)}, f32[256,2048]{1,0:T(8,128)}, u32[]{:S(2)}, u32[]{:S(2)}) collective-permute-start(f32[256,2048]{1,0:T(8,128)} %lead_product.5), channel_id=1, source_target_pairs={{0,4},{4,0},{8,12},{12,8},{16,20},{20,16},{24,28},{28,24},{1,5},{5... | collective-permute-start | bytes 6291464 | tf_op jit(solution)/shard_map/ppermute | solution.py:37
  77.6 5.0 %lead_product.7 = f32[256,2048]{1,0:T(8,128)} custom-call(s32[1]{0:T(128)} %bitcast.8.half_ref, f32[384,256]{1,0:T(8,128)S(1)} %pad_maximum_fusion.9.lead_ref, f32[384,4096]{1,0:T(8,128)} %assemble_front.3.front_ref), custom_call_target="tpu_custom_call" | custom-call | tf_op jit(solution)/shard_map/lead_product/pallas_call | solution.py:213
  90.6 4.3 %lead_product.6 = f32[256,2048]{1,0:T(8,128)S(1)} custom-call(s32[1]{0:T(128)} %bitcast.5.half_ref, f32[384,256]{1,0:T(8,128)S(1)} %pad_maximum_fusion.9.lead_ref, f32[384,4096]{1,0:T(8,128)} %assemble_front.3.front_ref), custom_call_target="tpu_custom_call" | custom-call | tf_op jit(solution)/shard_map/lead_product/pallas_call | solution.py:213
  98.6 5.4 %collective-permute-done.15 = f32[256,1024]{1,0:T(8,128)S(1)} collective-permute-done((f32[256,1024]{1,0:T(8,128)}, f32[256,1024]{1,0:T(8,128)S(1)}, u32[]{:S(2)}, u32[]{:S(2)}) %collective-permute-start.15) | collective-permute-done | bytes 1048608 | tf_op jit(solution)/shard_map/ppermute | solution.py:37
  106.2 14.6 %collective-permute-done.18 = f32[256,1024]{1,0:T(8,128)} collective-permute-done((f32[256,1024]{1,0:T(8,128)}, f32[256,1024]{1,0:T(8,128)}, u32[]{:S(2)}, u32[]{:S(2)}) %collective-permute-start.18) | collective-permute-done | bytes 1048608 | tf_op jit(solution)/shard_map/ppermute | solution.py:37
  125.2 6.1 %collective-permute-done.19 = f32[256,512]{1,0:T(8,128)} collective-permute-done((f32[256,512]{1,0:T(8,128)}, f32[256,512]{1,0:T(8,128)}, u32[]{:S(2)}, u32[]{:S(2)}) %collective-permute-start.19) | collective-permute-done | bytes 524320 | tf_op jit(solution)/shard_map/ppermute | solution.py:37
  136.1 5.1 %collective-permute-done.23 = f32[512,256]{1,0:T(8,128)} collective-permute-done((f32[512,256]{1,0:T(8,128)S(1)}, f32[512,256]{1,0:T(8,128)}, u32[]{:S(2)}, u32[]{:S(2)}) %collective-permute-start.23) | collective-permute-done | bytes 524320 | tf_op jit(solution)/shard_map/ppermute | solution.py:37
  153.3 21.6 %collective-permute-done.9 = f32[128,512]{1,0:T(8,128)S(1)} collective-permute-done((f32[128,512]{1,0:T(8,128)}, f32[128,512]{1,0:T(8,128)S(1)}, u32[]{:S(2)}, u32[]{:S(2)}) %collective-permute-start.9) | collective-permute-done | bytes 262176 | tf_op jit(solution)/shard_map/ppermute | solution.py:37
  186.3 4.8 %collective-permute-done.12 = f32[128,512]{1,0:T(8,128)S(1)} collective-permute-done((f32[128,512]{1,0:T(8,128)S(1)}, f32[128,512]{1,0:T(8,128)S(1)}, u32[]{:S(2)}, u32[]{:S(2)}) %collective-permute-start.12) | collective-permute-done | bytes 262176 | tf_op jit(solution)/shard_map/ppermute | solution.py:37
  195.0 12.2 %eliminate_panel.4.in_ref = f32[512,512]{1,0:T(8,128)S(1)} custom-call(f32[512,512]{1,0:T(8,128)S(1)} %maximum_select_fusion.in_ref), custom_call_target="tpu_custom_call" | custom-call | tf_op jit(solution)/shard_map/eliminate_panel/pallas_call | solution.py:284
  207.2 12.0 %eliminate_panel.5.in_ref = f32[512,512]{1,0:T(8,128)S(1)} custom-call(f32[512,512]{1,0:T(8,128)S(1)} %eliminate_panel.4.in_ref), custom_call_target="tpu_custom_call" | custom-call | tf_op jit(solution)/shard_map/eliminate_panel/pallas_call | solution.py:284
  219.3 11.6 %eliminate_panel.6.in_ref = f32[512,512]{1,0:T(8,128)S(1)} custom-call(f32[512,512]{1,0:T(8,128)S(1)} %eliminate_panel.5.in_ref), custom_call_target="tpu_custom_call" | custom-call | tf_op jit(solution)/shard_map/eliminate_panel/pallas_call | solution.py:284
  230.9 11.1 %eliminate_panel.7 = f32[512,512]{1,0:T(8,128)S(1)} custom-call(f32[512,512]{1,0:T(8,128)S(1)} %eliminate_panel.6.in_ref), custom_call_target="tpu_custom_call" | custom-call | tf_op jit(solution)/shard_map/eliminate_panel/pallas_call | solution.py:284
  244.6 8.7 %project_columns.4 = (f32[512,4096]{1,0:T(8,128)}, f32[384,4096]{1,0:T(8,128)}) custom-call(s32[4]{0:T(128)S(1)} %get-tuple-element.40.places_ref, f32[512,512]{1,0:T(8,128)S(1)} %broadcast_select_fusion.inverse_ref, f32[384,512]{1,0:T(8,128)S(1)} %get-tuple-element.45.basis_ref, ...), custom_call_target="tpu_custom_call", output_to_operand_aliasing={{1}: (4, {})} | custom-call | tf_op jit(solution)/shard_map/project_columns/pallas_call | solution.py:333
  253.3 9.2 %project_columns.5 = (f32[512,4096]{1,0:T(8,128)}, f32[384,4096]{1,0:T(8,128)}) custom-call(s32[4]{0:T(128)S(1)} %get-tuple-element.41.places_ref, f32[512,512]{1,0:T(8,128)S(1)} %broadcast_select_fusion.inverse_ref, f32[384,512]{1,0:T(8,128)S(1)} %get-tuple-element.45.basis_ref, ...), custom_call_target="tpu_custom_call", output_to_operand_aliasing={{1}: (4, {}), {0}: (5, {})} | custom-call | tf_op jit(solution)/shard_map/project_columns/pallas_call | solution.py:333
  262.5 8.9 %project_columns.6 = (f32[512,4096]{1,0:T(8,128)}, f32[384,4096]{1,0:T(8,128)}) custom-call(s32[4]{0:T(128)S(1)} %get-tuple-element.42.places_ref, f32[512,512]{1,0:T(8,128)S(1)} %broadcast_select_fusion.inverse_ref, f32[384,512]{1,0:T(8,128)S(1)} %get-tuple-element.45.basis_ref, ...), custom_call_target="tpu_custom_call", output_to_operand_aliasing={{1}: (4, {}), {0}: (5, {})} | custom-call | tf_op jit(solution)/shard_map/project_columns/pallas_call | solution.py:333
  271.4 8.9 %project_columns.7 = (f32[512,4096]{1,0:T(8,128)}, f32[384,4096]{1,0:T(8,128)}) custom-call(s32[4]{0:T(128)S(1)} %get-tuple-element.43.places_ref, f32[512,512]{1,0:T(8,128)S(1)} %broadcast_select_fusion.inverse_ref, f32[384,512]{1,0:T(8,128)S(1)} %get-tuple-element.45.basis_ref, ...), custom_call_target="tpu_custom_call", output_to_operand_aliasing={{1}: (4, {}), {0}: (5, {})} | custom-call | tf_op jit(solution)/shard_map/project_columns/pallas_call | solution.py:333
  (122 shorter events, 76.9 us)
Async XLA Ops:
  14.9 41.6 %all-to-all-start.1 = ((f32[8,16,4096]{2,1,0:T(8,128)}), f32[8,16,4096]{2,1,0:T(8,128)S(1)}, u32[]{:S(2)}, u32[]{:S(2)}) async-start(f32[8,16,4096]{2,1,0:T(8,128)} %bitcast.17), calls=%async_computation.1 | async-start | bytes 4194304 | tf_op jit(solution)/shard_map/all_to_all | solution.py:361
  21.9 9.0 %collective-permute-start = (f32[384,128]{1,0:T(8,128)S(1)}, f32[384,128]{1,0:T(8,128)}, u32[]{:S(2)}, u32[]{:S(2)}) collective-permute-start(f32[384,128]{1,0:T(8,128)S(1)} %slice.65), channel_id=1, source_target_pairs={{0,2},{4,6},{8,10},{12,14},{16,18},{20,22},{24,26},{28,30}} | collective-permute-start | bytes 589832 | tf_op jit(solution)/shard_map/ppermute | solution.py:114
  32.7 8.2 %collective-permute-start.2 = (f32[384,128]{1,0:T(8,128)}, f32[384,128]{1,0:T(8,128)S(1)}, u32[]{:S(2)}, u32[]{:S(2)}) collective-permute-start(f32[384,128]{1,0:T(8,128)} %get-tuple-element.34), channel_id=1, source_target_pairs={{0,2},{4,6},{8,10},{12,14},{16,18},{20,22},{24,26},{28,30}} | collective-permute-start | bytes 589832 | tf_op jit(solution)/shard_map/ppermute | solution.py:114
  34.0 11.2 %collective-permute-start.4 = (f32[384,128]{1,0:T(8,128)}, f32[384,128]{1,0:T(8,128)}, u32[]{:S(2)}, u32[]{:S(2)}) collective-permute-start(f32[384,128]{1,0:T(8,128)} %get-tuple-element.33), channel_id=1, source_target_pairs={{0,2},{4,6},{8,10},{12,14},{16,18},{20,22},{24,26},{28,30}} | collective-permute-start | bytes 589832 | tf_op jit(solution)/shard_map/ppermute | solution.py:114
  35.3 14.1 %collective-permute-start.6 = (f32[384,128]{1,0:T(8,128)S(1)}, f32[384,128]{1,0:T(8,128)}, u32[]{:S(2)}, u32[]{:S(2)}) collective-permute-start(f32[384,128]{1,0:T(8,128)S(1)} %get-tuple-element.32), channel_id=1, source_target_pairs={{0,2},{4,6},{8,10},{12,14},{16,18},{20,22},{24,26},{28,30}} | collective-permute-start | bytes 589832 | tf_op jit(solution)/shard_map/ppermute | solution.py:114
  36.6 18.5 %collective-permute-start.1 = (f32[384,128]{1,0:T(8,128)S(1)}, f32[384,128]{1,0:T(8,128)S(1)}, u32[]{:S(2)}, u32[]{:S(2)}) collective-permute-start(f32[384,128]{1,0:T(8,128)S(1)} %get-tuple-element.31), channel_id=1, source_target_pairs={{0,1},{2,3},{4,5},{6,7},{8,9},{10,11},{12,13},{14,15},{16,17},{18,... | collective-permute-start | bytes 589832 | tf_op jit(solution)/shard_map/ppermute | solution.py:114
  51.8 4.7 %collective-permute-start.5 = (f32[384,128]{1,0:T(8,128)S(1)}, f32[384,128]{1,0:T(8,128)S(1)}, u32[]{:S(2)}, u32[]{:S(2)}) collective-permute-start(f32[384,128]{1,0:T(8,128)S(1)} %get-tuple-element.36), channel_id=1, source_target_pairs={{0,1},{2,3},{4,5},{6,7},{8,9},{10,11},{12,13},{14,15},{16,17},{18,... | collective-permute-start | bytes 589832 | tf_op jit(solution)/shard_map/ppermute | solution.py:114
  53.1 24.4 %collective-permute-start.7 = (f32[384,128]{1,0:T(8,128)S(1)}, f32[384,128]{1,0:T(8,128)}, u32[]{:S(2)}, u32[]{:S(2)}) collective-permute-start(f32[384,128]{1,0:T(8,128)S(1)} %get-tuple-element.37), channel_id=1, source_target_pairs={{0,1},{2,3},{4,5},{6,7},{8,9},{10,11},{12,13},{14,15},{16,17},{18,... | collective-permute-start | bytes 589832 | tf_op jit(solution)/shard_map/ppermute | solution.py:114
  70.8 16.0 %collective-permute-start.14 = (f32[256,2048]{1,0:T(8,128)}, f32[256,2048]{1,0:T(8,128)}, u32[]{:S(2)}, u32[]{:S(2)}) collective-permute-start(f32[256,2048]{1,0:T(8,128)} %lead_product.5), channel_id=1, source_target_pairs={{0,4},{4,0},{8,12},{12,8},{16,20},{20,16},{24,28},{28,24},{1,5},{5... | collective-permute-start | bytes 6291464 | tf_op jit(solution)/shard_map/ppermute | solution.py:37
  82.6 12.2 %collective-permute-start.17 = (f32[256,2048]{1,0:T(8,128)}, f32[256,2048]{1,0:T(8,128)}, u32[]{:S(2)}, u32[]{:S(2)}) collective-permute-start(f32[256,2048]{1,0:T(8,128)} %lead_product.7), channel_id=1, source_target_pairs={{0,4},{4,0},{8,12},{12,8},{16,20},{20,16},{24,28},{28,24},{1,5},{5... | collective-permute-start | bytes 6291464 | tf_op jit(solution)/shard_map/ppermute | solution.py:37
  89.8 14.2 %collective-permute-start.15 = (f32[256,1024]{1,0:T(8,128)}, f32[256,1024]{1,0:T(8,128)S(1)}, u32[]{:S(2)}, u32[]{:S(2)}) collective-permute-start(f32[256,1024]{1,0:T(8,128)} %get-tuple-element.26), channel_id=1, source_target_pairs={{0,8},{4,20},{8,0},{12,28},{16,24},{20,4},{24,16},{28,12},{1,9},{5... | collective-permute-start | bytes 3145736 | tf_op jit(solution)/shard_map/ppermute | solution.py:37
  97.9 22.9 %collective-permute-start.18 = (f32[256,1024]{1,0:T(8,128)}, f32[256,1024]{1,0:T(8,128)}, u32[]{:S(2)}, u32[]{:S(2)}) collective-permute-start(f32[256,1024]{1,0:T(8,128)} %get-tuple-element.24), channel_id=1, source_target_pairs={{0,8},{4,20},{8,0},{12,28},{16,24},{20,4},{24,16},{28,12},{1,9},{5... | collective-permute-start | bytes 3145736 | tf_op jit(solution)/shard_map/ppermute | solution.py:37
  105.0 18.9 %collective-permute-start.16 = (f32[256,512]{1,0:T(8,128)}, f32[256,512]{1,0:T(8,128)}, u32[]{:S(2)}, u32[]{:S(2)}) collective-permute-start(f32[256,512]{1,0:T(8,128)} %dynamic-slice_add_fusion.5), channel_id=1, source_target_pairs={{0,16},{4,12},{8,24},{12,4},{16,0},{20,28},{24,8},{28,20},{1,17},{... | collective-permute-start | bytes 1572872 | tf_op jit(solution)/shard_map/ppermute | solution.py:37
  122.7 8.6 %collective-permute-start.19 = (f32[256,512]{1,0:T(8,128)}, f32[256,512]{1,0:T(8,128)}, u32[]{:S(2)}, u32[]{:S(2)}) collective-permute-start(f32[256,512]{1,0:T(8,128)} %dynamic-slice_add_fusion.4), channel_id=1, source_target_pairs={{0,16},{4,12},{8,24},{12,4},{16,0},{20,28},{24,8},{28,20},{1,17},{... | collective-permute-start | bytes 1572872 | tf_op jit(solution)/shard_map/ppermute | solution.py:37
  132.7 8.5 %collective-permute-start.23 = (f32[512,256]{1,0:T(8,128)S(1)}, f32[512,256]{1,0:T(8,128)}, u32[]{:S(2)}, u32[]{:S(2)}) collective-permute-start(f32[512,256]{1,0:T(8,128)S(1)} %get-tuple-element.29), channel_id=1, source_target_pairs={{0,16},{4,12},{8,24},{12,4},{16,0},{20,28},{24,8},{28,20},{1,17},{... | collective-permute-start | bytes 1572872 | tf_op jit(solution)/shard_map/ppermute | solution.py:37
  134.0 14.9 %collective-permute-start.20 = (f32[512,256]{1,0:T(8,128)S(1)}, f32[512,256]{1,0:T(8,128)S(1)}, u32[]{:S(2)}, u32[]{:S(2)}) collective-permute-start(f32[512,256]{1,0:T(8,128)S(1)} %get-tuple-element.30), channel_id=1, source_target_pairs={{0,16},{4,12},{8,24},{12,4},{16,0},{20,28},{24,8},{28,20},{1,17},{... | collective-permute-start | bytes 1572872 | tf_op jit(solution)/shard_map/ppermute | solution.py:37
  143.3 32.8 %collective-permute-start.24 = (f32[1024,256]{1,0:T(8,128)}, f32[1024,256]{1,0:T(8,128)}, u32[]{:S(2)}, u32[]{:S(2)}) collective-permute-start(f32[1024,256]{1,0:T(8,128)} %pad_maximum_fusion.3), channel_id=1, source_target_pairs={{0,8},{4,20},{8,0},{12,28},{16,24},{20,4},{24,16},{28,12},{1,9},{5... | collective-permute-start | bytes 3145736 | tf_op jit(solution)/shard_map/ppermute | solution.py:37
  144.9 5.9 %collective-permute-start.8 = (f32[256,512]{1,0:T(8,128)}, f32[256,512]{1,0:T(8,128)}, u32[]{:S(2)}, u32[]{:S(2)}) collective-permute-start(f32[256,512]{1,0:T(8,128)} %constant_dynamic-slice_fusion), channel_id=1, source_target_pairs={{0,4},{4,0},{8,12},{12,8},{16,20},{20,16},{24,28},{28,24},{1,5},{5... | collective-permute-start | bytes 1572872 | tf_op jit(solution)/shard_map/ppermute | solution.py:37
  150.0 28.4 %collective-permute-start.21 = (f32[1024,256]{1,0:T(8,128)}, f32[1024,256]{1,0:T(8,128)}, u32[]{:S(2)}, u32[]{:S(2)}) collective-permute-start(f32[1024,256]{1,0:T(8,128)} %pad_maximum_fusion.2), channel_id=1, source_target_pairs={{0,8},{4,20},{8,0},{12,28},{16,24},{20,4},{24,16},{28,12},{1,9},{5... | collective-permute-start | bytes 3145736 | tf_op jit(solution)/shard_map/ppermute | solution.py:37
  152.6 22.3 %collective-permute-start.9 = (f32[128,512]{1,0:T(8,128)}, f32[128,512]{1,0:T(8,128)S(1)}, u32[]{:S(2)}, u32[]{:S(2)}) collective-permute-start(f32[128,512]{1,0:T(8,128)} %get-tuple-element.28), channel_id=1, source_target_pairs={{0,8},{4,20},{8,0},{12,28},{16,24},{20,4},{24,16},{28,12},{1,9},{5... | collective-permute-start | bytes 786440 | tf_op jit(solution)/shard_map/ppermute | solution.py:37
  174.9 6.3 %collective-permute-start.10 = (f32[64,512]{1,0:T(8,128)S(1)}, f32[64,512]{1,0:T(8,128)S(1)}, u32[]{:S(2)}, u32[]{:S(2)}) collective-permute-start(f32[64,512]{1,0:T(8,128)S(1)} %dynamic-slice_add_fusion.8), channel_id=1, source_target_pairs={{0,16},{4,12},{8,24},{12,4},{16,0},{20,28},{24,8},{28,20},{1,17},{... | collective-permute-start | bytes 393224 | tf_op jit(solution)/shard_map/ppermute | solution.py:37
  177.8 75.5 %collective-permute-start.25 = (f32[2048,256]{1,0:T(8,128)S(1)}, f32[2048,256]{1,0:T(8,128)}, u32[]{:S(2)}, u32[]{:S(2)}) collective-permute-start(f32[2048,256]{1,0:T(8,128)S(1)} %pad_maximum_fusion.1.sums_ref), channel_id=1, source_target_pairs={{0,4},{4,0},{8,12},{12,8},{16,20},{20,16},{24,28},{28,24},{1,5},{5... | collective-permute-start | bytes 6291464 | tf_op jit(solution)/shard_map/ppermute | solution.py:37
  181.2 90.2 %collective-permute-start.22 = (f32[2048,256]{1,0:T(8,128)}, f32[2048,256]{1,0:T(8,128)}, u32[]{:S(2)}, u32[]{:S(2)}) collective-permute-start(f32[2048,256]{1,0:T(8,128)} %pad_maximum_fusion.sums_ref), channel_id=1, source_target_pairs={{0,4},{4,0},{8,12},{12,8},{16,20},{20,16},{24,28},{28,24},{1,5},{5... | collective-permute-start | bytes 6291464 | tf_op jit(solution)/shard_map/ppermute | solution.py:37
  185.5 5.6 %collective-permute-start.12 = (f32[128,512]{1,0:T(8,128)S(1)}, f32[128,512]{1,0:T(8,128)S(1)}, u32[]{:S(2)}, u32[]{:S(2)}) collective-permute-start(f32[128,512]{1,0:T(8,128)S(1)} %maximum_select_fusion.2), channel_id=1, source_target_pairs={{0,8},{4,20},{8,0},{12,28},{16,24},{20,4},{24,16},{28,12},{1,9},{5... | collective-permute-start | bytes 786440 | tf_op jit(solution)/shard_map/ppermute | solution.py:37
  (23 other events, 228.7 us)

commit v2 on v1

v2 whole, which is shorter than its diff:
```python
import functools
import math

import jax
import jax.numpy as jnp
import numpy as np
from jax import lax
from jax.experimental import pallas as pl
from jax.experimental.pallas import tpu as pltpu
from jax.sharding import PartitionSpec as P

PB = 128
PANELS = 4
LEAD = PB * PANELS
HALF = LEAD // 2
BLOCK = 256
VMEM_BYTES = 24 * 1024 * 1024
HIGHEST = lax.Precision.HIGHEST
F32 = jnp.float32
BF16 = jnp.bfloat16
SMEM = pltpu.SMEM
VMEM = pltpu.VMEM


def params():
    return pltpu.CompilerParams(vmem_limit_bytes=VMEM_BYTES)


def cost(flops):
    return pl.CostEstimate(flops=flops, bytes_accessed=1 << 20, transcendentals=0)


def mask_orders(count):
    others = [1 << b for b in range(1, count.bit_length() - 1)]
    half = len(others) // 2
    return ([1] + others, [1] + others[half:] + others[:half])


def swap(value, step, count):
    orders = mask_orders(count)
    pairs = [(d, d ^ orders[d & 1][step]) for d in range(count)]
    return lax.ppermute(value, "row", pairs)


def upper_side(step, count):
    orders = mask_orders(count)
    me = lax.axis_index("row")
    mask = jnp.where(me & 1 == 0, orders[0][step], orders[1][step])
    return ((me & mask) != 0).astype(jnp.int32)


def shard_table(count):
    orders = mask_orders(count)
    steps = len(orders[0])
    return np.array(
        [
            sum(((d & orders[d & 1][t]) != 0) << (steps - 1 - t) for t in range(steps))
            for d in range(count)
        ]
    )


def piece_order(count):
    orders = mask_orders(count)
    steps = len(orders[0])
    shard = shard_table(count)

    def pieces(device, done):
        if done == 0:
            return [device]
        mask = orders[device & 1][steps - done]
        return pieces(device, done - 1) + pieces(device ^ mask, done - 1)

    half = count // 2
    order = np.zeros((count, 2, half), np.int32)
    for d in range(count):
        for at, piece in enumerate(pieces(d, steps)):
            order[d, at // half, shard[piece] % half] = at % half
    return order


def split_add_kernel(side_ref, keep_ref, got_ref, keep_out, send_out):
    half = keep_out.shape[1]
    for which, out in ((side_ref[0], keep_out), (1 - side_ref[0], send_out)):
        part = pl.ds(pl.multiple_of(which * half, 128), half)
        out[...] = keep_ref[:, part] + got_ref[:, part]


def split_add(side, keep, got):
    half = jax.ShapeDtypeStruct((keep.shape[0], keep.shape[1] // 2), F32)
    return pl.pallas_call(
        split_add_kernel,
        out_shape=(half, half),
        in_specs=[
            pl.BlockSpec(memory_space=SMEM),
            pl.BlockSpec(memory_space=VMEM),
            pl.BlockSpec(memory_space=VMEM),
        ],
        out_specs=(pl.BlockSpec(memory_space=VMEM), pl.BlockSpec(memory_space=VMEM)),
        compiler_params=params(),
        name="split_add",
    )(side[None], keep, got)


def scatter_sum(keep, send, count):
    steps = count.bit_length() - 1
    for step in range(steps):
        got = swap(send, step, count)
        if step == steps - 1:
            return keep + got
        keep, send = split_add(upper_side(step + 1, count), keep, got)


def total(value, count):
    side = upper_side(0, count)
    half = value.shape[0] // 2
    keep = lax.dynamic_slice_in_dim(value, side * half, half, 0)
    send = lax.dynamic_slice_in_dim(value, (1 - side) * half, half, 0)
    mine = keep + swap(send, 0, count)
    for step in range(1, count.bit_length() - 1):
        mine = mine + swap(mine, step, count)
    got = swap(mine, 0, count)
    return jnp.where(
        side == 0,
        jnp.concatenate([mine, got], axis=0),
        jnp.concatenate([got, mine], axis=0),
    )


def spread(value, count):
    me = lax.axis_index("col")
    stride = count
    while stride > 1:
        half = stride // 2
        pairs = [(c, c + half) for c in range(0, count, stride)]
        got = lax.ppermute(value, "col", pairs)
        value = jnp.where(me % stride == half, got, value)
        stride = half
    return value


def parts3(x):
    hi = x.astype(BF16)
    rest = x - hi.astype(F32)
    mid = rest.astype(BF16)
    return hi, mid, (rest - mid.astype(F32)).astype(BF16)


def parts2(x):
    hi = x.astype(BF16)
    return hi, (x - hi.astype(F32)).astype(BF16)


def pack_kernel(row_count, capacity, sentinel, owner_ref, offset_ref, child_ref, out_ref, tag_ref, tally):
    out_ref[...] = jnp.zeros_like(out_ref)
    tag_ref[...] = jnp.full(tag_ref.shape, sentinel, F32)
    for d in range(row_count):
        tally[d] = 0

    def body(i, carry):
        owner = owner_ref[i]
        rank = tally[owner]
        tally[owner] = rank + 1
        slot = owner * capacity + rank
        out_ref[pl.ds(slot, 1), :] = child_ref[pl.ds(i, 1), :]
        tag_ref[pl.ds(slot, 1), :] = jnp.full((1, tag_ref.shape[1]), offset_ref[i].astype(F32))
        return carry

    lax.fori_loop(0, child_ref.shape[0], body, 0)


def pack(child_rows, owner, offset, row_count, capacity, sentinel):
    slots = row_count * capacity
    return pl.pallas_call(
        functools.partial(pack_kernel, row_count, capacity, float(sentinel)),
        out_shape=(
            jax.ShapeDtypeStruct((slots, child_rows.shape[1]), F32),
            jax.ShapeDtypeStruct((slots, PB), F32),
        ),
        in_specs=[
            pl.BlockSpec(memory_space=SMEM),
            pl.BlockSpec(memory_space=SMEM),
            pl.BlockSpec(memory_space=VMEM),
        ],
        out_specs=(pl.BlockSpec(memory_space=VMEM), pl.BlockSpec(memory_space=VMEM)),
        scratch_shapes=[pltpu.SMEM((row_count,), jnp.int32)],
        compiler_params=params(),
        name="pack_children",
    )(owner, offset, child_rows)


def triple(x, axis):
    hi, lo = parts2(x)
    return jnp.concatenate([hi, hi, lo] if axis == 1 else [hi, lo, hi], axis=axis)


def lead_kernel(front_ref, child_ref, tag_ref, lead_ref, left_ref, place_ref, gram_ref):
    rows = front_ref.shape[0]
    slots = child_ref.shape[0]
    place = jnp.transpose(tag_ref[...])[0:1, :]
    at = lax.broadcasted_iota(jnp.int32, (rows, slots), 0).astype(F32)
    onehot = jnp.where(at == place, 1.0, 0.0).astype(BF16)
    spots = jnp.concatenate([onehot, onehot, onehot], axis=1)
    place_ref[...] = spots
    parts = jnp.concatenate(parts3(child_ref[...])[::-1], axis=0)
    lead = front_ref[...] + jnp.dot(spots, parts, preferred_element_type=F32)
    lead_ref[...] = lead
    turned = jnp.transpose(lead)
    left_ref[...] = triple(turned, 1)
    gram_ref[:, :HALF] = dot_high(turned[:HALF], lead[:, :HALF], ((1,), (0,)))
    gram_ref[:, HALF:] = dot_high(turned[HALF:], lead, ((1,), (0,)))


def lead_setup(front, child, tags):
    rows = front.shape[0]
    slots = child.shape[0]
    return pl.pallas_call(
        lead_kernel,
        out_shape=(
            jax.ShapeDtypeStruct((rows, LEAD), F32),
            jax.ShapeDtypeStruct((LEAD, 3 * rows), BF16),
            jax.ShapeDtypeStruct((rows, 3 * slots), BF16),
            jax.ShapeDtypeStruct((HALF, LEAD + HALF), F32),
        ),
        in_specs=[pl.BlockSpec(memory_space=VMEM)] * 3,
        out_specs=(pl.BlockSpec(memory_space=VMEM),) * 4,
        compiler_params=params(),
        name="lead_setup",
    )(front, child, tags)


def product_kernel(has_front, base_ref, left_ref, place_ref, front_ref, child_ref, *rest):
    del base_ref
    out_ref, whole_ref = rest[1:] if has_front else rest
    parts = jnp.concatenate(parts3(child_ref[...])[::-1], axis=0)
    whole = front_ref[...] + jnp.dot(place_ref[...], parts, preferred_element_type=F32)
    whole_ref[...] = whole
    out_ref[...] = jnp.dot(left_ref[...], triple(whole, 0), preferred_element_type=F32)


def product(base, left, place, front, child, whole, width):
    rows, columns = front.shape
    slots = child.shape[0]
    has_front = whole is not None
    in_specs = [
        pl.BlockSpec(left.shape, lambda i, b: (0, 0)),
        pl.BlockSpec(place.shape, lambda i, b: (0, 0)),
        pl.BlockSpec((rows, BLOCK), lambda i, b: (0, b[0] + i)),
        pl.BlockSpec((slots, BLOCK), lambda i, b: (0, b[0] + i)),
    ]
    operands = [base[None], left, place, front, child]
    aliases = {}
    if has_front:
        in_specs.append(pl.BlockSpec(memory_space=pl.ANY))
        operands.append(whole)
        aliases = {5: 1}
    return pl.pallas_call(
        functools.partial(product_kernel, has_front),
        grid_spec=pltpu.PrefetchScalarGridSpec(
            num_scalar_prefetch=1,
            grid=(width // BLOCK,),
            in_specs=in_specs,
            out_specs=(
                pl.BlockSpec((LEAD, BLOCK), lambda i, b: (0, i)),
                pl.BlockSpec((rows, BLOCK), lambda i, b: (0, b[0] + i)),
            ),
        ),
        out_shape=(
            jax.ShapeDtypeStruct((LEAD, width), F32),
            jax.ShapeDtypeStruct((rows, columns), F32),
        ),
        input_output_aliases=aliases,
        compiler_params=params(),
        name="lead_product",
    )(*operands)


def dot_high(a, b, dims):
    return lax.dot_general(a, b, (dims, ((), ())), precision=HIGHEST, preferred_element_type=F32)


def spread_lane(tile, at):
    return jnp.broadcast_to(tile[:, at : at + 1], tile.shape)


def invert_factor(block):
    lane = lax.broadcasted_iota(jnp.int32, (8, PB), 1)
    sub = lax.broadcasted_iota(jnp.int32, (8, PB), 0)
    count = PB // 8
    tiles = [block[8 * t : 8 * t + 8, :] for t in range(count)]
    for b in range(count):
        first = 8 * b
        rows = tiles[b]
        cols = [spread_lane(rows, first + c) for c in range(8)]
        heads, inverses = {}, []
        for c in range(8):
            inverse = 1.0 / cols[c][c : c + 1, :]
            inverses.append(inverse)
            factor = jnp.where(sub > c, cols[c] * inverse, 0.0)
            here = lane == first + c
            source = jnp.where(here[0:1, :], 1.0, rows[c : c + 1, :])
            rows = jnp.where(here & (sub > c), 0.0, rows) - factor * source
            for d in range(c + 1, 8):
                heads[c, d] = cols[d][c : c + 1, :]
                cols[d] = cols[d] - factor * heads[c, d]
        tiles[b] = rows
        inside = (lane >= first) & (lane < first + 8)
        past = inside & (lane - first >= sub)
        used = jnp.where(past, jnp.where(lane - first == sub, 1.0, 0.0), rows)
        for t in range(b + 1, count):
            tile = tiles[t]
            factors = []
            for c in range(8):
                factor = spread_lane(tile, first + c)
                for d in range(c):
                    factor = factor - factors[d] * heads[d, c]
                factors.append(factor * inverses[c])
            tile = jnp.where(inside, 0.0, tile)
            for c in range(8):
                tile = tile - factors[c] * used[c : c + 1, :]
            tiles[t] = tile
    done = []
    for t in range(count):
        diagonal = lane == sub + 8 * t
        pivot = jnp.sum(jnp.where(diagonal, tiles[t], 0.0), axis=1, keepdims=True)
        scale = lax.rsqrt(pivot)
        scale = scale * (1.5 - 0.5 * pivot * scale * scale)
        unit = jnp.where(diagonal, 1.0, jnp.where(lane < sub + 8 * t, tiles[t], 0.0))
        done.append(unit * scale)
    return jnp.concatenate(done, axis=0)


def eliminate_kernel(k, in_ref, out_ref):
    lo, hi = k * PB, (k + 1) * PB
    if k == 0:
        cross = in_ref[:, HALF:LEAD]
        out_ref[:HALF, :HALF] = in_ref[:, :HALF]
        out_ref[HALF:, :HALF] = cross
        out_ref[:HALF, HALF:] = jnp.transpose(cross)
        out_ref[HALF:, HALF:] = in_ref[:, LEAD:]
        in_ref = out_ref
    else:
        out_ref[:lo, :] = in_ref[:lo, :]
    inverse = invert_factor(in_ref[lo:hi, lo:hi])
    pieces = []
    for j in range(PANELS):
        if j == k:
            pieces.append(inverse)
        else:
            pieces.append(dot_high(inverse, in_ref[lo:hi, j * PB : (j + 1) * PB], ((1,), (0,))))
    row = jnp.concatenate(pieces, axis=1)
    out_ref[lo:hi, :] = row
    if k < PANELS - 1:
        column = dot_high(in_ref[hi:, lo:hi], inverse, ((1,), (1,)))
        change = dot_high(column, row, ((1,), (0,)))
        later = in_ref[hi:, :]
        out_ref[hi:, :] = later - change
        out_ref[hi:, lo:hi] = -change[:, lo:hi]


def eliminate(matrix, k):
    return pl.pallas_call(
        functools.partial(eliminate_kernel, k),
        out_shape=jax.ShapeDtypeStruct((LEAD, LEAD), F32),
        in_specs=[pl.BlockSpec(memory_space=VMEM)],
        out_specs=pl.BlockSpec(memory_space=VMEM),
        compiler_params=params(),
        cost_estimate=cost(6 * 10**9),
        name="eliminate_panel",
    )(matrix)


def finish_kernel(scale, matrix_ref, lead_ref, top_ref, bottom_ref, basis3_ref, basis_ref):
    own = lax.broadcasted_iota(jnp.int32, (LEAD, LEAD), 0) // PB
    other = lax.broadcasted_iota(jnp.int32, (LEAD, LEAD), 1) // PB
    inverse = jnp.where(own >= other, matrix_ref[...], 0.0)
    top_ref[...] = triple(inverse[:HALF, :HALF], 1)
    bottom_ref[...] = triple(inverse[HALF:], 1)
    basis = dot_high(lead_ref[...], inverse, ((1,), (1,)))
    basis3_ref[...] = triple(basis, 1)
    basis_ref[...] = basis * scale


def finish(matrix, lead, scale):
    rows = lead.shape[0]
    return pl.pallas_call(
        functools.partial(finish_kernel, scale),
        out_shape=(
            jax.ShapeDtypeStruct((HALF, 3 * HALF), BF16),
            jax.ShapeDtypeStruct((HALF, 3 * LEAD), BF16),
            jax.ShapeDtypeStruct((rows, 3 * LEAD), BF16),
            jax.ShapeDtypeStruct((rows, LEAD), F32),
        ),
        in_specs=[pl.BlockSpec(memory_space=VMEM)] * 2,
        out_specs=(pl.BlockSpec(memory_space=VMEM),) * 4,
        compiler_params=params(),
        cost_estimate=cost(2 * 10**9),
        name="finish_factor",
    )(matrix, lead)


def project_kernel(has_upper, places_ref, top_ref, bottom_ref, basis_ref, *rest):
    del places_ref
    even_ref, odd_ref, front_ref = rest[:3]
    upper_ref, out_ref = rest[4 if has_upper else 3 :]
    sums = jnp.concatenate([even_ref[...], odd_ref[...]], axis=1)
    hi, lo = parts2(sums)
    upper_ref[:HALF, :] = jnp.dot(
        top_ref[...],
        jnp.concatenate([hi[:HALF], lo[:HALF], hi[:HALF]], axis=0),
        preferred_element_type=F32,
    )
    upper_ref[HALF:, :] = jnp.dot(
        bottom_ref[...], jnp.concatenate([hi, lo, hi], axis=0), preferred_element_type=F32
    )
    out_ref[...] = front_ref[...] - jnp.dot(
        basis_ref[...], triple(upper_ref[...], 0), preferred_element_type=F32
    )


def project(places, factor, sums, front, upper):
    top, bottom, basis = factor
    rows, columns = front.shape
    count = sums.shape[0] // LEAD
    has_upper = upper is not None
    in_specs = [
        pl.BlockSpec(top.shape, lambda i, p: (0, 0)),
        pl.BlockSpec(bottom.shape, lambda i, p: (0, 0)),
        pl.BlockSpec(basis.shape, lambda i, p: (0, 0)),
        pl.BlockSpec((LEAD, PB), lambda i, p: (p[1 + 2 * i], 0)),
        pl.BlockSpec((LEAD, PB), lambda i, p: (p[2 + 2 * i], 0)),
        pl.BlockSpec((rows, BLOCK), lambda i, p: (0, p[0] + i)),
    ]
    operands = [places, top, bottom, basis, sums, sums, front]
    aliases = {6: 1}
    if has_upper:
        in_specs.append(pl.BlockSpec(memory_space=pl.ANY))
        operands.append(upper)
        aliases[7] = 0
    return pl.pallas_call(
        functools.partial(project_kernel, has_upper),
        grid_spec=pltpu.PrefetchScalarGridSpec(
            num_scalar_prefetch=1,
            grid=(count // 2,),
            in_specs=in_specs,
            out_specs=(
                pl.BlockSpec((LEAD, BLOCK), lambda i, p: (0, p[0] + i)),
                pl.BlockSpec((rows, BLOCK), lambda i, p: (0, p[0] + i)),
            ),
        ),
        out_shape=(
            jax.ShapeDtypeStruct((LEAD, columns), F32),
            jax.ShapeDtypeStruct((rows, columns), F32),
        ),
        input_output_aliases=aliases,
        compiler_params=params(),
        cost_estimate=cost(3 * 10**9),
        name="project_columns",
    )(*operands)


def exchange(value, row_count):
    slots, width = value.shape
    shaped = value.reshape(row_count, slots // row_count, width)
    return lax.all_to_all(shaped, "row", split_axis=0, concat_axis=0, tiled=True).reshape(
        slots, width
    )


def on_device(front_matrix, child_rows, child_owner, child_offset):
    row_count = lax.axis_size("row")
    col_count = lax.axis_size("col")
    local_rows, local_cols = front_matrix.shape
    child_count = child_rows.shape[0]
    capacity = 2 * child_count // row_count
    me = lax.axis_index("row")

    owner, offset = child_owner[:, 0], child_offset[:, 0]
    lead_child = spread(child_rows[:, :LEAD], col_count)
    cut = local_rows // 2
    lead_front = jnp.concatenate(
        [
            spread(front_matrix[:cut, :LEAD], col_count),
            spread(front_matrix[cut:, :LEAD], col_count),
        ],
        axis=0,
    )
    packed, tags = pack(child_rows, owner, offset, row_count, capacity, local_rows)
    child = exchange(packed, row_count)
    packed, tags = pack(lead_child, owner, offset, row_count, capacity, local_rows)
    lead_child = exchange(jnp.concatenate([packed, tags], axis=1), row_count)
    lead, left, place, gram = lead_setup(lead_front, lead_child[:, :LEAD], lead_child[:, LEAD:])

    matrix = total(gram, row_count)
    for k in range(PANELS):
        matrix = eliminate(matrix, k)
    scale = math.sqrt(local_rows * row_count)
    top, bottom, basis, scaled = finish(matrix, lead, scale)

    chunks = max(1, min(4, local_cols // (PB * row_count)))
    width = local_cols // 2 // chunks
    blocks = width // BLOCK
    core = upper_side(0, row_count)
    front = None
    shards = []
    for c in range(chunks):
        made = []
        for half in (1 - core, core):
            base = (half * chunks + c) * blocks
            sums, front = product(base, left, place, front_matrix, child, front, width)
            made.append(sums)
        shards.append(scatter_sum(made[1], made[0], row_count))
    steps = row_count.bit_length() - 1
    held = []
    for c in range(chunks):
        buf = shards[c]
        for step in reversed(range(steps)):
            got = swap(buf, step, row_count)
            if step == 0:
                held.append((buf, got))
            else:
                buf = jnp.concatenate([buf, got], axis=0)
    order = jnp.asarray(piece_order(row_count))[me]
    upper = None
    for c in range(chunks):
        for which, half in enumerate((core, 1 - core)):
            base = (half * chunks + c) * blocks
            places = jnp.concatenate([base[None], order[which]])
            upper, front = project(places, (top, bottom, basis), held[c][which], front, upper)
    return upper, front, scaled


def solution(mesh):
    placed = (P("row", "col"), P("row", "col"), P("row", None), P("row", None))
    return jax.shard_map(
        on_device,
        mesh=mesh,
        in_specs=placed,
        out_specs=(P(None, "col"), P("row", "col"), P("row", None)),
        check_vma=False,
    )
```

time: 286 us -> 225 us (0.79); the launches traced: 280 us -> 222 us
  waiting for transfers between devices: 82.6 us -> 52.6 us
  Pallas kernels: 113 us -> 87.5 us
  starting transfers between devices: 39.9 us -> 56.1 us
  other arithmetic: 25 us -> 9.85 us
  local copies, waits for them, and re-layouts: 3.63 us -> 15.2 us
  blocking collectives: 10.2 us -> 0 us
  matrix products: 4.25 us -> 0 us
    ppermute x18 -> x28, waiting for transfers between devices: 62.1 us -> 27.1 us  [swap(): return lax.ppermute(value, 'row', pairs)]
    pallas_call x4, Pallas kernels: 46.9 us -> 20.1 us  [eliminate(): pl.pallas_call(functools.partial(eliminate_kernel, k), out_shape=jax.Shap...]
    ppermute x18 -> x28, starting transfers between devices: 23.6 us -> 34.2 us  [swap(): return lax.ppermute(value, 'row', pairs)]
    all_to_all x1 -> x0, blocking collectives: 10.2 us -> none  [exchange(): lax.all_to_all(shaped, 'row', split_axis=0, concat_axis=0, tiled=True)]
    unnamed x40 -> x28, local copies, waits for them, and re-layouts: 2.61 us -> 11.7 us
    all_to_all x1 -> x2, waiting for transfers between devices: 0.01 us -> 8.81 us  [exchange(): lax.all_to_all(shaped, 'row', split_axis=0, concat_axis=0, tiled=True)]
    concatenate x4 -> x8, other arithmetic: 7.48 us -> 0.42 us  [on_device(): buf = jnp.concatenate([buf, got], axis=0)]
    add x6 -> x3, other arithmetic: 10.8 us -> 4.97 us  [the longest x2 3.06 us: total(): mine = mine + swap(mine, step, count)]
  transfers between devices with their start and end apart: 27 -> 36, of which waited for: 14 -> 10; matrix products, arithmetic and copies ran while one was open for 10% -> 6% of each run, Pallas kernels for 37% -> 37%
where the time goes in v2:
time: 225 us; the launch traced here: 222 us
  Pallas kernels  87.5 us (39%)
  starting transfers between devices  56.1 us (25%)
  waiting for transfers between devices  52.6 us (23%)
  local copies, waits for them, and re-layouts  15.2 us (7%)
  other arithmetic  9.85 us (4%)
    pallas_call x8, Pallas kernels, project(): pl.pallas_call(functools.partial(project_kernel, has_upper), grid_spec=pl...  34.8 us
    ppermute x28, starting transfers between devices, swap(): return lax.ppermute(value, 'row', pairs)  34.2 us
    ppermute x28, waiting for transfers between devices, swap(): return lax.ppermute(value, 'row', pairs)  27.1 us
    pallas_call x8, Pallas kernels, product(): pl.pallas_call(functools.partial(product_kernel, has_front), grid_spec=pl...  22.8 us
    pallas_call x4, Pallas kernels, eliminate(): pl.pallas_call(functools.partial(eliminate_kernel, k), out_shape=jax.Shap...  20.1 us
    ppermute x6, waiting for transfers between devices, spread(): got = lax.ppermute(value, 'col', pairs)  16.7 us
    ppermute x6, starting transfers between devices, spread(): got = lax.ppermute(value, 'col', pairs)  12 us
    unnamed x28, local copies, waits for them, and re-layouts  11.7 us
  transfers between devices with their start and end apart: 36, of which 10 were waited for; matrix products, arithmetic and copies ran while one was open for 6% of the time, Pallas kernels for 37%

profile of v2, /device:TPU:21, one launch (start us, length us, event | category | flops | bytes accessed | tf_op | source)
XLA Modules:
  0.0 222.3 jit_solution(1839444490871424350)
XLA Ops:
  5.3 12.1 %collective-permute-done.4 = f32[64,512]{1,0:T(8,128)S(1)} collective-permute-done((f32[64,512]{1,0:T(8,128)S(1)}, f32[64,512]{1,0:T(8,128)S(1)}, u32[]{:S(2)}, u32[]{:S(2)}) %collective-permute-start.4) | collective-permute-done | bytes 131104 | tf_op jit(solution)/shard_map/ppermute | solution.py:136
  25.4 5.4 %all-to-all-start = ((f32[8,16,640]{2,1,0:T(8,128)}), f32[8,16,640]{2,1,0:T(8,128)S(1)}, u32[]{:S(2)}, u32[]{:S(2)}) async-start(f32[8,16,640]{2,1,0:T(8,128)} %bitcast.4), calls=%async_computation | async-start | bytes 655360 | tf_op jit(solution)/shard_map/all_to_all | solution.py:465
  30.8 4.8 %collective-permute-start.1 = (f32[192,512]{1,0:T(8,128)S(1)}, f32[192,512]{1,0:T(8,128)}, u32[]{:S(2)}, u32[]{:S(2)}) collective-permute-start(f32[192,512]{1,0:T(8,128)S(1)} %get-tuple-element.121), channel_id=1, source_target_pairs={{0,1},{2,3},{4,5},{6,7},{8,9},{10,11},{12,13},{14,15},{16,17},{18,... | collective-permute-start | bytes 1179656 | tf_op jit(solution)/shard_map/ppermute | solution.py:136
  42.2 4.5 %all-to-all-start.1 = ((f32[8,16,4096]{2,1,0:T(8,128)}), f32[8,16,4096]{2,1,0:T(8,128)S(1)}, u32[]{:S(2)}, u32[]{:S(2)}) async-start(f32[8,16,4096]{2,1,0:T(8,128)} %bitcast.28), calls=%async_computation.1 | async-start | bytes 4194304 | tf_op jit(solution)/shard_map/all_to_all | solution.py:465
  46.8 4.6 %collective-permute-done.3 = f32[192,512]{1,0:T(8,128)} collective-permute-done((f32[192,512]{1,0:T(8,128)S(1)}, f32[192,512]{1,0:T(8,128)}, u32[]{:S(2)}, u32[]{:S(2)}) %collective-permute-start.3) | collective-permute-done | bytes 393248 | tf_op jit(solution)/shard_map/ppermute | solution.py:136
  60.7 8.8 %all-to-all-done.1 = f32[8,16,4096]{2,1,0:T(8,128)S(1)} async-done(((f32[8,16,4096]{2,1,0:T(8,128)}), f32[8,16,4096]{2,1,0:T(8,128)S(1)}, u32[]{:S(2)}, u32[]{:S(2)}) %all-to-all-start.1) | async-done | bytes 2097184 | tf_op jit(solution)/shard_map/all_to_all | solution.py:465
  73.3 2.9 %lead_product.8 = (f32[512,512]{1,0:T(8,128)}, f32[384,4096]{1,0:T(8,128)}) custom-call(s32[1]{0:T(128)} %bitcast.16.base_ref, bf16[512,1152]{1,0:T(8,128)(2,1)S(1)} %get-tuple-element.69.left_ref, bf16[384,384]{1,0:T(8,128)(2,1)S(1)} %copy-done.3, f32[384,4096]{1,0:T(8,128)S(1)} %copy-done, f32[128,4096]{1,0:T(8,128)S(1)} %bitcast.20), custom_call_target="tpu_custom_call" | custom-call | tf_op jit(solution)/shard_map/lead_product/pallas_call | solution.py:257
  105.7 2.8 %lead_product.15 = (f32[512,512]{1,0:T(8,128)S(1)}, f32[384,4096]{1,0:T(8,128)}) custom-call(s32[1]{0:T(128)} %bitcast.8.base_ref, bf16[512,1152]{1,0:T(8,128)(2,1)S(1)} %get-tuple-element.69.left_ref, bf16[384,384]{1,0:T(8,128)(2,1)S(1)} %copy-done.4, f32[384,4096]{1,0:T(8,128)S(1)} %copy-done.1, ...), custom_call_target="tpu_custom_call", output_to_operand_aliasing={{1}: (5, {})} | custom-call | tf_op jit(solution)/shard_map/lead_product/pallas_call | solution.py:257
  111.4 5.5 %eliminate_panel.4.in_ref = f32[512,512]{1,0:T(8,128)S(1)} custom-call(f32[256,768]{1,0:T(8,128)S(1)} %maximum_select_fusion.in_ref), custom_call_target="tpu_custom_call" | custom-call | flops 6000000000 | bytes 1048576 | tf_op jit(solution)/shard_map/eliminate_panel/pallas_call | solution.py:362
  120.7 5.2 %eliminate_panel.5.in_ref = f32[512,512]{1,0:T(8,128)S(1)} custom-call(f32[512,512]{1,0:T(8,128)S(1)} %eliminate_panel.4.in_ref), custom_call_target="tpu_custom_call" | custom-call | flops 6000000000 | bytes 1048576 | tf_op jit(solution)/shard_map/eliminate_panel/pallas_call | solution.py:362
  128.3 6.4 %collective-permute-done.17.got_ref = f32[512,256]{1,0:T(8,128)S(1)} collective-permute-done((f32[512,256]{1,0:T(8,128)S(1)}, f32[512,256]{1,0:T(8,128)S(1)}, u32[]{:S(2)}, u32[]{:S(2)}) %collective-permute-start.17) | collective-permute-done | bytes 524320 | tf_op jit(solution)/shard_map/ppermute | solution.py:42
  136.1 6.6 %collective-permute-done.23.got_ref = f32[512,256]{1,0:T(8,128)S(1)} collective-permute-done((f32[512,256]{1,0:T(8,128)S(1)}, f32[512,256]{1,0:T(8,128)S(1)}, u32[]{:S(2)}, u32[]{:S(2)}) %collective-permute-start.23) | collective-permute-done | bytes 524320 | tf_op jit(solution)/shard_map/ppermute | solution.py:42
  144.6 5.1 %eliminate_panel.6.in_ref = f32[512,512]{1,0:T(8,128)S(1)} custom-call(f32[512,512]{1,0:T(8,128)S(1)} %eliminate_panel.5.in_ref), custom_call_target="tpu_custom_call" | custom-call | flops 6000000000 | bytes 1048576 | tf_op jit(solution)/shard_map/eliminate_panel/pallas_call | solution.py:362
  153.3 4.3 %eliminate_panel.7.matrix_ref = f32[512,512]{1,0:T(8,128)S(1)} custom-call(f32[512,512]{1,0:T(8,128)S(1)} %eliminate_panel.6.in_ref), custom_call_target="tpu_custom_call" | custom-call | flops 6000000000 | bytes 1048576 | tf_op jit(solution)/shard_map/eliminate_panel/pallas_call | solution.py:362
  165.6 10.9 %collective-permute-start.33 = (f32[2048,128]{1,0:T(8,128)S(1)}, f32[2048,128]{1,0:T(8,128)S(1)}, u32[]{:S(2)}, u32[]{:S(2)}) collective-permute-start(f32[2048,128]{1,0:T(8,128)S(1)} %pad_maximum_fusion.3.rest_0_.rest_1_), channel_id=1, source_target_pairs={{0,4},{4,0},{8,12},{12,8},{16,20},{20,16},{24,28},{28,24},{1,5},{5... | collective-permute-start | bytes 3145736 | tf_op jit(solution)/shard_map/ppermute | solution.py:42
  179.1 7.6 %collective-permute-done.26 = f32[1024,128]{1,0:T(8,128)S(1)} collective-permute-done((f32[1024,128]{1,0:T(8,128)S(1)}, f32[1024,128]{1,0:T(8,128)S(1)}, u32[]{:S(2)}, u32[]{:S(2)}) %collective-permute-start.26) | collective-permute-done | bytes 524320 | tf_op jit(solution)/shard_map/ppermute | solution.py:42
  187.5 4.3 %project_columns.8 = (f32[512,4096]{1,0:T(8,128)}, f32[384,4096]{1,0:T(8,128)}) custom-call(s32[5]{0:T(128)S(1)} %get-tuple-element.125.places_ref, bf16[256,768]{1,0:T(8,128)(2,1)S(1)} %get-tuple-element.66.top_ref, bf16[256,1536]{1,0:T(8,128)(2,1)S(1)} %get-tuple-element.67.bottom_ref, ...), custom_call_target="tpu_custom_call", output_to_operand_aliasing={{1}: (6, {})} | custom-call | flops 3000000000 | bytes 1048576 | tf_op jit(solution)/shard_map/project_columns/pallas_call | solution.py:440
  191.9 4.3 %project_columns.9 = (f32[512,4096]{1,0:T(8,128)}, f32[384,4096]{1,0:T(8,128)}) custom-call(s32[5]{0:T(128)S(1)} %get-tuple-element.129.places_ref, bf16[256,768]{1,0:T(8,128)(2,1)S(1)} %get-tuple-element.66.top_ref, bf16[256,1536]{1,0:T(8,128)(2,1)S(1)} %get-tuple-element.67.bottom_ref, ...), custom_call_target="tpu_custom_call", output_to_operand_aliasing={{1}: (6, {}), {0}: (7, {})} | custom-call | flops 3000000000 | bytes 1048576 | tf_op jit(solution)/shard_map/project_columns/pallas_call | solution.py:440
  196.2 4.4 %project_columns.10 = (f32[512,4096]{1,0:T(8,128)}, f32[384,4096]{1,0:T(8,128)}) custom-call(s32[5]{0:T(128)S(1)} %get-tuple-element.127.places_ref, bf16[256,768]{1,0:T(8,128)(2,1)S(1)} %get-tuple-element.66.top_ref, bf16[256,1536]{1,0:T(8,128)(2,1)S(1)} %get-tuple-element.67.bottom_ref, ...), custom_call_target="tpu_custom_call", output_to_operand_aliasing={{1}: (6, {}), {0}: (7, {})} | custom-call | flops 3000000000 | bytes 1048576 | tf_op jit(solution)/shard_map/project_columns/pallas_call | solution.py:440
  200.6 4.4 %project_columns.11 = (f32[512,4096]{1,0:T(8,128)}, f32[384,4096]{1,0:T(8,128)}) custom-call(s32[5]{0:T(128)S(1)} %get-tuple-element.131.places_ref, bf16[256,768]{1,0:T(8,128)(2,1)S(1)} %get-tuple-element.66.top_ref, bf16[256,1536]{1,0:T(8,128)(2,1)S(1)} %get-tuple-element.67.bottom_ref, ...), custom_call_target="tpu_custom_call", output_to_operand_aliasing={{1}: (6, {}), {0}: (7, {})} | custom-call | flops 3000000000 | bytes 1048576 | tf_op jit(solution)/shard_map/project_columns/pallas_call | solution.py:440
  204.9 4.4 %project_columns.12 = (f32[512,4096]{1,0:T(8,128)}, f32[384,4096]{1,0:T(8,128)}) custom-call(s32[5]{0:T(128)S(1)} %get-tuple-element.126.places_ref, bf16[256,768]{1,0:T(8,128)(2,1)S(1)} %get-tuple-element.66.top_ref, bf16[256,1536]{1,0:T(8,128)(2,1)S(1)} %get-tuple-element.67.bottom_ref, ...), custom_call_target="tpu_custom_call", output_to_operand_aliasing={{1}: (6, {}), {0}: (7, {})} | custom-call | flops 3000000000 | bytes 1048576 | tf_op jit(solution)/shard_map/project_columns/pallas_call | solution.py:440
  209.3 4.4 %project_columns.13 = (f32[512,4096]{1,0:T(8,128)}, f32[384,4096]{1,0:T(8,128)}) custom-call(s32[5]{0:T(128)S(1)} %get-tuple-element.130.places_ref, bf16[256,768]{1,0:T(8,128)(2,1)S(1)} %get-tuple-element.66.top_ref, bf16[256,1536]{1,0:T(8,128)(2,1)S(1)} %get-tuple-element.67.bottom_ref, ...), custom_call_target="tpu_custom_call", output_to_operand_aliasing={{1}: (6, {}), {0}: (7, {})} | custom-call | flops 3000000000 | bytes 1048576 | tf_op jit(solution)/shard_map/project_columns/pallas_call | solution.py:440
  213.6 4.4 %project_columns.14 = (f32[512,4096]{1,0:T(8,128)}, f32[384,4096]{1,0:T(8,128)}) custom-call(s32[5]{0:T(128)S(1)} %get-tuple-element.128.places_ref, bf16[256,768]{1,0:T(8,128)(2,1)S(1)} %get-tuple-element.66.top_ref, bf16[256,1536]{1,0:T(8,128)(2,1)S(1)} %get-tuple-element.67.bottom_ref, ...), custom_call_target="tpu_custom_call", output_to_operand_aliasing={{1}: (6, {}), {0}: (7, {})} | custom-call | flops 3000000000 | bytes 1048576 | tf_op jit(solution)/shard_map/project_columns/pallas_call | solution.py:440
  218.0 4.4 %project_columns.15 = (f32[512,4096]{1,0:T(8,128)}, f32[384,4096]{1,0:T(8,128)}) custom-call(s32[5]{0:T(128)S(1)} %get-tuple-element.132.places_ref, bf16[256,768]{1,0:T(8,128)(2,1)S(1)} %get-tuple-element.66.top_ref, bf16[256,1536]{1,0:T(8,128)(2,1)S(1)} %get-tuple-element.67.bottom_ref, ...), custom_call_target="tpu_custom_call", output_to_operand_aliasing={{1}: (6, {}), {0}: (7, {})} | custom-call | flops 3000000000 | bytes 1048576 | tf_op jit(solution)/shard_map/project_columns/pallas_call | solution.py:440
  (141 shorter events, 89.0 us)
Async XLA Ops:
  1.8 17.8 %collective-permute-start = (f32[192,512]{1,0:T(8,128)S(1)}, f32[192,512]{1,0:T(8,128)S(1)}, u32[]{:S(2)}, u32[]{:S(2)}) collective-permute-start(f32[192,512]{1,0:T(8,128)S(1)} %slice.30), channel_id=1, source_target_pairs={{0,2},{4,6},{8,10},{12,14},{16,18},{20,22},{24,26},{28,30}} | collective-permute-start | bytes 1179656 | tf_op jit(solution)/shard_map/ppermute | solution.py:136
  20.8 14.8 %collective-permute-start.2 = (f32[192,512]{1,0:T(8,128)S(1)}, f32[192,512]{1,0:T(8,128)S(1)}, u32[]{:S(2)}, u32[]{:S(2)}) collective-permute-start(f32[192,512]{1,0:T(8,128)S(1)} %get-tuple-element.122), channel_id=1, source_target_pairs={{0,2},{4,6},{8,10},{12,14},{16,18},{20,22},{24,26},{28,30}} | collective-permute-start | bytes 1179656 | tf_op jit(solution)/shard_map/ppermute | solution.py:136
  25.4 16.7 %all-to-all-start = ((f32[8,16,640]{2,1,0:T(8,128)}), f32[8,16,640]{2,1,0:T(8,128)S(1)}, u32[]{:S(2)}, u32[]{:S(2)}) async-start(f32[8,16,640]{2,1,0:T(8,128)} %bitcast.4), calls=%async_computation | async-start | bytes 655360 | tf_op jit(solution)/shard_map/all_to_all | solution.py:465
  30.8 15.9 %collective-permute-start.1 = (f32[192,512]{1,0:T(8,128)S(1)}, f32[192,512]{1,0:T(8,128)}, u32[]{:S(2)}, u32[]{:S(2)}) collective-permute-start(f32[192,512]{1,0:T(8,128)S(1)} %get-tuple-element.121), channel_id=1, source_target_pairs={{0,1},{2,3},{4,5},{6,7},{8,9},{10,11},{12,13},{14,15},{16,17},{18,... | collective-permute-start | bytes 1179656 | tf_op jit(solution)/shard_map/ppermute | solution.py:136
  36.6 14.7 %collective-permute-start.3 = (f32[192,512]{1,0:T(8,128)S(1)}, f32[192,512]{1,0:T(8,128)}, u32[]{:S(2)}, u32[]{:S(2)}) collective-permute-start(f32[192,512]{1,0:T(8,128)S(1)} %broadcast_select_fusion), channel_id=1, source_target_pairs={{0,1},{2,3},{4,5},{6,7},{8,9},{10,11},{12,13},{14,15},{16,17},{18,... | collective-permute-start | bytes 1179656 | tf_op jit(solution)/shard_map/ppermute | solution.py:136
  42.2 27.4 %all-to-all-start.1 = ((f32[8,16,4096]{2,1,0:T(8,128)}), f32[8,16,4096]{2,1,0:T(8,128)S(1)}, u32[]{:S(2)}, u32[]{:S(2)}) async-start(f32[8,16,4096]{2,1,0:T(8,128)} %bitcast.28), calls=%async_computation.1 | async-start | bytes 4194304 | tf_op jit(solution)/shard_map/all_to_all | solution.py:465
  60.7 18.2 %collective-permute-start.7 = (f32[128,768]{1,0:T(8,128)}, f32[128,768]{1,0:T(8,128)}, u32[]{:S(2)}, u32[]{:S(2)}) collective-permute-start(f32[128,768]{1,0:T(8,128)} %dynamic-slice_add_fusion), channel_id=1, source_target_pairs={{0,8},{4,20},{8,0},{12,28},{16,24},{20,4},{24,16},{28,12},{1,9},{5... | collective-permute-start | bytes 1179656 | tf_op jit(solution)/shard_map/ppermute | solution.py:42
  76.1 33.6 %collective-permute-start.28 = (f32[512,512]{1,0:T(8,128)}, f32[512,512]{1,0:T(8,128)}, u32[]{:S(2)}, u32[]{:S(2)}) collective-permute-start(f32[512,512]{1,0:T(8,128)} %get-tuple-element.98), channel_id=1, source_target_pairs={{0,4},{4,0},{8,12},{12,8},{16,20},{20,16},{24,28},{28,24},{1,5},{5... | collective-permute-start | bytes 3145736 | tf_op jit(solution)/shard_map/ppermute | solution.py:42
  80.8 23.5 %collective-permute-start.8 = (f32[128,768]{1,0:T(8,128)}, f32[128,768]{1,0:T(8,128)}, u32[]{:S(2)}, u32[]{:S(2)}) collective-permute-start(f32[128,768]{1,0:T(8,128)} %add.69), channel_id=1, source_target_pairs={{0,16},{4,12},{8,24},{12,4},{16,0},{20,28},{24,8},{28,20},{1,17},{... | collective-permute-start | bytes 1179656 | tf_op jit(solution)/shard_map/ppermute | solution.py:42
  102.5 14.4 %collective-permute-start.10 = (f32[512,512]{1,0:T(8,128)S(1)}, f32[512,512]{1,0:T(8,128)S(1)}, u32[]{:S(2)}, u32[]{:S(2)}) collective-permute-start(f32[512,512]{1,0:T(8,128)S(1)} %get-tuple-element.80), channel_id=1, source_target_pairs={{0,4},{4,0},{8,12},{12,8},{16,20},{20,16},{24,28},{28,24},{1,5},{5... | collective-permute-start | bytes 3145736 | tf_op jit(solution)/shard_map/ppermute | solution.py:42
  103.8 14.6 %collective-permute-start.16 = (f32[512,512]{1,0:T(8,128)S(1)}, f32[512,512]{1,0:T(8,128)S(1)}, u32[]{:S(2)}, u32[]{:S(2)}) collective-permute-start(f32[512,512]{1,0:T(8,128)S(1)} %get-tuple-element.86), channel_id=1, source_target_pairs={{0,4},{4,0},{8,12},{12,8},{16,20},{20,16},{24,28},{28,24},{1,5},{5... | collective-permute-start | bytes 3145736 | tf_op jit(solution)/shard_map/ppermute | solution.py:42
  103.8 15.1 %collective-permute-start.22 = (f32[512,512]{1,0:T(8,128)S(1)}, f32[512,512]{1,0:T(8,128)S(1)}, u32[]{:S(2)}, u32[]{:S(2)}) collective-permute-start(f32[512,512]{1,0:T(8,128)S(1)} %get-tuple-element.92), channel_id=1, source_target_pairs={{0,4},{4,0},{8,12},{12,8},{16,20},{20,16},{24,28},{28,24},{1,5},{5... | collective-permute-start | bytes 3145736 | tf_op jit(solution)/shard_map/ppermute | solution.py:42
  118.5 16.1 %collective-permute-start.17 = (f32[512,256]{1,0:T(8,128)S(1)}, f32[512,256]{1,0:T(8,128)S(1)}, u32[]{:S(2)}, u32[]{:S(2)}) collective-permute-start(f32[512,256]{1,0:T(8,128)S(1)} %get-tuple-element.88), channel_id=1, source_target_pairs={{0,8},{4,20},{8,0},{12,28},{16,24},{20,4},{24,16},{28,12},{1,9},{5... | collective-permute-start | bytes 1572872 | tf_op jit(solution)/shard_map/ppermute | solution.py:42
  119.0 23.7 %collective-permute-start.23 = (f32[512,256]{1,0:T(8,128)S(1)}, f32[512,256]{1,0:T(8,128)S(1)}, u32[]{:S(2)}, u32[]{:S(2)}) collective-permute-start(f32[512,256]{1,0:T(8,128)S(1)} %get-tuple-element.94), channel_id=1, source_target_pairs={{0,8},{4,20},{8,0},{12,28},{16,24},{20,4},{24,16},{28,12},{1,9},{5... | collective-permute-start | bytes 1572872 | tf_op jit(solution)/shard_map/ppermute | solution.py:42
  120.3 24.2 %collective-permute-start.30 = (f32[512,128]{1,0:T(8,128)S(1)}, f32[512,128]{1,0:T(8,128)S(1)}, u32[]{:S(2)}, u32[]{:S(2)}) collective-permute-start(f32[512,128]{1,0:T(8,128)S(1)} %get-tuple-element.102), channel_id=1, source_target_pairs={{0,16},{4,12},{8,24},{12,4},{16,0},{20,28},{24,8},{28,20},{1,17},{... | collective-permute-start | bytes 786440 | tf_op jit(solution)/shard_map/ppermute | solution.py:42
  126.0 23.7 %collective-permute-start.12 = (f32[512,128]{1,0:T(8,128)S(1)}, f32[512,128]{1,0:T(8,128)S(1)}, u32[]{:S(2)}, u32[]{:S(2)}) collective-permute-start(f32[512,128]{1,0:T(8,128)S(1)} %get-tuple-element.84), channel_id=1, source_target_pairs={{0,16},{4,12},{8,24},{12,4},{16,0},{20,28},{24,8},{28,20},{1,17},{... | collective-permute-start | bytes 786440 | tf_op jit(solution)/shard_map/ppermute | solution.py:42
  134.7 16.6 %collective-permute-start.18 = (f32[512,128]{1,0:T(8,128)S(1)}, f32[512,128]{1,0:T(8,128)S(1)}, u32[]{:S(2)}, u32[]{:S(2)}) collective-permute-start(f32[512,128]{1,0:T(8,128)S(1)} %get-tuple-element.90), channel_id=1, source_target_pairs={{0,16},{4,12},{8,24},{12,4},{16,0},{20,28},{24,8},{28,20},{1,17},{... | collective-permute-start | bytes 786440 | tf_op jit(solution)/shard_map/ppermute | solution.py:42
  157.7 21.3 %collective-permute-start.14 = (f32[1024,128]{1,0:T(8,128)S(1)}, f32[1024,128]{1,0:T(8,128)S(1)}, u32[]{:S(2)}, u32[]{:S(2)}) collective-permute-start(f32[1024,128]{1,0:T(8,128)S(1)} %pad_maximum_fusion.5), channel_id=1, source_target_pairs={{0,8},{4,20},{8,0},{12,28},{16,24},{20,4},{24,16},{28,12},{1,9},{5... | collective-permute-start | bytes 1572872 | tf_op jit(solution)/shard_map/ppermute | solution.py:42
  159.0 27.9 %collective-permute-start.20 = (f32[1024,128]{1,0:T(8,128)S(1)}, f32[1024,128]{1,0:T(8,128)S(1)}, u32[]{:S(2)}, u32[]{:S(2)}) collective-permute-start(f32[1024,128]{1,0:T(8,128)S(1)} %pad_maximum_fusion.6), channel_id=1, source_target_pairs={{0,8},{4,20},{8,0},{12,28},{16,24},{20,4},{24,16},{28,12},{1,9},{5... | collective-permute-start | bytes 1572872 | tf_op jit(solution)/shard_map/ppermute | solution.py:42
  161.0 25.7 %collective-permute-start.26 = (f32[1024,128]{1,0:T(8,128)S(1)}, f32[1024,128]{1,0:T(8,128)S(1)}, u32[]{:S(2)}, u32[]{:S(2)}) collective-permute-start(f32[1024,128]{1,0:T(8,128)S(1)} %pad_maximum_fusion.7), channel_id=1, source_target_pairs={{0,8},{4,20},{8,0},{12,28},{16,24},{20,4},{24,16},{28,12},{1,9},{5... | collective-permute-start | bytes 1572872 | tf_op jit(solution)/shard_map/ppermute | solution.py:42
  165.6 26.2 %collective-permute-start.33 = (f32[2048,128]{1,0:T(8,128)S(1)}, f32[2048,128]{1,0:T(8,128)S(1)}, u32[]{:S(2)}, u32[]{:S(2)}) collective-permute-start(f32[2048,128]{1,0:T(8,128)S(1)} %pad_maximum_fusion.3.rest_0_.rest_1_), channel_id=1, source_target_pairs={{0,4},{4,0},{8,12},{12,8},{16,20},{20,16},{24,28},{28,24},{1,5},{5... | collective-permute-start | bytes 3145736 | tf_op jit(solution)/shard_map/ppermute | solution.py:42
  179.0 39.0 %collective-permute-start.15 = (f32[2048,128]{1,0:T(8,128)S(1)}, f32[2048,128]{1,0:T(8,128)S(1)}, u32[]{:S(2)}, u32[]{:S(2)}) collective-permute-start(f32[2048,128]{1,0:T(8,128)S(1)} %pad_maximum_fusion.rest_0_.rest_1_), channel_id=1, source_target_pairs={{0,4},{4,0},{8,12},{12,8},{16,20},{20,16},{24,28},{28,24},{1,5},{5... | collective-permute-start | bytes 3145736 | tf_op jit(solution)/shard_map/ppermute | solution.py:42
  186.8 13.8 %collective-permute-start.27 = (f32[2048,128]{1,0:T(8,128)S(1)}, f32[2048,128]{1,0:T(8,128)S(1)}, u32[]{:S(2)}, u32[]{:S(2)}) collective-permute-start(f32[2048,128]{1,0:T(8,128)S(1)} %pad_maximum_fusion.2.rest_0_.rest_1_), channel_id=1, source_target_pairs={{0,4},{4,0},{8,12},{12,8},{16,20},{20,16},{24,28},{28,24},{1,5},{5... | collective-permute-start | bytes 3145736 | tf_op jit(solution)/shard_map/ppermute | solution.py:42
  187.0 22.3 %collective-permute-start.21 = (f32[2048,128]{1,0:T(8,128)S(1)}, f32[2048,128]{1,0:T(8,128)S(1)}, u32[]{:S(2)}, u32[]{:S(2)}) collective-permute-start(f32[2048,128]{1,0:T(8,128)S(1)} %pad_maximum_fusion.1.rest_0_.rest_1_), channel_id=1, source_target_pairs={{0,4},{4,0},{8,12},{12,8},{16,20},{20,16},{24,28},{28,24},{1,5},{5... | collective-permute-start | bytes 3145736 | tf_op jit(solution)/shard_map/ppermute | solution.py:42
  (26 other events, 248.1 us)

commit v3 on v0

v3 whole, which is shorter than its diff:
```python
import functools
import math

import jax
import jax.numpy as jnp
import numpy as np
from jax import lax
from jax.experimental import pallas as pl
from jax.experimental.pallas import tpu as pltpu
from jax.sharding import PartitionSpec as P

PB = 128
PANELS = 4
LEAD = PB * PANELS
HALF = LEAD // 2
BLOCK = 256
VMEM_BYTES = 24 * 1024 * 1024
HIGHEST = lax.Precision.HIGHEST
F32 = jnp.float32
BF16 = jnp.bfloat16
WHOLE = pl.BlockSpec(memory_space=pltpu.VMEM)
SCALARS = pl.BlockSpec(memory_space=pltpu.SMEM)
ANYWHERE = pl.BlockSpec(memory_space=pl.ANY)


def f32(*shape):
    return jax.ShapeDtypeStruct(shape, F32)


def bf16(*shape):
    return jax.ShapeDtypeStruct(shape, BF16)


class Chain:
    def __init__(self):
        self.token = None

    def __call__(self, name, body, operands, in_specs, outs, out_specs, scalars=(), grid=None, aliases=None):
        taken = len(scalars) + len(operands)
        given = len(outs)
        has_token = self.token is not None
        operands, in_specs = list(operands), list(in_specs)
        if has_token:
            operands.append(self.token)
            in_specs.append(ANYWHERE)

        def kernel(*refs):
            ins, rest = refs[:taken], refs[taken + has_token :]
            rest[given][...] = jnp.zeros((8, PB), F32)
            body(*ins, *rest[:given])

        token_spec = WHOLE if grid is None else pl.BlockSpec((8, PB), lambda *at: (0, 0))
        settings = dict(
            out_shape=tuple(outs) + (f32(8, PB),),
            input_output_aliases=aliases or {},
            compiler_params=pltpu.CompilerParams(vmem_limit_bytes=VMEM_BYTES),
            cost_estimate=pl.CostEstimate(flops=1 << 20, bytes_accessed=1 << 16, transcendentals=0),
            name=name,
        )
        out_specs = tuple(out_specs) + (token_spec,)
        if grid is None:
            settings.update(in_specs=in_specs, out_specs=out_specs)
        else:
            settings.update(
                grid_spec=pltpu.PrefetchScalarGridSpec(
                    num_scalar_prefetch=len(scalars),
                    grid=grid,
                    in_specs=in_specs,
                    out_specs=out_specs,
                )
            )
        results = pl.pallas_call(kernel, **settings)(*scalars, *operands)
        self.token = results[-1]
        return results[:-1] if given > 1 else results[0]


def mask_orders(count):
    others = [1 << b for b in range(1, count.bit_length() - 1)]
    half = len(others) // 2
    return ([1] + others, [1] + others[half:] + others[:half])


def swap(value, step, count):
    orders = mask_orders(count)
    pairs = [(d, d ^ orders[d & 1][step]) for d in range(count)]
    return lax.ppermute(value, "row", pairs)


def upper_side(step, count):
    orders = mask_orders(count)
    me = lax.axis_index("row")
    mask = jnp.where(me % 2 == 0, orders[0][step], orders[1][step])
    return ((me & mask) != 0).astype(jnp.int32)


def shard_table(count):
    orders = mask_orders(count)
    steps = len(orders[0])
    return np.array(
        [
            sum(((d & orders[d & 1][t]) != 0) << (steps - 1 - t) for t in range(steps))
            for d in range(count)
        ]
    )


def piece_order(count):
    orders = mask_orders(count)
    steps = len(orders[0])
    shard = shard_table(count)

    def pieces(device, done):
        if done == 0:
            return [device]
        mask = orders[device & 1][steps - done]
        return pieces(device, done - 1) + pieces(device ^ mask, done - 1)

    half = count // 2
    order = np.zeros((count, 2, half), np.int32)
    for d in range(count):
        for at, piece in enumerate(pieces(d, steps)):
            order[d, at // half, shard[piece] % half] = at % half
    return order


def spread(value, count):
    middle = count // 2
    first = lax.ppermute(value, "col", [(0, middle)])
    others = [c for c in range(count - 1, 0, -1) if c != middle]
    return [first] + [lax.ppermute(first, "col", [(middle, c)]) for c in others]


def exchange(value, row_count):
    slots, width = value.shape
    shaped = value.reshape(row_count, slots // row_count, width)
    return lax.all_to_all(shaped, "row", split_axis=0, concat_axis=0, tiled=True).reshape(
        slots, width
    )


def parts3(x):
    hi = x.astype(BF16)
    rest = x - hi.astype(F32)
    mid = rest.astype(BF16)
    return hi, mid, (rest - mid.astype(F32)).astype(BF16)


def parts2(x):
    hi = x.astype(BF16)
    return hi, (x - hi.astype(F32)).astype(BF16)


def triple(x, axis):
    hi, lo = parts2(x)
    return jnp.concatenate([hi, hi, lo] if axis == 1 else [hi, lo, hi], axis=axis)


def dot_high(a, b, dims):
    return lax.dot_general(a, b, (dims, ((), ())), precision=HIGHEST, preferred_element_type=F32)


def dot(a, b):
    return jnp.dot(a, b, preferred_element_type=F32)


def pick(own, gots):
    arrived = gots[0][...]
    for got in gots[1:]:
        arrived = arrived + got[...]
    return jnp.where(lax.axis_index("col") == 0, own[...], arrived)


def cut_body(child_ref, front_ref, *outs):
    at = 0
    stacked = [(child_ref, child_ref.shape[0]), (front_ref, front_ref.shape[0])]
    starts = [0, child_ref.shape[0]]
    for out in outs:
        for (ref, length), start in zip(stacked, starts):
            lo, hi = max(at, start), min(at + out.shape[0], start + length)
            if lo < hi:
                out[lo - at : hi - at, :] = ref[lo - start : hi - start, :]
        at += out.shape[0]


def place_rows(row_count, capacity, owner_ref, read, write, width, child_count):
    def body(i, counts):
        owner = owner_ref[i]
        rank = jnp.int32(0)
        for d in range(row_count):
            rank = jnp.where(owner == d, counts[d], rank)
        write(owner * capacity + rank, read(i), i)
        return tuple(counts[d] + (owner == d).astype(jnp.int32) for d in range(row_count))

    lax.fori_loop(0, child_count, body, (jnp.int32(0),) * row_count)


def pack_body(row_count, capacity, owner_ref, child_ref, out_ref):
    out_ref[...] = jnp.zeros_like(out_ref)

    def write(slot, row, i):
        out_ref[pl.ds(slot, 1), :] = row

    place_rows(
        row_count, capacity, owner_ref, lambda i: child_ref[pl.ds(i, 1), :], write,
        out_ref.shape[1], child_ref.shape[0],
    )


def pack_lead_body(row_count, capacity, sentinel, child_count, owner_ref, offset_ref, *refs):
    own, gots = refs[0], refs[1:-4]
    out_ref, child_ref, rows_ref, tag_ref = refs[-4:]
    child_ref[...] = pick(own, gots)
    rows_ref[...] = jnp.zeros_like(rows_ref)
    tag_ref[...] = jnp.full(tag_ref.shape, sentinel, F32)

    def write(slot, row, i):
        rows_ref[pl.ds(slot, 1), :] = row
        tag_ref[pl.ds(slot, 1), :] = jnp.full((1, PB), offset_ref[i].astype(F32))

    place_rows(
        row_count, capacity, owner_ref, lambda i: child_ref[pl.ds(i, 1), :], write,
        LEAD, child_count,
    )
    out_ref[:, :LEAD] = rows_ref[...]
    out_ref[:, LEAD:] = tag_ref[...]


def lead_body(child_count, chunk_count, *refs):
    each = (len(refs) - 6) // chunk_count
    chunks = [refs[i * each : (i + 1) * each] for i in range(chunk_count)]
    slots_ref = refs[each * chunk_count]
    lead_ref, left_ref, place_ref, keep_ref, send_ref = refs[each * chunk_count + 1 :]
    front = jnp.concatenate([pick(c[0], c[1:]) for c in chunks], axis=0)[child_count:]
    rows, slots = front.shape[0], slots_ref.shape[0]
    place = jnp.transpose(slots_ref[:, LEAD:])[0:1, :]
    at = lax.broadcasted_iota(jnp.int32, (rows, slots), 0).astype(F32)
    onehot = jnp.where(at == place, 1.0, 0.0).astype(BF16)
    spots = jnp.concatenate([onehot, onehot, onehot], axis=1)
    place_ref[...] = spots
    lead = front + dot(spots, jnp.concatenate(parts3(slots_ref[:, :LEAD])[::-1], axis=0))
    lead_ref[...] = lead
    turned = jnp.transpose(lead)
    left_ref[...] = triple(turned, 1)
    first = dot_high(turned[:HALF], lead[:, :HALF], ((1,), (0,)))
    second = dot_high(turned[HALF:], lead, ((1,), (0,)))
    side = lax.axis_index("row") % 2 == 0
    for out, flip in ((keep_ref, False), (send_ref, True)):
        low = jnp.logical_xor(side, flip)
        out[:, :HALF] = jnp.where(low, first[:PB], first[PB:])
        out[:, HALF:] = jnp.where(low, second[:PB], second[PB:])


def add_body(a_ref, b_ref, out_ref):
    out_ref[...] = a_ref[...] + b_ref[...]


def join_body(a_ref, b_ref, out_ref):
    half = a_ref.shape[0]
    out_ref[:half, :] = a_ref[...]
    out_ref[half:, :] = b_ref[...]


def split_add_body(step, count, keep_ref, got_ref, keep_out, send_out):
    half = keep_out.shape[1]
    side = upper_side(step, count)
    for which, out in ((side, keep_out), (1 - side, send_out)):
        part = pl.ds(pl.multiple_of(which * half, 128), half)
        out[...] = keep_ref[:, part] + got_ref[:, part]


def product_body(blocks, halves, base_ref, left_ref, place_ref, front_ref, child_ref, *rest):
    del base_ref
    outs, whole_ref = rest[-1 - halves : -1], rest[-1]
    parts = jnp.concatenate(parts3(child_ref[...])[::-1], axis=0)
    whole = front_ref[...] + dot(place_ref[...], parts)
    whole_ref[...] = whole
    result = dot(left_ref[...], triple(whole, 0))
    if halves == 1:
        outs[0][...] = result
    else:
        first = pl.program_id(0) < blocks

        @pl.when(first)
        def _():
            outs[0][...] = result

        @pl.when(jnp.logical_not(first))
        def _():
            outs[1][...] = result


def spread_lane(tile, at):
    return jnp.broadcast_to(tile[:, at : at + 1], tile.shape)


def invert_factor(block):
    lane = lax.broadcasted_iota(jnp.int32, (8, PB), 1)
    sub = lax.broadcasted_iota(jnp.int32, (8, PB), 0)
    count = PB // 8
    tiles = [block[8 * t : 8 * t + 8, :] for t in range(count)]
    for b in range(count):
        first = 8 * b
        rows = tiles[b]
        cols = [spread_lane(rows, first + c) for c in range(8)]
        heads, inverses = {}, []
        for c in range(8):
            inverse = 1.0 / cols[c][c : c + 1, :]
            inverses.append(inverse)
            factor = jnp.where(sub > c, cols[c] * inverse, 0.0)
            here = lane == first + c
            source = jnp.where(here[0:1, :], 1.0, rows[c : c + 1, :])
            rows = jnp.where(here & (sub > c), 0.0, rows) - factor * source
            for d in range(c + 1, 8):
                heads[c, d] = cols[d][c : c + 1, :]
                cols[d] = cols[d] - factor * heads[c, d]
        tiles[b] = rows
        inside = (lane >= first) & (lane < first + 8)
        past = inside & (lane - first >= sub)
        used = jnp.where(past, jnp.where(lane - first == sub, 1.0, 0.0), rows)
        for t in range(b + 1, count):
            tile = tiles[t]
            factors = []
            for c in range(8):
                factor = spread_lane(tile, first + c)
                for d in range(c):
                    factor = factor - factors[d] * heads[d, c]
                factors.append(factor * inverses[c])
            tile = jnp.where(inside, 0.0, tile)
            for c in range(8):
                tile = tile - factors[c] * used[c : c + 1, :]
            tiles[t] = tile
    done = []
    for t in range(count):
        diagonal = lane == sub + 8 * t
        pivot = jnp.sum(jnp.where(diagonal, tiles[t], 0.0), axis=1, keepdims=True)
        scale = lax.rsqrt(pivot)
        scale = scale * (1.5 - 0.5 * pivot * scale * scale)
        unit = jnp.where(diagonal, 1.0, jnp.where(lane < sub + 8 * t, tiles[t], 0.0))
        done.append(unit * scale)
    return jnp.concatenate(done, axis=0)


def eliminate_body(k, *refs):
    out_ref = refs[-1]
    lo, hi = k * PB, (k + 1) * PB
    if k == 0:
        mine, got = refs[0][...], refs[1][...]
        low = lax.axis_index("row") % 2 == 0
        packed = jnp.concatenate([jnp.where(low, mine, got), jnp.where(low, got, mine)], axis=0)
        cross = packed[:, HALF:LEAD]
        out_ref[:HALF, :HALF] = packed[:, :HALF]
        out_ref[HALF:, :HALF] = cross
        out_ref[:HALF, HALF:] = jnp.transpose(cross)
        out_ref[HALF:, HALF:] = packed[:, LEAD:]
        in_ref = out_ref
    else:
        in_ref = refs[0]
        out_ref[:lo, :] = in_ref[:lo, :]
    inverse = invert_factor(in_ref[lo:hi, lo:hi])
    pieces = []
    for j in range(PANELS):
        if j == k:
            pieces.append(inverse)
        else:
            pieces.append(dot_high(inverse, in_ref[lo:hi, j * PB : (j + 1) * PB], ((1,), (0,))))
    row = jnp.concatenate(pieces, axis=1)
    out_ref[lo:hi, :] = row
    if k < PANELS - 1:
        column = dot_high(in_ref[hi:, lo:hi], inverse, ((1,), (1,)))
        change = dot_high(column, row, ((1,), (0,)))
        later = in_ref[hi:, :]
        out_ref[hi:, :] = later - change
        out_ref[hi:, lo:hi] = -change[:, lo:hi]


def finish_body(scale, matrix_ref, lead_ref, top_ref, bottom_ref, basis3_ref, basis_ref):
    own = lax.broadcasted_iota(jnp.int32, (LEAD, LEAD), 0) // PB
    other = lax.broadcasted_iota(jnp.int32, (LEAD, LEAD), 1) // PB
    inverse = jnp.where(own >= other, matrix_ref[...], 0.0)
    top_ref[...] = triple(inverse[:HALF, :HALF], 1)
    bottom_ref[...] = triple(inverse[HALF:], 1)
    basis = dot_high(lead_ref[...], inverse, ((1,), (1,)))
    basis3_ref[...] = triple(basis, 1)
    basis_ref[...] = basis * scale


def project_body(blocks, places_ref, top_ref, bottom_ref, basis_ref, *refs):
    del places_ref
    near_even, near_odd, far_even, far_odd, front_ref = refs[:5]
    upper_ref, out_ref = refs[-2:]
    near = pl.program_id(0) < blocks
    sums = jnp.concatenate(
        [
            jnp.where(near, near_even[...], far_even[...]),
            jnp.where(near, near_odd[...], far_odd[...]),
        ],
        axis=1,
    )
    hi, lo = parts2(sums)
    upper_ref[:HALF, :] = dot(
        top_ref[...], jnp.concatenate([hi[:HALF], lo[:HALF], hi[:HALF]], axis=0)
    )
    upper_ref[HALF:, :] = dot(bottom_ref[...], jnp.concatenate([hi, lo, hi], axis=0))
    out_ref[...] = front_ref[...] - dot(basis_ref[...], triple(upper_ref[...], 0))


def plan(tasks, link_rate, near_rate, lag):
    ready_link = {"near": 0.0, "far": 0.0}
    arrival, order, now = {}, [], 0.0
    left = dict(tasks)
    ended = {}

    def when(name):
        latest = 0.0
        for before, way, size in tasks[name][2]:
            if before not in ended:
                return None
            latest = max(latest, arrival.get((before, way), ended[before]))
        return latest

    while left:
        known = [(when(name), left[name][0], at, name) for at, name in enumerate(left)]
        known = [entry for entry in known if entry[0] is not None]
        free = [entry for entry in known if entry[0] <= now]
        chosen = min(free, key=lambda e: (e[1], e[2])) if free else min(known)
        name = chosen[3]
        now = max(now, chosen[0]) + tasks[name][1]
        ended[name] = now
        order.append((name, now))
        del left[name]
        sent = {}
        for other in tasks:
            for before, way, size in tasks[other][2]:
                if before == name and way:
                    sent[way] = max(size, sent.get(way, 0))
        for way, size in sent.items():
            begin = max(now, ready_link[way])
            ready_link[way] = begin + size / (near_rate if way == "near" else link_rate)
            arrival[name, way] = ready_link[way] + lag
    return order


def task_list(steps, chunks, width):
    tasks = {}
    gram = HALF // 2 * (LEAD + HALF) * 4e-6
    for t in range(steps):
        before = [("lead", None, 0), ("lead", "near", gram)] if t == 0 else [
            (("gram", t - 1), None, 0), (("gram", t - 1), "far", gram)
        ]
        tasks["gram", t] = (0, 1.0, before)
    tasks["lead"] = (0, 0.0, [])
    for k in range(PANELS):
        before = [(("factor", k - 1), None, 0)] if k else [(("gram", steps - 1), "near", gram)]
        tasks["factor", k] = (3, 5.2, before)
    tasks["finish"] = (3, 2.4, [(("factor", PANELS - 1), None, 0)])
    for c in range(chunks):
        if c == 0:
            tasks["send", c] = (2, 2.9, [("lead", None, 0)])
            tasks["keep", c] = (2, 2.9, [(("send", c), None, 0)])
        else:
            tasks["send", c] = (2, 4.8, [("lead", None, 0)])
        size = LEAD * width * 4e-6
        last = ("send", c)
        for t in range(1, steps):
            way = "near" if t == 1 else "far"
            before = [(last, way, size)] + ([(("keep", c), None, 0)] if t == 1 and c == 0 else [])
            tasks["split", c, t] = (1, 1.4, before)
            size = size / 2
            last = ("split", c, t)
        tasks["sum", c] = (1, 0.8, [(last, "far", size)])
        last = ("sum", c)
        for t in reversed(range(1, steps)):
            tasks["join", c, t] = (1, 0.9, [(last, "far", size)])
            size = size * 2
            last = ("join", c, t)
        tasks["project", c] = (4, 6.2, [(last, "near", size), ("finish", None, 0)])
    return tasks


def on_device(front_matrix, child_rows, child_owner, child_offset):
    row_count = lax.axis_size("row")
    col_count = lax.axis_size("col")
    local_rows, local_cols = front_matrix.shape
    child_count = child_rows.shape[0]
    capacity = 2 * child_count // row_count
    slots = row_count * capacity
    steps = row_count.bit_length() - 1
    owner, offset = child_owner[:, 0], child_offset[:, 0]
    run = Chain()

    stacked = child_count + local_rows
    pieces = 3
    size = -(-stacked // pieces // 16) * 16
    sizes = [size] * (pieces - 1) + [stacked - size * (pieces - 1)]
    own = run(
        "cut_lead", cut_body, [child_rows, front_matrix],
        [pl.BlockSpec((child_count, LEAD), lambda i: (0, 0)), pl.BlockSpec((local_rows, LEAD), lambda i: (0, 0))],
        [f32(n, LEAD) for n in sizes], [pl.BlockSpec((n, LEAD), lambda i: (0, 0)) for n in sizes],
        grid=(1,),
    )
    got = [spread(piece, col_count) for piece in own]
    packed = run(
        "pack_children", functools.partial(pack_body, row_count, capacity),
        [owner, child_rows], [SCALARS, WHOLE], [f32(slots, local_cols)], [WHOLE],
    )
    child = exchange(packed, row_count)
    packed, _, _, _ = run(
        "pack_lead",
        functools.partial(pack_lead_body, row_count, capacity, float(local_rows), child_count),
        [owner, offset, own[0]] + got[0], [SCALARS, SCALARS] + [WHOLE] * (1 + len(got[0])),
        [f32(slots, LEAD + PB), f32(sizes[0], LEAD), f32(slots, LEAD), f32(slots, PB)], [WHOLE] * 4,
    )
    lead_child = exchange(packed, row_count)
    operands = [ref for piece, arrived in zip(own, got) for ref in [piece] + arrived]
    lead, left, place, gram, gram_send = run(
        "lead_setup", functools.partial(lead_body, child_count, pieces),
        operands + [lead_child], [WHOLE] * (len(operands) + 1),
        [f32(local_rows, LEAD), bf16(LEAD, 3 * local_rows), bf16(local_rows, 3 * slots),
         f32(HALF // 2, LEAD + HALF), f32(HALF // 2, LEAD + HALF)],
        [WHOLE] * 5,
    )

    chunks = max(1, min(4, local_cols // (PB * row_count)))
    width = local_cols // 2 // chunks
    blocks = width // BLOCK
    core = upper_side(0, row_count)
    order = jnp.asarray(piece_order(row_count))[lax.axis_index("row")]
    scale = math.sqrt(local_rows * row_count)
    front = upper = matrix = factor = scaled = None
    gram_got = swap(gram_send, 0, row_count)
    keep, arrived, far = {}, {}, {}

    def make(halves, c, front):
        at = [(half * chunks + c) * blocks for half in halves]
        bases = jnp.concatenate([base + jnp.arange(blocks, dtype=jnp.int32) for base in at])
        operands = [left, place, front_matrix, child]
        in_specs = [
            pl.BlockSpec(left.shape, lambda i, b: (0, 0)),
            pl.BlockSpec(place.shape, lambda i, b: (0, 0)),
            pl.BlockSpec((local_rows, BLOCK), lambda i, b: (0, b[i])),
            pl.BlockSpec((slots, BLOCK), lambda i, b: (0, b[i])),
        ]
        aliases = {}
        if front is not None:
            operands.append(front)
            in_specs.append(ANYWHERE)
            aliases = {5: len(halves)}
        out_specs = [pl.BlockSpec((LEAD, BLOCK), lambda i, b: (0, jnp.minimum(i, blocks - 1)))]
        if len(halves) == 2:
            out_specs.append(pl.BlockSpec((LEAD, BLOCK), lambda i, b: (0, jnp.maximum(i - blocks, 0))))
        out_specs.append(pl.BlockSpec((local_rows, BLOCK), lambda i, b: (0, b[i])))
        return run(
            "lead_product", functools.partial(product_body, blocks, len(halves)), operands, in_specs,
            [f32(LEAD, width)] * len(halves) + [f32(local_rows, local_cols)], out_specs,
            scalars=[bases], grid=(blocks * len(halves),), aliases=aliases,
        )

    def cast(c, value, step):
        keep[c], arrived[c] = value, swap(value, step, row_count)

    for task, _ in plan(task_list(steps, chunks, width), 0.09, 0.4, 5.0):
        kind, c = task[0], task[1]
        if task == "lead":
            continue
        if task == "finish":
            top, bottom, basis, scaled = run(
                "finish_factor", functools.partial(finish_body, scale), [matrix, lead], [WHOLE] * 2,
                [bf16(HALF, 3 * HALF), bf16(HALF, 3 * LEAD), bf16(local_rows, 3 * LEAD), f32(local_rows, LEAD)],
                [WHOLE] * 4,
            )
        elif kind == "gram":
            gram = run("add_gram", add_body, [gram, gram_got], [WHOLE] * 2, [f32(*gram.shape)], [WHOLE])
            gram_got = swap(gram, (c + 1) % steps, row_count)
        elif kind == "factor":
            operands = [gram, gram_got] if c == 0 else [matrix]
            matrix = run(
                "eliminate_panel", functools.partial(eliminate_body, c), operands,
                [WHOLE] * len(operands), [f32(LEAD, LEAD)], [WHOLE],
            )
        elif kind == "send":
            if c == 0:
                send, front = make([1 - core], c, front)
            else:
                send, keep[c], front = make([1 - core, core], c, front)
            arrived[c] = swap(send, 0, row_count)
        elif kind == "keep":
            keep[c], front = make([core], c, front)
        elif kind == "split":
            t = task[2]
            shape = f32(LEAD, keep[c].shape[1] // 2)
            keep[c], send = run(
                "split_add", functools.partial(split_add_body, t, row_count), [keep[c], arrived[c]],
                [WHOLE] * 2, [shape, shape], [WHOLE] * 2,
            )
            arrived[c] = swap(send, t, row_count)
        elif kind == "sum":
            value = run("add_shard", add_body, [keep[c], arrived[c]], [WHOLE] * 2, [f32(*keep[c].shape)], [WHOLE])
            cast(c, value, steps - 1)
        elif kind == "join":
            rows = keep[c].shape[0]
            value = run("join_pieces", join_body, [keep[c], arrived[c]], [WHOLE] * 2, [f32(2 * rows, PB)], [WHOLE])
            cast(c, value, task[2] - 1)
        elif kind == "project":
            starts = [(half * chunks + c) * blocks for half in (core, 1 - core)]
            columns = jnp.concatenate([s + jnp.arange(blocks, dtype=jnp.int32) for s in starts])
            scalars = [jnp.concatenate([columns, order[0], order[1]])]
            near = 2 * blocks
            far_at = near + 2 * blocks

            def near_piece(odd):
                return lambda i, p: (p[near + 2 * jnp.minimum(i, blocks - 1) + odd], 0)

            def far_piece(odd):
                return lambda i, p: (p[far_at + 2 * jnp.maximum(i - blocks, 0) + odd], 0)

            operands = [top, bottom, basis, keep[c], keep[c], arrived[c], arrived[c], front]
            in_specs = [
                pl.BlockSpec(top.shape, lambda i, p: (0, 0)),
                pl.BlockSpec(bottom.shape, lambda i, p: (0, 0)),
                pl.BlockSpec(basis.shape, lambda i, p: (0, 0)),
                pl.BlockSpec((LEAD, PB), near_piece(0)),
                pl.BlockSpec((LEAD, PB), near_piece(1)),
                pl.BlockSpec((LEAD, PB), far_piece(0)),
                pl.BlockSpec((LEAD, PB), far_piece(1)),
                pl.BlockSpec((local_rows, BLOCK), lambda i, p: (0, p[i])),
            ]
            aliases = {8: 1}
            if upper is not None:
                operands.append(upper)
                in_specs.append(ANYWHERE)
                aliases[9] = 0
            upper, front = run(
                "project_columns", functools.partial(project_body, blocks), operands, in_specs,
                [f32(LEAD, local_cols), f32(local_rows, local_cols)],
                [pl.BlockSpec((LEAD, BLOCK), lambda i, p: (0, p[i])), pl.BlockSpec((local_rows, BLOCK), lambda i, p: (0, p[i]))],
                scalars=scalars, grid=(2 * blocks,), aliases=aliases,
            )
    return upper, front, scaled


def solution(mesh):
    placed = (P("row", "col"), P("row", "col"), P("row", None), P("row", None))
    return jax.shard_map(
        on_device,
        mesh=mesh,
        in_specs=placed,
        out_specs=(P(None, "col"), P("row", "col"), P("row", None)),
        check_vma=False,
    )
```

time: 825 us -> 244 us (0.30)
  waiting for transfers between devices: 563 us -> 67.1 us
  other arithmetic: 114 us -> 0.4 us
  Pallas kernels: 0 us -> 89.3 us
  matrix products: 86.5 us -> 0 us
  starting transfers between devices: 11.5 us -> 43 us
  between operations: 14.8 us -> 1.04 us
  blocking collectives: 0 us -> 11.8 us
    psum x12 -> x0, waiting for transfers between devices: 541 us -> none  [the longest x3 176 us: factor_panel(): gram_total = lax.psum(gram_part, 'row')]
    another operation x21 -> x0, other arithmetic: 91.5 us -> none  [the longest x12 49.6 us: factor_panel(): lower_factor = jnp.linalg.cholesky(gram_total)]
    pallas_call x0 -> x41, Pallas kernels: none -> 89.3 us  [__call__(): results = pl.pallas_call(kernel, **settings)(*scalars, *operands)]
    dot_general x20 -> x0, matrix products: 81.3 us -> none  [product(): jnp.dot(left_op, right_op, precision=lax.Precision.HIGHEST, preferred_ele...]
    ppermute x0 -> x37, waiting for transfers between devices: none -> 67.1 us  [the longest x28 38.1 us: swap(): return lax.ppermute(value, 'row', pairs)]
    ppermute x0 -> x37, starting transfers between devices: none -> 37.7 us  [the longest x28 24.6 us: swap(): return lax.ppermute(value, 'row', pairs)]
    all_to_all x2 -> x1, waiting for transfers between devices: 21.6 us -> 0.01 us  [exchange(): lax.all_to_all(shaped, 'row', split_axis=0, concat_axis=0, tiled=True)]
    all_to_all x0 -> x1, blocking collectives: none -> 11.8 us  [exchange(): lax.all_to_all(shaped, 'row', split_axis=0, concat_axis=0, tiled=True)]
  transfers between devices with their start and end apart: 14 -> 38, of which waited for: 13 -> 18; matrix products, arithmetic and copies ran while one was open for 7% -> 0% of each run, Pallas kernels for 0% -> 31%
where the time goes in v3:
time: 244 us; the launch traced here: 241 us
  Pallas kernels  89.3 us (37%)
  waiting for transfers between devices  67.1 us (27%)
  starting transfers between devices  43 us (18%)
  local copies, waits for them, and re-layouts  28.3 us (12%)
  blocking collectives  11.8 us (5%)
    pallas_call x41, Pallas kernels, __call__(): results = pl.pallas_call(kernel, **settings)(*scalars, *operands)  89.3 us
    ppermute x28, waiting for transfers between devices, swap(): return lax.ppermute(value, 'row', pairs)  38.1 us
    unnamed x72, local copies, waits for them, and re-layouts  27.6 us
    ppermute x28, starting transfers between devices, swap(): return lax.ppermute(value, 'row', pairs)  24.6 us
    ppermute x3, waiting for transfers between devices, spread(): first = lax.ppermute(value, 'col', [(0, middle)])  21.6 us
    all_to_all x1, blocking collectives, exchange(): lax.all_to_all(shaped, 'row', split_axis=0, concat_axis=0, tiled=True)  11.8 us
    ppermute x6, starting transfers between devices, spread(): return [first] + [lax.ppermute(first, 'col', [(middle, c)]) for c in others]  9.22 us
    ppermute x6, waiting for transfers between devices, spread(): return [first] + [lax.ppermute(first, 'col', [(middle, c)]) for c in others]  7.38 us
  transfers between devices with their start and end apart: 38, of which 18 were waited for; matrix products, arithmetic and copies ran while one was open for 0% of the time, Pallas kernels for 31%

profile of v3, /device:TPU:21, one launch (start us, length us, event | category | flops | bytes accessed | tf_op | source)
XLA Modules:
  0.0 240.9 jit_solution(11367117805191266413)
XLA Ops:
  6.7 10.1 %collective-permute-done.refs_3_.refs_1_ = f32[160,512]{1,0:T(8,128)S(1)} collective-permute-done((f32[160,512]{1,0:T(8,128)S(1)}, f32[160,512]{1,0:T(8,128)S(1)}, u32[]{:S(2)}, u32[]{:S(2)}) %collective-permute-start) | collective-permute-done | bytes 327712 | tf_op jit(solution)/shard_map/ppermute | solution.py:128
  28.1 11.8 %all_to_all.10 = f32[8,16,640]{2,1,0:T(8,128)} all-to-all(f32[8,16,640]{2,1,0:T(8,128)S(1)} %bitcast.19), channel_id=1, replica_groups=mesh['row'=8,'col'=4] {'row'}, dimensions={0} | all-to-all | bytes 655360 | tf_op jit(solution)/shard_map/all_to_all | solution.py:136
  39.9 5.3 %all-to-all-start.1 = ((f32[8,16,4096]{2,1,0:T(8,128)}), f32[8,16,4096]{2,1,0:T(8,128)S(1)}, u32[]{:S(2)}, u32[]{:S(2)}) async-start(f32[8,16,4096]{2,1,0:T(8,128)} %bitcast.17), calls=%async_computation.1 | async-start | bytes 4194304 | tf_op jit(solution)/shard_map/all_to_all | solution.py:136
  47.8 9.1 %collective-permute-done.3.refs_5_ = f32[160,512]{1,0:T(8,128)S(1)} collective-permute-done((f32[160,512]{1,0:T(8,128)S(1)}, f32[160,512]{1,0:T(8,128)S(1)}, u32[]{:S(2)}, u32[]{:S(2)}) %collective-permute-start.3) | collective-permute-done | bytes 327712 | tf_op jit(solution)/shard_map/ppermute | solution.py:128
  66.6 3.8 %collective-permute-done.8.refs_11_ = f32[128,512]{1,0:T(8,128)} collective-permute-done((f32[128,512]{1,0:T(8,128)}, f32[128,512]{1,0:T(8,128)}, u32[]{:S(2)}, u32[]{:S(2)}) %collective-permute-start.8) | collective-permute-done | bytes 262176 | tf_op jit(solution)/shard_map/ppermute | solution.py:130
  92.2 3.4 %lead_product.5 = (f32[512,512]{1,0:T(8,128)}, f32[384,4096]{1,0:T(8,128)}, f32[8,128]{1,0:T(8,128)S(1)}) custom-call(s32[2]{0:T(128)S(1)} %get-tuple-element.234.refs_0_, bf16[512,1152]{1,0:T(8,128)(2,1)S(1)} %get-tuple-element.122.refs_1_, bf16[384,384]{1,0:T(8,128)(2,1)S(1)} %copy-done.4, f32[384,4096]{1,0:T(8,128)S(1)} %copy-done.1, ...), custom_call_target="tpu_custom_call" | custom-call | flops 1048576 | bytes 65536 | tf_op jit(solution)/shard_map/lead_product/pallas_call | solution.py:72
  100.9 3.5 %lead_product.6 = (f32[512,512]{1,0:T(8,128)S(1)}, f32[384,4096]{1,0:T(8,128)}, f32[8,128]{1,0:T(8,128)S(1)}) custom-call(s32[2]{0:T(128)S(1)} %get-tuple-element.235.refs_0_, bf16[512,1152]{1,0:T(8,128)(2,1)S(1)} %get-tuple-element.122.refs_1_, bf16[384,384]{1,0:T(8,128)(2,1)S(1)} %copy-done.5, ...), custom_call_target="tpu_custom_call", output_to_operand_aliasing={{1}: (5, {})} | custom-call | flops 1048576 | bytes 65536 | tf_op jit(solution)/shard_map/lead_product/pallas_call | solution.py:72
  104.4 5.8 %lead_product.7 = (f32[512,512]{1,0:T(8,128)S(1)}, f32[512,512]{1,0:T(8,128)S(1)}, f32[384,4096]{1,0:T(8,128)}, f32[8,128]{1,0:T(8,128)S(1)}) custom-call(s32[4]{0:T(128)S(1)} %pad_add_fusion.refs_0_, bf16[512,1152]{1,0:T(8,128)(2,1)S(1)} %get-tuple-element.122.refs_1_, bf16[384,384]{1,0:T(8,128)(2,1)S(1)} %copy-done.5, ...), custom_call_target="tpu_custom_call", output_to_operand_aliasing={{2}: (5, {})} | custom-call | flops 1048576 | bytes 65536 | tf_op jit(solution)/shard_map/lead_product/pallas_call | solution.py:72
  112.1 5.8 %lead_product.8 = (f32[512,512]{1,0:T(8,128)S(1)}, f32[512,512]{1,0:T(8,128)S(1)}, f32[384,4096]{1,0:T(8,128)}, f32[8,128]{1,0:T(8,128)S(1)}) custom-call(s32[4]{0:T(128)S(1)} %pad_add_fusion.2.refs_0_, bf16[512,1152]{1,0:T(8,128)(2,1)S(1)} %get-tuple-element.122.refs_1_, bf16[384,384]{1,0:T(8,128)(2,1)S(1)} %copy-done.5, ...), custom_call_target="tpu_custom_call", output_to_operand_aliasing={{2}: (5, {})} | custom-call | flops 1048576 | bytes 65536 | tf_op jit(solution)/shard_map/lead_product/pallas_call | solution.py:72
  118.0 5.8 %lead_product.9 = (f32[512,512]{1,0:T(8,128)S(1)}, f32[512,512]{1,0:T(8,128)S(1)}, f32[384,4096]{1,0:T(8,128)}, f32[8,128]{1,0:T(8,128)S(1)}) custom-call(s32[4]{0:T(128)S(1)} %pad_add_fusion.1.refs_0_, bf16[512,1152]{1,0:T(8,128)(2,1)S(1)} %get-tuple-element.122.refs_1_, bf16[384,384]{1,0:T(8,128)(2,1)S(1)} %copy-done.5, ...), custom_call_target="tpu_custom_call", output_to_operand_aliasing={{2}: (5, {})} | custom-call | flops 1048576 | bytes 65536 | tf_op jit(solution)/shard_map/lead_product/pallas_call | solution.py:72
  125.7 5.5 %collective-permute-done.10.refs_1_ = f32[128,768]{1,0:T(8,128)S(1)} collective-permute-done((f32[128,768]{1,0:T(8,128)S(1)}, f32[128,768]{1,0:T(8,128)S(1)}, u32[]{:S(2)}, u32[]{:S(2)}) %collective-permute-start.10) | collective-permute-done | bytes 393248 | tf_op jit(solution)/shard_map/ppermute | solution.py:86
  134.4 3.8 %collective-permute-done.14.refs_1_ = f32[512,256]{1,0:T(8,128)S(1)} collective-permute-done((f32[512,256]{1,0:T(8,128)S(1)}, f32[512,256]{1,0:T(8,128)S(1)}, u32[]{:S(2)}, u32[]{:S(2)}) %collective-permute-start.14) | collective-permute-done | bytes 524320 | tf_op jit(solution)/shard_map/ppermute | solution.py:86
  138.4 4.0 %collective-permute-done.12.refs_1_ = f32[128,768]{1,0:T(8,128)S(1)} collective-permute-done((f32[128,768]{1,0:T(8,128)S(1)}, f32[128,768]{1,0:T(8,128)S(1)}, u32[]{:S(2)}, u32[]{:S(2)}) %collective-permute-start.12) | collective-permute-done | bytes 393248 | tf_op jit(solution)/shard_map/ppermute | solution.py:86
  147.9 5.5 %eliminate_panel.4 = (f32[512,512]{1,0:T(8,128)S(1)}, f32[8,128]{1,0:T(8,128)S(1)}) custom-call(f32[128,768]{1,0:T(8,128)S(1)} %get-tuple-element.154.refs_0_, f32[128,768]{1,0:T(8,128)S(1)} %collective-permute-done.17.refs_1_, f32[8,128]{1,0:T(8,128)S(1)} %get-tuple-element.158.refs_2_), custom_call_target="tpu_custom_call" | custom-call | flops 1048576 | bytes 65536 | tf_op jit(solution)/shard_map/eliminate_panel/pallas_call | solution.py:72
  157.6 5.2 %eliminate_panel.5 = (f32[512,512]{1,0:T(8,128)S(1)}, f32[8,128]{1,0:T(8,128)S(1)}) custom-call(f32[512,512]{1,0:T(8,128)S(1)} %get-tuple-element.159.refs_0_, f32[8,128]{1,0:T(8,128)S(1)} %get-tuple-element.163.refs_1_), custom_call_target="tpu_custom_call" | custom-call | flops 1048576 | bytes 65536 | tf_op jit(solution)/shard_map/eliminate_panel/pallas_call | solution.py:72
  162.9 5.1 %eliminate_panel.6 = (f32[512,512]{1,0:T(8,128)S(1)}, f32[8,128]{1,0:T(8,128)S(1)}) custom-call(f32[512,512]{1,0:T(8,128)S(1)} %get-tuple-element.164.refs_0_, f32[8,128]{1,0:T(8,128)S(1)} %get-tuple-element.168.refs_1_), custom_call_target="tpu_custom_call" | custom-call | flops 1048576 | bytes 65536 | tf_op jit(solution)/shard_map/eliminate_panel/pallas_call | solution.py:72
  168.2 4.3 %eliminate_panel.7 = (f32[512,512]{1,0:T(8,128)S(1)}, f32[8,128]{1,0:T(8,128)S(1)}) custom-call(f32[512,512]{1,0:T(8,128)S(1)} %get-tuple-element.169.refs_0_, f32[8,128]{1,0:T(8,128)S(1)} %get-tuple-element.179.refs_1_), custom_call_target="tpu_custom_call" | custom-call | flops 1048576 | bytes 65536 | tf_op jit(solution)/shard_map/eliminate_panel/pallas_call | solution.py:72
  184.3 4.9 %collective-permute-done.28.refs_1_ = f32[512,128]{1,0:T(8,128)S(1)} collective-permute-done((f32[512,128]{1,0:T(8,128)S(1)}, f32[512,128]{1,0:T(8,128)S(1)}, u32[]{:S(2)}, u32[]{:S(2)}) %collective-permute-start.28) | collective-permute-done | bytes 262176 | tf_op jit(solution)/shard_map/ppermute | solution.py:86
  193.0 6.4 %collective-permute-done.32.refs_1_ = f32[1024,128]{1,0:T(8,128)} collective-permute-done((f32[1024,128]{1,0:T(8,128)}, f32[1024,128]{1,0:T(8,128)}, u32[]{:S(2)}, u32[]{:S(2)}) %collective-permute-start.32) | collective-permute-done | bytes 524320 | tf_op jit(solution)/shard_map/ppermute | solution.py:86
  201.7 6.9 %project_columns.4 = (f32[512,4096]{1,0:T(8,128)}, f32[384,4096]{1,0:T(8,128)}, f32[8,128]{1,0:T(8,128)S(1)}) custom-call(s32[12]{0:T(128)S(1)} %get-tuple-element.224.refs_0_, bf16[256,768]{1,0:T(8,128)(2,1)S(1)} %get-tuple-element.187.refs_1_, bf16[256,1536]{1,0:T(8,128)(2,1)S(1)} %get-tuple-element.188.refs_2_, ...), custom_call_target="tpu_custom_call", output_to_operand_aliasing={{1}: (8, {})} | custom-call | flops 1048576 | bytes 65536 | tf_op jit(solution)/shard_map/project_columns/pallas_call | solution.py:72
  211.5 4.1 %collective-permute-done.27.refs_1_ = f32[512,128]{1,0:T(8,128)S(1)} collective-permute-done((f32[512,128]{1,0:T(8,128)S(1)}, f32[512,128]{1,0:T(8,128)S(1)}, u32[]{:S(2)}, u32[]{:S(2)}) %collective-permute-start.27) | collective-permute-done | bytes 262176 | tf_op jit(solution)/shard_map/ppermute | solution.py:86
  216.9 6.6 %project_columns.5 = (f32[512,4096]{1,0:T(8,128)}, f32[384,4096]{1,0:T(8,128)}, f32[8,128]{1,0:T(8,128)S(1)}) custom-call(s32[12]{0:T(128)S(1)} %get-tuple-element.223.refs_0_, bf16[256,768]{1,0:T(8,128)(2,1)S(1)} %get-tuple-element.187.refs_1_, bf16[256,1536]{1,0:T(8,128)(2,1)S(1)} %get-tuple-element.188.refs_2_, ...), custom_call_target="tpu_custom_call", output_to_operand_aliasing={{1}: (8, {}), {0}: (9, {})} | custom-call | flops 1048576 | bytes 65536 | tf_op jit(solution)/shard_map/project_columns/pallas_call | solution.py:72
  223.5 6.6 %project_columns.6 = (f32[512,4096]{1,0:T(8,128)}, f32[384,4096]{1,0:T(8,128)}, f32[8,128]{1,0:T(8,128)S(1)}) custom-call(s32[12]{0:T(128)S(1)} %get-tuple-element.225.refs_0_, bf16[256,768]{1,0:T(8,128)(2,1)S(1)} %get-tuple-element.187.refs_1_, bf16[256,1536]{1,0:T(8,128)(2,1)S(1)} %get-tuple-element.188.refs_2_, ...), custom_call_target="tpu_custom_call", output_to_operand_aliasing={{1}: (8, {}), {0}: (9, {})} | custom-call | flops 1048576 | bytes 65536 | tf_op jit(solution)/shard_map/project_columns/pallas_call | solution.py:72
  234.3 6.6 %project_columns.7 = (f32[512,4096]{1,0:T(8,128)}, f32[384,4096]{1,0:T(8,128)}, f32[8,128]{1,0:T(8,128)}) custom-call(s32[12]{0:T(128)S(1)} %add_add_fusion.refs_0_, bf16[256,768]{1,0:T(8,128)(2,1)S(1)} %get-tuple-element.187.refs_1_, bf16[256,1536]{1,0:T(8,128)(2,1)S(1)} %get-tuple-element.188.refs_2_, ...), custom_call_target="tpu_custom_call", output_to_operand_aliasing={{1}: (8, {}), {0}: (9, {})} | custom-call | flops 1048576 | bytes 65536 | tf_op jit(solution)/shard_map/project_columns/pallas_call | solution.py:72
  (178 shorter events, 100.1 us)
Async XLA Ops:
  39.9 48.5 %all-to-all-start.1 = ((f32[8,16,4096]{2,1,0:T(8,128)}), f32[8,16,4096]{2,1,0:T(8,128)S(1)}, u32[]{:S(2)}, u32[]{:S(2)}) async-start(f32[8,16,4096]{2,1,0:T(8,128)} %bitcast.17), calls=%async_computation.1 | async-start | bytes 4194304 | tf_op jit(solution)/shard_map/all_to_all | solution.py:136
  45.2 11.7 %collective-permute-start.3 = (f32[160,512]{1,0:T(8,128)S(1)}, f32[160,512]{1,0:T(8,128)S(1)}, u32[]{:S(2)}, u32[]{:S(2)}) collective-permute-start(f32[160,512]{1,0:T(8,128)S(1)} %get-tuple-element.114.refs_4_), channel_id=1, source_target_pairs={{0,2},{4,6},{8,10},{12,14},{16,18},{20,22},{24,26},{28,30}} | collective-permute-start | bytes 983048 | tf_op jit(solution)/shard_map/ppermute | solution.py:128
  46.5 16.2 %collective-permute-start.6 = (f32[128,512]{1,0:T(8,128)}, f32[128,512]{1,0:T(8,128)}, u32[]{:S(2)}, u32[]{:S(2)}) collective-permute-start(f32[128,512]{1,0:T(8,128)} %get-tuple-element.115.refs_8_), channel_id=1, source_target_pairs={{0,2},{4,6},{8,10},{12,14},{16,18},{20,22},{24,26},{28,30}} | collective-permute-start | bytes 786440 | tf_op jit(solution)/shard_map/ppermute | solution.py:128
  56.9 14.8 %collective-permute-start.5 = (f32[160,512]{1,0:T(8,128)S(1)}, f32[160,512]{1,0:T(8,128)S(1)}, u32[]{:S(2)}, u32[]{:S(2)}) collective-permute-start(f32[160,512]{1,0:T(8,128)S(1)} %collective-permute-done.3.refs_5_), channel_id=1, source_target_pairs={{2,1},{6,5},{10,9},{14,13},{18,17},{22,21},{26,25},{30,29}} | collective-permute-start | bytes 983048 | tf_op jit(solution)/shard_map/ppermute | solution.py:130
  58.2 14.3 %collective-permute-start.4 = (f32[160,512]{1,0:T(8,128)S(1)}, f32[160,512]{1,0:T(8,128)S(1)}, u32[]{:S(2)}, u32[]{:S(2)}) collective-permute-start(f32[160,512]{1,0:T(8,128)S(1)} %collective-permute-done.3.refs_5_), channel_id=1, source_target_pairs={{2,3},{6,7},{10,11},{14,15},{18,19},{22,23},{26,27},{30,31}} | collective-permute-start | bytes 983048 | tf_op jit(solution)/shard_map/ppermute | solution.py:130
  95.6 15.1 %collective-permute-start.11 = (f32[512,512]{1,0:T(8,128)}, f32[512,512]{1,0:T(8,128)}, u32[]{:S(2)}, u32[]{:S(2)}) collective-permute-start(f32[512,512]{1,0:T(8,128)} %get-tuple-element.134), channel_id=1, source_target_pairs={{0,4},{4,0},{8,12},{12,8},{16,20},{20,16},{24,28},{28,24},{1,5},{5... | collective-permute-start | bytes 3145736 | tf_op jit(solution)/shard_map/ppermute | solution.py:86
  97.0 13.7 %collective-permute-start.9 = (f32[128,768]{1,0:T(8,128)}, f32[128,768]{1,0:T(8,128)S(1)}, u32[]{:S(2)}, u32[]{:S(2)}) collective-permute-start(f32[128,768]{1,0:T(8,128)} %copy-done.33), channel_id=1, source_target_pairs={{0,4},{4,0},{8,12},{12,8},{16,20},{20,16},{24,28},{28,24},{1,5},{5... | collective-permute-start | bytes 1179656 | tf_op jit(solution)/shard_map/ppermute | solution.py:86
  110.1 22.3 %collective-permute-start.16 = (f32[512,512]{1,0:T(8,128)S(1)}, f32[512,512]{1,0:T(8,128)S(1)}, u32[]{:S(2)}, u32[]{:S(2)}) collective-permute-start(f32[512,512]{1,0:T(8,128)S(1)} %get-tuple-element.148), channel_id=1, source_target_pairs={{0,4},{4,0},{8,12},{12,8},{16,20},{20,16},{24,28},{28,24},{1,5},{5... | collective-permute-start | bytes 3145736 | tf_op jit(solution)/shard_map/ppermute | solution.py:86
  117.9 15.1 %collective-permute-start.15 = (f32[512,512]{1,0:T(8,128)S(1)}, f32[512,512]{1,0:T(8,128)S(1)}, u32[]{:S(2)}, u32[]{:S(2)}) collective-permute-start(f32[512,512]{1,0:T(8,128)S(1)} %get-tuple-element.146), channel_id=1, source_target_pairs={{0,4},{4,0},{8,12},{12,8},{16,20},{20,16},{24,28},{28,24},{1,5},{5... | collective-permute-start | bytes 3145736 | tf_op jit(solution)/shard_map/ppermute | solution.py:86
  123.7 14.5 %collective-permute-start.13 = (f32[512,512]{1,0:T(8,128)S(1)}, f32[512,512]{1,0:T(8,128)S(1)}, u32[]{:S(2)}, u32[]{:S(2)}) collective-permute-start(f32[512,512]{1,0:T(8,128)S(1)} %get-tuple-element.142), channel_id=1, source_target_pairs={{0,4},{4,0},{8,12},{12,8},{16,20},{20,16},{24,28},{28,24},{1,5},{5... | collective-permute-start | bytes 3145736 | tf_op jit(solution)/shard_map/ppermute | solution.py:86
  124.5 13.6 %collective-permute-start.14 = (f32[512,256]{1,0:T(8,128)S(1)}, f32[512,256]{1,0:T(8,128)S(1)}, u32[]{:S(2)}, u32[]{:S(2)}) collective-permute-start(f32[512,256]{1,0:T(8,128)S(1)} %get-tuple-element.144), channel_id=1, source_target_pairs={{0,8},{4,20},{8,0},{12,28},{16,24},{20,4},{24,16},{28,12},{1,9},{5... | collective-permute-start | bytes 1572872 | tf_op jit(solution)/shard_map/ppermute | solution.py:86
  132.6 14.0 %collective-permute-start.18 = (f32[512,256]{1,0:T(8,128)S(1)}, f32[512,256]{1,0:T(8,128)S(1)}, u32[]{:S(2)}, u32[]{:S(2)}) collective-permute-start(f32[512,256]{1,0:T(8,128)S(1)} %get-tuple-element.156), channel_id=1, source_target_pairs={{0,8},{4,20},{8,0},{12,28},{16,24},{20,4},{24,16},{28,12},{1,9},{5... | collective-permute-start | bytes 1572872 | tf_op jit(solution)/shard_map/ppermute | solution.py:86
  133.1 22.2 %collective-permute-start.19 = (f32[512,256]{1,0:T(8,128)S(1)}, f32[512,256]{1,0:T(8,128)S(1)}, u32[]{:S(2)}, u32[]{:S(2)}) collective-permute-start(f32[512,256]{1,0:T(8,128)S(1)} %get-tuple-element.161), channel_id=1, source_target_pairs={{0,8},{4,20},{8,0},{12,28},{16,24},{20,4},{24,16},{28,12},{1,9},{5... | collective-permute-start | bytes 1572872 | tf_op jit(solution)/shard_map/ppermute | solution.py:86
  144.3 23.8 %collective-permute-start.22 = (f32[512,256]{1,0:T(8,128)S(1)}, f32[512,256]{1,0:T(8,128)S(1)}, u32[]{:S(2)}, u32[]{:S(2)}) collective-permute-start(f32[512,256]{1,0:T(8,128)S(1)} %get-tuple-element.173), channel_id=1, source_target_pairs={{0,8},{4,20},{8,0},{12,28},{16,24},{20,4},{24,16},{28,12},{1,9},{5... | collective-permute-start | bytes 1572872 | tf_op jit(solution)/shard_map/ppermute | solution.py:86
  144.6 18.2 %collective-permute-start.20 = (f32[512,128]{1,0:T(8,128)S(1)}, f32[512,128]{1,0:T(8,128)S(1)}, u32[]{:S(2)}, u32[]{:S(2)}) collective-permute-start(f32[512,128]{1,0:T(8,128)S(1)} %get-tuple-element.166), channel_id=1, source_target_pairs={{0,16},{4,12},{8,24},{12,4},{16,0},{20,28},{24,8},{28,20},{1,17},{... | collective-permute-start | bytes 786440 | tf_op jit(solution)/shard_map/ppermute | solution.py:86
  146.7 21.4 %collective-permute-start.23 = (f32[512,128]{1,0:T(8,128)S(1)}, f32[512,128]{1,0:T(8,128)S(1)}, u32[]{:S(2)}, u32[]{:S(2)}) collective-permute-start(f32[512,128]{1,0:T(8,128)S(1)} %get-tuple-element.175), channel_id=1, source_target_pairs={{0,16},{4,12},{8,24},{12,4},{16,0},{20,28},{24,8},{28,20},{1,17},{... | collective-permute-start | bytes 786440 | tf_op jit(solution)/shard_map/ppermute | solution.py:86
  155.4 12.8 %collective-permute-start.21 = (f32[512,128]{1,0:T(8,128)S(1)}, f32[512,128]{1,0:T(8,128)S(1)}, u32[]{:S(2)}, u32[]{:S(2)}) collective-permute-start(f32[512,128]{1,0:T(8,128)S(1)} %get-tuple-element.171), channel_id=1, source_target_pairs={{0,16},{4,12},{8,24},{12,4},{16,0},{20,28},{24,8},{28,20},{1,17},{... | collective-permute-start | bytes 786440 | tf_op jit(solution)/shard_map/ppermute | solution.py:86
  172.6 17.4 %collective-permute-start.30 = (f32[1024,128]{1,0:T(8,128)S(1)}, f32[1024,128]{1,0:T(8,128)S(1)}, u32[]{:S(2)}, u32[]{:S(2)}) collective-permute-start(f32[1024,128]{1,0:T(8,128)S(1)} %get-tuple-element.197.refs_0_), channel_id=1, source_target_pairs={{0,8},{4,20},{8,0},{12,28},{16,24},{20,4},{24,16},{28,12},{1,9},{5... | collective-permute-start | bytes 1572872 | tf_op jit(solution)/shard_map/ppermute | solution.py:86
  174.4 14.8 %collective-permute-start.28 = (f32[512,128]{1,0:T(8,128)S(1)}, f32[512,128]{1,0:T(8,128)S(1)}, u32[]{:S(2)}, u32[]{:S(2)}) collective-permute-start(f32[512,128]{1,0:T(8,128)S(1)} %get-tuple-element.194.refs_0_), channel_id=1, source_target_pairs={{0,16},{4,12},{8,24},{12,4},{16,0},{20,28},{24,8},{28,20},{1,17},{... | collective-permute-start | bytes 786440 | tf_op jit(solution)/shard_map/ppermute | solution.py:86
  190.1 11.6 %collective-permute-start.31 = (f32[2048,128]{1,0:T(8,128)S(1)}, f32[2048,128]{1,0:T(8,128)}, u32[]{:S(2)}, u32[]{:S(2)}) collective-permute-start(f32[2048,128]{1,0:T(8,128)S(1)} %get-tuple-element.199.refs_4_.refs_5_), channel_id=1, source_target_pairs={{0,4},{4,0},{8,12},{12,8},{16,20},{20,16},{24,28},{28,24},{1,5},{5... | collective-permute-start | bytes 3145736 | tf_op jit(solution)/shard_map/ppermute | solution.py:86
  191.7 17.0 %collective-permute-start.29 = (f32[1024,128]{1,0:T(8,128)}, f32[1024,128]{1,0:T(8,128)}, u32[]{:S(2)}, u32[]{:S(2)}) collective-permute-start(f32[1024,128]{1,0:T(8,128)} %get-tuple-element.196.refs_0_), channel_id=1, source_target_pairs={{0,8},{4,20},{8,0},{12,28},{16,24},{20,4},{24,16},{28,12},{1,9},{5... | collective-permute-start | bytes 1572872 | tf_op jit(solution)/shard_map/ppermute | solution.py:86
  200.7 16.2 %collective-permute-start.35 = (f32[2048,128]{1,0:T(8,128)S(1)}, f32[2048,128]{1,0:T(8,128)S(1)}, u32[]{:S(2)}, u32[]{:S(2)}) collective-permute-start(f32[2048,128]{1,0:T(8,128)S(1)} %get-tuple-element.208.refs_4_.refs_5_), channel_id=1, source_target_pairs={{0,4},{4,0},{8,12},{12,8},{16,20},{20,16},{24,28},{28,24},{1,5},{5... | collective-permute-start | bytes 3145736 | tf_op jit(solution)/shard_map/ppermute | solution.py:86
  209.9 13.6 %collective-permute-start.34 = (f32[2048,128]{1,0:T(8,128)S(1)}, f32[2048,128]{1,0:T(8,128)S(1)}, u32[]{:S(2)}, u32[]{:S(2)}) collective-permute-start(f32[2048,128]{1,0:T(8,128)S(1)} %get-tuple-element.207.refs_4_.refs_5_), channel_id=1, source_target_pairs={{0,4},{4,0},{8,12},{12,8},{16,20},{20,16},{24,28},{28,24},{1,5},{5... | collective-permute-start | bytes 3145736 | tf_op jit(solution)/shard_map/ppermute | solution.py:86
  215.6 14.4 %collective-permute-start.33 = (f32[1024,128]{1,0:T(8,128)S(1)}, f32[1024,128]{1,0:T(8,128)S(1)}, u32[]{:S(2)}, u32[]{:S(2)}) collective-permute-start(f32[1024,128]{1,0:T(8,128)S(1)} %get-tuple-element.206.refs_0_), channel_id=1, source_target_pairs={{0,8},{4,20},{8,0},{12,28},{16,24},{20,4},{24,16},{28,12},{1,9},{5... | collective-permute-start | bytes 1572872 | tf_op jit(solution)/shard_map/ppermute | solution.py:86
  (50 other events, 346.0 us)

commit v4 on v3

--- a/solution.py
+++ b/solution.py
@@ -15,6 +15,7 @@
 HALF = LEAD // 2
 BLOCK = 256
 VMEM_BYTES = 24 * 1024 * 1024
+CHUNKS = 2
 HIGHEST = lax.Precision.HIGHEST
 F32 = jnp.float32
 BF16 = jnp.bfloat16
@@ -31,15 +32,23 @@
     return jax.ShapeDtypeStruct(shape, BF16)
 
 
+def full(shape):
+    return pl.BlockSpec(shape, lambda *at: (0,) * len(shape))
+
+
 class Chain:
     def __init__(self):
         self.token = None
 
-    def __call__(self, name, body, operands, in_specs, outs, out_specs, scalars=(), grid=None, aliases=None):
+    def __call__(self, name, body, operands, in_specs, outs, out_specs, scalars=(), grid=None, aliases=None, scratch=()):
         taken = len(scalars) + len(operands)
         given = len(outs)
         has_token = self.token is not None
         operands, in_specs = list(operands), list(in_specs)
+        if grid is None:
+            grid = (1,)
+            in_specs = [full(x.shape) if spec is WHOLE else spec for x, spec in zip(operands, in_specs)]
+            out_specs = [full(x.shape) for x in outs]
         if has_token:
             operands.append(self.token)
             in_specs.append(ANYWHERE)
@@ -47,9 +56,8 @@
         def kernel(*refs):
             ins, rest = refs[:taken], refs[taken + has_token :]
             rest[given][...] = jnp.zeros((8, PB), F32)
-            body(*ins, *rest[:given])
-
-        token_spec = WHOLE if grid is None else pl.BlockSpec((8, PB), lambda *at: (0, 0))
+            body(*ins, *rest[:given], *rest[given + 1 :])
+
         settings = dict(
             out_shape=tuple(outs) + (f32(8, PB),),
             input_output_aliases=aliases or {},
@@ -57,19 +65,14 @@
             cost_estimate=pl.CostEstimate(flops=1 << 20, bytes_accessed=1 << 16, transcendentals=0),
             name=name,
         )
-        out_specs = tuple(out_specs) + (token_spec,)
-        if grid is None:
-            settings.update(in_specs=in_specs, out_specs=out_specs)
-        else:
-            settings.update(
-                grid_spec=pltpu.PrefetchScalarGridSpec(
-                    num_scalar_prefetch=len(scalars),
-                    grid=grid,
-                    in_specs=in_specs,
-                    out_specs=out_specs,
-                )
-            )
-        results = pl.pallas_call(kernel, **settings)(*scalars, *operands)
+        grid_spec = pltpu.PrefetchScalarGridSpec(
+            num_scalar_prefetch=len(scalars),
+            grid=grid,
+            in_specs=in_specs,
+            out_specs=tuple(out_specs) + (full((8, PB)),),
+            scratch_shapes=scratch,
+        )
+        results = pl.pallas_call(kernel, grid_spec=grid_spec, **settings)(*scalars, *operands)
         self.token = results[-1]
         return results[:-1] if given > 1 else results[0]
 
@@ -123,11 +126,10 @@
     return order
 
 
-def spread(value, count):
+def relay(first, count):
     middle = count // 2
-    first = lax.ppermute(value, "col", [(0, middle)])
     others = [c for c in range(count - 1, 0, -1) if c != middle]
-    return [first] + [lax.ppermute(first, "col", [(middle, c)]) for c in others]
+    return [lax.ppermute(first, "col", [(middle, c)]) for c in others]
 
 
 def exchange(value, row_count):
@@ -170,74 +172,51 @@
     return jnp.where(lax.axis_index("col") == 0, own[...], arrived)
 
 
-def cut_body(child_ref, front_ref, *outs):
+def pack_body(row_count, capacity, sentinel, pieces, owner_ref, offset_ref, child_ref, front_ref, *refs):
+    outs, (out_ref, rows_ref, tag_ref) = refs[:pieces], refs[pieces:]
     at = 0
-    stacked = [(child_ref, child_ref.shape[0]), (front_ref, front_ref.shape[0])]
-    starts = [0, child_ref.shape[0]]
     for out in outs:
-        for (ref, length), start in zip(stacked, starts):
-            lo, hi = max(at, start), min(at + out.shape[0], start + length)
-            if lo < hi:
-                out[lo - at : hi - at, :] = ref[lo - start : hi - start, :]
+        out[...] = front_ref[at : at + out.shape[0], :]
         at += out.shape[0]
-
-
-def place_rows(row_count, capacity, owner_ref, read, write, width, child_count):
+    rows_ref[...] = jnp.zeros_like(rows_ref)
+    tag_ref[...] = jnp.full(tag_ref.shape, sentinel, F32)
+
     def body(i, counts):
         owner = owner_ref[i]
         rank = jnp.int32(0)
         for d in range(row_count):
             rank = jnp.where(owner == d, counts[d], rank)
-        write(owner * capacity + rank, read(i), i)
+        slot = owner * capacity + rank
+        rows_ref[pl.ds(slot, 1), :] = child_ref[pl.ds(i, 1), :]
+        tag_ref[pl.ds(slot, 1), :] = jnp.full((1, PB), offset_ref[i].astype(F32))
         return tuple(counts[d] + (owner == d).astype(jnp.int32) for d in range(row_count))
 
-    lax.fori_loop(0, child_count, body, (jnp.int32(0),) * row_count)
-
-
-def pack_body(row_count, capacity, owner_ref, child_ref, out_ref):
-    out_ref[...] = jnp.zeros_like(out_ref)
-
-    def write(slot, row, i):
-        out_ref[pl.ds(slot, 1), :] = row
-
-    place_rows(
-        row_count, capacity, owner_ref, lambda i: child_ref[pl.ds(i, 1), :], write,
-        out_ref.shape[1], child_ref.shape[0],
-    )
-
-
-def pack_lead_body(row_count, capacity, sentinel, child_count, owner_ref, offset_ref, *refs):
-    own, gots = refs[0], refs[1:-4]
-    out_ref, child_ref, rows_ref, tag_ref = refs[-4:]
-    child_ref[...] = pick(own, gots)
-    rows_ref[...] = jnp.zeros_like(rows_ref)
-    tag_ref[...] = jnp.full(tag_ref.shape, sentinel, F32)
-
-    def write(slot, row, i):
-        rows_ref[pl.ds(slot, 1), :] = row
-        tag_ref[pl.ds(slot, 1), :] = jnp.full((1, PB), offset_ref[i].astype(F32))
-
-    place_rows(
-        row_count, capacity, owner_ref, lambda i: child_ref[pl.ds(i, 1), :], write,
-        LEAD, child_count,
-    )
-    out_ref[:, :LEAD] = rows_ref[...]
-    out_ref[:, LEAD:] = tag_ref[...]
-
-
-def lead_body(child_count, chunk_count, *refs):
-    each = (len(refs) - 6) // chunk_count
-    chunks = [refs[i * each : (i + 1) * each] for i in range(chunk_count)]
-    slots_ref = refs[each * chunk_count]
-    lead_ref, left_ref, place_ref, keep_ref, send_ref = refs[each * chunk_count + 1 :]
-    front = jnp.concatenate([pick(c[0], c[1:]) for c in chunks], axis=0)[child_count:]
-    rows, slots = front.shape[0], slots_ref.shape[0]
-    place = jnp.transpose(slots_ref[:, LEAD:])[0:1, :]
+    lax.fori_loop(0, child_ref.shape[0], body, (jnp.int32(0),) * row_count)
+    width = rows_ref.shape[1]
+    out_ref[:, :width] = rows_ref[...]
+    out_ref[:, width:] = tag_ref[...]
+
+
+def gather_body(rows_in, tags_in, *refs):
+    rows_ref, tag_ref = refs[-2:]
+    rows_ref[...] = rows_in[...]
+    tag_ref[...] = tags_in[...]
+
+
+def lead_body(chunk_count, *refs):
+    each = (len(refs) - 6) // (chunk_count + 1)
+    chunks = [refs[i * each : (i + 1) * each] for i in range(chunk_count + 1)]
+    tag_ref = refs[each * (chunk_count + 1)]
+    lead_ref, left_ref, place_ref, keep_ref, send_ref = refs[-5:]
+    slots_value = pick(chunks[-1][0], chunks[-1][1:])
+    front = jnp.concatenate([pick(c[0], c[1:]) for c in chunks[:-1]], axis=0)
+    rows, slots = front.shape[0], slots_value.shape[0]
     at = lax.broadcasted_iota(jnp.int32, (rows, slots), 0).astype(F32)
-    onehot = jnp.where(at == place, 1.0, 0.0).astype(BF16)
+
+    onehot = jnp.where(at == jnp.transpose(tag_ref[...])[0:1, :], 1.0, 0.0).astype(BF16)
     spots = jnp.concatenate([onehot, onehot, onehot], axis=1)
     place_ref[...] = spots
-    lead = front + dot(spots, jnp.concatenate(parts3(slots_ref[:, :LEAD])[::-1], axis=0))
+    lead = front + dot(spots, jnp.concatenate(parts3(slots_value)[::-1], axis=0))
     lead_ref[...] = lead
     turned = jnp.transpose(lead)
     left_ref[...] = triple(turned, 1)
@@ -268,25 +247,18 @@
         out[...] = keep_ref[:, part] + got_ref[:, part]
 
 
-def product_body(blocks, halves, base_ref, left_ref, place_ref, front_ref, child_ref, *rest):
+def product_body(blocks, count, base_ref, left_ref, place_ref, front_ref, child_ref, *rest):
     del base_ref
-    outs, whole_ref = rest[-1 - halves : -1], rest[-1]
+    outs, whole_ref = rest[-1 - count : -1], rest[-1]
     parts = jnp.concatenate(parts3(child_ref[...])[::-1], axis=0)
     whole = front_ref[...] + dot(place_ref[...], parts)
     whole_ref[...] = whole
     result = dot(left_ref[...], triple(whole, 0))
-    if halves == 1:
-        outs[0][...] = result
-    else:
-        first = pl.program_id(0) < blocks
-
-        @pl.when(first)
+    for at, out in enumerate(outs):
+
+        @pl.when(pl.program_id(0) // blocks == at)
         def _():
-            outs[0][...] = result
-
-        @pl.when(jnp.logical_not(first))
-        def _():
-            outs[1][...] = result
+            out[...] = result
 
 
 def spread_lane(tile, at):
@@ -453,17 +425,14 @@
         before = [(("factor", k - 1), None, 0)] if k else [(("gram", steps - 1), "near", gram)]
         tasks["factor", k] = (3, 5.2, before)
     tasks["finish"] = (3, 2.4, [(("factor", PANELS - 1), None, 0)])
+    tasks["send", 0] = (2, 8.0, [("lead", None, 0)])
+    tasks["keep", 0] = (2, 8.0, [(("send", 0), None, 0)])
     for c in range(chunks):
-        if c == 0:
-            tasks["send", c] = (2, 2.9, [("lead", None, 0)])
-            tasks["keep", c] = (2, 2.9, [(("send", c), None, 0)])
-        else:
-            tasks["send", c] = (2, 4.8, [("lead", None, 0)])
         size = LEAD * width * 4e-6
-        last = ("send", c)
+        last = ("send", 0)
         for t in range(1, steps):
             way = "near" if t == 1 else "far"
-            before = [(last, way, size)] + ([(("keep", c), None, 0)] if t == 1 and c == 0 else [])
+            before = [(last, way, size)] + ([(("keep", 0), None, 0)] if t == 1 else [])
             tasks["split", c, t] = (1, 1.4, before)
             size = size / 2
             last = ("split", c, t)
@@ -477,6 +446,22 @@
     return tasks
 
 
+ORDER = (
+    "G0 P0 G1 K0 S01 S11 G2 S02 S12 E0 A0 E1 A1 J02 E2 J12 E3 F J01 J11 X0 X1 "
+)
+KINDS = {"P": "send", "K": "keep", "S": "split", "G": "gram", "E": "factor", "A": "sum", "J": "join", "X": "project"}
+
+
+def sequence(steps, chunks, width):
+    tasks = task_list(steps, chunks, width)
+    named = []
+    for word in ORDER.split():
+        named.append("finish" if word == "F" else (KINDS[word[0]],) + tuple(int(d) for d in word[1:]))
+    if set(named) == set(tasks) - {"lead"}:
+        return named
+    return [task for task, _ in plan(tasks, 0.09, 0.4, 5.0)]
+
+
 def on_device(front_matrix, child_rows, child_owner, child_offset):
     row_count = lax.axis_size("row")
     col_count = lax.axis_size("col")
@@ -488,39 +473,37 @@
     owner, offset = child_owner[:, 0], child_offset[:, 0]
     run = Chain()
 
-    stacked = child_count + local_rows
-    pieces = 3
-    size = -(-stacked // pieces // 16) * 16
-    sizes = [size] * (pieces - 1) + [stacked - size * (pieces - 1)]
-    own = run(
-        "cut_lead", cut_body, [child_rows, front_matrix],
-        [pl.BlockSpec((child_count, LEAD), lambda i: (0, 0)), pl.BlockSpec((local_rows, LEAD), lambda i: (0, 0))],
-        [f32(n, LEAD) for n in sizes], [pl.BlockSpec((n, LEAD), lambda i: (0, 0)) for n in sizes],
-        grid=(1,),
-    )
-    got = [spread(piece, col_count) for piece in own]
-    packed = run(
-        "pack_children", functools.partial(pack_body, row_count, capacity),
-        [owner, child_rows], [SCALARS, WHOLE], [f32(slots, local_cols)], [WHOLE],
-    )
+    pieces = 2
+    sizes = [local_rows // pieces] * pieces
+    *own, packed = run(
+        "pack_children", functools.partial(pack_body, row_count, capacity, float(local_rows), pieces),
+        [owner, offset, child_rows, front_matrix],
+        [SCALARS, SCALARS, full(child_rows.shape), full((local_rows, LEAD))],
+        [f32(n, LEAD) for n in sizes] + [f32(slots, local_cols + PB)],
+        [full((n, LEAD)) for n in sizes] + [full((slots, local_cols + PB))],
+        grid=(1,), scratch=[pltpu.VMEM((slots, local_cols), F32), pltpu.VMEM((slots, PB), F32)],
+    )
+    got = [[lax.ppermute(piece, "col", [(0, col_count // 2)])] for piece in own]
     child = exchange(packed, row_count)
-    packed, _, _, _ = run(
-        "pack_lead",
-        functools.partial(pack_lead_body, row_count, capacity, float(local_rows), child_count),
-        [owner, offset, own[0]] + got[0], [SCALARS, SCALARS] + [WHOLE] * (1 + len(got[0])),
-        [f32(slots, LEAD + PB), f32(sizes[0], LEAD), f32(slots, LEAD), f32(slots, PB)], [WHOLE] * 4,
-    )
-    lead_child = exchange(packed, row_count)
+    rows, tags = run(
+        "gather_lead", gather_body, [child, child] + [first for first, in got],
+        [full((slots, LEAD)), pl.BlockSpec((slots, PB), lambda i: (0, local_cols // PB))] + [ANYWHERE] * pieces,
+        [f32(slots, LEAD), f32(slots, PB)], [full((slots, LEAD)), full((slots, PB))], grid=(1,),
+    )
+    own.append(rows)
+    got.append([lax.ppermute(rows, "col", [(0, col_count // 2)])])
+    for arrived_here in got:
+        arrived_here.extend(relay(arrived_here[0], col_count))
     operands = [ref for piece, arrived in zip(own, got) for ref in [piece] + arrived]
     lead, left, place, gram, gram_send = run(
-        "lead_setup", functools.partial(lead_body, child_count, pieces),
-        operands + [lead_child], [WHOLE] * (len(operands) + 1),
+        "lead_setup", functools.partial(lead_body, pieces),
+        operands + [tags], [WHOLE] * (len(operands) + 1),
         [f32(local_rows, LEAD), bf16(LEAD, 3 * local_rows), bf16(local_rows, 3 * slots),
          f32(HALF // 2, LEAD + HALF), f32(HALF // 2, LEAD + HALF)],
         [WHOLE] * 5,
     )
 
-    chunks = max(1, min(4, local_cols // (PB * row_count)))
+    chunks = max(1, min(CHUNKS, local_cols // (PB * row_count)))
     width = local_cols // 2 // chunks
     blocks = width // BLOCK
     core = upper_side(0, row_count)
@@ -530,13 +513,12 @@
     gram_got = swap(gram_send, 0, row_count)
     keep, arrived, far = {}, {}, {}
 
-    def make(halves, c, front):
-        at = [(half * chunks + c) * blocks for half in halves]
-        bases = jnp.concatenate([base + jnp.arange(blocks, dtype=jnp.int32) for base in at])
+    def make(half, front):
+        base = (half * chunks * blocks + jnp.arange(chunks * blocks)).astype(jnp.int32)
         operands = [left, place, front_matrix, child]
         in_specs = [
-            pl.BlockSpec(left.shape, lambda i, b: (0, 0)),
-            pl.BlockSpec(place.shape, lambda i, b: (0, 0)),
+            full(left.shape),
+            full(place.shape),
             pl.BlockSpec((local_rows, BLOCK), lambda i, b: (0, b[i])),
             pl.BlockSpec((slots, BLOCK), lambda i, b: (0, b[i])),
         ]
@@ -544,21 +526,23 @@
         if front is not None:
             operands.append(front)
             in_specs.append(ANYWHERE)
-            aliases = {5: len(halves)}
-        out_specs = [pl.BlockSpec((LEAD, BLOCK), lambda i, b: (0, jnp.minimum(i, blocks - 1)))]
-        if len(halves) == 2:
-            out_specs.append(pl.BlockSpec((LEAD, BLOCK), lambda i, b: (0, jnp.maximum(i - blocks, 0))))
+            aliases = {5: chunks}
+
+        def out_block(at):
+            return lambda i, b: (0, jnp.clip(i - at * blocks, 0, blocks - 1))
+
+        out_specs = [pl.BlockSpec((LEAD, BLOCK), out_block(at)) for at in range(chunks)]
         out_specs.append(pl.BlockSpec((local_rows, BLOCK), lambda i, b: (0, b[i])))
         return run(
-            "lead_product", functools.partial(product_body, blocks, len(halves)), operands, in_specs,
-            [f32(LEAD, width)] * len(halves) + [f32(local_rows, local_cols)], out_specs,
-            scalars=[bases], grid=(blocks * len(halves),), aliases=aliases,
+            "lead_product", functools.partial(product_body, blocks, chunks), operands, in_specs,
+            [f32(LEAD, width)] * chunks + [f32(local_rows, local_cols)], out_specs,
+            scalars=[base], grid=(blocks * chunks,), aliases=aliases,
         )
 
     def cast(c, value, step):
         keep[c], arrived[c] = value, swap(value, step, row_count)
 
-    for task, _ in plan(task_list(steps, chunks, width), 0.09, 0.4, 5.0):
+    for task in sequence(steps, chunks, width):
         kind, c = task[0], task[1]
         if task == "lead":
             continue
@@ -578,13 +562,13 @@
                 [WHOLE] * len(operands), [f32(LEAD, LEAD)], [WHOLE],
             )
         elif kind == "send":
-            if c == 0:
-                send, front = make([1 - core], c, front)
-            else:
-                send, keep[c], front = make([1 - core, core], c, front)
-            arrived[c] = swap(send, 0, row_count)
+            *made, front = make(1 - core, front)
+            for at, value in enumerate(made):
+                arrived[at] = swap(value, 0, row_count)
         elif kind == "keep":
-            keep[c], front = make([core], c, front)
+            *made, front = make(core, front)
+            for at, value in enumerate(made):
+                keep[at] = value
         elif kind == "split":
             t = task[2]
             shape = f32(LEAD, keep[c].shape[1] // 2)
@@ -597,21 +581,29 @@
             value = run("add_shard", add_body, [keep[c], arrived[c]], [WHOLE] * 2, [f32(*keep[c].shape)], [WHOLE])
             cast(c, value, steps - 1)
         elif kind == "join":
-            rows = keep[c].shape[0]
-            value = run("join_pieces", join_body, [keep[c], arrived[c]], [WHOLE] * 2, [f32(2 * rows, PB)], [WHOLE])
+            rows, value_width = keep[c].shape
+            value = run("join_pieces", join_body, [keep[c], arrived[c]], [WHOLE] * 2, [f32(2 * rows, value_width)], [WHOLE])
             cast(c, value, task[2] - 1)
         elif kind == "project":
             starts = [(half * chunks + c) * blocks for half in (core, 1 - core)]
             columns = jnp.concatenate([s + jnp.arange(blocks, dtype=jnp.int32) for s in starts])
             scalars = [jnp.concatenate([columns, order[0], order[1]])]
-            near = 2 * blocks
-            far_at = near + 2 * blocks
+            near, per = 2 * blocks, keep[c].shape[1] // PB
+            far_at = near + 2 * blocks // per
 
             def near_piece(odd):
-                return lambda i, p: (p[near + 2 * jnp.minimum(i, blocks - 1) + odd], 0)
+                def at(i, p):
+                    place = 2 * jnp.minimum(i, blocks - 1) + odd
+                    return p[near + place // per], place % per
+
+                return at
 
             def far_piece(odd):
-                return lambda i, p: (p[far_at + 2 * jnp.maximum(i - blocks, 0) + odd], 0)
+                def at(i, p):
+                    place = 2 * jnp.maximum(i - blocks, 0) + odd
+                    return p[far_at + place // per], place % per
+
+                return at
 
             operands = [top, bottom, basis, keep[c], keep[c], arrived[c], arrived[c], front]
             in_specs = [

time: 244 us -> 232 us (0.951)
  waiting for transfers between devices: 67.1 us -> 81.1 us
  blocking collectives: 11.8 us -> 0 us
  Pallas kernels: 89.3 us -> 81.4 us
  starting transfers between devices: 43 us -> 39.7 us
    all_to_all x1 -> x0, blocking collectives: 11.8 us -> none  [exchange(): lax.all_to_all(shaped, 'row', split_axis=0, concat_axis=0, tiled=True)]
    ppermute x28 -> x16, waiting for transfers between devices: 38.1 us -> 47.7 us  [swap(): return lax.ppermute(value, 'row', pairs)]
    pallas_call x41 -> x25, Pallas kernels: 89.3 us -> 81.4 us  [__call__(): pl.pallas_call(kernel, grid_spec=grid_spec, **settings)(*scalars, *operands)]
    ppermute x28 -> x16, starting transfers between devices: 24.6 us -> 22 us  [swap(): return lax.ppermute(value, 'row', pairs)]
    ppermute x9, waiting for transfers between devices: 28.9 us -> 31.4 us  [the longest x2 17.6 us: on_device(): got = [[lax.ppermute(piece, 'col', [(0, col_count // 2)])] for piece in own]]
    unnamed x72 -> x56, local copies, waits for them, and re-layouts: 27.6 us -> 25.8 us
  transfers between devices with their start and end apart: 38 -> 26, of which waited for: 18 -> 15; matrix products, arithmetic and copies ran while one was open for 0% -> 0% of each run, Pallas kernels for 31% -> 23%
where the time goes in v4:
time: 232 us; the launch traced here: 230 us
  Pallas kernels  81.4 us (35%)
  waiting for transfers between devices  81.1 us (35%)
  starting transfers between devices  39.7 us (17%)
  local copies, waits for them, and re-layouts  26.5 us (11%)
    pallas_call x25, Pallas kernels, __call__(): pl.pallas_call(kernel, grid_spec=grid_spec, **settings)(*scalars, *operands)  81.4 us
    ppermute x16, waiting for transfers between devices, swap(): return lax.ppermute(value, 'row', pairs)  47.7 us
    unnamed x56, local copies, waits for them, and re-layouts  25.8 us
    ppermute x16, starting transfers between devices, swap(): return lax.ppermute(value, 'row', pairs)  22 us
    ppermute x2, waiting for transfers between devices, on_device(): got = [[lax.ppermute(piece, 'col', [(0, col_count // 2)])] for piece in own]  17.6 us
    ppermute x6, waiting for transfers between devices, relay(): return [lax.ppermute(first, 'col', [(middle, c)]) for c in others]  12.3 us
    ppermute x6, starting transfers between devices, relay(): return [lax.ppermute(first, 'col', [(middle, c)]) for c in others]  9.13 us
  transfers between devices with their start and end apart: 26, of which 15 were waited for; matrix products, arithmetic and copies ran while one was open for 0% of the time, Pallas kernels for 23%

profile of v4, /device:TPU:21, one launch (start us, length us, event | category | flops | bytes accessed | tf_op | source)
XLA Modules:
  0.0 229.8 jit_solution(16400480041042299488)
XLA Ops:
  0.6 2.8 %copy-done = f32[384,4096]{1,0:T(8,128)S(1)} copy-done((f32[384,4096]{1,0:T(8,128)S(1)}, f32[384,4096]{1,0:T(8,128)}, u32[]{:S(2)}) %copy-start) | copy-done | bytes 6291480
  10.4 4.5 %all-to-all-start = ((f32[8,16,4224]{2,1,0:T(8,128)}), f32[8,16,4224]{2,1,0:T(8,128)S(1)}, u32[]{:S(2)}, u32[]{:S(2)}) async-start(f32[8,16,4224]{2,1,0:T(8,128)} %bitcast.12), calls=%async_computation | async-start | bytes 4325376 | tf_op jit(solution)/shard_map/all_to_all | solution.py:138
  17.5 10.5 %collective-permute-done.refs_2_.refs_1_ = f32[192,512]{1,0:T(8,128)S(1)} collective-permute-done((f32[192,512]{1,0:T(8,128)S(1)}, f32[192,512]{1,0:T(8,128)S(1)}, u32[]{:S(2)}, u32[]{:S(2)}) %collective-permute-start) | collective-permute-done | bytes 393248 | tf_op jit(solution)/shard_map/ppermute | solution.py:486
  29.3 7.1 %collective-permute-done.3.refs_3_.refs_5_ = f32[192,512]{1,0:T(8,128)S(1)} collective-permute-done((f32[192,512]{1,0:T(8,128)}, f32[192,512]{1,0:T(8,128)S(1)}, u32[]{:S(2)}, u32[]{:S(2)}) %collective-permute-start.3) | collective-permute-done | bytes 393248 | tf_op jit(solution)/shard_map/ppermute | solution.py:486
  50.1 6.7 %collective-permute-done.4.refs_6_ = f32[192,512]{1,0:T(8,128)S(1)} collective-permute-done((f32[192,512]{1,0:T(8,128)S(1)}, f32[192,512]{1,0:T(8,128)S(1)}, u32[]{:S(2)}, u32[]{:S(2)}) %collective-permute-start.4) | collective-permute-done | bytes 393248 | tf_op jit(solution)/shard_map/ppermute | solution.py:132
  56.8 5.6 %collective-permute-done.7.refs_10_ = f32[128,512]{1,0:T(8,128)S(1)} collective-permute-done((f32[128,512]{1,0:T(8,128)S(1)}, f32[128,512]{1,0:T(8,128)S(1)}, u32[]{:S(2)}, u32[]{:S(2)}) %collective-permute-start.7) | collective-permute-done | bytes 262176 | tf_op jit(solution)/shard_map/ppermute | solution.py:132
  65.4 2.9 %lead_setup.1 = (f32[384,512]{1,0:T(8,128)S(1)}, bf16[512,1152]{1,0:T(8,128)(2,1)S(1)}, bf16[384,384]{1,0:T(8,128)(2,1)S(1)}, f32[128,768]{1,0:T(8,128)S(1)}, f32[128,768]{1,0:T(8,128)}, /*index=5*/f32[8,128]{1,0:T(8,128)S(1)}) custom-call(f32[192,512]{1,0:T(8,128)S(1)} %copy-done.19, f32[192,512]{1,0:T(8,128)S(1)} %copy-done.7, ...), custom_call_target="tpu_custom_call" | custom-call | flops 1048576 | bytes 65536 | tf_op jit(solution)/shard_map/lead_setup/pallas_call | solution.py:75
  70.6 3.6 %collective-permute-start.9 = (f32[128,768]{1,0:T(8,128)}, f32[128,768]{1,0:T(8,128)}, u32[]{:S(2)}, u32[]{:S(2)}) collective-permute-start(f32[128,768]{1,0:T(8,128)} %get-tuple-element.80), channel_id=1, source_target_pairs={{0,4},{4,0},{8,12},{12,8},{16,20},{20,16},{24,28},{28,24},{1,5},{5... | collective-permute-start | bytes 1179656 | tf_op jit(solution)/shard_map/ppermute | solution.py:89
  78.6 2.8 %copy-done.1 = f32[384,4096]{1,0:T(8,128)S(1)} copy-done((f32[384,4096]{1,0:T(8,128)S(1)}, f32[384,4096]{1,0:T(8,128)}, u32[]{:S(2)}) %copy-start.1) | copy-done | bytes 6291480
  82.4 10.6 %lead_product.2 = (f32[512,1024]{1,0:T(8,128)}, f32[512,1024]{1,0:T(8,128)}, f32[384,4096]{1,0:T(8,128)}, f32[8,128]{1,0:T(8,128)S(1)}) custom-call(s32[8]{0:T(128)S(1)} %iota_add_fusion.3.refs_0_, bf16[512,1152]{1,0:T(8,128)(2,1)S(1)} %get-tuple-element.83.refs_1_, bf16[384,384]{1,0:T(8,128)(2,1)S(1)} %copy-done.13, f32[384,4096]{1,0:T(8,128)S(1)} %copy-done.1, ...), custom_call_target="tpu_custom_call" | custom-call | flops 1048576 | bytes 65536 | tf_op jit(solution)/shard_map/lead_product/pallas_call | solution.py:75
  93.8 6.9 %collective-permute-done.10.refs_1_ = f32[128,768]{1,0:T(8,128)} collective-permute-done((f32[128,768]{1,0:T(8,128)}, f32[128,768]{1,0:T(8,128)}, u32[]{:S(2)}, u32[]{:S(2)}) %collective-permute-start.10) | collective-permute-done | bytes 393248 | tf_op jit(solution)/shard_map/ppermute | solution.py:89
  105.6 10.5 %lead_product.3 = (f32[512,1024]{1,0:T(8,128)S(1)}, f32[512,1024]{1,0:T(8,128)S(1)}, f32[384,4096]{1,0:T(8,128)}, f32[8,128]{1,0:T(8,128)S(1)}) custom-call(s32[8]{0:T(128)S(1)} %iota_add_fusion.2.refs_0_, bf16[512,1152]{1,0:T(8,128)(2,1)S(1)} %get-tuple-element.83.refs_1_, bf16[384,384]{1,0:T(8,128)(2,1)S(1)} %copy-done.14, ...), custom_call_target="tpu_custom_call", output_to_operand_aliasing={{2}: (5, {})} | custom-call | flops 1048576 | bytes 65536 | tf_op jit(solution)/shard_map/lead_product/pallas_call | solution.py:75
  123.5 9.7 %collective-permute-done.11.refs_1_ = f32[128,768]{1,0:T(8,128)S(1)} collective-permute-done((f32[128,768]{1,0:T(8,128)S(1)}, f32[128,768]{1,0:T(8,128)S(1)}, u32[]{:S(2)}, u32[]{:S(2)}) %collective-permute-start.11) | collective-permute-done | bytes 393248 | tf_op jit(solution)/shard_map/ppermute | solution.py:89
  133.3 2.8 %collective-permute-done.16.refs_1_ = f32[512,512]{1,0:T(8,128)S(1)} collective-permute-done((f32[512,512]{1,0:T(8,128)S(1)}, f32[512,512]{1,0:T(8,128)S(1)}, u32[]{:S(2)}, u32[]{:S(2)}) %collective-permute-start.16) | collective-permute-done | bytes 1048608 | tf_op jit(solution)/shard_map/ppermute | solution.py:89
  138.6 14.0 %collective-permute-done.15.refs_1_ = f32[512,512]{1,0:T(8,128)S(1)} collective-permute-done((f32[512,512]{1,0:T(8,128)S(1)}, f32[512,512]{1,0:T(8,128)S(1)}, u32[]{:S(2)}, u32[]{:S(2)}) %collective-permute-start.15) | collective-permute-done | bytes 1048608 | tf_op jit(solution)/shard_map/ppermute | solution.py:89
  158.8 5.5 %eliminate_panel.4 = (f32[512,512]{1,0:T(8,128)S(1)}, f32[8,128]{1,0:T(8,128)S(1)}) custom-call(f32[128,768]{1,0:T(8,128)S(1)} %get-tuple-element.97.refs_0_, f32[128,768]{1,0:T(8,128)S(1)} %collective-permute-done.14.refs_1_, f32[8,128]{1,0:T(8,128)S(1)} %get-tuple-element.104.refs_2_), custom_call_target="tpu_custom_call" | custom-call | flops 1048576 | bytes 65536 | tf_op jit(solution)/shard_map/eliminate_panel/pallas_call | solution.py:75
  166.2 5.2 %eliminate_panel.5 = (f32[512,512]{1,0:T(8,128)S(1)}, f32[8,128]{1,0:T(8,128)S(1)}) custom-call(f32[512,512]{1,0:T(8,128)S(1)} %get-tuple-element.105.refs_0_, f32[8,128]{1,0:T(8,128)S(1)} %get-tuple-element.109.refs_1_), custom_call_target="tpu_custom_call" | custom-call | flops 1048576 | bytes 65536 | tf_op jit(solution)/shard_map/eliminate_panel/pallas_call | solution.py:75
  173.3 5.1 %eliminate_panel.6 = (f32[512,512]{1,0:T(8,128)S(1)}, f32[8,128]{1,0:T(8,128)S(1)}) custom-call(f32[512,512]{1,0:T(8,128)S(1)} %get-tuple-element.110.refs_0_, f32[8,128]{1,0:T(8,128)S(1)} %get-tuple-element.116.refs_1_), custom_call_target="tpu_custom_call" | custom-call | flops 1048576 | bytes 65536 | tf_op jit(solution)/shard_map/eliminate_panel/pallas_call | solution.py:75
  178.4 3.9 %collective-permute-done.20.refs_1_ = f32[512,256]{1,0:T(8,128)S(1)} collective-permute-done((f32[512,256]{1,0:T(8,128)S(1)}, f32[512,256]{1,0:T(8,128)S(1)}, u32[]{:S(2)}, u32[]{:S(2)}) %collective-permute-start.20) | collective-permute-done | bytes 524320 | tf_op jit(solution)/shard_map/ppermute | solution.py:89
  182.5 4.3 %eliminate_panel.7 = (f32[512,512]{1,0:T(8,128)S(1)}, f32[8,128]{1,0:T(8,128)S(1)}) custom-call(f32[512,512]{1,0:T(8,128)S(1)} %get-tuple-element.117.refs_0_, f32[8,128]{1,0:T(8,128)S(1)} %get-tuple-element.120.refs_1_), custom_call_target="tpu_custom_call" | custom-call | flops 1048576 | bytes 65536 | tf_op jit(solution)/shard_map/eliminate_panel/pallas_call | solution.py:75
  192.4 3.6 %collective-permute-start.24 = (f32[2048,256]{1,0:T(8,128)}, f32[2048,256]{1,0:T(8,128)}, u32[]{:S(2)}, u32[]{:S(2)}) collective-permute-start(f32[2048,256]{1,0:T(8,128)} %get-tuple-element.132.refs_4_.refs_5_), channel_id=1, source_target_pairs={{0,4},{4,0},{8,12},{12,8},{16,20},{20,16},{24,28},{28,24},{1,5},{5... | collective-permute-start | bytes 6291464 | tf_op jit(solution)/shard_map/ppermute | solution.py:89
  196.0 5.8 %collective-permute-done.21.refs_1_ = f32[1024,256]{1,0:T(8,128)S(1)} collective-permute-done((f32[1024,256]{1,0:T(8,128)S(1)}, f32[1024,256]{1,0:T(8,128)S(1)}, u32[]{:S(2)}, u32[]{:S(2)}) %collective-permute-start.21) | collective-permute-done | bytes 1048608 | tf_op jit(solution)/shard_map/ppermute | solution.py:89
  205.8 12.0 %project_columns.2 = (f32[512,4096]{1,0:T(8,128)}, f32[384,4096]{1,0:T(8,128)}, f32[8,128]{1,0:T(8,128)S(1)}) custom-call(s32[16]{0:T(128)S(1)} %get-tuple-element.141.refs_0_, bf16[256,768]{1,0:T(8,128)(2,1)S(1)} %copy-done.11, bf16[256,1536]{1,0:T(8,128)(2,1)S(1)} %copy-done.4, ...), custom_call_target="tpu_custom_call", output_to_operand_aliasing={{1}: (8, {})} | custom-call | flops 1048576 | bytes 65536 | tf_op jit(solution)/shard_map/project_columns/pallas_call | solution.py:75
  217.8 12.0 %project_columns.3 = (f32[512,4096]{1,0:T(8,128)}, f32[384,4096]{1,0:T(8,128)}, f32[8,128]{1,0:T(8,128)}) custom-call(s32[16]{0:T(128)S(1)} %get-tuple-element.142.refs_0_, bf16[256,768]{1,0:T(8,128)(2,1)S(1)} %copy-done.11, bf16[256,1536]{1,0:T(8,128)(2,1)S(1)} %copy-done.4, ...), custom_call_target="tpu_custom_call", output_to_operand_aliasing={{1}: (8, {}), {0}: (9, {})} | custom-call | flops 1048576 | bytes 65536 | tf_op jit(solution)/shard_map/project_columns/pallas_call | solution.py:75
  (116 shorter events, 70.6 us)
Async XLA Ops:
  10.4 28.1 %all-to-all-start = ((f32[8,16,4224]{2,1,0:T(8,128)}), f32[8,16,4224]{2,1,0:T(8,128)S(1)}, u32[]{:S(2)}, u32[]{:S(2)}) async-start(f32[8,16,4224]{2,1,0:T(8,128)} %bitcast.12), calls=%async_computation | async-start | bytes 4325376 | tf_op jit(solution)/shard_map/all_to_all | solution.py:138
  14.9 13.1 %collective-permute-start = (f32[192,512]{1,0:T(8,128)S(1)}, f32[192,512]{1,0:T(8,128)S(1)}, u32[]{:S(2)}, u32[]{:S(2)}) collective-permute-start(f32[192,512]{1,0:T(8,128)S(1)} %get-tuple-element.72.refs_0_), channel_id=1, source_target_pairs={{0,2},{4,6},{8,10},{12,14},{16,18},{20,22},{24,26},{28,30}} | collective-permute-start | bytes 1179656 | tf_op jit(solution)/shard_map/ppermute | solution.py:486
  16.2 20.3 %collective-permute-start.3 = (f32[192,512]{1,0:T(8,128)}, f32[192,512]{1,0:T(8,128)S(1)}, u32[]{:S(2)}, u32[]{:S(2)}) collective-permute-start(f32[192,512]{1,0:T(8,128)} %copy-done.20), channel_id=1, source_target_pairs={{0,2},{4,6},{8,10},{12,14},{16,18},{20,22},{24,26},{28,30}} | collective-permute-start | bytes 1179656 | tf_op jit(solution)/shard_map/ppermute | solution.py:486
  28.0 20.0 %collective-permute-start.2 = (f32[192,512]{1,0:T(8,128)S(1)}, f32[192,512]{1,0:T(8,128)S(1)}, u32[]{:S(2)}, u32[]{:S(2)}) collective-permute-start(f32[192,512]{1,0:T(8,128)S(1)} %collective-permute-done.refs_2_.refs_1_), channel_id=1, source_target_pairs={{2,1},{6,5},{10,9},{14,13},{18,17},{22,21},{26,25},{30,29}} | collective-permute-start | bytes 1179656 | tf_op jit(solution)/shard_map/ppermute | solution.py:132
  38.5 8.1 %collective-permute-start.6 = (f32[128,512]{1,0:T(8,128)S(1)}, f32[128,512]{1,0:T(8,128)S(1)}, u32[]{:S(2)}, u32[]{:S(2)}) collective-permute-start(f32[128,512]{1,0:T(8,128)S(1)} %get-tuple-element.76.refs_8_), channel_id=1, source_target_pairs={{0,2},{4,6},{8,10},{12,14},{16,18},{20,22},{24,26},{28,30}} | collective-permute-start | bytes 786440 | tf_op jit(solution)/shard_map/ppermute | solution.py:494
  40.0 10.1 %collective-permute-start.1 = (f32[192,512]{1,0:T(8,128)S(1)}, f32[192,512]{1,0:T(8,128)S(1)}, u32[]{:S(2)}, u32[]{:S(2)}) collective-permute-start(f32[192,512]{1,0:T(8,128)S(1)} %collective-permute-done.refs_2_.refs_1_), channel_id=1, source_target_pairs={{2,3},{6,7},{10,11},{14,15},{18,19},{22,23},{26,27},{30,31}} | collective-permute-start | bytes 1179656 | tf_op jit(solution)/shard_map/ppermute | solution.py:132
  42.6 7.5 %collective-permute-start.5 = (f32[192,512]{1,0:T(8,128)S(1)}, f32[192,512]{1,0:T(8,128)S(1)}, u32[]{:S(2)}, u32[]{:S(2)}) collective-permute-start(f32[192,512]{1,0:T(8,128)S(1)} %collective-permute-done.3.refs_3_.refs_5_), channel_id=1, source_target_pairs={{2,1},{6,5},{10,9},{14,13},{18,17},{22,21},{26,25},{30,29}} | collective-permute-start | bytes 1179656 | tf_op jit(solution)/shard_map/ppermute | solution.py:132
  43.9 12.8 %collective-permute-start.4 = (f32[192,512]{1,0:T(8,128)S(1)}, f32[192,512]{1,0:T(8,128)S(1)}, u32[]{:S(2)}, u32[]{:S(2)}) collective-permute-start(f32[192,512]{1,0:T(8,128)S(1)} %collective-permute-done.3.refs_3_.refs_5_), channel_id=1, source_target_pairs={{2,3},{6,7},{10,11},{14,15},{18,19},{22,23},{26,27},{30,31}} | collective-permute-start | bytes 1179656 | tf_op jit(solution)/shard_map/ppermute | solution.py:132
  46.7 10.1 %collective-permute-start.8 = (f32[128,512]{1,0:T(8,128)S(1)}, f32[128,512]{1,0:T(8,128)S(1)}, u32[]{:S(2)}, u32[]{:S(2)}) collective-permute-start(f32[128,512]{1,0:T(8,128)S(1)} %collective-permute-done.6.refs_9_), channel_id=1, source_target_pairs={{2,1},{6,5},{10,9},{14,13},{18,17},{22,21},{26,25},{30,29}} | collective-permute-start | bytes 786440 | tf_op jit(solution)/shard_map/ppermute | solution.py:132
  48.7 13.6 %collective-permute-start.7 = (f32[128,512]{1,0:T(8,128)S(1)}, f32[128,512]{1,0:T(8,128)S(1)}, u32[]{:S(2)}, u32[]{:S(2)}) collective-permute-start(f32[128,512]{1,0:T(8,128)S(1)} %collective-permute-done.6.refs_9_), channel_id=1, source_target_pairs={{2,3},{6,7},{10,11},{14,15},{18,19},{22,23},{26,27},{30,31}} | collective-permute-start | bytes 786440 | tf_op jit(solution)/shard_map/ppermute | solution.py:132
  93.0 23.1 %collective-permute-start.13 = (f32[512,1024]{1,0:T(8,128)}, f32[512,1024]{1,0:T(8,128)}, u32[]{:S(2)}, u32[]{:S(2)}) collective-permute-start(f32[512,1024]{1,0:T(8,128)} %get-tuple-element.93), channel_id=1, source_target_pairs={{0,4},{4,0},{8,12},{12,8},{16,20},{20,16},{24,28},{28,24},{1,5},{5... | collective-permute-start | bytes 6291464 | tf_op jit(solution)/shard_map/ppermute | solution.py:89
  93.3 25.0 %collective-permute-start.12 = (f32[512,1024]{1,0:T(8,128)}, f32[512,1024]{1,0:T(8,128)}, u32[]{:S(2)}, u32[]{:S(2)}) collective-permute-start(f32[512,1024]{1,0:T(8,128)} %get-tuple-element.91), channel_id=1, source_target_pairs={{0,4},{4,0},{8,12},{12,8},{16,20},{20,16},{24,28},{28,24},{1,5},{5... | collective-permute-start | bytes 6291464 | tf_op jit(solution)/shard_map/ppermute | solution.py:89
  93.5 7.2 %collective-permute-start.10 = (f32[128,768]{1,0:T(8,128)}, f32[128,768]{1,0:T(8,128)}, u32[]{:S(2)}, u32[]{:S(2)}) collective-permute-start(f32[128,768]{1,0:T(8,128)} %get-tuple-element.82.refs_0_), channel_id=1, source_target_pairs={{0,8},{4,20},{8,0},{12,28},{16,24},{20,4},{24,16},{28,12},{1,9},{5... | collective-permute-start | bytes 1179656 | tf_op jit(solution)/shard_map/ppermute | solution.py:89
  117.9 18.2 %collective-permute-start.16 = (f32[512,512]{1,0:T(8,128)S(1)}, f32[512,512]{1,0:T(8,128)S(1)}, u32[]{:S(2)}, u32[]{:S(2)}) collective-permute-start(f32[512,512]{1,0:T(8,128)S(1)} %get-tuple-element.101), channel_id=1, source_target_pairs={{0,8},{4,20},{8,0},{12,28},{16,24},{20,4},{24,16},{28,12},{1,9},{5... | collective-permute-start | bytes 3145736 | tf_op jit(solution)/shard_map/ppermute | solution.py:89
  120.1 32.4 %collective-permute-start.15 = (f32[512,512]{1,0:T(8,128)S(1)}, f32[512,512]{1,0:T(8,128)S(1)}, u32[]{:S(2)}, u32[]{:S(2)}) collective-permute-start(f32[512,512]{1,0:T(8,128)S(1)} %get-tuple-element.99), channel_id=1, source_target_pairs={{0,8},{4,20},{8,0},{12,28},{16,24},{20,4},{24,16},{28,12},{1,9},{5... | collective-permute-start | bytes 3145736 | tf_op jit(solution)/shard_map/ppermute | solution.py:89
  121.3 12.0 %collective-permute-start.11 = (f32[128,768]{1,0:T(8,128)S(1)}, f32[128,768]{1,0:T(8,128)S(1)}, u32[]{:S(2)}, u32[]{:S(2)}) collective-permute-start(f32[128,768]{1,0:T(8,128)S(1)} %get-tuple-element.87.refs_0_), channel_id=1, source_target_pairs={{0,16},{4,12},{8,24},{12,4},{16,0},{20,28},{24,8},{28,20},{1,17},{... | collective-permute-start | bytes 1179656 | tf_op jit(solution)/shard_map/ppermute | solution.py:89
  136.2 28.1 %collective-permute-start.17 = (f32[512,256]{1,0:T(8,128)S(1)}, f32[512,256]{1,0:T(8,128)S(1)}, u32[]{:S(2)}, u32[]{:S(2)}) collective-permute-start(f32[512,256]{1,0:T(8,128)S(1)} %get-tuple-element.107), channel_id=1, source_target_pairs={{0,16},{4,12},{8,24},{12,4},{16,0},{20,28},{24,8},{28,20},{1,17},{... | collective-permute-start | bytes 1572872 | tf_op jit(solution)/shard_map/ppermute | solution.py:89
  152.7 18.7 %collective-permute-start.19 = (f32[512,256]{1,0:T(8,128)S(1)}, f32[512,256]{1,0:T(8,128)S(1)}, u32[]{:S(2)}, u32[]{:S(2)}) collective-permute-start(f32[512,256]{1,0:T(8,128)S(1)} %get-tuple-element.113), channel_id=1, source_target_pairs={{0,16},{4,12},{8,24},{12,4},{16,0},{20,28},{24,8},{28,20},{1,17},{... | collective-permute-start | bytes 1572872 | tf_op jit(solution)/shard_map/ppermute | solution.py:89
  164.4 8.7 %collective-permute-start.18 = (f32[512,256]{1,0:T(8,128)S(1)}, f32[512,256]{1,0:T(8,128)S(1)}, u32[]{:S(2)}, u32[]{:S(2)}) collective-permute-start(f32[512,256]{1,0:T(8,128)S(1)} %get-tuple-element.111.refs_0_), channel_id=1, source_target_pairs={{0,16},{4,12},{8,24},{12,4},{16,0},{20,28},{24,8},{28,20},{1,17},{... | collective-permute-start | bytes 1572872 | tf_op jit(solution)/shard_map/ppermute | solution.py:89
  171.4 10.9 %collective-permute-start.20 = (f32[512,256]{1,0:T(8,128)S(1)}, f32[512,256]{1,0:T(8,128)S(1)}, u32[]{:S(2)}, u32[]{:S(2)}) collective-permute-start(f32[512,256]{1,0:T(8,128)S(1)} %get-tuple-element.118.refs_0_), channel_id=1, source_target_pairs={{0,16},{4,12},{8,24},{12,4},{16,0},{20,28},{24,8},{28,20},{1,17},{... | collective-permute-start | bytes 1572872 | tf_op jit(solution)/shard_map/ppermute | solution.py:89
  173.1 17.8 %collective-permute-start.22 = (f32[1024,256]{1,0:T(8,128)S(1)}, f32[1024,256]{1,0:T(8,128)S(1)}, u32[]{:S(2)}, u32[]{:S(2)}) collective-permute-start(f32[1024,256]{1,0:T(8,128)S(1)} %get-tuple-element.128.refs_0_), channel_id=1, source_target_pairs={{0,8},{4,20},{8,0},{12,28},{16,24},{20,4},{24,16},{28,12},{1,9},{5... | collective-permute-start | bytes 3145736 | tf_op jit(solution)/shard_map/ppermute | solution.py:89
  182.4 19.4 %collective-permute-start.21 = (f32[1024,256]{1,0:T(8,128)S(1)}, f32[1024,256]{1,0:T(8,128)S(1)}, u32[]{:S(2)}, u32[]{:S(2)}) collective-permute-start(f32[1024,256]{1,0:T(8,128)S(1)} %get-tuple-element.127.refs_0_), channel_id=1, source_target_pairs={{0,8},{4,20},{8,0},{12,28},{16,24},{20,4},{24,16},{28,12},{1,9},{5... | collective-permute-start | bytes 3145736 | tf_op jit(solution)/shard_map/ppermute | solution.py:89
  192.4 11.3 %collective-permute-start.24 = (f32[2048,256]{1,0:T(8,128)}, f32[2048,256]{1,0:T(8,128)}, u32[]{:S(2)}, u32[]{:S(2)}) collective-permute-start(f32[2048,256]{1,0:T(8,128)} %get-tuple-element.132.refs_4_.refs_5_), channel_id=1, source_target_pairs={{0,4},{4,0},{8,12},{12,8},{16,20},{20,16},{24,28},{28,24},{1,5},{5... | collective-permute-start | bytes 6291464 | tf_op jit(solution)/shard_map/ppermute | solution.py:89
  201.9 15.9 %collective-permute-start.23 = (f32[2048,256]{1,0:T(8,128)S(1)}, f32[2048,256]{1,0:T(8,128)}, u32[]{:S(2)}, u32[]{:S(2)}) collective-permute-start(f32[2048,256]{1,0:T(8,128)S(1)} %get-tuple-element.131.refs_4_.refs_5_), channel_id=1, source_target_pairs={{0,4},{4,0},{8,12},{12,8},{16,20},{20,16},{24,28},{28,24},{1,5},{5... | collective-permute-start | bytes 6291464 | tf_op jit(solution)/shard_map/ppermute | solution.py:89
  (30 other events, 119.9 us)

commit v5 on v4

--- a/solution.py
+++ b/solution.py
@@ -14,14 +14,15 @@
 LEAD = PB * PANELS
 HALF = LEAD // 2
 BLOCK = 256
-VMEM_BYTES = 24 * 1024 * 1024
-CHUNKS = 2
+VMEM_BYTES = 32 * 1024 * 1024
+CHUNKS = 4
 HIGHEST = lax.Precision.HIGHEST
 F32 = jnp.float32
 BF16 = jnp.bfloat16
 WHOLE = pl.BlockSpec(memory_space=pltpu.VMEM)
 SCALARS = pl.BlockSpec(memory_space=pltpu.SMEM)
 ANYWHERE = pl.BlockSpec(memory_space=pl.ANY)
+IN_HBM = pl.BlockSpec(memory_space=pltpu.HBM)
 
 
 def f32(*shape):
@@ -40,41 +41,50 @@
     def __init__(self):
         self.token = None
 
-    def __call__(self, name, body, operands, in_specs, outs, out_specs, scalars=(), grid=None, aliases=None, scratch=()):
-        taken = len(scalars) + len(operands)
-        given = len(outs)
-        has_token = self.token is not None
-        operands, in_specs = list(operands), list(in_specs)
-        if grid is None:
-            grid = (1,)
-            in_specs = [full(x.shape) if spec is WHOLE else spec for x, spec in zip(operands, in_specs)]
-            out_specs = [full(x.shape) for x in outs]
+    def __call__(self, name, body, operands, in_specs, outs, out_specs, scalars=(), grid=(1,), aliases=None, scratch=()):
+        count, has_token = len(operands), self.token is not None
+        smem = [at for at, spec in enumerate(in_specs) if spec is SCALARS]
+        moved = [at for at, spec in enumerate(in_specs) if spec is not SCALARS and spec is not ANYWHERE]
+        blocks_in = [full(operands[at].shape) if in_specs[at] is WHOLE else in_specs[at] for at in moved]
+        blocks_out = [full(out.shape) if spec is WHOLE else spec for out, spec in zip(outs, out_specs)]
+        first = len(scalars)
+
+        def kernel(*refs):
+            counts, ins = refs[:first], refs[first : first + count]
+            results = refs[first + count + has_token :][: len(outs)]
+            held = refs[first + count + has_token + len(outs) + 1 :]
+
+            def located(spec):
+                return pl.BlockSpec(spec.block_shape, lambda *at: spec.index_map(*at, *counts))
+
+            def step(*blocks):
+                body(*counts, *[ins[at] for at in smem], *blocks, *held)
+
+            pltpu.emit_pipeline(
+                step,
+                grid=grid,
+                in_specs=[located(spec) for spec in blocks_in],
+                out_specs=[located(spec) for spec in blocks_out],
+            )(*[ins[at] for at in moved], *results)
+
+        places = [SCALARS] * first + [SCALARS if at in smem else IN_HBM for at in range(count)]
+        arrays = list(scalars) + list(operands)
         if has_token:
-            operands.append(self.token)
-            in_specs.append(ANYWHERE)
-
-        def kernel(*refs):
-            ins, rest = refs[:taken], refs[taken + has_token :]
-            rest[given][...] = jnp.zeros((8, PB), F32)
-            body(*ins, *rest[:given], *rest[given + 1 :])
-
-        settings = dict(
+            arrays.append(self.token)
+            places.append(IN_HBM)
+        results = pl.pallas_call(
+            kernel,
             out_shape=tuple(outs) + (f32(8, PB),),
+            in_specs=places,
+            out_specs=(IN_HBM,) * (len(outs) + 1),
+            scratch_shapes=scratch,
             input_output_aliases=aliases or {},
             compiler_params=pltpu.CompilerParams(vmem_limit_bytes=VMEM_BYTES),
             cost_estimate=pl.CostEstimate(flops=1 << 20, bytes_accessed=1 << 16, transcendentals=0),
             name=name,
-        )
-        grid_spec = pltpu.PrefetchScalarGridSpec(
-            num_scalar_prefetch=len(scalars),
-            grid=grid,
-            in_specs=in_specs,
-            out_specs=tuple(out_specs) + (full((8, PB)),),
-            scratch_shapes=scratch,
-        )
-        results = pl.pallas_call(kernel, grid_spec=grid_spec, **settings)(*scalars, *operands)
+        )(*arrays)
         self.token = results[-1]
-        return results[:-1] if given > 1 else results[0]
+        return results[:-1] if len(outs) > 1 else results[0]
 
 
 def mask_orders(count):
@@ -126,10 +136,11 @@
     return order
 
 
-def relay(first, count):
+def spread(value, count):
     middle = count // 2
+    first = lax.ppermute(value, "col", [(0, middle)])
     others = [c for c in range(count - 1, 0, -1) if c != middle]
-    return [lax.ppermute(first, "col", [(middle, c)]) for c in others]
+    return [first] + [lax.ppermute(first, "col", [(middle, c)]) for c in others]
 
 
 def exchange(value, row_count):
@@ -172,8 +183,21 @@
     return jnp.where(lax.axis_index("col") == 0, own[...], arrived)
 
 
+def place_rows(row_count, capacity, owner_ref, child_count, write):
+    def body(i, counts):
+        owner = owner_ref[i]
+        rank = jnp.int32(0)
+        for d in range(row_count):
+            rank = jnp.where(owner == d, counts[d], rank)
+        write(i, owner, rank)
+        return tuple(counts[d] + (owner == d).astype(jnp.int32) for d in range(row_count))
+
+    lax.fori_loop(0, child_count, body, (jnp.int32(0),) * row_count)
+
+
 def pack_body(row_count, capacity, sentinel, pieces, owner_ref, offset_ref, child_ref, front_ref, *refs):
-    outs, (out_ref, rows_ref, tag_ref) = refs[:pieces], refs[pieces:]
+    outs, (lead_ref, out_ref, rows_ref, tag_ref) = refs[:pieces], refs[pieces:]
+    lead_ref[...] = child_ref[:, :LEAD]
     at = 0
     for out in outs:
         out[...] = front_ref[at : at + out.shape[0], :]
@@ -181,35 +205,48 @@
     rows_ref[...] = jnp.zeros_like(rows_ref)
     tag_ref[...] = jnp.full(tag_ref.shape, sentinel, F32)
 
-    def body(i, counts):
-        owner = owner_ref[i]
-        rank = jnp.int32(0)
-        for d in range(row_count):
-            rank = jnp.where(owner == d, counts[d], rank)
+    def write(i, owner, rank):
         slot = owner * capacity + rank
         rows_ref[pl.ds(slot, 1), :] = child_ref[pl.ds(i, 1), :]
         tag_ref[pl.ds(slot, 1), :] = jnp.full((1, PB), offset_ref[i].astype(F32))
-        return tuple(counts[d] + (owner == d).astype(jnp.int32) for d in range(row_count))
-
-    lax.fori_loop(0, child_ref.shape[0], body, (jnp.int32(0),) * row_count)
+
+    place_rows(row_count, capacity, owner_ref, child_ref.shape[0], write)
     width = rows_ref.shape[1]
     out_ref[:, :width] = rows_ref[...]
     out_ref[:, width:] = tag_ref[...]
 
 
-def gather_body(rows_in, tags_in, *refs):
-    rows_ref, tag_ref = refs[-2:]
-    rows_ref[...] = rows_in[...]
-    tag_ref[...] = tags_in[...]
-
-
-def lead_body(chunk_count, *refs):
-    each = (len(refs) - 6) // (chunk_count + 1)
-    chunks = [refs[i * each : (i + 1) * each] for i in range(chunk_count + 1)]
-    tag_ref = refs[each * (chunk_count + 1)]
+def pack_lead_body(row_count, capacity, child_count, owner_ref, *refs):
+    outs = refs[-2 - row_count : -2]
+    own, gots = refs[0], refs[1 : len(refs) - 2 - row_count]
+    child_ref, rows_ref = refs[-2:]
+    child_ref[...] = pick(own, gots)
+    rows_ref[...] = jnp.zeros_like(rows_ref)
+    me = lax.axis_index("row")
+
+    def write(i, owner, rank):
+        rows_ref[pl.ds((owner ^ me) * capacity + rank, 1), :] = child_ref[pl.ds(i, 1), :]
+
+    place_rows(row_count, capacity, owner_ref, child_count, write)
+    for at, out in enumerate(outs):
+        out[...] = rows_ref[at * capacity : (at + 1) * capacity, :]
+
+
+def lead_body(chunk_count, row_count, *refs):
+    each = (len(refs) - 6 - row_count) // chunk_count
+    chunks = [refs[i * each : (i + 1) * each] for i in range(chunk_count)]
+    pieces = refs[chunk_count * each : chunk_count * each + row_count]
+    tag_ref = refs[chunk_count * each + row_count]
     lead_ref, left_ref, place_ref, keep_ref, send_ref = refs[-5:]
-    slots_value = pick(chunks[-1][0], chunks[-1][1:])
-    front = jnp.concatenate([pick(c[0], c[1:]) for c in chunks[:-1]], axis=0)
+    me = lax.axis_index("row")
+    values = [ref[...] for ref in pieces]
+    bit = 1
+    while bit < row_count:
+        swapped = [values[at ^ bit] for at in range(row_count)]
+        values = [jnp.where((me & bit) != 0, b, a) for a, b in zip(values, swapped)]
+        bit *= 2
+    slots_value = jnp.concatenate(values, axis=0)
+    front = jnp.concatenate([pick(c[0], c[1:]) for c in chunks], axis=0)
     rows, slots = front.shape[0], slots_value.shape[0]
     at = lax.broadcasted_iota(jnp.int32, (rows, slots), 0).astype(F32)
 
@@ -447,7 +484,7 @@
 
 
 ORDER = (
-    "G0 P0 G1 K0 S01 S11 G2 S02 S12 E0 A0 E1 A1 J02 E2 J12 E3 F J01 J11 X0 X1 "
+    "G0 P0 G1 K0 S01 S11 S21 S31 G2 S02 S12 E0 S22 S32 A0 E1 A1 A2 E2 A3 J02 J12 E3 J22 J01 F J32 J11 X0 J21 X1 J31 X2 X3"
 )
 KINDS = {"P": "send", "K": "keep", "S": "split", "G": "gram", "E": "factor", "A": "sum", "J": "join", "X": "project"}
 
@@ -475,29 +512,34 @@
 
     pieces = 2
     sizes = [local_rows // pieces] * pieces
-    *own, packed = run(
+    *own, lead_child, packed = run(
         "pack_children", functools.partial(pack_body, row_count, capacity, float(local_rows), pieces),
         [owner, offset, child_rows, front_matrix],
-        [SCALARS, SCALARS, full(child_rows.shape), full((local_rows, LEAD))],
-        [f32(n, LEAD) for n in sizes] + [f32(slots, local_cols + PB)],
-        [full((n, LEAD)) for n in sizes] + [full((slots, local_cols + PB))],
-        grid=(1,), scratch=[pltpu.VMEM((slots, local_cols), F32), pltpu.VMEM((slots, PB), F32)],
-    )
-    got = [[lax.ppermute(piece, "col", [(0, col_count // 2)])] for piece in own]
+        [SCALARS, SCALARS, WHOLE, full((local_rows, LEAD))],
+        [f32(n, LEAD) for n in sizes] + [f32(child_count, LEAD), f32(slots, local_cols + PB)],
+        [WHOLE] * (pieces + 2),
+        scratch=[pltpu.VMEM((slots, local_cols), F32), pltpu.VMEM((slots, PB), F32)],
+    )
     child = exchange(packed, row_count)
-    rows, tags = run(
-        "gather_lead", gather_body, [child, child] + [first for first, in got],
-        [full((slots, LEAD)), pl.BlockSpec((slots, PB), lambda i: (0, local_cols // PB))] + [ANYWHERE] * pieces,
-        [f32(slots, LEAD), f32(slots, PB)], [full((slots, LEAD)), full((slots, PB))], grid=(1,),
-    )
-    own.append(rows)
-    got.append([lax.ppermute(rows, "col", [(0, col_count // 2)])])
-    for arrived_here in got:
-        arrived_here.extend(relay(arrived_here[0], col_count))
+    lead_got = spread(lead_child, col_count)
+    got = [spread(piece, col_count) for piece in own]
+    lead_pieces = list(
+        run(
+            "pack_lead", functools.partial(pack_lead_body, row_count, capacity, child_count),
+            [owner, lead_child] + lead_got + [child] + got[0],
+            [SCALARS] + [WHOLE] * (1 + len(lead_got)) + [ANYWHERE] * (1 + len(got[0])),
+            [f32(capacity, LEAD)] * row_count, [WHOLE] * row_count,
+            scratch=[pltpu.VMEM((child_count, LEAD), F32), pltpu.VMEM((slots, LEAD), F32)],
+        )
+    )
+    for mask in range(1, row_count):
+        pairs = [(d, d ^ mask) for d in range(row_count)]
+        lead_pieces[mask] = lax.ppermute(lead_pieces[mask], "row", pairs)
     operands = [ref for piece, arrived in zip(own, got) for ref in [piece] + arrived]
     lead, left, place, gram, gram_send = run(
-        "lead_setup", functools.partial(lead_body, pieces),
-        operands + [tags], [WHOLE] * (len(operands) + 1),
+        "lead_setup", functools.partial(lead_body, pieces, row_count),
+        operands + lead_pieces + [child],
+        [WHOLE] * (len(operands) + row_count) + [pl.BlockSpec((slots, PB), lambda i: (0, local_cols // PB))],
         [f32(local_rows, LEAD), bf16(LEAD, 3 * local_rows), bf16(local_rows, 3 * slots),
          f32(HALF // 2, LEAD + HALF), f32(HALF // 2, LEAD + HALF)],
         [WHOLE] * 5,

time: 232 us -> 244 us (1.052)
  waiting for transfers between devices: 81.1 us -> 45.7 us
  Pallas kernels: 81.4 us -> 107 us
  starting transfers between devices: 39.7 us -> 57.1 us
    ppermute x16 -> x28, waiting for transfers between devices: 47.7 us -> 20.9 us  [swap(): return lax.ppermute(value, 'row', pairs)]
    pallas_call x25 -> x37, Pallas kernels: 81.4 us -> 107 us  [__call__(): pl.pallas_call(kernel, out_shape=tuple(outs) + (f32(8, PB),), in_specs=pl...]
    ppermute x9 -> x16, starting transfers between devices: 13.1 us -> 22.4 us  [the longest x7 9.29 us: on_device(): lead_pieces[mask] = lax.ppermute(lead_pieces[mask], 'row', pairs)]
    ppermute x16 -> x28, starting transfers between devices: 22 us -> 30.1 us  [swap(): return lax.ppermute(value, 'row', pairs)]
    ppermute x9 -> x16, waiting for transfers between devices: 31.4 us -> 24.7 us  [the longest x3 15.1 us: spread(): first = lax.ppermute(value, 'col', [(0, middle)])]
    unnamed x56 -> x66, local copies, waits for them, and re-layouts: 25.8 us -> 27.9 us
  transfers between devices with their start and end apart: 26 -> 45, of which waited for: 15 -> 12; matrix products, arithmetic and copies ran while one was open for 0% -> 0% of each run, Pallas kernels for 23% -> 31%
where the time goes in v5:
time: 244 us; the launch traced here: 240 us
  Pallas kernels  107 us (44%)
  starting transfers between devices  57.1 us (23%)
  waiting for transfers between devices  45.7 us (19%)
  local copies, waits for them, and re-layouts  28.5 us (12%)
    pallas_call x37, Pallas kernels, __call__(): pl.pallas_call(kernel, out_shape=tuple(outs) + (f32(8, PB),), in_specs=pl...  107 us
    ppermute x28, starting transfers between devices, swap(): return lax.ppermute(value, 'row', pairs)  30.1 us
    unnamed x66, local copies, waits for them, and re-layouts  27.9 us
    ppermute x28, waiting for transfers between devices, swap(): return lax.ppermute(value, 'row', pairs)  20.9 us
    ppermute x3, waiting for transfers between devices, spread(): first = lax.ppermute(value, 'col', [(0, middle)])  15.1 us
    ppermute x7, starting transfers between devices, on_device(): lead_pieces[mask] = lax.ppermute(lead_pieces[mask], 'row', pairs)  9.29 us
    ppermute x6, starting transfers between devices, spread(): return [first] + [lax.ppermute(first, 'col', [(middle, c)]) for c in others]  9.27 us
    ppermute x6, waiting for transfers between devices, spread(): return [first] + [lax.ppermute(first, 'col', [(middle, c)]) for c in others]  6.89 us
  transfers between devices with their start and end apart: 45, of which 12 were waited for; matrix products, arithmetic and copies ran while one was open for 0% of the time, Pallas kernels for 31%

profile of v5, /device:TPU:21, one launch (start us, length us, event | category | flops | bytes accessed | tf_op | source)
XLA Modules:
  0.0 240.1 jit_solution(4573373275625507869)
XLA Ops:
  6.0 3.7 %pack_children.1 = (f32[192,512]{1,0:T(8,128)S(1)}, f32[192,512]{1,0:T(8,128)}, f32[64,512]{1,0:T(8,128)S(1)}, f32[128,4224]{1,0:T(8,128)S(1)}, f32[8,128]{1,0:T(8,128)S(1)}) custom-call(s32[64]{0:T(128)S(1)} %bitcast.13, s32[64]{0:T(128)S(1)} %bitcast.15, f32[64,4096]{1,0:T(8,128)S(1)} %copy-done.13, f32[384,4096]{1,0:T(8,128)S(1)} %copy-done), custom_call_target="tpu_custom_call" | custom-call | flops 1048576 | bytes 65536 | tf_op jit(solution)/shard_map/pack_children/pallas_call | solution.py:75
  11.1 4.5 %all-to-all-start = ((f32[8,16,4224]{2,1,0:T(8,128)}), f32[8,16,4224]{2,1,0:T(8,128)S(1)}, u32[]{:S(2)}, u32[]{:S(2)}) async-start(f32[8,16,4224]{2,1,0:T(8,128)} %bitcast.12), calls=%async_computation | async-start | bytes 4325376 | tf_op jit(solution)/shard_map/all_to_all | solution.py:149
  19.5 9.2 %collective-permute-done.refs_6_.refs_1_ = f32[192,512]{1,0:T(8,128)S(1)} collective-permute-done((f32[192,512]{1,0:T(8,128)S(1)}, f32[192,512]{1,0:T(8,128)S(1)}, u32[]{:S(2)}, u32[]{:S(2)}) %collective-permute-start) | collective-permute-done | bytes 393248 | tf_op jit(solution)/shard_map/ppermute | solution.py:141
  31.3 5.9 %collective-permute-done.3.refs_5_ = f32[192,512]{1,0:T(8,128)} collective-permute-done((f32[192,512]{1,0:T(8,128)}, f32[192,512]{1,0:T(8,128)}, u32[]{:S(2)}, u32[]{:S(2)}) %collective-permute-start.3) | collective-permute-done | bytes 393248 | tf_op jit(solution)/shard_map/ppermute | solution.py:141
  42.6 5.6 %collective-permute-done.7.refs_3_ = f32[64,512]{1,0:T(8,128)S(1)} collective-permute-done((f32[64,512]{1,0:T(8,128)S(1)}, f32[64,512]{1,0:T(8,128)S(1)}, u32[]{:S(2)}, u32[]{:S(2)}) %collective-permute-start.7) | collective-permute-done | bytes 131104 | tf_op jit(solution)/shard_map/ppermute | solution.py:143
  55.7 3.0 %pack_lead.1 = (f32[16,512]{1,0:T(8,128)S(1)}, f32[16,512]{1,0:T(8,128)S(1)}, f32[16,512]{1,0:T(8,128)S(1)}, f32[16,512]{1,0:T(8,128)S(1)}, f32[16,512]{1,0:T(8,...) custom-call(s32[64]{0:T(128)S(1)} %bitcast.14, ...), custom_call_target="tpu_custom_call" | custom-call | flops 1048576 | bytes 65536 | tf_op jit(solution)/shard_map/pack_lead/pallas_call | solution.py:75
  60.0 3.6 %collective-permute-start.11 = (f32[16,512]{1,0:T(8,128)S(1)}, f32[16,512]{1,0:T(8,128)S(1)}, u32[]{:S(2)}, u32[]{:S(2)}) collective-permute-start(f32[16,512]{1,0:T(8,128)S(1)} %get-tuple-element.121), channel_id=1, source_target_pairs={{0,12},{4,8},{8,4},{12,0},{16,28},{20,24},{24,20},{28,16},{1,13},{... | collective-permute-start | bytes 98312 | tf_op jit(solution)/shard_map/ppermute | solution.py:537
  74.7 8.5 %lead_setup.1 = (f32[384,512]{1,0:T(8,128)S(1)}, bf16[512,1152]{1,0:T(8,128)(2,1)S(1)}, bf16[384,384]{1,0:T(8,128)(2,1)S(1)}, f32[128,768]{1,0:T(8,128)S(1)}, f32[128,768]{1,0:T(8,128)}, /*index=5*/f32[8,128]{1,0:T(8,128)S(1)}) custom-call(f32[192,512]{1,0:T(8,128)S(1)} %copy-done.21, f32[192,512]{1,0:T(8,128)S(1)} %copy-done.5, f32[192,512]{1,0:T(8,128)S(1)} %copy-done.7, ...), custom_call_target="tpu_custom_call" | custom-call | flops 1048576 | bytes 65536 | tf_op jit(solution)/shard_map/lead_setup/pallas_call | solution.py:75
  90.9 2.8 %copy-done.1 = f32[384,4096]{1,0:T(8,128)S(1)} copy-done((f32[384,4096]{1,0:T(8,128)S(1)}, f32[384,4096]{1,0:T(8,128)}, u32[]{:S(2)}) %copy-start.1) | copy-done | bytes 6291480
  94.6 11.6 %lead_product.2 = (f32[512,512]{1,0:T(8,128)}, f32[512,512]{1,0:T(8,128)}, f32[512,512]{1,0:T(8,128)}, f32[512,512]{1,0:T(8,128)}, f32[384,4096]{1,0:T(8,128)}, /*index=5*/f32[8,128]{1,0:T(8,128)S(1)}) custom-call(s32[8]{0:T(128)S(1)} %iota_add_fusion.7.refs_0_, bf16[512,1152]{1,0:T(8,128)(2,1)S(1)} %get-tuple-element.131.refs_1_, ...), custom_call_target="tpu_custom_call" | custom-call | flops 1048576 | bytes 65536 | tf_op jit(solution)/shard_map/lead_product/pallas_call | solution.py:75
  108.2 6.2 %collective-permute-done.17.refs_1_ = f32[128,768]{1,0:T(8,128)} collective-permute-done((f32[128,768]{1,0:T(8,128)}, f32[128,768]{1,0:T(8,128)}, u32[]{:S(2)}, u32[]{:S(2)}) %collective-permute-start.17) | collective-permute-done | bytes 393248 | tf_op jit(solution)/shard_map/ppermute | solution.py:99
  121.2 11.7 %lead_product.3 = (f32[512,512]{1,0:T(8,128)S(1)}, f32[512,512]{1,0:T(8,128)S(1)}, f32[512,512]{1,0:T(8,128)S(1)}, f32[512,512]{1,0:T(8,128)S(1)}, f32[384,4096]{1,0:T(8,128)}, /*index=5*/f32[8,128]{1,0:T(8,128)S(1)}) custom-call(s32[8]{0:T(128)S(1)} %iota_add_fusion.6.refs_0_, ...), custom_call_target="tpu_custom_call", output_to_operand_aliasing={{4}: (5, {})} | custom-call | flops 1048576 | bytes 65536 | tf_op jit(solution)/shard_map/lead_product/pallas_call | solution.py:75
  142.8 3.0 %collective-permute-start.23 = (f32[128,768]{1,0:T(8,128)S(1)}, f32[128,768]{1,0:T(8,128)S(1)}, u32[]{:S(2)}, u32[]{:S(2)}) collective-permute-start(f32[128,768]{1,0:T(8,128)S(1)} %get-tuple-element.151.refs_0_), channel_id=1, source_target_pairs={{0,4},{4,0},{8,12},{12,8},{16,20},{20,16},{24,28},{28,24},{1,5},{5... | collective-permute-start | bytes 1179656 | tf_op jit(solution)/shard_map/ppermute | solution.py:99
  149.5 6.0 %eliminate_panel.4 = (f32[512,512]{1,0:T(8,128)S(1)}, f32[8,128]{1,0:T(8,128)S(1)}) custom-call(f32[128,768]{1,0:T(8,128)S(1)} %get-tuple-element.151.refs_0_, f32[128,768]{1,0:T(8,128)S(1)} %collective-permute-done.23.refs_1_, f32[8,128]{1,0:T(8,128)S(1)} %get-tuple-element.158.refs_2_), custom_call_target="tpu_custom_call" | custom-call | flops 1048576 | bytes 65536 | tf_op jit(solution)/shard_map/eliminate_panel/pallas_call | solution.py:75
  158.4 6.8 %collective-permute-done.27.refs_1_ = f32[512,256]{1,0:T(8,128)S(1)} collective-permute-done((f32[512,256]{1,0:T(8,128)S(1)}, f32[512,256]{1,0:T(8,128)S(1)}, u32[]{:S(2)}, u32[]{:S(2)}) %collective-permute-start.27) | collective-permute-done | bytes 524320 | tf_op jit(solution)/shard_map/ppermute | solution.py:99
  167.2 5.3 %eliminate_panel.5 = (f32[512,512]{1,0:T(8,128)S(1)}, f32[8,128]{1,0:T(8,128)S(1)}) custom-call(f32[512,512]{1,0:T(8,128)S(1)} %get-tuple-element.159.refs_0_, f32[8,128]{1,0:T(8,128)S(1)} %get-tuple-element.169.refs_1_), custom_call_target="tpu_custom_call" | custom-call | flops 1048576 | bytes 65536 | tf_op jit(solution)/shard_map/eliminate_panel/pallas_call | solution.py:75
  173.8 5.0 %eliminate_panel.6 = (f32[512,512]{1,0:T(8,128)S(1)}, f32[8,128]{1,0:T(8,128)S(1)}) custom-call(f32[512,512]{1,0:T(8,128)S(1)} %get-tuple-element.170.refs_0_, f32[8,128]{1,0:T(8,128)S(1)} %get-tuple-element.177.refs_1_), custom_call_target="tpu_custom_call" | custom-call | flops 1048576 | bytes 65536 | tf_op jit(solution)/shard_map/eliminate_panel/pallas_call | solution.py:75
  182.3 4.5 %eliminate_panel.7 = (f32[512,512]{1,0:T(8,128)S(1)}, f32[8,128]{1,0:T(8,128)S(1)}) custom-call(f32[512,512]{1,0:T(8,128)S(1)} %get-tuple-element.178.refs_0_, f32[8,128]{1,0:T(8,128)S(1)} %get-tuple-element.186.refs_1_), custom_call_target="tpu_custom_call" | custom-call | flops 1048576 | bytes 65536 | tf_op jit(solution)/shard_map/eliminate_panel/pallas_call | solution.py:75
  190.6 9.8 %collective-permute-start.40 = (f32[2048,128]{1,0:T(8,128)S(1)}, f32[2048,128]{1,0:T(8,128)}, u32[]{:S(2)}, u32[]{:S(2)}) collective-permute-start(f32[2048,128]{1,0:T(8,128)S(1)} %get-tuple-element.203.refs_4_.refs_5_), channel_id=1, source_target_pairs={{0,4},{4,0},{8,12},{12,8},{16,20},{20,16},{24,28},{28,24},{1,5},{5... | collective-permute-start | bytes 3145736 | tf_op jit(solution)/shard_map/ppermute | solution.py:99
  200.4 2.9 %finish_factor.1 = (bf16[256,768]{1,0:T(8,128)(2,1)S(1)}, bf16[256,1536]{1,0:T(8,128)(2,1)S(1)}, bf16[384,1536]{1,0:T(8,128)(2,1)S(1)}, f32[384,512]{1,0:T(8,128)}, f32[8,128]{1,0:T(8,128)S(1)}) custom-call(f32[512,512]{1,0:T(8,128)S(1)} %get-tuple-element.187.refs_0_, f32[384,512]{1,0:T(8,128)S(1)} %copy-done.15, f32[8,128]{1,0:T(8,128)S(1)} %get-tuple-element.193.refs_2_), custom_call_target="tpu_custom_call" | custom-call | flops 1048576 | bytes 65536 | tf_op jit(solution)/shard_map/finish_factor/pallas_call | solution.py:75
  207.7 7.3 %project_columns.4 = (f32[512,4096]{1,0:T(8,128)}, f32[384,4096]{1,0:T(8,128)}, f32[8,128]{1,0:T(8,128)S(1)}) custom-call(s32[12]{0:T(128)S(1)} %get-tuple-element.225.refs_0_, bf16[256,768]{1,0:T(8,128)(2,1)S(1)} %get-tuple-element.194.refs_1_, bf16[256,1536]{1,0:T(8,128)(2,1)S(1)} %get-tuple-element.195.refs_2_, ...), custom_call_target="tpu_custom_call", output_to_operand_aliasing={{1}: (8, {})} | custom-call | flops 1048576 | bytes 65536 | tf_op jit(solution)/shard_map/project_columns/pallas_call | solution.py:75
  216.6 7.4 %project_columns.5 = (f32[512,4096]{1,0:T(8,128)}, f32[384,4096]{1,0:T(8,128)}, f32[8,128]{1,0:T(8,128)S(1)}) custom-call(s32[12]{0:T(128)S(1)} %get-tuple-element.224.refs_0_, bf16[256,768]{1,0:T(8,128)(2,1)S(1)} %get-tuple-element.194.refs_1_, bf16[256,1536]{1,0:T(8,128)(2,1)S(1)} %get-tuple-element.195.refs_2_, ...), custom_call_target="tpu_custom_call", output_to_operand_aliasing={{1}: (8, {}), {0}: (9, {})} | custom-call | flops 1048576 | bytes 65536 | tf_op jit(solution)/shard_map/project_columns/pallas_call | solution.py:75
  225.3 7.3 %project_columns.6 = (f32[512,4096]{1,0:T(8,128)}, f32[384,4096]{1,0:T(8,128)}, f32[8,128]{1,0:T(8,128)S(1)}) custom-call(s32[12]{0:T(128)S(1)} %get-tuple-element.223.refs_0_, bf16[256,768]{1,0:T(8,128)(2,1)S(1)} %get-tuple-element.194.refs_1_, bf16[256,1536]{1,0:T(8,128)(2,1)S(1)} %get-tuple-element.195.refs_2_, ...), custom_call_target="tpu_custom_call", output_to_operand_aliasing={{1}: (8, {}), {0}: (9, {})} | custom-call | flops 1048576 | bytes 65536 | tf_op jit(solution)/shard_map/project_columns/pallas_call | solution.py:75
  232.6 7.4 %project_columns.7 = (f32[512,4096]{1,0:T(8,128)}, f32[384,4096]{1,0:T(8,128)}, f32[8,128]{1,0:T(8,128)}) custom-call(s32[12]{0:T(128)S(1)} %add_add_fusion.refs_0_, bf16[256,768]{1,0:T(8,128)(2,1)S(1)} %get-tuple-element.194.refs_1_, bf16[256,1536]{1,0:T(8,128)(2,1)S(1)} %get-tuple-element.195.refs_2_, ...), custom_call_target="tpu_custom_call", output_to_operand_aliasing={{1}: (8, {}), {0}: (9, {})} | custom-call | flops 1048576 | bytes 65536 | tf_op jit(solution)/shard_map/project_columns/pallas_call | solution.py:75
  (179 shorter events, 89.5 us)
Async XLA Ops:
  11.1 41.7 %all-to-all-start = ((f32[8,16,4224]{2,1,0:T(8,128)}), f32[8,16,4224]{2,1,0:T(8,128)S(1)}, u32[]{:S(2)}, u32[]{:S(2)}) async-start(f32[8,16,4224]{2,1,0:T(8,128)} %bitcast.12), calls=%async_computation | async-start | bytes 4325376 | tf_op jit(solution)/shard_map/all_to_all | solution.py:149
  15.6 13.1 %collective-permute-start = (f32[192,512]{1,0:T(8,128)S(1)}, f32[192,512]{1,0:T(8,128)S(1)}, u32[]{:S(2)}, u32[]{:S(2)}) collective-permute-start(f32[192,512]{1,0:T(8,128)S(1)} %get-tuple-element.113.refs_0_), channel_id=1, source_target_pairs={{0,2},{4,6},{8,10},{12,14},{16,18},{20,22},{24,26},{28,30}} | collective-permute-start | bytes 1179656 | tf_op jit(solution)/shard_map/ppermute | solution.py:141
  16.9 20.4 %collective-permute-start.3 = (f32[192,512]{1,0:T(8,128)}, f32[192,512]{1,0:T(8,128)}, u32[]{:S(2)}, u32[]{:S(2)}) collective-permute-start(f32[192,512]{1,0:T(8,128)} %get-tuple-element.114.refs_4_), channel_id=1, source_target_pairs={{0,2},{4,6},{8,10},{12,14},{16,18},{20,22},{24,26},{28,30}} | collective-permute-start | bytes 1179656 | tf_op jit(solution)/shard_map/ppermute | solution.py:141
  18.2 23.1 %collective-permute-start.6 = (f32[64,512]{1,0:T(8,128)S(1)}, f32[64,512]{1,0:T(8,128)S(1)}, u32[]{:S(2)}, u32[]{:S(2)}) collective-permute-start(f32[64,512]{1,0:T(8,128)S(1)} %get-tuple-element.115.refs_1_), channel_id=1, source_target_pairs={{0,2},{4,6},{8,10},{12,14},{16,18},{20,22},{24,26},{28,30}} | collective-permute-start | bytes 393224 | tf_op jit(solution)/shard_map/ppermute | solution.py:141
  28.7 24.0 %collective-permute-start.1 = (f32[192,512]{1,0:T(8,128)S(1)}, f32[192,512]{1,0:T(8,128)S(1)}, u32[]{:S(2)}, u32[]{:S(2)}) collective-permute-start(f32[192,512]{1,0:T(8,128)S(1)} %collective-permute-done.refs_6_.refs_1_), channel_id=1, source_target_pairs={{2,3},{6,7},{10,11},{14,15},{18,19},{22,23},{26,27},{30,31}} | collective-permute-start | bytes 1179656 | tf_op jit(solution)/shard_map/ppermute | solution.py:143
  30.0 22.7 %collective-permute-start.2 = (f32[192,512]{1,0:T(8,128)S(1)}, f32[192,512]{1,0:T(8,128)S(1)}, u32[]{:S(2)}, u32[]{:S(2)}) collective-permute-start(f32[192,512]{1,0:T(8,128)S(1)} %collective-permute-done.refs_6_.refs_1_), channel_id=1, source_target_pairs={{2,1},{6,5},{10,9},{14,13},{18,17},{22,21},{26,25},{30,29}} | collective-permute-start | bytes 1179656 | tf_op jit(solution)/shard_map/ppermute | solution.py:143
  37.2 26.8 %collective-permute-start.4 = (f32[192,512]{1,0:T(8,128)}, f32[192,512]{1,0:T(8,128)}, u32[]{:S(2)}, u32[]{:S(2)}) collective-permute-start(f32[192,512]{1,0:T(8,128)} %collective-permute-done.3.refs_5_), channel_id=1, source_target_pairs={{2,3},{6,7},{10,11},{14,15},{18,19},{22,23},{26,27},{30,31}} | collective-permute-start | bytes 1179656 | tf_op jit(solution)/shard_map/ppermute | solution.py:143
  39.3 25.8 %collective-permute-start.5 = (f32[192,512]{1,0:T(8,128)}, f32[192,512]{1,0:T(8,128)}, u32[]{:S(2)}, u32[]{:S(2)}) collective-permute-start(f32[192,512]{1,0:T(8,128)} %collective-permute-done.3.refs_5_), channel_id=1, source_target_pairs={{2,1},{6,5},{10,9},{14,13},{18,17},{22,21},{26,25},{30,29}} | collective-permute-start | bytes 1179656 | tf_op jit(solution)/shard_map/ppermute | solution.py:143
  106.2 26.7 %collective-permute-start.22 = (f32[512,512]{1,0:T(8,128)}, f32[512,512]{1,0:T(8,128)}, u32[]{:S(2)}, u32[]{:S(2)}) collective-permute-start(f32[512,512]{1,0:T(8,128)} %get-tuple-element.145), channel_id=1, source_target_pairs={{0,4},{4,0},{8,12},{12,8},{16,20},{20,16},{24,28},{28,24},{1,5},{5... | collective-permute-start | bytes 3145736 | tf_op jit(solution)/shard_map/ppermute | solution.py:99
  106.5 28.9 %collective-permute-start.21 = (f32[512,512]{1,0:T(8,128)}, f32[512,512]{1,0:T(8,128)}, u32[]{:S(2)}, u32[]{:S(2)}) collective-permute-start(f32[512,512]{1,0:T(8,128)} %get-tuple-element.143), channel_id=1, source_target_pairs={{0,4},{4,0},{8,12},{12,8},{16,20},{20,16},{24,28},{28,24},{1,5},{5... | collective-permute-start | bytes 3145736 | tf_op jit(solution)/shard_map/ppermute | solution.py:99
  106.7 30.8 %collective-permute-start.20 = (f32[512,512]{1,0:T(8,128)}, f32[512,512]{1,0:T(8,128)}, u32[]{:S(2)}, u32[]{:S(2)}) collective-permute-start(f32[512,512]{1,0:T(8,128)} %get-tuple-element.141), channel_id=1, source_target_pairs={{0,4},{4,0},{8,12},{12,8},{16,20},{20,16},{24,28},{28,24},{1,5},{5... | collective-permute-start | bytes 3145736 | tf_op jit(solution)/shard_map/ppermute | solution.py:99
  107.1 33.0 %collective-permute-start.19 = (f32[512,512]{1,0:T(8,128)}, f32[512,512]{1,0:T(8,128)}, u32[]{:S(2)}, u32[]{:S(2)}) collective-permute-start(f32[512,512]{1,0:T(8,128)} %get-tuple-element.139), channel_id=1, source_target_pairs={{0,4},{4,0},{8,12},{12,8},{16,20},{20,16},{24,28},{28,24},{1,5},{5... | collective-permute-start | bytes 3145736 | tf_op jit(solution)/shard_map/ppermute | solution.py:99
  116.7 25.5 %collective-permute-start.18 = (f32[128,768]{1,0:T(8,128)S(1)}, f32[128,768]{1,0:T(8,128)S(1)}, u32[]{:S(2)}, u32[]{:S(2)}) collective-permute-start(f32[128,768]{1,0:T(8,128)S(1)} %get-tuple-element.135.refs_0_), channel_id=1, source_target_pairs={{0,16},{4,12},{8,24},{12,4},{16,0},{20,28},{24,8},{28,20},{1,17},{... | collective-permute-start | bytes 1179656 | tf_op jit(solution)/shard_map/ppermute | solution.py:99
  139.0 18.1 %collective-permute-start.28 = (f32[512,256]{1,0:T(8,128)S(1)}, f32[512,256]{1,0:T(8,128)S(1)}, u32[]{:S(2)}, u32[]{:S(2)}) collective-permute-start(f32[512,256]{1,0:T(8,128)S(1)} %get-tuple-element.165), channel_id=1, source_target_pairs={{0,8},{4,20},{8,0},{12,28},{16,24},{20,4},{24,16},{28,12},{1,9},{5... | collective-permute-start | bytes 1572872 | tf_op jit(solution)/shard_map/ppermute | solution.py:99
  141.5 23.7 %collective-permute-start.27 = (f32[512,256]{1,0:T(8,128)S(1)}, f32[512,256]{1,0:T(8,128)S(1)}, u32[]{:S(2)}, u32[]{:S(2)}) collective-permute-start(f32[512,256]{1,0:T(8,128)S(1)} %get-tuple-element.163), channel_id=1, source_target_pairs={{0,8},{4,20},{8,0},{12,28},{16,24},{20,4},{24,16},{28,12},{1,9},{5... | collective-permute-start | bytes 1572872 | tf_op jit(solution)/shard_map/ppermute | solution.py:99
  146.0 20.3 %collective-permute-start.26 = (f32[512,128]{1,0:T(8,128)S(1)}, f32[512,128]{1,0:T(8,128)S(1)}, u32[]{:S(2)}, u32[]{:S(2)}) collective-permute-start(f32[512,128]{1,0:T(8,128)S(1)} %get-tuple-element.161), channel_id=1, source_target_pairs={{0,16},{4,12},{8,24},{12,4},{16,0},{20,28},{24,8},{28,20},{1,17},{... | collective-permute-start | bytes 786440 | tf_op jit(solution)/shard_map/ppermute | solution.py:99
  148.6 23.9 %collective-permute-start.30 = (f32[512,128]{1,0:T(8,128)S(1)}, f32[512,128]{1,0:T(8,128)S(1)}, u32[]{:S(2)}, u32[]{:S(2)}) collective-permute-start(f32[512,128]{1,0:T(8,128)S(1)} %get-tuple-element.174), channel_id=1, source_target_pairs={{0,16},{4,12},{8,24},{12,4},{16,0},{20,28},{24,8},{28,20},{1,17},{... | collective-permute-start | bytes 786440 | tf_op jit(solution)/shard_map/ppermute | solution.py:99
  157.4 16.3 %collective-permute-start.29 = (f32[512,128]{1,0:T(8,128)S(1)}, f32[512,128]{1,0:T(8,128)S(1)}, u32[]{:S(2)}, u32[]{:S(2)}) collective-permute-start(f32[512,128]{1,0:T(8,128)S(1)} %get-tuple-element.172), channel_id=1, source_target_pairs={{0,16},{4,12},{8,24},{12,4},{16,0},{20,28},{24,8},{28,20},{1,17},{... | collective-permute-start | bytes 786440 | tf_op jit(solution)/shard_map/ppermute | solution.py:99
  165.5 13.4 %collective-permute-start.33 = (f32[512,128]{1,0:T(8,128)S(1)}, f32[512,128]{1,0:T(8,128)S(1)}, u32[]{:S(2)}, u32[]{:S(2)}) collective-permute-start(f32[512,128]{1,0:T(8,128)S(1)} %get-tuple-element.182), channel_id=1, source_target_pairs={{0,16},{4,12},{8,24},{12,4},{16,0},{20,28},{24,8},{28,20},{1,17},{... | collective-permute-start | bytes 786440 | tf_op jit(solution)/shard_map/ppermute | solution.py:99
  166.4 12.5 %collective-permute-start.32 = (f32[512,128]{1,0:T(8,128)S(1)}, f32[512,128]{1,0:T(8,128)S(1)}, u32[]{:S(2)}, u32[]{:S(2)}) collective-permute-start(f32[512,128]{1,0:T(8,128)S(1)} %get-tuple-element.180.refs_0_), channel_id=1, source_target_pairs={{0,16},{4,12},{8,24},{12,4},{16,0},{20,28},{24,8},{28,20},{1,17},{... | collective-permute-start | bytes 786440 | tf_op jit(solution)/shard_map/ppermute | solution.py:99
  180.3 23.9 %collective-permute-start.38 = (f32[1024,128]{1,0:T(8,128)S(1)}, f32[1024,128]{1,0:T(8,128)S(1)}, u32[]{:S(2)}, u32[]{:S(2)}) collective-permute-start(f32[1024,128]{1,0:T(8,128)S(1)} %get-tuple-element.200.refs_0_), channel_id=1, source_target_pairs={{0,8},{4,20},{8,0},{12,28},{16,24},{20,4},{24,16},{28,12},{1,9},{5... | collective-permute-start | bytes 1572872 | tf_op jit(solution)/shard_map/ppermute | solution.py:99
  181.5 21.8 %collective-permute-start.36 = (f32[512,128]{1,0:T(8,128)S(1)}, f32[512,128]{1,0:T(8,128)S(1)}, u32[]{:S(2)}, u32[]{:S(2)}) collective-permute-start(f32[512,128]{1,0:T(8,128)S(1)} %get-tuple-element.197.refs_0_), channel_id=1, source_target_pairs={{0,16},{4,12},{8,24},{12,4},{16,0},{20,28},{24,8},{28,20},{1,17},{... | collective-permute-start | bytes 786440 | tf_op jit(solution)/shard_map/ppermute | solution.py:99
  190.6 17.1 %collective-permute-start.40 = (f32[2048,128]{1,0:T(8,128)S(1)}, f32[2048,128]{1,0:T(8,128)}, u32[]{:S(2)}, u32[]{:S(2)}) collective-permute-start(f32[2048,128]{1,0:T(8,128)S(1)} %get-tuple-element.203.refs_4_.refs_5_), channel_id=1, source_target_pairs={{0,4},{4,0},{8,12},{12,8},{16,20},{20,16},{24,28},{28,24},{1,5},{5... | collective-permute-start | bytes 3145736 | tf_op jit(solution)/shard_map/ppermute | solution.py:99
  206.4 17.6 %collective-permute-start.37 = (f32[1024,128]{1,0:T(8,128)}, f32[1024,128]{1,0:T(8,128)S(1)}, u32[]{:S(2)}, u32[]{:S(2)}) collective-permute-start(f32[1024,128]{1,0:T(8,128)} %copy-done.18), channel_id=1, source_target_pairs={{0,8},{4,20},{8,0},{12,28},{16,24},{20,4},{24,16},{28,12},{1,9},{5... | collective-permute-start | bytes 1572872 | tf_op jit(solution)/shard_map/ppermute | solution.py:99
  (54 other events, 382.6 us)

commit v6 on v2

--- a/solution.py
+++ b/solution.py
@@ -14,7 +14,8 @@
 LEAD = PB * PANELS
 HALF = LEAD // 2
 BLOCK = 256
-VMEM_BYTES = 24 * 1024 * 1024
+LAG = 2
+VMEM_BYTES = 48 * 1024 * 1024
 HIGHEST = lax.Precision.HIGHEST
 F32 = jnp.float32
 BF16 = jnp.bfloat16
@@ -151,7 +152,8 @@
     return hi, (x - hi.astype(F32)).astype(BF16)
 
 
-def pack_kernel(row_count, capacity, sentinel, owner_ref, offset_ref, child_ref, out_ref, tag_ref, tally):
+def pack_kernel(row_count, capacity, sentinel, owner_ref, offset_ref, child_ref, *rest):
+    out_ref, tag_ref, tally = rest[-3:]
     out_ref[...] = jnp.zeros_like(out_ref)
     tag_ref[...] = jnp.full(tag_ref.shape, sentinel, F32)
     for d in range(row_count):
@@ -169,7 +171,7 @@
     lax.fori_loop(0, child_ref.shape[0], body, 0)
 
 
-def pack(child_rows, owner, offset, row_count, capacity, sentinel):
+def pack(child_rows, owner, offset, row_count, capacity, sentinel, after=()):
     slots = row_count * capacity
     return pl.pallas_call(
         functools.partial(pack_kernel, row_count, capacity, float(sentinel)),
@@ -181,12 +183,13 @@
             pl.BlockSpec(memory_space=SMEM),
             pl.BlockSpec(memory_space=SMEM),
             pl.BlockSpec(memory_space=VMEM),
-        ],
+        ]
+        + [pl.BlockSpec(memory_space=pl.ANY)] * len(after),
         out_specs=(pl.BlockSpec(memory_space=VMEM), pl.BlockSpec(memory_space=VMEM)),
         scratch_shapes=[pltpu.SMEM((row_count,), jnp.int32)],
         compiler_params=params(),
         name="pack_children",
-    )(owner, offset, child_rows)
+    )(owner, offset, child_rows, *after)
 
 
 def triple(x, axis):
@@ -229,50 +232,74 @@
     )(front, child, tags)
 
 
-def product_kernel(has_front, base_ref, left_ref, place_ref, front_ref, child_ref, *rest):
+def product_kernel(blocks, chunks, base_ref, left_ref, place_ref, front_ref, child_ref, *rest):
     del base_ref
-    out_ref, whole_ref = rest[1:] if has_front else rest
+    outs, whole_ref = rest[-1 - chunks : -1], rest[-1]
     parts = jnp.concatenate(parts3(child_ref[...])[::-1], axis=0)
     whole = front_ref[...] + jnp.dot(place_ref[...], parts, preferred_element_type=F32)
     whole_ref[...] = whole
-    out_ref[...] = jnp.dot(left_ref[...], triple(whole, 0), preferred_element_type=F32)
-
-
-def product(base, left, place, front, child, whole, width):
+    result = jnp.dot(left_ref[...], triple(whole, 0), preferred_element_type=F32)
+    for at, out in enumerate(outs):
+
+        @pl.when(pl.program_id(0) // blocks == at)
+        def _():
+            out[...] = result
+
+
+def product(half, left, place, front, child, whole, chunks):
     rows, columns = front.shape
     slots = child.shape[0]
-    has_front = whole is not None
+    steps = columns // 2 // BLOCK
+    blocks = steps // chunks
     in_specs = [
-        pl.BlockSpec(left.shape, lambda i, b: (0, 0)),
-        pl.BlockSpec(place.shape, lambda i, b: (0, 0)),
-        pl.BlockSpec((rows, BLOCK), lambda i, b: (0, b[0] + i)),
-        pl.BlockSpec((slots, BLOCK), lambda i, b: (0, b[0] + i)),
+        pl.BlockSpec(left.shape, lambda i, h: (0, 0)),
+        pl.BlockSpec(place.shape, lambda i, h: (0, 0)),
+        pl.BlockSpec((rows, BLOCK), lambda i, h: (0, h[0] * steps + i)),
+        pl.BlockSpec((slots, BLOCK), lambda i, h: (0, h[0] * steps + i)),
     ]
-    operands = [base[None], left, place, front, child]
+    operands = [half[None], left, place, front, child]
     aliases = {}
-    if has_front:
+    if whole is not None:
         in_specs.append(pl.BlockSpec(memory_space=pl.ANY))
         operands.append(whole)
-        aliases = {5: 1}
-    return pl.pallas_call(
-        functools.partial(product_kernel, has_front),
+        aliases = {5: chunks}
+
+    def out_block(at):
+        return lambda i, h: (0, jnp.clip(i - at * blocks, 0, blocks - 1))
+
+    return pl.pallas_call(
+        functools.partial(product_kernel, blocks, chunks),
         grid_spec=pltpu.PrefetchScalarGridSpec(
             num_scalar_prefetch=1,
-            grid=(width // BLOCK,),
+            grid=(steps,),
             in_specs=in_specs,
-            out_specs=(
-                pl.BlockSpec((LEAD, BLOCK), lambda i, b: (0, i)),
-                pl.BlockSpec((rows, BLOCK), lambda i, b: (0, b[0] + i)),
-            ),
+            out_specs=tuple(pl.BlockSpec((LEAD, BLOCK), out_block(at)) for at in range(chunks))
+            + (pl.BlockSpec((rows, BLOCK), lambda i, h: (0, h[0] * steps + i)),),
         ),
-        out_shape=(
-            jax.ShapeDtypeStruct((LEAD, width), F32),
-            jax.ShapeDtypeStruct((rows, columns), F32),
-        ),
+        out_shape=(jax.ShapeDtypeStruct((LEAD, columns // 2 // chunks), F32),) * chunks
+        + (jax.ShapeDtypeStruct((rows, columns), F32),),
         input_output_aliases=aliases,
         compiler_params=params(),
         name="lead_product",
     )(*operands)
+
+
+def join_kernel(a_ref, b_ref, after_ref, out_ref):
+    del after_ref
+    half = a_ref.shape[0]
+    out_ref[:half, :] = a_ref[...]
+    out_ref[half:, :] = b_ref[...]
+
+
+def join(a, b, after):
+    return pl.pallas_call(
+        join_kernel,
+        out_shape=jax.ShapeDtypeStruct((2 * a.shape[0], a.shape[1]), F32),
+        in_specs=[pl.BlockSpec(memory_space=VMEM)] * 2 + [pl.BlockSpec(memory_space=pl.ANY)],
+        out_specs=pl.BlockSpec(memory_space=VMEM),
+        compiler_params=params(),
+        name="join_pieces",
+    )(a, b, after)
 
 
 def dot_high(a, b, dims):
@@ -399,11 +426,19 @@
     )(matrix, lead)
 
 
-def project_kernel(has_upper, places_ref, top_ref, bottom_ref, basis_ref, *rest):
+def project_kernel(blocks, places_ref, top_ref, bottom_ref, basis_ref, *rest):
     del places_ref
-    even_ref, odd_ref, front_ref = rest[:3]
-    upper_ref, out_ref = rest[4 if has_upper else 3 :]
-    sums = jnp.concatenate([even_ref[...], odd_ref[...]], axis=1)
+    near_even, near_odd, far_even, far_odd, front_ref = rest[:5]
+    upper_ref, out_ref, done_ref = rest[-3:]
+    done_ref[...] = jnp.zeros_like(done_ref)
+    near = pl.program_id(0) < blocks
+    sums = jnp.concatenate(
+        [
+            jnp.where(near, near_even[...], far_even[...]),
+            jnp.where(near, near_odd[...], far_odd[...]),
+        ],
+        axis=1,
+    )
     hi, lo = parts2(sums)
     upper_ref[:HALF, :] = jnp.dot(
         top_ref[...],
@@ -418,39 +453,51 @@
     )
 
 
-def project(places, factor, sums, front, upper):
+def project(columns_at, order, factor, near, far, front, upper):
     top, bottom, basis = factor
     rows, columns = front.shape
-    count = sums.shape[0] // LEAD
-    has_upper = upper is not None
+    blocks = near.shape[0] // LEAD // 2
+    near_at, far_at = 2 * blocks, 4 * blocks
+
+    def near_piece(odd):
+        return lambda i, p: (p[near_at + 2 * jnp.minimum(i, blocks - 1) + odd], 0)
+
+    def far_piece(odd):
+        return lambda i, p: (p[far_at + 2 * jnp.maximum(i - blocks, 0) + odd], 0)
+
     in_specs = [
         pl.BlockSpec(top.shape, lambda i, p: (0, 0)),
         pl.BlockSpec(bottom.shape, lambda i, p: (0, 0)),
         pl.BlockSpec(basis.shape, lambda i, p: (0, 0)),
-        pl.BlockSpec((LEAD, PB), lambda i, p: (p[1 + 2 * i], 0)),
-        pl.BlockSpec((LEAD, PB), lambda i, p: (p[2 + 2 * i], 0)),
-        pl.BlockSpec((rows, BLOCK), lambda i, p: (0, p[0] + i)),
+        pl.BlockSpec((LEAD, PB), near_piece(0)),
+        pl.BlockSpec((LEAD, PB), near_piece(1)),
+        pl.BlockSpec((LEAD, PB), far_piece(0)),
+        pl.BlockSpec((LEAD, PB), far_piece(1)),
+        pl.BlockSpec((rows, BLOCK), lambda i, p: (0, p[i])),
     ]
-    operands = [places, top, bottom, basis, sums, sums, front]
-    aliases = {6: 1}
-    if has_upper:
+    places = jnp.concatenate([columns_at, order[0], order[1]])
+    operands = [places, top, bottom, basis, near, near, far, far, front]
+    aliases = {8: 1}
+    if upper is not None:
         in_specs.append(pl.BlockSpec(memory_space=pl.ANY))
         operands.append(upper)
-        aliases[7] = 0
-    return pl.pallas_call(
-        functools.partial(project_kernel, has_upper),
+        aliases[9] = 0
+    return pl.pallas_call(
+        functools.partial(project_kernel, blocks),
         grid_spec=pltpu.PrefetchScalarGridSpec(
             num_scalar_prefetch=1,
-            grid=(count // 2,),
+            grid=(2 * blocks,),
             in_specs=in_specs,
             out_specs=(
-                pl.BlockSpec((LEAD, BLOCK), lambda i, p: (0, p[0] + i)),
-                pl.BlockSpec((rows, BLOCK), lambda i, p: (0, p[0] + i)),
+                pl.BlockSpec((LEAD, BLOCK), lambda i, p: (0, p[i])),
+                pl.BlockSpec((rows, BLOCK), lambda i, p: (0, p[i])),
+                pl.BlockSpec((8, PB), lambda i, p: (0, 0)),
             ),
         ),
         out_shape=(
             jax.ShapeDtypeStruct((LEAD, columns), F32),
             jax.ShapeDtypeStruct((rows, columns), F32),
+            jax.ShapeDtypeStruct((8, PB), F32),
         ),
         input_output_aliases=aliases,
         compiler_params=params(),
@@ -487,7 +534,7 @@
     )
     packed, tags = pack(child_rows, owner, offset, row_count, capacity, local_rows)
     child = exchange(packed, row_count)
-    packed, tags = pack(lead_child, owner, offset, row_count, capacity, local_rows)
+    packed, tags = pack(lead_child, owner, offset, row_count, capacity, local_rows, (child,))
     lead_child = exchange(jnp.concatenate([packed, tags], axis=1), row_count)
     lead, left, place, gram = lead_setup(lead_front, lead_child[:, :LEAD], lead_child[:, LEAD:])
 
@@ -501,32 +548,25 @@
     width = local_cols // 2 // chunks
     blocks = width // BLOCK
     core = upper_side(0, row_count)
-    front = None
-    shards = []
-    for c in range(chunks):
-        made = []
-        for half in (1 - core, core):
-            base = (half * chunks + c) * blocks
-            sums, front = product(base, left, place, front_matrix, child, front, width)
-            made.append(sums)
-        shards.append(scatter_sum(made[1], made[0], row_count))
+    *send, front = product(1 - core, left, place, front_matrix, child, None, chunks)
+    *keep, front = product(core, left, place, front_matrix, child, front, chunks)
+    shards = [scatter_sum(keep[c], send[c], row_count) for c in range(chunks)]
     steps = row_count.bit_length() - 1
-    held = []
+    order = jnp.asarray(piece_order(row_count))[me]
+    upper = None
+    done = []
     for c in range(chunks):
         buf = shards[c]
         for step in reversed(range(steps)):
             got = swap(buf, step, row_count)
-            if step == 0:
-                held.append((buf, got))
-            else:
+            if step == 1 and c >= LAG:
+                buf = join(buf, got, done[c - LAG])
+            elif step > 0:
                 buf = jnp.concatenate([buf, got], axis=0)
-    order = jnp.asarray(piece_order(row_count))[me]
-    upper = None
-    for c in range(chunks):
-        for which, half in enumerate((core, 1 - core)):
-            base = (half * chunks + c) * blocks
-            places = jnp.concatenate([base[None], order[which]])
-            upper, front = project(places, (top, bottom, basis), held[c][which], front, upper)
+        starts = [(half * chunks + c) * blocks for half in (core, 1 - core)]
+        columns_at = jnp.concatenate([s + jnp.arange(blocks, dtype=jnp.int32) for s in starts])
+        upper, front, at = project(columns_at, order, (top, bottom, basis), buf, got, front, upper)
+        done.append(at)
     return upper, front, scaled
 
 

time: 225 us -> 235 us (1.044)
  waiting for transfers between devices: 52.6 us -> 61.2 us
  other arithmetic: 9.85 us -> 13 us
    ppermute x6, waiting for transfers between devices: 16.7 us -> 28.2 us  [spread(): got = lax.ppermute(value, 'col', pairs)]
    pallas_call x16 -> x8, Pallas kernels: 57.6 us -> 49.1 us  [the longest x4 26.3 us: project(): pl.pallas_call(functools.partial(project_kernel, blocks), grid_spec=pltpu...]
    pallas_call x8, Pallas kernels: 2.06 us -> 8.56 us  [split_add(): pl.pallas_call(split_add_kernel, out_shape=(half, half), in_specs=[pl.Blo...]
    all_to_all x2, waiting for transfers between devices: 8.81 us -> 3.95 us  [exchange(): lax.all_to_all(shaped, 'row', split_axis=0, concat_axis=0, tiled=True)]
    all_to_all x2, starting transfers between devices: 9.89 us -> 14 us  [exchange(): lax.all_to_all(shaped, 'row', split_axis=0, concat_axis=0, tiled=True)]
    ppermute x6, starting transfers between devices: 12 us -> 8.55 us  [spread(): got = lax.ppermute(value, 'col', pairs)]
    unnamed x28 -> x30, local copies, waits for them, and re-layouts: 11.7 us -> 9.57 us
  transfers between devices with their start and end apart: 36 -> 36, of which waited for: 10 -> 9; matrix products, arithmetic and copies ran while one was open for 6% -> 7% of each run, Pallas kernels for 37% -> 32%
where the time goes in v6:
time: 235 us; the launch traced here: 231 us
  Pallas kernels  85.4 us (36%)
  waiting for transfers between devices  61.2 us (26%)
  starting transfers between devices  55.7 us (24%)
  local copies, waits for them, and re-layouts  14.8 us (6%)
  other arithmetic  13 us (6%)
    ppermute x28, starting transfers between devices, swap(): return lax.ppermute(value, 'row', pairs)  33.1 us
    ppermute x28, waiting for transfers between devices, swap(): return lax.ppermute(value, 'row', pairs)  29.1 us
    ppermute x6, waiting for transfers between devices, spread(): got = lax.ppermute(value, 'col', pairs)  28.2 us
    pallas_call x4, Pallas kernels, project(): pl.pallas_call(functools.partial(project_kernel, blocks), grid_spec=pltpu...  26.3 us
    pallas_call x2, Pallas kernels, product(): pl.pallas_call(functools.partial(product_kernel, blocks, chunks), grid_sp...  22.6 us
    pallas_call x4, Pallas kernels, eliminate(): pl.pallas_call(functools.partial(eliminate_kernel, k), out_shape=jax.Shap...  20.1 us
    all_to_all x2, starting transfers between devices, exchange(): lax.all_to_all(shaped, 'row', split_axis=0, concat_axis=0, tiled=True)  14 us
    unnamed x30, local copies, waits for them, and re-layouts  9.57 us
  transfers between devices with their start and end apart: 36, of which 9 were waited for; matrix products, arithmetic and copies ran while one was open for 7% of the time, Pallas kernels for 32%

profile of v6, /device:TPU:21, one launch (start us, length us, event | category | flops | bytes accessed | tf_op | source)
XLA Modules:
  0.0 231.3 jit_solution(17347000974147477718)
XLA Ops:
  6.6 4.5 %all-to-all-start = ((f32[8,16,4096]{2,1,0:T(8,128)}), f32[8,16,4096]{2,1,0:T(8,128)S(1)}, u32[]{:S(2)}, u32[]{:S(2)}) async-start(f32[8,16,4096]{2,1,0:T(8,128)} %bitcast.17), calls=%async_computation | async-start | bytes 4194304 | tf_op jit(solution)/shard_map/all_to_all | solution.py:512
  13.5 11.8 %collective-permute-done = f32[192,512]{1,0:T(8,128)S(1)} collective-permute-done((f32[192,512]{1,0:T(8,128)S(1)}, f32[192,512]{1,0:T(8,128)S(1)}, u32[]{:S(2)}, u32[]{:S(2)}) %collective-permute-start) | collective-permute-done | bytes 393248 | tf_op jit(solution)/shard_map/ppermute | solution.py:137
  30.1 11.5 %collective-permute-done.4 = f32[64,512]{1,0:T(8,128)S(1)} collective-permute-done((f32[64,512]{1,0:T(8,128)S(1)}, f32[64,512]{1,0:T(8,128)S(1)}, u32[]{:S(2)}, u32[]{:S(2)}) %collective-permute-start.4) | collective-permute-done | bytes 131104 | tf_op jit(solution)/shard_map/ppermute | solution.py:137
  48.3 4.9 %collective-permute-done.1 = f32[192,512]{1,0:T(8,128)S(1)} collective-permute-done((f32[192,512]{1,0:T(8,128)S(1)}, f32[192,512]{1,0:T(8,128)S(1)}, u32[]{:S(2)}, u32[]{:S(2)}) %collective-permute-start.1) | collective-permute-done | bytes 393248 | tf_op jit(solution)/shard_map/ppermute | solution.py:137
  55.2 9.5 %all-to-all-start.1 = ((f32[8,16,640]{2,1,0:T(8,128)}), f32[8,16,640]{2,1,0:T(8,128)}, u32[]{:S(2)}, u32[]{:S(2)}) async-start(f32[8,16,640]{2,1,0:T(8,128)} %bitcast.6), calls=%async_computation.1 | async-start | bytes 655360 | tf_op jit(solution)/shard_map/all_to_all | solution.py:512
  65.7 3.9 %all-to-all-done.1 = f32[8,16,640]{2,1,0:T(8,128)} async-done(((f32[8,16,640]{2,1,0:T(8,128)}), f32[8,16,640]{2,1,0:T(8,128)}, u32[]{:S(2)}, u32[]{:S(2)}) %all-to-all-start.1) | async-done | bytes 327712 | tf_op jit(solution)/shard_map/all_to_all | solution.py:512
  78.8 11.8 %lead_product.2 = (f32[512,512]{1,0:T(8,128)}, f32[512,512]{1,0:T(8,128)}, f32[512,512]{1,0:T(8,128)}, f32[512,512]{1,0:T(8,128)}, f32[384,4096]{1,0:T(8,128)}) custom-call(s32[1]{0:T(128)} %bitcast.11.base_ref, bf16[512,1152]{1,0:T(8,128)(2,1)S(1)} %get-tuple-element.58.left_ref, bf16[384,384]{1,0:T(8,128)(2,1)S(1)} %get-tuple-element.59.place_ref, ...), custom_call_target="tpu_custom_call" | custom-call | tf_op jit(solution)/shard_map/lead_product/pallas_call | solution.py:270
  95.5 5.4 %collective-permute-done.7 = f32[128,768]{1,0:T(8,128)} collective-permute-done((f32[128,768]{1,0:T(8,128)}, f32[128,768]{1,0:T(8,128)}, u32[]{:S(2)}, u32[]{:S(2)}) %collective-permute-start.7) | collective-permute-done | bytes 393248 | tf_op jit(solution)/shard_map/ppermute | solution.py:43
  104.8 10.8 %lead_product.3 = (f32[512,512]{1,0:T(8,128)S(1)}, f32[512,512]{1,0:T(8,128)S(1)}, f32[512,512]{1,0:T(8,128)S(1)}, f32[512,512]{1,0:T(8,128)S(1)}, f32[384,4096]{1,0:T(8,128)}) custom-call(s32[1]{0:T(128)} %bitcast.10.base_ref, bf16[512,1152]{1,0:T(8,128)(2,1)S(1)} %get-tuple-element.58.left_ref, ...), custom_call_target="tpu_custom_call", output_to_operand_aliasing={{4}: (5, {})} | custom-call | tf_op jit(solution)/shard_map/lead_product/pallas_call | solution.py:270
  126.7 3.3 %collective-permute-start.9 = (f32[128,768]{1,0:T(8,128)S(1)}, f32[128,768]{1,0:T(8,128)}, u32[]{:S(2)}, u32[]{:S(2)}) collective-permute-start(f32[128,768]{1,0:T(8,128)S(1)} %add.117), channel_id=1, source_target_pairs={{0,4},{4,0},{8,12},{12,8},{16,20},{20,16},{24,28},{28,24},{1,5},{5... | collective-permute-start | bytes 1179656 | tf_op jit(solution)/shard_map/ppermute | solution.py:43
  135.8 4.5 %collective-permute-done.22.got_ref = f32[512,256]{1,0:T(8,128)S(1)} collective-permute-done((f32[512,256]{1,0:T(8,128)}, f32[512,256]{1,0:T(8,128)S(1)}, u32[]{:S(2)}, u32[]{:S(2)}) %collective-permute-start.22) | collective-permute-done | bytes 524320 | tf_op jit(solution)/shard_map/ppermute | solution.py:43
  142.5 7.1 %collective-permute-done.29.got_ref = f32[512,256]{1,0:T(8,128)S(1)} collective-permute-done((f32[512,256]{1,0:T(8,128)}, f32[512,256]{1,0:T(8,128)S(1)}, u32[]{:S(2)}, u32[]{:S(2)}) %collective-permute-start.29) | collective-permute-done | bytes 524320 | tf_op jit(solution)/shard_map/ppermute | solution.py:43
  152.8 5.5 %eliminate_panel.4.in_ref = f32[512,512]{1,0:T(8,128)S(1)} custom-call(f32[256,768]{1,0:T(8,128)S(1)} %maximum_select_fusion.in_ref), custom_call_target="tpu_custom_call" | custom-call | flops 6000000000 | bytes 1048576 | tf_op jit(solution)/shard_map/eliminate_panel/pallas_call | solution.py:389
  160.0 5.2 %eliminate_panel.5.in_ref = f32[512,512]{1,0:T(8,128)S(1)} custom-call(f32[512,512]{1,0:T(8,128)S(1)} %eliminate_panel.4.in_ref), custom_call_target="tpu_custom_call" | custom-call | flops 6000000000 | bytes 1048576 | tf_op jit(solution)/shard_map/eliminate_panel/pallas_call | solution.py:389
  168.7 5.1 %eliminate_panel.6.in_ref = f32[512,512]{1,0:T(8,128)S(1)} custom-call(f32[512,512]{1,0:T(8,128)S(1)} %eliminate_panel.5.in_ref), custom_call_target="tpu_custom_call" | custom-call | flops 6000000000 | bytes 1048576 | tf_op jit(solution)/shard_map/eliminate_panel/pallas_call | solution.py:389
  174.2 10.2 %collective-permute-done.25 = f32[1024,128]{1,0:T(8,128)S(1)} collective-permute-done((f32[1024,128]{1,0:T(8,128)S(1)}, f32[1024,128]{1,0:T(8,128)S(1)}, u32[]{:S(2)}, u32[]{:S(2)}) %collective-permute-start.25) | collective-permute-done | bytes 524320 | tf_op jit(solution)/shard_map/ppermute | solution.py:43
  184.5 5.8 %collective-permute-start.26 = (f32[2048,128]{1,0:T(8,128)S(1)}, f32[2048,128]{1,0:T(8,128)S(1)}, u32[]{:S(2)}, u32[]{:S(2)}) collective-permute-start(f32[2048,128]{1,0:T(8,128)S(1)} %pad_maximum_fusion.1.rest_0_.rest_1_), channel_id=1, source_target_pairs={{0,4},{4,0},{8,12},{12,8},{16,20},{20,16},{24,28},{28,24},{1,5},{5... | collective-permute-start | bytes 3145736 | tf_op jit(solution)/shard_map/ppermute | solution.py:43
  190.4 4.3 %eliminate_panel.7.matrix_ref = f32[512,512]{1,0:T(8,128)S(1)} custom-call(f32[512,512]{1,0:T(8,128)S(1)} %eliminate_panel.6.in_ref), custom_call_target="tpu_custom_call" | custom-call | flops 6000000000 | bytes 1048576 | tf_op jit(solution)/shard_map/eliminate_panel/pallas_call | solution.py:389
  196.3 2.4 %finish_factor.1 = (bf16[256,768]{1,0:T(8,128)(2,1)S(1)}, bf16[256,1536]{1,0:T(8,128)(2,1)S(1)}, bf16[384,1536]{1,0:T(8,128)(2,1)S(1)}, f32[384,512]{1,0:T(8,128)}) custom-call(f32[512,512]{1,0:T(8,128)S(1)} %eliminate_panel.7.matrix_ref, f32[384,512]{1,0:T(8,128)S(1)} %copy-done.14), custom_call_target="tpu_custom_call" | custom-call | flops 2000000000 | bytes 1048576 | tf_op jit(solution)/shard_map/finish_factor/pallas_call | solution.py:413
  200.6 2.4 %collective-permute-start.14 = (f32[1024,128]{1,0:T(8,128)S(1)}, f32[1024,128]{1,0:T(8,128)S(1)}, u32[]{:S(2)}, u32[]{:S(2)}) collective-permute-start(f32[1024,128]{1,0:T(8,128)S(1)} %pad_maximum_fusion.3.a_ref), channel_id=1, source_target_pairs={{0,8},{4,20},{8,0},{12,28},{16,24},{20,4},{24,16},{28,12},{1,9},{5... | collective-permute-start | bytes 1572872 | tf_op jit(solution)/shard_map/ppermute | solution.py:43
  203.0 6.6 %project_columns.4 = (f32[512,4096]{1,0:T(8,128)}, f32[384,4096]{1,0:T(8,128)}, f32[8,128]{1,0:T(8,128)S(1)}) custom-call(s32[12]{0:T(128)S(1)} %get-tuple-element.101.places_ref, bf16[256,768]{1,0:T(8,128)(2,1)S(1)} %get-tuple-element.55.top_ref, bf16[256,1536]{1,0:T(8,128)(2,1)S(1)} %get-tuple-element.56.bottom_ref, ...), custom_call_target="tpu_custom_call", output_to_operand_aliasing={{1}: (8, {})} | custom-call | flops 3000000000 | bytes 1048576 | tf_op jit(solution)/shard_map/project_columns/pallas_call | solution.py:485
  211.4 6.6 %project_columns.5 = (f32[512,4096]{1,0:T(8,128)}, f32[384,4096]{1,0:T(8,128)}, f32[8,128]{1,0:T(8,128)S(1)}) custom-call(s32[12]{0:T(128)S(1)} %get-tuple-element.100.places_ref, bf16[256,768]{1,0:T(8,128)(2,1)S(1)} %get-tuple-element.55.top_ref, bf16[256,1536]{1,0:T(8,128)(2,1)S(1)} %get-tuple-element.56.bottom_ref, ...), custom_call_target="tpu_custom_call", output_to_operand_aliasing={{1}: (8, {}), {0}: (9, {})} | custom-call | flops 3000000000 | bytes 1048576 | tf_op jit(solution)/shard_map/project_columns/pallas_call | solution.py:485
  218.1 6.6 %project_columns.6 = (f32[512,4096]{1,0:T(8,128)}, f32[384,4096]{1,0:T(8,128)}, f32[8,128]{1,0:T(8,128)}) custom-call(s32[12]{0:T(128)S(1)} %get-tuple-element.99.places_ref, bf16[256,768]{1,0:T(8,128)(2,1)S(1)} %get-tuple-element.55.top_ref, bf16[256,1536]{1,0:T(8,128)(2,1)S(1)} %get-tuple-element.56.bottom_ref, ...), custom_call_target="tpu_custom_call", output_to_operand_aliasing={{1}: (8, {}), {0}: (9, {})} | custom-call | flops 3000000000 | bytes 1048576 | tf_op jit(solution)/shard_map/project_columns/pallas_call | solution.py:485
  224.7 6.6 %project_columns.7 = (f32[512,4096]{1,0:T(8,128)}, f32[384,4096]{1,0:T(8,128)}, f32[8,128]{1,0:T(8,128)}) custom-call(s32[12]{0:T(128)S(1)} %get-tuple-element.102.places_ref, bf16[256,768]{1,0:T(8,128)(2,1)S(1)} %get-tuple-element.55.top_ref, bf16[256,1536]{1,0:T(8,128)(2,1)S(1)} %get-tuple-element.56.bottom_ref, ...), custom_call_target="tpu_custom_call", output_to_operand_aliasing={{1}: (8, {}), {0}: (9, {})} | custom-call | flops 3000000000 | bytes 1048576 | tf_op jit(solution)/shard_map/project_columns/pallas_call | solution.py:485
  (138 shorter events, 73.9 us)
Async XLA Ops:
  6.6 46.6 %all-to-all-start = ((f32[8,16,4096]{2,1,0:T(8,128)}), f32[8,16,4096]{2,1,0:T(8,128)S(1)}, u32[]{:S(2)}, u32[]{:S(2)}) async-start(f32[8,16,4096]{2,1,0:T(8,128)} %bitcast.17), calls=%async_computation | async-start | bytes 4194304 | tf_op jit(solution)/shard_map/all_to_all | solution.py:512
  26.5 18.6 %collective-permute-start.2 = (f32[192,512]{1,0:T(8,128)S(1)}, f32[192,512]{1,0:T(8,128)S(1)}, u32[]{:S(2)}, u32[]{:S(2)}) collective-permute-start(f32[192,512]{1,0:T(8,128)S(1)} %get-tuple-element.98), channel_id=1, source_target_pairs={{0,2},{4,6},{8,10},{12,14},{16,18},{20,22},{24,26},{28,30}} | collective-permute-start | bytes 1179656 | tf_op jit(solution)/shard_map/ppermute | solution.py:137
  46.2 18.5 %collective-permute-start.3 = (f32[192,512]{1,0:T(8,128)S(1)}, f32[192,512]{1,0:T(8,128)}, u32[]{:S(2)}, u32[]{:S(2)}) collective-permute-start(f32[192,512]{1,0:T(8,128)S(1)} %broadcast_select_fusion), channel_id=1, source_target_pairs={{0,1},{2,3},{4,5},{6,7},{8,9},{10,11},{12,13},{14,15},{16,17},{18,... | collective-permute-start | bytes 1179656 | tf_op jit(solution)/shard_map/ppermute | solution.py:137
  55.2 14.4 %all-to-all-start.1 = ((f32[8,16,640]{2,1,0:T(8,128)}), f32[8,16,640]{2,1,0:T(8,128)}, u32[]{:S(2)}, u32[]{:S(2)}) async-start(f32[8,16,640]{2,1,0:T(8,128)} %bitcast.6), calls=%async_computation.1 | async-start | bytes 655360 | tf_op jit(solution)/shard_map/all_to_all | solution.py:512
  77.1 14.6 %collective-permute-start.6 = (f32[128,768]{1,0:T(8,128)}, f32[128,768]{1,0:T(8,128)}, u32[]{:S(2)}, u32[]{:S(2)}) collective-permute-start(f32[128,768]{1,0:T(8,128)} %constant_dynamic-slice_fusion), channel_id=1, source_target_pairs={{0,4},{4,0},{8,12},{12,8},{16,20},{20,16},{24,28},{28,24},{1,5},{5... | collective-permute-start | bytes 1179656 | tf_op jit(solution)/shard_map/ppermute | solution.py:43
  90.7 24.9 %collective-permute-start.10 = (f32[512,512]{1,0:T(8,128)}, f32[512,512]{1,0:T(8,128)}, u32[]{:S(2)}, u32[]{:S(2)}) collective-permute-start(f32[512,512]{1,0:T(8,128)} %get-tuple-element.62), channel_id=1, source_target_pairs={{0,4},{4,0},{8,12},{12,8},{16,20},{20,16},{24,28},{28,24},{1,5},{5... | collective-permute-start | bytes 3145736 | tf_op jit(solution)/shard_map/ppermute | solution.py:43
  90.7 29.0 %collective-permute-start.15 = (f32[512,512]{1,0:T(8,128)}, f32[512,512]{1,0:T(8,128)}, u32[]{:S(2)}, u32[]{:S(2)}) collective-permute-start(f32[512,512]{1,0:T(8,128)} %get-tuple-element.68), channel_id=1, source_target_pairs={{0,4},{4,0},{8,12},{12,8},{16,20},{20,16},{24,28},{28,24},{1,5},{5... | collective-permute-start | bytes 3145736 | tf_op jit(solution)/shard_map/ppermute | solution.py:43
  91.2 30.9 %collective-permute-start.21 = (f32[512,512]{1,0:T(8,128)}, f32[512,512]{1,0:T(8,128)S(1)}, u32[]{:S(2)}, u32[]{:S(2)}) collective-permute-start(f32[512,512]{1,0:T(8,128)} %get-tuple-element.74), channel_id=1, source_target_pairs={{0,4},{4,0},{8,12},{12,8},{16,20},{20,16},{24,28},{28,24},{1,5},{5... | collective-permute-start | bytes 3145736 | tf_op jit(solution)/shard_map/ppermute | solution.py:43
  91.3 33.0 %collective-permute-start.28 = (f32[512,512]{1,0:T(8,128)}, f32[512,512]{1,0:T(8,128)S(1)}, u32[]{:S(2)}, u32[]{:S(2)}) collective-permute-start(f32[512,512]{1,0:T(8,128)} %get-tuple-element.84), channel_id=1, source_target_pairs={{0,4},{4,0},{8,12},{12,8},{16,20},{20,16},{24,28},{28,24},{1,5},{5... | collective-permute-start | bytes 3145736 | tf_op jit(solution)/shard_map/ppermute | solution.py:43
  102.9 22.7 %collective-permute-start.8 = (f32[128,768]{1,0:T(8,128)}, f32[128,768]{1,0:T(8,128)}, u32[]{:S(2)}, u32[]{:S(2)}) collective-permute-start(f32[128,768]{1,0:T(8,128)} %add.116), channel_id=1, source_target_pairs={{0,16},{4,12},{8,24},{12,4},{16,0},{20,28},{24,8},{28,20},{1,17},{... | collective-permute-start | bytes 1179656 | tf_op jit(solution)/shard_map/ppermute | solution.py:43
  123.1 17.2 %collective-permute-start.22 = (f32[512,256]{1,0:T(8,128)}, f32[512,256]{1,0:T(8,128)S(1)}, u32[]{:S(2)}, u32[]{:S(2)}) collective-permute-start(f32[512,256]{1,0:T(8,128)} %get-tuple-element.76), channel_id=1, source_target_pairs={{0,8},{4,20},{8,0},{12,28},{16,24},{20,4},{24,16},{28,12},{1,9},{5... | collective-permute-start | bytes 1572872 | tf_op jit(solution)/shard_map/ppermute | solution.py:43
  125.3 24.3 %collective-permute-start.29 = (f32[512,256]{1,0:T(8,128)}, f32[512,256]{1,0:T(8,128)S(1)}, u32[]{:S(2)}, u32[]{:S(2)}) collective-permute-start(f32[512,256]{1,0:T(8,128)} %get-tuple-element.86), channel_id=1, source_target_pairs={{0,8},{4,20},{8,0},{12,28},{16,24},{20,4},{24,16},{28,12},{1,9},{5... | collective-permute-start | bytes 1572872 | tf_op jit(solution)/shard_map/ppermute | solution.py:43
  126.7 24.9 %collective-permute-start.9 = (f32[128,768]{1,0:T(8,128)S(1)}, f32[128,768]{1,0:T(8,128)}, u32[]{:S(2)}, u32[]{:S(2)}) collective-permute-start(f32[128,768]{1,0:T(8,128)S(1)} %add.117), channel_id=1, source_target_pairs={{0,4},{4,0},{8,12},{12,8},{16,20},{20,16},{24,28},{28,24},{1,5},{5... | collective-permute-start | bytes 1179656 | tf_op jit(solution)/shard_map/ppermute | solution.py:43
  133.0 61.7 %collective-permute-start.12 = (f32[512,128]{1,0:T(8,128)S(1)}, f32[512,128]{1,0:T(8,128)S(1)}, u32[]{:S(2)}, u32[]{:S(2)}) collective-permute-start(f32[512,128]{1,0:T(8,128)S(1)} %get-tuple-element.66), channel_id=1, source_target_pairs={{0,16},{4,12},{8,24},{12,4},{16,0},{20,28},{24,8},{28,20},{1,17},{... | collective-permute-start | bytes 786440 | tf_op jit(solution)/shard_map/ppermute | solution.py:43
  134.5 23.9 %collective-permute-start.17 = (f32[512,128]{1,0:T(8,128)S(1)}, f32[512,128]{1,0:T(8,128)S(1)}, u32[]{:S(2)}, u32[]{:S(2)}) collective-permute-start(f32[512,128]{1,0:T(8,128)S(1)} %get-tuple-element.72), channel_id=1, source_target_pairs={{0,16},{4,12},{8,24},{12,4},{16,0},{20,28},{24,8},{28,20},{1,17},{... | collective-permute-start | bytes 786440 | tf_op jit(solution)/shard_map/ppermute | solution.py:43
  140.3 18.1 %collective-permute-start.23 = (f32[512,128]{1,0:T(8,128)S(1)}, f32[512,128]{1,0:T(8,128)S(1)}, u32[]{:S(2)}, u32[]{:S(2)}) collective-permute-start(f32[512,128]{1,0:T(8,128)S(1)} %get-tuple-element.78), channel_id=1, source_target_pairs={{0,16},{4,12},{8,24},{12,4},{16,0},{20,28},{24,8},{28,20},{1,17},{... | collective-permute-start | bytes 786440 | tf_op jit(solution)/shard_map/ppermute | solution.py:43
  149.6 24.2 %collective-permute-start.30 = (f32[512,128]{1,0:T(8,128)S(1)}, f32[512,128]{1,0:T(8,128)S(1)}, u32[]{:S(2)}, u32[]{:S(2)}) collective-permute-start(f32[512,128]{1,0:T(8,128)S(1)} %get-tuple-element.88), channel_id=1, source_target_pairs={{0,16},{4,12},{8,24},{12,4},{16,0},{20,28},{24,8},{28,20},{1,17},{... | collective-permute-start | bytes 786440 | tf_op jit(solution)/shard_map/ppermute | solution.py:43
  165.3 25.0 %collective-permute-start.19 = (f32[1024,128]{1,0:T(8,128)S(1)}, f32[1024,128]{1,0:T(8,128)S(1)}, u32[]{:S(2)}, u32[]{:S(2)}) collective-permute-start(f32[1024,128]{1,0:T(8,128)S(1)} %pad_maximum_fusion.4), channel_id=1, source_target_pairs={{0,8},{4,20},{8,0},{12,28},{16,24},{20,4},{24,16},{28,12},{1,9},{5... | collective-permute-start | bytes 1572872 | tf_op jit(solution)/shard_map/ppermute | solution.py:43
  167.5 16.9 %collective-permute-start.25 = (f32[1024,128]{1,0:T(8,128)S(1)}, f32[1024,128]{1,0:T(8,128)S(1)}, u32[]{:S(2)}, u32[]{:S(2)}) collective-permute-start(f32[1024,128]{1,0:T(8,128)S(1)} %pad_maximum_fusion.5), channel_id=1, source_target_pairs={{0,8},{4,20},{8,0},{12,28},{16,24},{20,4},{24,16},{28,12},{1,9},{5... | collective-permute-start | bytes 1572872 | tf_op jit(solution)/shard_map/ppermute | solution.py:43
  173.8 21.0 %collective-permute-start.31 = (f32[512,128]{1,0:T(8,128)S(1)}, f32[512,128]{1,0:T(8,128)S(1)}, u32[]{:S(2)}, u32[]{:S(2)}) collective-permute-start(f32[512,128]{1,0:T(8,128)S(1)} %add.137), channel_id=1, source_target_pairs={{0,16},{4,12},{8,24},{12,4},{16,0},{20,28},{24,8},{28,20},{1,17},{... | collective-permute-start | bytes 786440 | tf_op jit(solution)/shard_map/ppermute | solution.py:43
  184.5 18.5 %collective-permute-start.26 = (f32[2048,128]{1,0:T(8,128)S(1)}, f32[2048,128]{1,0:T(8,128)S(1)}, u32[]{:S(2)}, u32[]{:S(2)}) collective-permute-start(f32[2048,128]{1,0:T(8,128)S(1)} %pad_maximum_fusion.1.rest_0_.rest_1_), channel_id=1, source_target_pairs={{0,4},{4,0},{8,12},{12,8},{16,20},{20,16},{24,28},{28,24},{1,5},{5... | collective-permute-start | bytes 3145736 | tf_op jit(solution)/shard_map/ppermute | solution.py:43
  190.3 21.0 %collective-permute-start.20 = (f32[2048,128]{1,0:T(8,128)S(1)}, f32[2048,128]{1,0:T(8,128)S(1)}, u32[]{:S(2)}, u32[]{:S(2)}) collective-permute-start(f32[2048,128]{1,0:T(8,128)S(1)} %pad_maximum_fusion.rest_0_.rest_1_), channel_id=1, source_target_pairs={{0,4},{4,0},{8,12},{12,8},{16,20},{20,16},{24,28},{28,24},{1,5},{5... | collective-permute-start | bytes 3145736 | tf_op jit(solution)/shard_map/ppermute | solution.py:43
  194.9 14.6 %collective-permute-start.32 = (f32[1024,128]{1,0:T(8,128)S(1)}, f32[1024,128]{1,0:T(8,128)S(1)}, u32[]{:S(2)}, u32[]{:S(2)}) collective-permute-start(f32[1024,128]{1,0:T(8,128)S(1)} %pad_maximum_fusion.6.a_ref), channel_id=1, source_target_pairs={{0,8},{4,20},{8,0},{12,28},{16,24},{20,4},{24,16},{28,12},{1,9},{5... | collective-permute-start | bytes 1572872 | tf_op jit(solution)/shard_map/ppermute | solution.py:43
  200.6 17.4 %collective-permute-start.14 = (f32[1024,128]{1,0:T(8,128)S(1)}, f32[1024,128]{1,0:T(8,128)S(1)}, u32[]{:S(2)}, u32[]{:S(2)}) collective-permute-start(f32[1024,128]{1,0:T(8,128)S(1)} %pad_maximum_fusion.3.a_ref), channel_id=1, source_target_pairs={{0,8},{4,20},{8,0},{12,28},{16,24},{20,4},{24,16},{28,12},{1,9},{5... | collective-permute-start | bytes 1572872 | tf_op jit(solution)/shard_map/ppermute | solution.py:43
  (27 other events, 270.3 us)

commit v7 on v6

--- a/solution.py
+++ b/solution.py
@@ -80,64 +80,84 @@
     return order
 
 
-def split_add_kernel(side_ref, keep_ref, got_ref, keep_out, send_out):
-    half = keep_out.shape[1]
-    for which, out in ((side_ref[0], keep_out), (1 - side_ref[0], send_out)):
-        part = pl.ds(pl.multiple_of(which * half, 128), half)
-        out[...] = keep_ref[:, part] + got_ref[:, part]
-
-
-def split_add(side, keep, got):
+def in_vmem(count):
+    return [pl.BlockSpec(memory_space=VMEM)] * count
+
+
+def ordered(name, body, operands, outs, after=()):
+    count = len(operands)
+
+    def kernel(*refs):
+        body(*refs[:count], *refs[count + len(after) :])
+
+    results = pl.pallas_call(
+        kernel,
+        out_shape=tuple(outs),
+        in_specs=in_vmem(count) + [pl.BlockSpec(memory_space=pl.ANY)] * len(after),
+        out_specs=tuple(in_vmem(len(outs))),
+        compiler_params=params(),
+        name=name,
+    )(*operands, *after)
+    return results if len(outs) > 1 else results[0]
+
+
+def add_body(a_ref, b_ref, out_ref):
+    out_ref[...] = a_ref[...] + b_ref[...]
+
+
+def split_add(step, count, keep, got, after):
+    def body(keep_ref, got_ref, keep_out, send_out):
+        half = keep_out.shape[1]
+        side = upper_side(step, count)
+        for which, out in ((side, keep_out), (1 - side, send_out)):
+            part = pl.ds(pl.multiple_of(which * half, 128), half)
+            out[...] = keep_ref[:, part] + got_ref[:, part]
+
     half = jax.ShapeDtypeStruct((keep.shape[0], keep.shape[1] // 2), F32)
-    return pl.pallas_call(
-        split_add_kernel,
-        out_shape=(half, half),
-        in_specs=[
-            pl.BlockSpec(memory_space=SMEM),
-            pl.BlockSpec(memory_space=VMEM),
-            pl.BlockSpec(memory_space=VMEM),
-        ],
-        out_specs=(pl.BlockSpec(memory_space=VMEM), pl.BlockSpec(memory_space=VMEM)),
-        compiler_params=params(),
-        name="split_add",
-    )(side[None], keep, got)
-
-
-def scatter_sum(keep, send, count):
+    return ordered("split_add", body, [keep, got], [half, half], after)
+
+
+def scatter_rest(keep, send, count, after):
     steps = count.bit_length() - 1
-    for step in range(steps):
+    for step in range(1, steps):
         got = swap(send, step, count)
         if step == steps - 1:
-            return keep + got
-        keep, send = split_add(upper_side(step + 1, count), keep, got)
-
-
-def total(value, count):
+            return keep + got, keep
+        keep, send = split_add(step + 1, count, keep, got, after if step == steps - 2 else ())
+
+
+def total(value, count, first_after, last_after):
     side = upper_side(0, count)
     half = value.shape[0] // 2
     keep = lax.dynamic_slice_in_dim(value, side * half, half, 0)
     send = lax.dynamic_slice_in_dim(value, (1 - side) * half, half, 0)
     mine = keep + swap(send, 0, count)
     for step in range(1, count.bit_length() - 1):
-        mine = mine + swap(mine, step, count)
-    got = swap(mine, 0, count)
-    return jnp.where(
-        side == 0,
-        jnp.concatenate([mine, got], axis=0),
-        jnp.concatenate([got, mine], axis=0),
-    )
-
-
-def spread(value, count):
-    me = lax.axis_index("col")
+        got = swap(mine, step, count)
+        mine = ordered(
+            "add_gram", add_body, [mine, got], [jax.ShapeDtypeStruct(mine.shape, F32)],
+            first_after * (step == 1) + last_after * (step == count.bit_length() - 2),
+        )
+    return mine, swap(mine, 0, count)
+
+
+def spread(value, count, after):
     stride = count
-    while stride > 1:
+    while True:
         half = stride // 2
-        pairs = [(c, c + half) for c in range(0, count, stride)]
-        got = lax.ppermute(value, "col", pairs)
-        value = jnp.where(me % stride == half, got, value)
+        got = lax.ppermute(value, "col", [(c, c + half) for c in range(0, count, stride)])
+        if half == 1:
+            return value, got
+        value = relay(value, got, stride, after)
         stride = half
-    return value
+
+
+def relay(value, got, stride, after):
+    def body(value_ref, got_ref, out_ref):
+        here = lax.axis_index("col") % stride == stride // 2
+        out_ref[...] = jnp.where(here, got_ref[...], value_ref[...])
+
+    return ordered("relay", body, [value, got], [jax.ShapeDtypeStruct(value.shape, F32)], after)
 
 
 def parts3(x):
@@ -152,10 +172,7 @@
     return hi, (x - hi.astype(F32)).astype(BF16)
 
 
-def pack_kernel(row_count, capacity, sentinel, owner_ref, offset_ref, child_ref, *rest):
-    out_ref, tag_ref, tally = rest[-3:]
-    out_ref[...] = jnp.zeros_like(out_ref)
-    tag_ref[...] = jnp.full(tag_ref.shape, sentinel, F32)
+def place_rows(row_count, capacity, owner_ref, tally, child_count, write):
     for d in range(row_count):
         tally[d] = 0
 
@@ -163,33 +180,68 @@
         owner = owner_ref[i]
         rank = tally[owner]
         tally[owner] = rank + 1
-        slot = owner * capacity + rank
-        out_ref[pl.ds(slot, 1), :] = child_ref[pl.ds(i, 1), :]
-        tag_ref[pl.ds(slot, 1), :] = jnp.full((1, tag_ref.shape[1]), offset_ref[i].astype(F32))
+        write(i, owner, rank)
         return carry
 
-    lax.fori_loop(0, child_ref.shape[0], body, 0)
-
-
-def pack(child_rows, owner, offset, row_count, capacity, sentinel, after=()):
+    lax.fori_loop(0, child_count, body, 0)
+
+
+def pack_kernel(row_count, capacity, owner_ref, child_ref, out_ref, tally):
+    out_ref[...] = jnp.zeros_like(out_ref)
+
+    def write(i, owner, rank):
+        out_ref[pl.ds(owner * capacity + rank, 1), :] = child_ref[pl.ds(i, 1), :]
+
+    place_rows(row_count, capacity, owner_ref, tally, child_ref.shape[0], write)
+
+
+def pack(child_rows, owner, row_count, capacity):
+    return pl.pallas_call(
+        functools.partial(pack_kernel, row_count, capacity),
+        out_shape=jax.ShapeDtypeStruct((row_count * capacity, child_rows.shape[1]), F32),
+        in_specs=[pl.BlockSpec(memory_space=SMEM)] + in_vmem(1),
+        out_specs=in_vmem(1)[0],
+        scratch_shapes=[pltpu.SMEM((row_count,), jnp.int32)],
+        compiler_params=params(),
+        name="pack_children",
+    )(owner, child_rows)
+
+
+def pack_lead_kernel(row_count, capacity, sentinel, owner_ref, offset_ref, even_ref, odd_ref, *refs):
+    outs, (child_ref, rows_ref, tag_ref, tally) = refs[:row_count], refs[row_count:]
+    child_ref[...] = jnp.where(lax.axis_index("col") % 2 == 0, even_ref[...], odd_ref[...])
+    rows_ref[...] = jnp.zeros_like(rows_ref)
+    tag_ref[...] = jnp.full(tag_ref.shape, sentinel, F32)
+    me = lax.axis_index("row")
+
+    def write(i, owner, rank):
+        slot = (owner ^ me) * capacity + rank
+        rows_ref[pl.ds(slot, 1), :] = child_ref[pl.ds(i, 1), :]
+        tag_ref[pl.ds(slot, 1), :] = jnp.full((1, PB), offset_ref[i].astype(F32))
+
+    place_rows(row_count, capacity, owner_ref, tally, child_ref.shape[0], write)
+    for at, out in enumerate(outs):
+        part = slice(at * capacity, (at + 1) * capacity)
+        out[:, :LEAD] = rows_ref[part, :]
+        out[:, LEAD:] = tag_ref[part, :]
+
+
+def pack_lead(even, odd, owner, offset, row_count, capacity, sentinel):
     slots = row_count * capacity
     return pl.pallas_call(
-        functools.partial(pack_kernel, row_count, capacity, float(sentinel)),
-        out_shape=(
-            jax.ShapeDtypeStruct((slots, child_rows.shape[1]), F32),
-            jax.ShapeDtypeStruct((slots, PB), F32),
-        ),
-        in_specs=[
-            pl.BlockSpec(memory_space=SMEM),
-            pl.BlockSpec(memory_space=SMEM),
-            pl.BlockSpec(memory_space=VMEM),
-        ]
-        + [pl.BlockSpec(memory_space=pl.ANY)] * len(after),
-        out_specs=(pl.BlockSpec(memory_space=VMEM), pl.BlockSpec(memory_space=VMEM)),
-        scratch_shapes=[pltpu.SMEM((row_count,), jnp.int32)],
-        compiler_params=params(),
-        name="pack_children",
-    )(owner, offset, child_rows, *after)
+        functools.partial(pack_lead_kernel, row_count, capacity, float(sentinel)),
+        out_shape=(jax.ShapeDtypeStruct((capacity, LEAD + PB), F32),) * row_count,
+        in_specs=[pl.BlockSpec(memory_space=SMEM)] * 2 + in_vmem(2),
+        out_specs=tuple(in_vmem(row_count)),
+        scratch_shapes=[
+            pltpu.VMEM(even.shape, F32),
+            pltpu.VMEM((slots, LEAD), F32),
+            pltpu.VMEM((slots, PB), F32),
+            pltpu.SMEM((row_count,), jnp.int32),
+        ],
+        compiler_params=params(),
+        name="pack_lead",
+    )(owner, offset, even, odd)
 
 
 def triple(x, axis):
@@ -197,16 +249,29 @@
     return jnp.concatenate([hi, hi, lo] if axis == 1 else [hi, lo, hi], axis=axis)
 
 
-def lead_kernel(front_ref, child_ref, tag_ref, lead_ref, left_ref, place_ref, gram_ref):
-    rows = front_ref.shape[0]
-    slots = child_ref.shape[0]
-    place = jnp.transpose(tag_ref[...])[0:1, :]
+def lead_kernel(row_count, *refs):
+    front_refs, piece_refs = refs[:4], refs[4 : 4 + row_count]
+    lead_ref, left_ref, place_ref, gram_ref = refs[4 + row_count :]
+    even = lax.axis_index("col") % 2 == 0
+    front = jnp.concatenate(
+        [jnp.where(even, a[...], b[...]) for a, b in zip(front_refs[::2], front_refs[1::2])], axis=0
+    )
+    me = lax.axis_index("row")
+    pieces = [ref[...] for ref in piece_refs]
+    bit = 1
+    while bit < row_count:
+        swapped = [pieces[at ^ bit] for at in range(row_count)]
+        pieces = [jnp.where((me & bit) != 0, b, a) for a, b in zip(pieces, swapped)]
+        bit *= 2
+    child = jnp.concatenate(pieces, axis=0)
+    rows, slots = front.shape[0], child.shape[0]
+    place = jnp.transpose(child[:, LEAD:])[0:1, :]
     at = lax.broadcasted_iota(jnp.int32, (rows, slots), 0).astype(F32)
     onehot = jnp.where(at == place, 1.0, 0.0).astype(BF16)
     spots = jnp.concatenate([onehot, onehot, onehot], axis=1)
     place_ref[...] = spots
-    parts = jnp.concatenate(parts3(child_ref[...])[::-1], axis=0)
-    lead = front_ref[...] + jnp.dot(spots, parts, preferred_element_type=F32)
+    parts = jnp.concatenate(parts3(child[:, :LEAD])[::-1], axis=0)
+    lead = front + jnp.dot(spots, parts, preferred_element_type=F32)
     lead_ref[...] = lead
     turned = jnp.transpose(lead)
     left_ref[...] = triple(turned, 1)
@@ -214,22 +279,22 @@
     gram_ref[:, HALF:] = dot_high(turned[HALF:], lead, ((1,), (0,)))
 
 
-def lead_setup(front, child, tags):
-    rows = front.shape[0]
-    slots = child.shape[0]
+def lead_setup(fronts, pieces, rows):
+    slots = len(pieces) * pieces[0].shape[0]
+    operands = list(fronts) + list(pieces)
     return pl.pallas_call(
-        lead_kernel,
+        functools.partial(lead_kernel, len(pieces)),
         out_shape=(
             jax.ShapeDtypeStruct((rows, LEAD), F32),
             jax.ShapeDtypeStruct((LEAD, 3 * rows), BF16),
             jax.ShapeDtypeStruct((rows, 3 * slots), BF16),
             jax.ShapeDtypeStruct((HALF, LEAD + HALF), F32),
         ),
-        in_specs=[pl.BlockSpec(memory_space=VMEM)] * 3,
-        out_specs=(pl.BlockSpec(memory_space=VMEM),) * 4,
+        in_specs=in_vmem(len(operands)),
+        out_specs=tuple(in_vmem(4)),
         compiler_params=params(),
         name="lead_setup",
-    )(front, child, tags)
+    )(*operands)
 
 
 def product_kernel(blocks, chunks, base_ref, left_ref, place_ref, front_ref, child_ref, *rest):
@@ -284,22 +349,14 @@
     )(*operands)
 
 
-def join_kernel(a_ref, b_ref, after_ref, out_ref):
-    del after_ref
-    half = a_ref.shape[0]
-    out_ref[:half, :] = a_ref[...]
-    out_ref[half:, :] = b_ref[...]
-
-
 def join(a, b, after):
-    return pl.pallas_call(
-        join_kernel,
-        out_shape=jax.ShapeDtypeStruct((2 * a.shape[0], a.shape[1]), F32),
-        in_specs=[pl.BlockSpec(memory_space=VMEM)] * 2 + [pl.BlockSpec(memory_space=pl.ANY)],
-        out_specs=pl.BlockSpec(memory_space=VMEM),
-        compiler_params=params(),
-        name="join_pieces",
-    )(a, b, after)
+    def body(a_ref, b_ref, out_ref):
+        half = a_ref.shape[0]
+        out_ref[:half, :] = a_ref[...]
+        out_ref[half:, :] = b_ref[...]
+
+    shape = jax.ShapeDtypeStruct((2 * a.shape[0], a.shape[1]), F32)
+    return ordered("join_pieces", body, [a, b], [shape], after)
 
 
 def dot_high(a, b, dims):
@@ -357,14 +414,18 @@
     return jnp.concatenate(done, axis=0)
 
 
-def eliminate_kernel(k, in_ref, out_ref):
+def eliminate_kernel(k, *refs):
+    in_ref, out_ref = refs[0], refs[-1]
     lo, hi = k * PB, (k + 1) * PB
     if k == 0:
-        cross = in_ref[:, HALF:LEAD]
-        out_ref[:HALF, :HALF] = in_ref[:, :HALF]
+        mine, got = refs[0][...], refs[1][...]
+        low = lax.axis_index("row") % 2 == 0
+        packed = jnp.concatenate([jnp.where(low, mine, got), jnp.where(low, got, mine)], axis=0)
+        cross = packed[:, HALF:LEAD]
+        out_ref[:HALF, :HALF] = packed[:, :HALF]
         out_ref[HALF:, :HALF] = cross
         out_ref[:HALF, HALF:] = jnp.transpose(cross)
-        out_ref[HALF:, HALF:] = in_ref[:, LEAD:]
+        out_ref[HALF:, HALF:] = packed[:, LEAD:]
         in_ref = out_ref
     else:
         out_ref[:lo, :] = in_ref[:lo, :]
@@ -385,16 +446,16 @@
         out_ref[hi:, lo:hi] = -change[:, lo:hi]
 
 
-def eliminate(matrix, k):
+def eliminate(operands, k):
     return pl.pallas_call(
         functools.partial(eliminate_kernel, k),
         out_shape=jax.ShapeDtypeStruct((LEAD, LEAD), F32),
-        in_specs=[pl.BlockSpec(memory_space=VMEM)],
-        out_specs=pl.BlockSpec(memory_space=VMEM),
+        in_specs=in_vmem(len(operands)),
+        out_specs=in_vmem(1)[0],
         compiler_params=params(),
         cost_estimate=cost(6 * 10**9),
         name="eliminate_panel",
-    )(matrix)
+    )(*operands)
 
 
 def finish_kernel(scale, matrix_ref, lead_ref, top_ref, bottom_ref, basis3_ref, basis_ref):
@@ -453,11 +514,13 @@
     )
 
 
-def project(columns_at, order, factor, near, far, front, upper):
+def project(places, c, chunks, factor, near, far, front, upper):
     top, bottom, basis = factor
     rows, columns = front.shape
     blocks = near.shape[0] // LEAD // 2
-    near_at, far_at = 2 * blocks, 4 * blocks
+    begin = c * 2 * blocks
+    near_at = chunks * 2 * blocks
+    far_at = near_at + 2 * blocks
 
     def near_piece(odd):
         return lambda i, p: (p[near_at + 2 * jnp.minimum(i, blocks - 1) + odd], 0)
@@ -473,9 +536,8 @@
         pl.BlockSpec((LEAD, PB), near_piece(1)),
         pl.BlockSpec((LEAD, PB), far_piece(0)),
         pl.BlockSpec((LEAD, PB), far_piece(1)),
-        pl.BlockSpec((rows, BLOCK), lambda i, p: (0, p[i])),
+        pl.BlockSpec((rows, BLOCK), lambda i, p: (0, p[begin + i])),
     ]
-    places = jnp.concatenate([columns_at, order[0], order[1]])
     operands = [places, top, bottom, basis, near, near, far, far, front]
     aliases = {8: 1}
     if upper is not None:
@@ -489,8 +551,8 @@
             grid=(2 * blocks,),
             in_specs=in_specs,
             out_specs=(
-                pl.BlockSpec((LEAD, BLOCK), lambda i, p: (0, p[i])),
-                pl.BlockSpec((rows, BLOCK), lambda i, p: (0, p[i])),
+                pl.BlockSpec((LEAD, BLOCK), lambda i, p: (0, p[begin + i])),
+                pl.BlockSpec((rows, BLOCK), lambda i, p: (0, p[begin + i])),
                 pl.BlockSpec((8, PB), lambda i, p: (0, 0)),
             ),
         ),
@@ -523,26 +585,31 @@
     me = lax.axis_index("row")
 
     owner, offset = child_owner[:, 0], child_offset[:, 0]
-    lead_child = spread(child_rows[:, :LEAD], col_count)
+    packed = pack(child_rows, owner, row_count, capacity)
+    child = exchange(packed, row_count)
+    lead_rows = child_rows[:, :LEAD]
+    first = lax.ppermute(lead_rows, "col", [(0, col_count // 2)])
     cut = local_rows // 2
-    lead_front = jnp.concatenate(
-        [
-            spread(front_matrix[:cut, :LEAD], col_count),
-            spread(front_matrix[cut:, :LEAD], col_count),
-        ],
-        axis=0,
-    )
-    packed, tags = pack(child_rows, owner, offset, row_count, capacity, local_rows)
-    child = exchange(packed, row_count)
-    packed, tags = pack(lead_child, owner, offset, row_count, capacity, local_rows, (child,))
-    lead_child = exchange(jnp.concatenate([packed, tags], axis=1), row_count)
-    lead, left, place, gram = lead_setup(lead_front, lead_child[:, :LEAD], lead_child[:, LEAD:])
-
-    matrix = total(gram, row_count)
-    for k in range(PANELS):
-        matrix = eliminate(matrix, k)
-    scale = math.sqrt(local_rows * row_count)
-    top, bottom, basis, scaled = finish(matrix, lead, scale)
+
+    def cut_body(front_ref, low_ref, high_ref):
+        low_ref[...] = front_ref[:cut, :]
+        high_ref[...] = front_ref[cut:, :]
+
+    low, high = ordered(
+        "cut_lead", cut_body, [front_matrix[:, :LEAD]],
+        [jax.ShapeDtypeStruct((cut, LEAD), F32)] * 2, (first,),
+    )
+    passed = relay(lead_rows, first, col_count, ())
+    stride = col_count // 2
+    pairs = [(c, c + stride // 2) for c in range(0, col_count, stride)]
+    pieces = list(
+        pack_lead(passed, lax.ppermute(passed, "col", pairs), owner, offset, row_count, capacity, local_rows)
+    )
+    for mask in range(1, row_count):
+        pairs = [(d, d ^ mask) for d in range(row_count)]
+        pieces[mask] = lax.ppermute(pieces[mask], "row", pairs)
+    fronts = spread(low, col_count, (passed,)) + spread(high, col_count, (child, pieces[0]))
+    lead, left, place, gram = lead_setup(fronts, pieces, local_rows)
 
     chunks = max(1, min(4, local_cols // (PB * row_count)))
     width = local_cols // 2 // chunks
@@ -550,22 +617,48 @@
     core = upper_side(0, row_count)
     *send, front = product(1 - core, left, place, front_matrix, child, None, chunks)
     *keep, front = product(core, left, place, front_matrix, child, front, chunks)
-    shards = [scatter_sum(keep[c], send[c], row_count) for c in range(chunks)]
+
+    halves = [split_add(1, row_count, keep[c], swap(send[c], 0, row_count), ()) for c in range(chunks)]
+
+    matrix = total(gram, row_count, (keep[0],), tuple(h[0] for h in halves))
+    made = []
+    for k in range(PANELS):
+        matrix = [eliminate(matrix, k)]
+        made.append(matrix[0])
+    matrix = matrix[0]
+    scale = math.sqrt(local_rows * row_count)
+    top, bottom, basis, scaled = finish(matrix, lead, scale)
+
+    shards = [
+        scatter_rest(*halves[c], row_count, (made[min(c, PANELS - 1)],))
+        for c in range(chunks)
+    ]
     steps = row_count.bit_length() - 1
-    order = jnp.asarray(piece_order(row_count))[me]
+    columns_at = [
+        [
+            ((d & 1) ^ side) * chunks * blocks + c * blocks + b
+            for c in range(chunks)
+            for side in range(2)
+            for b in range(blocks)
+        ]
+        for d in range(row_count)
+    ]
+    order = piece_order(row_count).reshape(row_count, -1)
+    table = np.concatenate([np.array(columns_at, np.int32), order], axis=1)
+    places = lax.dynamic_index_in_dim(jnp.asarray(table), me, 0, keepdims=False)
     upper = None
     done = []
     for c in range(chunks):
-        buf = shards[c]
+        buf = shards[c][0]
         for step in reversed(range(steps)):
             got = swap(buf, step, row_count)
-            if step == 1 and c >= LAG:
-                buf = join(buf, got, done[c - LAG])
+            if step == steps - 1 and step > 1:
+                buf = join(buf, got, tuple(keep for _, keep in shards))
+            elif step == 1 and c >= LAG:
+                buf = join(buf, got, (done[c - LAG],))
             elif step > 0:
                 buf = jnp.concatenate([buf, got], axis=0)
-        starts = [(half * chunks + c) * blocks for half in (core, 1 - core)]
-        columns_at = jnp.concatenate([s + jnp.arange(blocks, dtype=jnp.int32) for s in starts])
-        upper, front, at = project(columns_at, order, (top, bottom, basis), buf, got, front, upper)
+        upper, front, at = project(places, c, chunks, (top, bottom, basis), buf, got, front, upper)
         done.append(at)
     return upper, front, scaled
 

time: 235 us -> 218 us (0.928)
  the two profiles are of different devices: /device:TPU:21 before, /device:TPU:0 now
where the time goes in v7:
time: 218 us; the launch traced here: 217 us
  Pallas kernels  84.1 us (39%)
  waiting for transfers between devices  59.3 us (27%)
  starting transfers between devices  50.5 us (23%)
  local copies, waits for them, and re-layouts  19.6 us (9%)
  other arithmetic  2.36 us (1%)
    ppermute x28, waiting for transfers between devices, swap(): return lax.ppermute(value, 'row', pairs)  34.5 us
    pallas_call x4, Pallas kernels, project(): pl.pallas_call(functools.partial(project_kernel, blocks), grid_spec=pltpu...  27.1 us
    pallas_call x2, Pallas kernels, product(): pl.pallas_call(functools.partial(product_kernel, blocks, chunks), grid_sp...  22.6 us
    ppermute x28, starting transfers between devices, swap(): return lax.ppermute(value, 'row', pairs)  20.4 us
    pallas_call x4, Pallas kernels, eliminate(): pl.pallas_call(functools.partial(eliminate_kernel, k), out_shape=jax.Shap...  20.1 us
    ppermute x1, waiting for transfers between devices, on_device(): lax.ppermute(passed, 'col', pairs)  16.8 us
    unnamed x48, local copies, waits for them, and re-layouts  16 us
    ppermute x4, starting transfers between devices, spread(): lax.ppermute(value, 'col', [(c, c + half) for c in range(0, count, stride)])  13.1 us
  transfers between devices with their start and end apart: 42, of which 14 were waited for; matrix products, arithmetic and copies ran while one was open for 2% of the time, Pallas kernels for 34%

profile of v7, /device:TPU:0, one launch (start us, length us, event | category | flops | bytes accessed | tf_op | source)
XLA Modules:
  0.0 217.0 jit_solution(14540302611842053)
XLA Ops:
  5.3 5.2 %all-to-all-start = ((f32[8,16,4096]{2,1,0:T(8,128)}), f32[8,16,4096]{2,1,0:T(8,128)S(1)}, u32[]{:S(2)}, u32[]{:S(2)}) async-start(f32[8,16,4096]{2,1,0:T(8,128)} %bitcast.11), calls=%async_computation | async-start | bytes 4194304 | tf_op jit(solution)/shard_map/all_to_all | solution.py:574
  11.4 4.5 %collective-permute-start = (f32[64,512]{1,0:T(8,128)S(1)}, f32[64,512]{1,0:T(8,128)S(1)}, u32[]{:S(2)}, u32[]{:S(2)}) collective-permute-start(f32[64,512]{1,0:T(8,128)S(1)} %slice.7.refs_0_), channel_id=1, source_target_pairs={{0,2},{4,6},{8,10},{12,14},{16,18},{20,22},{24,26},{28,30}} | collective-permute-start | bytes 393224 | tf_op jit(solution)/shard_map/ppermute | solution.py:591
  17.1 2.2 %collective-permute-done.refs_1_ = f32[64,512]{1,0:T(8,128)S(1)} collective-permute-done((f32[64,512]{1,0:T(8,128)S(1)}, f32[64,512]{1,0:T(8,128)S(1)}, u32[]{:S(2)}, u32[]{:S(2)}) %collective-permute-start) | collective-permute-done | bytes 131104 | tf_op jit(solution)/shard_map/ppermute | solution.py:591
  19.3 5.3 %collective-permute-start.1 = (f32[192,512]{1,0:T(8,128)S(1)}, f32[192,512]{1,0:T(8,128)S(1)}, u32[]{:S(2)}, u32[]{:S(2)}) collective-permute-start(f32[192,512]{1,0:T(8,128)S(1)} %get-tuple-element.57.refs_0_), channel_id=1, source_target_pairs={{0,2},{4,6},{8,10},{12,14},{16,18},{20,22},{24,26},{28,30}} | collective-permute-start | bytes 1179656 | tf_op jit(solution)/shard_map/ppermute | solution.py:148
  27.3 16.8 %collective-permute-done.4.odd_ref = f32[64,512]{1,0:T(8,128)S(1)} collective-permute-done((f32[64,512]{1,0:T(8,128)S(1)}, f32[64,512]{1,0:T(8,128)S(1)}, u32[]{:S(2)}, u32[]{:S(2)}) %collective-permute-start.4) | collective-permute-done | bytes 131104 | tf_op jit(solution)/shard_map/ppermute | solution.py:606
  47.3 5.2 %collective-permute-start.2 = (f32[192,512]{1,0:T(8,128)S(1)}, f32[192,512]{1,0:T(8,128)}, u32[]{:S(2)}, u32[]{:S(2)}) collective-permute-start(f32[192,512]{1,0:T(8,128)S(1)} %relay.4.refs_0_), channel_id=1, source_target_pairs={{0,1},{2,3},{4,5},{6,7},{8,9},{10,11},{12,13},{14,15},{16,17},{18,... | collective-permute-start | bytes 1179656 | tf_op jit(solution)/shard_map/ppermute | solution.py:148
  64.5 2.3 %collective-permute-done.11.refs_10_ = f32[16,640]{1,0:T(8,128)} collective-permute-done((f32[16,640]{1,0:T(8,128)}, f32[16,640]{1,0:T(8,128)}, u32[]{:S(2)}, u32[]{:S(2)}) %collective-permute-start.11) | collective-permute-done | bytes 40992 | tf_op jit(solution)/shard_map/ppermute | solution.py:610
  72.1 3.1 %lead_setup.1 = (f32[384,512]{1,0:T(8,128)S(1)}, bf16[512,1152]{1,0:T(8,128)(2,1)S(1)}, bf16[384,384]{1,0:T(8,128)(2,1)S(1)}, f32[256,768]{1,0:T(8,128)S(1)}) custom-call(f32[192,512]{1,0:T(8,128)S(1)} %copy-done.5, f32[192,512]{1,0:T(8,128)} %collective-permute-done.2.refs_1_, f32[192,512]{1,0:T(8,128)S(1)} %copy-done.3, f32[192,512]{1,0:T(8,128)S(1)} %copy-done.15, ...), custom_call_target="tpu_custom_call" | custom-call | tf_op jit(solution)/shard_map/lead_setup/pallas_call | solution.py:285
  78.0 11.8 %lead_product.2 = (f32[512,512]{1,0:T(8,128)}, f32[512,512]{1,0:T(8,128)}, f32[512,512]{1,0:T(8,128)}, f32[512,512]{1,0:T(8,128)}, f32[384,4096]{1,0:T(8,128)}) custom-call(s32[1]{0:T(128)} %bitcast.6.base_ref, bf16[512,1152]{1,0:T(8,128)(2,1)S(1)} %get-tuple-element.68.left_ref, bf16[384,384]{1,0:T(8,128)(2,1)S(1)} %get-tuple-element.69.place_ref, ...), custom_call_target="tpu_custom_call" | custom-call | tf_op jit(solution)/shard_map/lead_product/pallas_call | solution.py:335
  94.2 10.8 %lead_product.3 = (f32[512,512]{1,0:T(8,128)S(1)}, f32[512,512]{1,0:T(8,128)S(1)}, f32[512,512]{1,0:T(8,128)S(1)}, f32[512,512]{1,0:T(8,128)S(1)}, f32[384,4096]{1,0:T(8,128)}) custom-call(s32[1]{0:T(128)} %bitcast.5.base_ref, bf16[512,1152]{1,0:T(8,128)(2,1)S(1)} %get-tuple-element.68.left_ref, ...), custom_call_target="tpu_custom_call", output_to_operand_aliasing={{4}: (5, {})} | custom-call | tf_op jit(solution)/shard_map/lead_product/pallas_call | solution.py:335
  109.0 3.8 %collective-permute-done.15.refs_1_ = f32[128,768]{1,0:T(8,128)S(1)} collective-permute-done((f32[128,768]{1,0:T(8,128)S(1)}, f32[128,768]{1,0:T(8,128)S(1)}, u32[]{:S(2)}, u32[]{:S(2)}) %collective-permute-start.15) | collective-permute-done | bytes 393248 | tf_op jit(solution)/shard_map/ppermute | solution.py:43
  117.1 5.5 %eliminate_panel.4.refs_0_.refs_2_ = f32[512,512]{1,0:T(8,128)S(1)} custom-call(f32[128,768]{1,0:T(8,128)S(1)} %add_gram.3.refs_0_, f32[128,768]{1,0:T(8,128)S(1)} %collective-permute-done.20.refs_1_), custom_call_target="tpu_custom_call" | custom-call | flops 6000000000 | bytes 1048576 | tf_op jit(solution)/shard_map/eliminate_panel/pallas_call | solution.py:450
  122.6 5.2 %eliminate_panel.5.refs_0_.refs_2_ = f32[512,512]{1,0:T(8,128)S(1)} custom-call(f32[512,512]{1,0:T(8,128)S(1)} %eliminate_panel.4.refs_0_.refs_2_), custom_call_target="tpu_custom_call" | custom-call | flops 6000000000 | bytes 1048576 | tf_op jit(solution)/shard_map/eliminate_panel/pallas_call | solution.py:450
  128.8 5.1 %eliminate_panel.6.refs_0_.refs_2_ = f32[512,512]{1,0:T(8,128)S(1)} custom-call(f32[512,512]{1,0:T(8,128)S(1)} %eliminate_panel.5.refs_0_.refs_2_), custom_call_target="tpu_custom_call" | custom-call | flops 6000000000 | bytes 1048576 | tf_op jit(solution)/shard_map/eliminate_panel/pallas_call | solution.py:450
  138.2 4.3 %eliminate_panel.7.matrix_ref.refs_2_ = f32[512,512]{1,0:T(8,128)S(1)} custom-call(f32[512,512]{1,0:T(8,128)S(1)} %eliminate_panel.6.refs_0_.refs_2_), custom_call_target="tpu_custom_call" | custom-call | flops 6000000000 | bytes 1048576 | tf_op jit(solution)/shard_map/eliminate_panel/pallas_call | solution.py:450
  142.6 4.9 %collective-permute-done.21.refs_1_ = f32[512,256]{1,0:T(8,128)S(1)} collective-permute-done((f32[512,256]{1,0:T(8,128)S(1)}, f32[512,256]{1,0:T(8,128)S(1)}, u32[]{:S(2)}, u32[]{:S(2)}) %collective-permute-start.21) | collective-permute-done | bytes 524320 | tf_op jit(solution)/shard_map/ppermute | solution.py:43
  150.3 8.3 %collective-permute-done.29.refs_1_ = f32[512,128]{1,0:T(8,128)S(1)} collective-permute-done((f32[512,128]{1,0:T(8,128)S(1)}, f32[512,128]{1,0:T(8,128)S(1)}, u32[]{:S(2)}, u32[]{:S(2)}) %collective-permute-start.29) | collective-permute-done | bytes 262176 | tf_op jit(solution)/shard_map/ppermute | solution.py:43
  160.7 10.0 %collective-permute-done.30 = f32[1024,128]{1,0:T(8,128)S(1)} collective-permute-done((f32[1024,128]{1,0:T(8,128)S(1)}, f32[1024,128]{1,0:T(8,128)S(1)}, u32[]{:S(2)}, u32[]{:S(2)}) %collective-permute-start.30) | collective-permute-done | bytes 524320 | tf_op jit(solution)/shard_map/ppermute | solution.py:43
  173.0 4.6 %collective-permute-done.22 = f32[512,128]{1,0:T(8,128)} collective-permute-done((f32[512,128]{1,0:T(8,128)}, f32[512,128]{1,0:T(8,128)}, u32[]{:S(2)}, u32[]{:S(2)}) %collective-permute-start.22) | collective-permute-done | bytes 262176 | tf_op jit(solution)/shard_map/ppermute | solution.py:43
  185.7 2.4 %finish_factor.1 = (bf16[256,768]{1,0:T(8,128)(2,1)S(1)}, bf16[256,1536]{1,0:T(8,128)(2,1)S(1)}, bf16[384,1536]{1,0:T(8,128)(2,1)S(1)}, f32[384,512]{1,0:T(8,128)}) custom-call(f32[512,512]{1,0:T(8,128)S(1)} %copy-done.10, f32[384,512]{1,0:T(8,128)S(1)} %copy-done.20), custom_call_target="tpu_custom_call" | custom-call | flops 2000000000 | bytes 1048576 | tf_op jit(solution)/shard_map/finish_factor/pallas_call | solution.py:474
  189.1 7.0 %project_columns.4 = (f32[512,4096]{1,0:T(8,128)}, f32[384,4096]{1,0:T(8,128)}, f32[8,128]{1,0:T(8,128)S(1)}) custom-call(s32[24]{0:T(128)S(1)} %fusion.places_ref, bf16[256,768]{1,0:T(8,128)(2,1)S(1)} %get-tuple-element.84.top_ref, bf16[256,1536]{1,0:T(8,128)(2,1)S(1)} %get-tuple-element.85.bottom_ref, ...), custom_call_target="tpu_custom_call", output_to_operand_aliasing={{1}: (8, {})} | custom-call | flops 3000000000 | bytes 1048576 | tf_op jit(solution)/shard_map/project_columns/pallas_call | solution.py:547
  196.2 7.0 %project_columns.5 = (f32[512,4096]{1,0:T(8,128)}, f32[384,4096]{1,0:T(8,128)}, f32[8,128]{1,0:T(8,128)S(1)}) custom-call(s32[24]{0:T(128)S(1)} %fusion.places_ref, bf16[256,768]{1,0:T(8,128)(2,1)S(1)} %get-tuple-element.84.top_ref, bf16[256,1536]{1,0:T(8,128)(2,1)S(1)} %get-tuple-element.85.bottom_ref, ...), custom_call_target="tpu_custom_call", output_to_operand_aliasing={{1}: (8, {}), {0}: (9, {})} | custom-call | flops 3000000000 | bytes 1048576 | tf_op jit(solution)/shard_map/project_columns/pallas_call | solution.py:547
  203.8 6.6 %project_columns.6 = (f32[512,4096]{1,0:T(8,128)}, f32[384,4096]{1,0:T(8,128)}, f32[8,128]{1,0:T(8,128)}) custom-call(s32[24]{0:T(128)S(1)} %fusion.places_ref, bf16[256,768]{1,0:T(8,128)(2,1)S(1)} %get-tuple-element.84.top_ref, bf16[256,1536]{1,0:T(8,128)(2,1)S(1)} %get-tuple-element.85.bottom_ref, ...), custom_call_target="tpu_custom_call", output_to_operand_aliasing={{1}: (8, {}), {0}: (9, {})} | custom-call | flops 3000000000 | bytes 1048576 | tf_op jit(solution)/shard_map/project_columns/pallas_call | solution.py:547
  210.4 6.6 %project_columns.7 = (f32[512,4096]{1,0:T(8,128)}, f32[384,4096]{1,0:T(8,128)}, f32[8,128]{1,0:T(8,128)}) custom-call(s32[24]{0:T(128)S(1)} %fusion.places_ref, bf16[256,768]{1,0:T(8,128)(2,1)S(1)} %get-tuple-element.84.top_ref, bf16[256,1536]{1,0:T(8,128)(2,1)S(1)} %get-tuple-element.85.bottom_ref, ...), custom_call_target="tpu_custom_call", output_to_operand_aliasing={{1}: (8, {}), {0}: (9, {})} | custom-call | flops 3000000000 | bytes 1048576 | tf_op jit(solution)/shard_map/project_columns/pallas_call | solution.py:547
  (153 shorter events, 67.5 us)
Async XLA Ops:
  5.3 47.9 %all-to-all-start = ((f32[8,16,4096]{2,1,0:T(8,128)}), f32[8,16,4096]{2,1,0:T(8,128)S(1)}, u32[]{:S(2)}, u32[]{:S(2)}) async-start(f32[8,16,4096]{2,1,0:T(8,128)} %bitcast.11), calls=%async_computation | async-start | bytes 4194304 | tf_op jit(solution)/shard_map/all_to_all | solution.py:574
  19.3 27.9 %collective-permute-start.1 = (f32[192,512]{1,0:T(8,128)S(1)}, f32[192,512]{1,0:T(8,128)S(1)}, u32[]{:S(2)}, u32[]{:S(2)}) collective-permute-start(f32[192,512]{1,0:T(8,128)S(1)} %get-tuple-element.57.refs_0_), channel_id=1, source_target_pairs={{0,2},{4,6},{8,10},{12,14},{16,18},{20,22},{24,26},{28,30}} | collective-permute-start | bytes 1179656 | tf_op jit(solution)/shard_map/ppermute | solution.py:148
  24.7 27.8 %collective-permute-start.3 = (f32[192,512]{1,0:T(8,128)S(1)}, f32[192,512]{1,0:T(8,128)S(1)}, u32[]{:S(2)}, u32[]{:S(2)}) collective-permute-start(f32[192,512]{1,0:T(8,128)S(1)} %get-tuple-element.58.refs_0_), channel_id=1, source_target_pairs={{0,2},{4,6},{8,10},{12,14},{16,18},{20,22},{24,26},{28,30}} | collective-permute-start | bytes 1179656 | tf_op jit(solution)/shard_map/ppermute | solution.py:148
  26.0 18.1 %collective-permute-start.4 = (f32[64,512]{1,0:T(8,128)S(1)}, f32[64,512]{1,0:T(8,128)S(1)}, u32[]{:S(2)}, u32[]{:S(2)}) collective-permute-start(f32[64,512]{1,0:T(8,128)S(1)} %relay.3.refs_2_.even_ref), channel_id=1, source_target_pairs={{0,1},{2,3},{4,5},{6,7},{8,9},{10,11},{12,13},{14,15},{16,17},{18,... | collective-permute-start | bytes 393224 | tf_op jit(solution)/shard_map/ppermute | solution.py:606
  47.3 21.1 %collective-permute-start.2 = (f32[192,512]{1,0:T(8,128)S(1)}, f32[192,512]{1,0:T(8,128)}, u32[]{:S(2)}, u32[]{:S(2)}) collective-permute-start(f32[192,512]{1,0:T(8,128)S(1)} %relay.4.refs_0_), channel_id=1, source_target_pairs={{0,1},{2,3},{4,5},{6,7},{8,9},{10,11},{12,13},{14,15},{16,17},{18,... | collective-permute-start | bytes 1179656 | tf_op jit(solution)/shard_map/ppermute | solution.py:148
  54.5 13.9 %collective-permute-start.5 = (f32[192,512]{1,0:T(8,128)S(1)}, f32[192,512]{1,0:T(8,128)S(1)}, u32[]{:S(2)}, u32[]{:S(2)}) collective-permute-start(f32[192,512]{1,0:T(8,128)S(1)} %relay.5.refs_2_), channel_id=1, source_target_pairs={{0,1},{2,3},{4,5},{6,7},{8,9},{10,11},{12,13},{14,15},{16,17},{18,... | collective-permute-start | bytes 1179656 | tf_op jit(solution)/shard_map/ppermute | solution.py:148
  77.8 13.0 %collective-permute-start.13 = (f32[128,768]{1,0:T(8,128)}, f32[128,768]{1,0:T(8,128)}, u32[]{:S(2)}, u32[]{:S(2)}) collective-permute-start(f32[128,768]{1,0:T(8,128)} %constant_dynamic-slice_fusion), channel_id=1, source_target_pairs={{0,4},{4,0},{8,12},{12,8},{16,20},{20,16},{24,28},{28,24},{1,5},{5... | collective-permute-start | bytes 1179656 | tf_op jit(solution)/shard_map/ppermute | solution.py:43
  89.8 16.2 %collective-permute-start.16 = (f32[512,512]{1,0:T(8,128)}, f32[512,512]{1,0:T(8,128)}, u32[]{:S(2)}, u32[]{:S(2)}) collective-permute-start(f32[512,512]{1,0:T(8,128)} %get-tuple-element.72), channel_id=1, source_target_pairs={{0,4},{4,0},{8,12},{12,8},{16,20},{20,16},{24,28},{28,24},{1,5},{5... | collective-permute-start | bytes 3145736 | tf_op jit(solution)/shard_map/ppermute | solution.py:43
  90.2 17.1 %collective-permute-start.17 = (f32[512,512]{1,0:T(8,128)}, f32[512,512]{1,0:T(8,128)}, u32[]{:S(2)}, u32[]{:S(2)}) collective-permute-start(f32[512,512]{1,0:T(8,128)} %get-tuple-element.75), channel_id=1, source_target_pairs={{0,4},{4,0},{8,12},{12,8},{16,20},{20,16},{24,28},{28,24},{1,5},{5... | collective-permute-start | bytes 3145736 | tf_op jit(solution)/shard_map/ppermute | solution.py:43
  90.3 18.3 %collective-permute-start.18 = (f32[512,512]{1,0:T(8,128)}, f32[512,512]{1,0:T(8,128)S(1)}, u32[]{:S(2)}, u32[]{:S(2)}) collective-permute-start(f32[512,512]{1,0:T(8,128)} %get-tuple-element.78), channel_id=1, source_target_pairs={{0,4},{4,0},{8,12},{12,8},{16,20},{20,16},{24,28},{28,24},{1,5},{5... | collective-permute-start | bytes 3145736 | tf_op jit(solution)/shard_map/ppermute | solution.py:43
  90.7 18.1 %collective-permute-start.19 = (f32[512,512]{1,0:T(8,128)}, f32[512,512]{1,0:T(8,128)S(1)}, u32[]{:S(2)}, u32[]{:S(2)}) collective-permute-start(f32[512,512]{1,0:T(8,128)} %get-tuple-element.81), channel_id=1, source_target_pairs={{0,4},{4,0},{8,12},{12,8},{16,20},{20,16},{24,28},{28,24},{1,5},{5... | collective-permute-start | bytes 3145736 | tf_op jit(solution)/shard_map/ppermute | solution.py:43
  92.0 13.0 %collective-permute-start.14 = (f32[128,768]{1,0:T(8,128)S(1)}, f32[128,768]{1,0:T(8,128)S(1)}, u32[]{:S(2)}, u32[]{:S(2)}) collective-permute-start(f32[128,768]{1,0:T(8,128)S(1)} %dynamic-slice_add_fusion.refs_0_), channel_id=1, source_target_pairs={{0,8},{4,20},{8,0},{12,28},{16,24},{20,4},{24,16},{28,12},{1,9},{5... | collective-permute-start | bytes 1179656 | tf_op jit(solution)/shard_map/ppermute | solution.py:43
  113.0 14.8 %collective-permute-start.24 = (f32[512,256]{1,0:T(8,128)S(1)}, f32[512,256]{1,0:T(8,128)S(1)}, u32[]{:S(2)}, u32[]{:S(2)}) collective-permute-start(f32[512,256]{1,0:T(8,128)S(1)} %get-tuple-element.90), channel_id=1, source_target_pairs={{0,8},{4,20},{8,0},{12,28},{16,24},{20,4},{24,16},{28,12},{1,9},{5... | collective-permute-start | bytes 1572872 | tf_op jit(solution)/shard_map/ppermute | solution.py:43
  113.9 20.1 %collective-permute-start.25 = (f32[512,256]{1,0:T(8,128)S(1)}, f32[512,256]{1,0:T(8,128)S(1)}, u32[]{:S(2)}, u32[]{:S(2)}) collective-permute-start(f32[512,256]{1,0:T(8,128)S(1)} %get-tuple-element.92), channel_id=1, source_target_pairs={{0,8},{4,20},{8,0},{12,28},{16,24},{20,4},{24,16},{28,12},{1,9},{5... | collective-permute-start | bytes 1572872 | tf_op jit(solution)/shard_map/ppermute | solution.py:43
  115.1 27.4 %collective-permute-start.26 = (f32[512,256]{1,0:T(8,128)S(1)}, f32[512,256]{1,0:T(8,128)S(1)}, u32[]{:S(2)}, u32[]{:S(2)}) collective-permute-start(f32[512,256]{1,0:T(8,128)S(1)} %get-tuple-element.94), channel_id=1, source_target_pairs={{0,8},{4,20},{8,0},{12,28},{16,24},{20,4},{24,16},{28,12},{1,9},{5... | collective-permute-start | bytes 1572872 | tf_op jit(solution)/shard_map/ppermute | solution.py:43
  115.9 31.6 %collective-permute-start.21 = (f32[512,256]{1,0:T(8,128)S(1)}, f32[512,256]{1,0:T(8,128)S(1)}, u32[]{:S(2)}, u32[]{:S(2)}) collective-permute-start(f32[512,256]{1,0:T(8,128)S(1)} %get-tuple-element.87), channel_id=1, source_target_pairs={{0,8},{4,20},{8,0},{12,28},{16,24},{20,4},{24,16},{28,12},{1,9},{5... | collective-permute-start | bytes 1572872 | tf_op jit(solution)/shard_map/ppermute | solution.py:43
  134.1 15.2 %collective-permute-start.28 = (f32[512,128]{1,0:T(8,128)S(1)}, f32[512,128]{1,0:T(8,128)S(1)}, u32[]{:S(2)}, u32[]{:S(2)}) collective-permute-start(f32[512,128]{1,0:T(8,128)S(1)} %get-tuple-element.96), channel_id=1, source_target_pairs={{0,16},{4,12},{8,24},{12,4},{16,0},{20,28},{24,8},{28,20},{1,17},{... | collective-permute-start | bytes 786440 | tf_op jit(solution)/shard_map/ppermute | solution.py:43
  148.3 11.5 %collective-permute-start.34 = (f32[1024,128]{1,0:T(8,128)S(1)}, f32[1024,128]{1,0:T(8,128)S(1)}, u32[]{:S(2)}, u32[]{:S(2)}) collective-permute-start(f32[1024,128]{1,0:T(8,128)S(1)} %join_pieces.8), channel_id=1, source_target_pairs={{0,8},{4,20},{8,0},{12,28},{16,24},{20,4},{24,16},{28,12},{1,9},{5... | collective-permute-start | bytes 1572872 | tf_op jit(solution)/shard_map/ppermute | solution.py:43
  158.6 12.1 %collective-permute-start.30 = (f32[1024,128]{1,0:T(8,128)S(1)}, f32[1024,128]{1,0:T(8,128)S(1)}, u32[]{:S(2)}, u32[]{:S(2)}) collective-permute-start(f32[1024,128]{1,0:T(8,128)S(1)} %join_pieces.7), channel_id=1, source_target_pairs={{0,8},{4,20},{8,0},{12,28},{16,24},{20,4},{24,16},{28,12},{1,9},{5... | collective-permute-start | bytes 1572872 | tf_op jit(solution)/shard_map/ppermute | solution.py:43
  159.9 29.1 %collective-permute-start.35 = (f32[2048,128]{1,0:T(8,128)S(1)}, f32[2048,128]{1,0:T(8,128)}, u32[]{:S(2)}, u32[]{:S(2)}) collective-permute-start(f32[2048,128]{1,0:T(8,128)S(1)} %pad_maximum_fusion.1.rest_0_.rest_1_), channel_id=1, source_target_pairs={{0,4},{4,0},{8,12},{12,8},{16,20},{20,16},{24,28},{28,24},{1,5},{5... | collective-permute-start | bytes 3145736 | tf_op jit(solution)/shard_map/ppermute | solution.py:43
  160.0 11.7 %collective-permute-start.37 = (f32[512,128]{1,0:T(8,128)S(1)}, f32[512,128]{1,0:T(8,128)S(1)}, u32[]{:S(2)}, u32[]{:S(2)}) collective-permute-start(f32[512,128]{1,0:T(8,128)S(1)} %get-tuple-element.102), channel_id=1, source_target_pairs={{0,16},{4,12},{8,24},{12,4},{16,0},{20,28},{24,8},{28,20},{1,17},{... | collective-permute-start | bytes 786440 | tf_op jit(solution)/shard_map/ppermute | solution.py:43
  170.8 25.4 %collective-permute-start.31 = (f32[2048,128]{1,0:T(8,128)S(1)}, f32[2048,128]{1,0:T(8,128)}, u32[]{:S(2)}, u32[]{:S(2)}) collective-permute-start(f32[2048,128]{1,0:T(8,128)S(1)} %pad_maximum_fusion.rest_0_.rest_1_), channel_id=1, source_target_pairs={{0,4},{4,0},{8,12},{12,8},{16,20},{20,16},{24,28},{28,24},{1,5},{5... | collective-permute-start | bytes 3145736 | tf_op jit(solution)/shard_map/ppermute | solution.py:43
  181.4 14.6 %collective-permute-start.39 = (f32[1024,128]{1,0:T(8,128)S(1)}, f32[1024,128]{1,0:T(8,128)S(1)}, u32[]{:S(2)}, u32[]{:S(2)}) collective-permute-start(f32[1024,128]{1,0:T(8,128)S(1)} %join_pieces.10.refs_0_), channel_id=1, source_target_pairs={{0,8},{4,20},{8,0},{12,28},{16,24},{20,4},{24,16},{28,12},{1,9},{5... | collective-permute-start | bytes 1572872 | tf_op jit(solution)/shard_map/ppermute | solution.py:43
  188.1 15.0 %collective-permute-start.27 = (f32[1024,128]{1,0:T(8,128)S(1)}, f32[1024,128]{1,0:T(8,128)S(1)}, u32[]{:S(2)}, u32[]{:S(2)}) collective-permute-start(f32[1024,128]{1,0:T(8,128)S(1)} %join_pieces.6.refs_0_), channel_id=1, source_target_pairs={{0,8},{4,20},{8,0},{12,28},{16,24},{20,4},{24,16},{28,12},{1,9},{5... | collective-permute-start | bytes 1572872 | tf_op jit(solution)/shard_map/ppermute | solution.py:43
  (42 other events, 314.1 us)

commit v8 on v7

--- a/solution.py
+++ b/solution.py
@@ -15,6 +15,7 @@
 HALF = LEAD // 2
 BLOCK = 256
 LAG = 2
+WIDE = 512
 VMEM_BYTES = 48 * 1024 * 1024
 HIGHEST = lax.Precision.HIGHEST
 F32 = jnp.float32
@@ -141,23 +142,31 @@
     return mine, swap(mine, 0, count)
 
 
-def spread(value, count, after):
-    stride = count
-    while True:
-        half = stride // 2
-        got = lax.ppermute(value, "col", [(c, c + half) for c in range(0, count, stride)])
-        if half == 1:
-            return value, got
-        value = relay(value, got, stride, after)
-        stride = half
-
-
-def relay(value, got, stride, after):
+def spread(value, got, count, after, paired):
+    middle = count // 2
+
     def body(value_ref, got_ref, out_ref):
-        here = lax.axis_index("col") % stride == stride // 2
+        here = lax.axis_index("col") == middle
         out_ref[...] = jnp.where(here, got_ref[...], value_ref[...])
 
-    return ordered("relay", body, [value, got], [jax.ShapeDtypeStruct(value.shape, F32)], after)
+    passed = ordered("relay", body, [value, got], [jax.ShapeDtypeStruct(value.shape, F32)], after)
+    others = [c for c in range(count - 1, 0, -1) if c != middle]
+    if paired and count == 4:
+        return [passed, lax.ppermute(passed, "col", [(0, 1), (2, 3)])]
+    return [passed] + [lax.ppermute(passed, "col", [(middle, c)]) for c in others]
+
+
+def pick(refs, count):
+    me = lax.axis_index("col")
+    held = (me == 0) | (me == count // 2)
+    arrived = refs[1][...]
+    for ref in refs[2:]:
+        arrived = arrived + ref[...]
+    return jnp.where(held, refs[0][...], arrived)
+
+
+def first_hop(value, count):
+    return lax.ppermute(value, "col", [(0, count // 2)])
 
 
 def parts3(x):
@@ -207,9 +216,10 @@
     )(owner, child_rows)
 
 
-def pack_lead_kernel(row_count, capacity, sentinel, owner_ref, offset_ref, even_ref, odd_ref, *refs):
+def pack_lead_kernel(row_count, capacity, sentinel, col_count, given_count, owner_ref, offset_ref, *refs):
+    given, refs = refs[:given_count], refs[given_count:]
     outs, (child_ref, rows_ref, tag_ref, tally) = refs[:row_count], refs[row_count:]
-    child_ref[...] = jnp.where(lax.axis_index("col") % 2 == 0, even_ref[...], odd_ref[...])
+    child_ref[...] = pick(given, col_count)
     rows_ref[...] = jnp.zeros_like(rows_ref)
     tag_ref[...] = jnp.full(tag_ref.shape, sentinel, F32)
     me = lax.axis_index("row")
@@ -226,22 +236,22 @@
         out[:, LEAD:] = tag_ref[part, :]
 
 
-def pack_lead(even, odd, owner, offset, row_count, capacity, sentinel):
+def pack_lead(given, owner, offset, row_count, capacity, sentinel, col_count):
     slots = row_count * capacity
     return pl.pallas_call(
-        functools.partial(pack_lead_kernel, row_count, capacity, float(sentinel)),
+        functools.partial(pack_lead_kernel, row_count, capacity, float(sentinel), col_count, len(given)),
         out_shape=(jax.ShapeDtypeStruct((capacity, LEAD + PB), F32),) * row_count,
-        in_specs=[pl.BlockSpec(memory_space=SMEM)] * 2 + in_vmem(2),
+        in_specs=[pl.BlockSpec(memory_space=SMEM)] * 2 + in_vmem(len(given)),
         out_specs=tuple(in_vmem(row_count)),
         scratch_shapes=[
-            pltpu.VMEM(even.shape, F32),
+            pltpu.VMEM(given[0].shape, F32),
             pltpu.VMEM((slots, LEAD), F32),
             pltpu.VMEM((slots, PB), F32),
             pltpu.SMEM((row_count,), jnp.int32),
         ],
         compiler_params=params(),
         name="pack_lead",
-    )(owner, offset, even, odd)
+    )(owner, offset, *given)
 
 
 def triple(x, axis):
@@ -249,12 +259,11 @@
     return jnp.concatenate([hi, hi, lo] if axis == 1 else [hi, lo, hi], axis=axis)
 
 
-def lead_kernel(row_count, *refs):
-    front_refs, piece_refs = refs[:4], refs[4 : 4 + row_count]
-    lead_ref, left_ref, place_ref, gram_ref = refs[4 + row_count :]
-    even = lax.axis_index("col") % 2 == 0
+def lead_kernel(row_count, col_count, each, *refs):
+    front_refs, piece_refs = refs[: 2 * each], refs[2 * each : 2 * each + row_count]
+    lead_ref, left_ref, place_ref, gram_ref = refs[2 * each + row_count :]
     front = jnp.concatenate(
-        [jnp.where(even, a[...], b[...]) for a, b in zip(front_refs[::2], front_refs[1::2])], axis=0
+        [pick(front_refs[:each], col_count), pick(front_refs[each:], col_count)], axis=0
     )
     me = lax.axis_index("row")
     pieces = [ref[...] for ref in piece_refs]
@@ -279,11 +288,11 @@
     gram_ref[:, HALF:] = dot_high(turned[HALF:], lead, ((1,), (0,)))
 
 
-def lead_setup(fronts, pieces, rows):
+def lead_setup(fronts, pieces, rows, col_count):
     slots = len(pieces) * pieces[0].shape[0]
     operands = list(fronts) + list(pieces)
     return pl.pallas_call(
-        functools.partial(lead_kernel, len(pieces)),
+        functools.partial(lead_kernel, len(pieces), col_count, len(fronts) // 2),
         out_shape=(
             jax.ShapeDtypeStruct((rows, LEAD), F32),
             jax.ShapeDtypeStruct((LEAD, 3 * rows), BF16),
@@ -314,13 +323,13 @@
 def product(half, left, place, front, child, whole, chunks):
     rows, columns = front.shape
     slots = child.shape[0]
-    steps = columns // 2 // BLOCK
+    steps = columns // 2 // WIDE
     blocks = steps // chunks
     in_specs = [
         pl.BlockSpec(left.shape, lambda i, h: (0, 0)),
         pl.BlockSpec(place.shape, lambda i, h: (0, 0)),
-        pl.BlockSpec((rows, BLOCK), lambda i, h: (0, h[0] * steps + i)),
-        pl.BlockSpec((slots, BLOCK), lambda i, h: (0, h[0] * steps + i)),
+        pl.BlockSpec((rows, WIDE), lambda i, h: (0, h[0] * steps + i)),
+        pl.BlockSpec((slots, WIDE), lambda i, h: (0, h[0] * steps + i)),
     ]
     operands = [half[None], left, place, front, child]
     aliases = {}
@@ -338,8 +347,8 @@
             num_scalar_prefetch=1,
             grid=(steps,),
             in_specs=in_specs,
-            out_specs=tuple(pl.BlockSpec((LEAD, BLOCK), out_block(at)) for at in range(chunks))
-            + (pl.BlockSpec((rows, BLOCK), lambda i, h: (0, h[0] * steps + i)),),
+            out_specs=tuple(pl.BlockSpec((LEAD, WIDE), out_block(at)) for at in range(chunks))
+            + (pl.BlockSpec((rows, WIDE), lambda i, h: (0, h[0] * steps + i)),),
         ),
         out_shape=(jax.ShapeDtypeStruct((LEAD, columns // 2 // chunks), F32),) * chunks
         + (jax.ShapeDtypeStruct((rows, columns), F32),),
@@ -588,7 +597,7 @@
     packed = pack(child_rows, owner, row_count, capacity)
     child = exchange(packed, row_count)
     lead_rows = child_rows[:, :LEAD]
-    first = lax.ppermute(lead_rows, "col", [(0, col_count // 2)])
+    first = first_hop(lead_rows, col_count)
     cut = local_rows // 2
 
     def cut_body(front_ref, low_ref, high_ref):
@@ -599,17 +608,16 @@
         "cut_lead", cut_body, [front_matrix[:, :LEAD]],
         [jax.ShapeDtypeStruct((cut, LEAD), F32)] * 2, (first,),
     )
-    passed = relay(lead_rows, first, col_count, ())
-    stride = col_count // 2
-    pairs = [(c, c + stride // 2) for c in range(0, col_count, stride)]
-    pieces = list(
-        pack_lead(passed, lax.ppermute(passed, "col", pairs), owner, offset, row_count, capacity, local_rows)
-    )
+    given = spread(lead_rows, first, col_count, (), False)
+    pieces = list(pack_lead(given, owner, offset, row_count, capacity, local_rows, col_count))
     for mask in range(1, row_count):
         pairs = [(d, d ^ mask) for d in range(row_count)]
         pieces[mask] = lax.ppermute(pieces[mask], "row", pairs)
-    fronts = spread(low, col_count, (passed,)) + spread(high, col_count, (child, pieces[0]))
-    lead, left, place, gram = lead_setup(fronts, pieces, local_rows)
+    low_got, high_got = first_hop(low, col_count), first_hop(high, col_count)
+    own_piece = pieces[0]
+    fronts = spread(low, low_got, col_count, (given[0],), True)
+    fronts += spread(high, high_got, col_count, (child, own_piece), True)
+    lead, left, place, gram = lead_setup(fronts, pieces, local_rows, col_count)
 
     chunks = max(1, min(4, local_cols // (PB * row_count)))
     width = local_cols // 2 // chunks
@@ -653,7 +661,7 @@
         for step in reversed(range(steps)):
             got = swap(buf, step, row_count)
             if step == steps - 1 and step > 1:
-                buf = join(buf, got, tuple(keep for _, keep in shards))
+                buf = join(buf, got, tuple(keep for _, keep in shards) + (top,))
             elif step == 1 and c >= LAG:
                 buf = join(buf, got, (done[c - LAG],))
             elif step > 0:

time: 218 us -> 208 us (0.954)
  the two profiles are of different devices: /device:TPU:0 before, /device:TPU:21 now
where the time goes in v8:
time: 208 us; the launch traced here: 206 us
  Pallas kernels  79.4 us (38%)
  starting transfers between devices  58.4 us (28%)
  waiting for transfers between devices  44.3 us (21%)
  local copies, waits for them, and re-layouts  19.9 us (10%)
  other arithmetic  3.1 us (1%)
    ppermute x28, starting transfers between devices, swap(): return lax.ppermute(value, 'row', pairs)  34.5 us
    pallas_call x4, Pallas kernels, project(): pl.pallas_call(functools.partial(project_kernel, blocks), grid_spec=pltpu...  27.3 us
    ppermute x28, waiting for transfers between devices, swap(): return lax.ppermute(value, 'row', pairs)  22.4 us
    pallas_call x4, Pallas kernels, eliminate(): pl.pallas_call(functools.partial(eliminate_kernel, k), out_shape=jax.Shap...  20.1 us
    pallas_call x2, Pallas kernels, product(): pl.pallas_call(functools.partial(product_kernel, blocks, chunks), grid_sp...  16.4 us
    unnamed x60, local copies, waits for them, and re-layouts  16.3 us
    ppermute x3, waiting for transfers between devices, first_hop(): return lax.ppermute(value, 'col', [(0, count // 2)])  14.5 us
    ppermute x7, starting transfers between devices, on_device(): pieces[mask] = lax.ppermute(pieces[mask], 'row', pairs)  9.48 us
  transfers between devices with their start and end apart: 43, of which 19 were waited for; matrix products, arithmetic and copies ran while one was open for 3% of the time, Pallas kernels for 33%

profile of v8, /device:TPU:21, one launch (start us, length us, event | category | flops | bytes accessed | tf_op | source)
XLA Modules:
  0.0 206.2 jit_solution(2428595002947856948)
XLA Ops:
  5.3 4.5 %all-to-all-start = ((f32[8,16,4096]{2,1,0:T(8,128)}), f32[8,16,4096]{2,1,0:T(8,128)S(1)}, u32[]{:S(2)}, u32[]{:S(2)}) async-start(f32[8,16,4096]{2,1,0:T(8,128)} %bitcast.11), calls=%async_computation | async-start | bytes 4194304 | tf_op jit(solution)/shard_map/all_to_all | solution.py:583
  13.2 5.0 %collective-permute-done.refs_1_ = f32[64,512]{1,0:T(8,128)S(1)} collective-permute-done((f32[64,512]{1,0:T(8,128)S(1)}, f32[64,512]{1,0:T(8,128)S(1)}, u32[]{:S(2)}, u32[]{:S(2)}) %collective-permute-start) | collective-permute-done | bytes 131104 | tf_op jit(solution)/shard_map/ppermute | solution.py:169
  27.3 3.2 %collective-permute-done.1.refs_1_ = f32[192,512]{1,0:T(8,128)S(1)} collective-permute-done((f32[192,512]{1,0:T(8,128)S(1)}, f32[192,512]{1,0:T(8,128)S(1)}, u32[]{:S(2)}, u32[]{:S(2)}) %collective-permute-start.1) | collective-permute-done | bytes 393248 | tf_op jit(solution)/shard_map/ppermute | solution.py:169
  32.6 6.3 %collective-permute-done.3.refs_1_ = f32[192,512]{1,0:T(8,128)S(1)} collective-permute-done((f32[192,512]{1,0:T(8,128)S(1)}, f32[192,512]{1,0:T(8,128)S(1)}, u32[]{:S(2)}, u32[]{:S(2)}) %collective-permute-start.3) | collective-permute-done | bytes 393248 | tf_op jit(solution)/shard_map/ppermute | solution.py:169
  43.1 3.8 %collective-permute-start.7 = (f32[16,640]{1,0:T(8,128)S(1)}, f32[16,640]{1,0:T(8,128)S(1)}, u32[]{:S(2)}, u32[]{:S(2)}) collective-permute-start(f32[16,640]{1,0:T(8,128)S(1)} %get-tuple-element.60), channel_id=1, source_target_pairs={{0,4},{4,0},{8,12},{12,8},{16,20},{20,16},{24,28},{28,24},{1,5},{5... | collective-permute-start | bytes 122888 | tf_op jit(solution)/shard_map/ppermute | solution.py:615
  61.8 3.1 %lead_setup.1 = (f32[384,512]{1,0:T(8,128)S(1)}, bf16[512,1152]{1,0:T(8,128)(2,1)S(1)}, bf16[384,384]{1,0:T(8,128)(2,1)S(1)}, f32[256,768]{1,0:T(8,128)S(1)}) custom-call(f32[192,512]{1,0:T(8,128)S(1)} %copy-done.13, f32[192,512]{1,0:T(8,128)} %collective-permute-done.2.refs_1_, f32[192,512]{1,0:T(8,128)S(1)} %copy-done.11, f32[192,512]{1,0:T(8,128)S(1)} %copy-done.21, ...), custom_call_target="tpu_custom_call" | custom-call | tf_op jit(solution)/shard_map/lead_setup/pallas_call | solution.py:294
  67.5 8.9 %lead_product.2 = (f32[512,512]{1,0:T(8,128)}, f32[512,512]{1,0:T(8,128)}, f32[512,512]{1,0:T(8,128)}, f32[512,512]{1,0:T(8,128)}, f32[384,4096]{1,0:T(8,128)}) custom-call(s32[1]{0:T(128)} %bitcast.6.base_ref, bf16[512,1152]{1,0:T(8,128)(2,1)S(1)} %get-tuple-element.68.left_ref, bf16[384,384]{1,0:T(8,128)(2,1)S(1)} %get-tuple-element.69.place_ref, ...), custom_call_target="tpu_custom_call" | custom-call | tf_op jit(solution)/shard_map/lead_product/pallas_call | solution.py:344
  80.5 7.5 %lead_product.3 = (f32[512,512]{1,0:T(8,128)S(1)}, f32[512,512]{1,0:T(8,128)S(1)}, f32[512,512]{1,0:T(8,128)S(1)}, f32[512,512]{1,0:T(8,128)S(1)}, f32[384,4096]{1,0:T(8,128)}) custom-call(s32[1]{0:T(128)} %bitcast.5.base_ref, bf16[512,1152]{1,0:T(8,128)(2,1)S(1)} %get-tuple-element.68.left_ref, ...), custom_call_target="tpu_custom_call", output_to_operand_aliasing={{4}: (5, {})} | custom-call | tf_op jit(solution)/shard_map/lead_product/pallas_call | solution.py:344
  92.4 2.7 %collective-permute-done.16.refs_1_ = f32[128,768]{1,0:T(8,128)S(1)} collective-permute-done((f32[128,768]{1,0:T(8,128)S(1)}, f32[128,768]{1,0:T(8,128)S(1)}, u32[]{:S(2)}, u32[]{:S(2)}) %collective-permute-start.16) | collective-permute-done | bytes 393248 | tf_op jit(solution)/shard_map/ppermute | solution.py:44
  99.6 5.5 %eliminate_panel.4.refs_0_.refs_2_ = f32[512,512]{1,0:T(8,128)S(1)} custom-call(f32[128,768]{1,0:T(8,128)S(1)} %add_gram.3.refs_0_, f32[128,768]{1,0:T(8,128)S(1)} %collective-permute-done.21.refs_1_), custom_call_target="tpu_custom_call" | custom-call | flops 6000000000 | bytes 1048576 | tf_op jit(solution)/shard_map/eliminate_panel/pallas_call | solution.py:459
  105.1 5.2 %eliminate_panel.5.refs_0_.refs_2_ = f32[512,512]{1,0:T(8,128)S(1)} custom-call(f32[512,512]{1,0:T(8,128)S(1)} %eliminate_panel.4.refs_0_.refs_2_), custom_call_target="tpu_custom_call" | custom-call | flops 6000000000 | bytes 1048576 | tf_op jit(solution)/shard_map/eliminate_panel/pallas_call | solution.py:459
  111.2 5.1 %eliminate_panel.6.refs_0_.refs_2_ = f32[512,512]{1,0:T(8,128)S(1)} custom-call(f32[512,512]{1,0:T(8,128)S(1)} %eliminate_panel.5.refs_0_.refs_2_), custom_call_target="tpu_custom_call" | custom-call | flops 6000000000 | bytes 1048576 | tf_op jit(solution)/shard_map/eliminate_panel/pallas_call | solution.py:459
  119.7 4.3 %eliminate_panel.7.matrix_ref.refs_2_ = f32[512,512]{1,0:T(8,128)S(1)} custom-call(f32[512,512]{1,0:T(8,128)S(1)} %eliminate_panel.6.refs_0_.refs_2_), custom_call_target="tpu_custom_call" | custom-call | flops 6000000000 | bytes 1048576 | tf_op jit(solution)/shard_map/eliminate_panel/pallas_call | solution.py:459
  124.2 3.7 %collective-permute-done.22.refs_1_ = f32[512,256]{1,0:T(8,128)S(1)} collective-permute-done((f32[512,256]{1,0:T(8,128)S(1)}, f32[512,256]{1,0:T(8,128)S(1)}, u32[]{:S(2)}, u32[]{:S(2)}) %collective-permute-start.22) | collective-permute-done | bytes 524320 | tf_op jit(solution)/shard_map/ppermute | solution.py:44
  128.0 2.4 %finish_factor.1 = (bf16[256,768]{1,0:T(8,128)(2,1)S(1)}, bf16[256,1536]{1,0:T(8,128)(2,1)S(1)}, bf16[384,1536]{1,0:T(8,128)(2,1)S(1)}, f32[384,512]{1,0:T(8,128)}) custom-call(f32[512,512]{1,0:T(8,128)S(1)} %eliminate_panel.7.matrix_ref.refs_2_, f32[384,512]{1,0:T(8,128)S(1)} %copy-done.26), custom_call_target="tpu_custom_call" | custom-call | flops 2000000000 | bytes 1048576 | tf_op jit(solution)/shard_map/finish_factor/pallas_call | solution.py:483
  132.1 5.5 %collective-permute-done.30.refs_1_ = f32[512,128]{1,0:T(8,128)S(1)} collective-permute-done((f32[512,128]{1,0:T(8,128)S(1)}, f32[512,128]{1,0:T(8,128)S(1)}, u32[]{:S(2)}, u32[]{:S(2)}) %collective-permute-start.30) | collective-permute-done | bytes 262176 | tf_op jit(solution)/shard_map/ppermute | solution.py:44
  140.8 5.5 %collective-permute-start.36 = (f32[2048,128]{1,0:T(8,128)}, f32[2048,128]{1,0:T(8,128)}, u32[]{:S(2)}, u32[]{:S(2)}) collective-permute-start(f32[2048,128]{1,0:T(8,128)} %pad_maximum_fusion.1.rest_0_.rest_1_), channel_id=1, source_target_pairs={{0,4},{4,0},{8,12},{12,8},{16,20},{20,16},{24,28},{28,24},{1,5},{5... | collective-permute-start | bytes 3145736 | tf_op jit(solution)/shard_map/ppermute | solution.py:44
  147.5 8.1 %collective-permute-start.32 = (f32[2048,128]{1,0:T(8,128)S(1)}, f32[2048,128]{1,0:T(8,128)}, u32[]{:S(2)}, u32[]{:S(2)}) collective-permute-start(f32[2048,128]{1,0:T(8,128)S(1)} %pad_maximum_fusion.rest_0_.rest_1_), channel_id=1, source_target_pairs={{0,4},{4,0},{8,12},{12,8},{16,20},{20,16},{24,28},{28,24},{1,5},{5... | collective-permute-start | bytes 3145736 | tf_op jit(solution)/shard_map/ppermute | solution.py:44
  157.3 3.9 %collective-permute-done.23 = f32[512,128]{1,0:T(8,128)S(1)} collective-permute-done((f32[512,128]{1,0:T(8,128)S(1)}, f32[512,128]{1,0:T(8,128)S(1)}, u32[]{:S(2)}, u32[]{:S(2)}) %collective-permute-start.23) | collective-permute-done | bytes 262176 | tf_op jit(solution)/shard_map/ppermute | solution.py:44
  173.8 7.1 %project_columns.4 = (f32[512,4096]{1,0:T(8,128)}, f32[384,4096]{1,0:T(8,128)}, f32[8,128]{1,0:T(8,128)S(1)}) custom-call(s32[24]{0:T(128)S(1)} %fusion.places_ref, bf16[256,768]{1,0:T(8,128)(2,1)S(1)} %get-tuple-element.84.refs_6_.top_ref, bf16[256,1536]{1,0:T(8,128)(2,1)S(1)} %get-tuple-element.85.bottom_ref, ...), custom_call_target="tpu_custom_call", output_to_operand_aliasing={{1}: (8, {})} | custom-call | flops 3000000000 | bytes 1048576 | tf_op jit(solution)/shard_map/project_columns/pallas_call | solution.py:556
  182.2 3.6 %collective-permute-start.41 = (f32[2048,128]{1,0:T(8,128)S(1)}, f32[2048,128]{1,0:T(8,128)S(1)}, u32[]{:S(2)}, u32[]{:S(2)}) collective-permute-start(f32[2048,128]{1,0:T(8,128)S(1)} %join_pieces.11.rest_0_.rest_1_), channel_id=1, source_target_pairs={{0,4},{4,0},{8,12},{12,8},{16,20},{20,16},{24,28},{28,24},{1,5},{5... | collective-permute-start | bytes 3145736 | tf_op jit(solution)/shard_map/ppermute | solution.py:44
  185.9 6.9 %project_columns.5 = (f32[512,4096]{1,0:T(8,128)}, f32[384,4096]{1,0:T(8,128)}, f32[8,128]{1,0:T(8,128)S(1)}) custom-call(s32[24]{0:T(128)S(1)} %fusion.places_ref, bf16[256,768]{1,0:T(8,128)(2,1)S(1)} %get-tuple-element.84.refs_6_.top_ref, bf16[256,1536]{1,0:T(8,128)(2,1)S(1)} %get-tuple-element.85.bottom_ref, ...), custom_call_target="tpu_custom_call", output_to_operand_aliasing={{1}: (8, {}), {0}: (9, {})} | custom-call | flops 3000000000 | bytes 1048576 | tf_op jit(solution)/shard_map/project_columns/pallas_call | solution.py:556
  193.0 6.6 %project_columns.6 = (f32[512,4096]{1,0:T(8,128)}, f32[384,4096]{1,0:T(8,128)}, f32[8,128]{1,0:T(8,128)}) custom-call(s32[24]{0:T(128)S(1)} %fusion.places_ref, bf16[256,768]{1,0:T(8,128)(2,1)S(1)} %get-tuple-element.84.refs_6_.top_ref, bf16[256,1536]{1,0:T(8,128)(2,1)S(1)} %get-tuple-element.85.bottom_ref, ...), custom_call_target="tpu_custom_call", output_to_operand_aliasing={{1}: (8, {}), {0}: (9, {})} | custom-call | flops 3000000000 | bytes 1048576 | tf_op jit(solution)/shard_map/project_columns/pallas_call | solution.py:556
  199.6 6.6 %project_columns.7 = (f32[512,4096]{1,0:T(8,128)}, f32[384,4096]{1,0:T(8,128)}, f32[8,128]{1,0:T(8,128)}) custom-call(s32[24]{0:T(128)S(1)} %fusion.places_ref, bf16[256,768]{1,0:T(8,128)(2,1)S(1)} %get-tuple-element.84.refs_6_.top_ref, bf16[256,1536]{1,0:T(8,128)(2,1)S(1)} %get-tuple-element.85.bottom_ref, ...), custom_call_target="tpu_custom_call", output_to_operand_aliasing={{1}: (8, {}), {0}: (9, {})} | custom-call | flops 3000000000 | bytes 1048576 | tf_op jit(solution)/shard_map/project_columns/pallas_call | solution.py:556
  (167 shorter events, 79.7 us)
Async XLA Ops:
  5.3 34.4 %all-to-all-start = ((f32[8,16,4096]{2,1,0:T(8,128)}), f32[8,16,4096]{2,1,0:T(8,128)S(1)}, u32[]{:S(2)}, u32[]{:S(2)}) async-start(f32[8,16,4096]{2,1,0:T(8,128)} %bitcast.11), calls=%async_computation | async-start | bytes 4194304 | tf_op jit(solution)/shard_map/all_to_all | solution.py:583
  18.3 12.2 %collective-permute-start.1 = (f32[192,512]{1,0:T(8,128)S(1)}, f32[192,512]{1,0:T(8,128)S(1)}, u32[]{:S(2)}, u32[]{:S(2)}) collective-permute-start(f32[192,512]{1,0:T(8,128)S(1)} %get-tuple-element.57.refs_0_), channel_id=1, source_target_pairs={{0,2},{4,6},{8,10},{12,14},{16,18},{20,22},{24,26},{28,30}} | collective-permute-start | bytes 1179656 | tf_op jit(solution)/shard_map/ppermute | solution.py:169
  19.6 19.3 %collective-permute-start.3 = (f32[192,512]{1,0:T(8,128)S(1)}, f32[192,512]{1,0:T(8,128)S(1)}, u32[]{:S(2)}, u32[]{:S(2)}) collective-permute-start(f32[192,512]{1,0:T(8,128)S(1)} %get-tuple-element.58.refs_0_), channel_id=1, source_target_pairs={{0,2},{4,6},{8,10},{12,14},{16,18},{20,22},{24,26},{28,30}} | collective-permute-start | bytes 1179656 | tf_op jit(solution)/shard_map/ppermute | solution.py:169
  30.6 27.5 %collective-permute-start.2 = (f32[192,512]{1,0:T(8,128)S(1)}, f32[192,512]{1,0:T(8,128)}, u32[]{:S(2)}, u32[]{:S(2)}) collective-permute-start(f32[192,512]{1,0:T(8,128)S(1)} %relay.4.refs_0_), channel_id=1, source_target_pairs={{0,1},{2,3},{4,5},{6,7},{8,9},{10,11},{12,13},{14,15},{16,17},{18,... | collective-permute-start | bytes 1179656 | tf_op jit(solution)/shard_map/ppermute | solution.py:155
  41.0 17.0 %collective-permute-start.6 = (f32[192,512]{1,0:T(8,128)S(1)}, f32[192,512]{1,0:T(8,128)S(1)}, u32[]{:S(2)}, u32[]{:S(2)}) collective-permute-start(f32[192,512]{1,0:T(8,128)S(1)} %relay.5.refs_2_), channel_id=1, source_target_pairs={{0,1},{2,3},{4,5},{6,7},{8,9},{10,11},{12,13},{14,15},{16,17},{18,... | collective-permute-start | bytes 1179656 | tf_op jit(solution)/shard_map/ppermute | solution.py:155
  67.5 10.0 %collective-permute-start.14 = (f32[128,768]{1,0:T(8,128)}, f32[128,768]{1,0:T(8,128)}, u32[]{:S(2)}, u32[]{:S(2)}) collective-permute-start(f32[128,768]{1,0:T(8,128)} %constant_dynamic-slice_fusion), channel_id=1, source_target_pairs={{0,4},{4,0},{8,12},{12,8},{16,20},{20,16},{24,28},{28,24},{1,5},{5... | collective-permute-start | bytes 1179656 | tf_op jit(solution)/shard_map/ppermute | solution.py:44
  76.4 12.9 %collective-permute-start.17 = (f32[512,512]{1,0:T(8,128)}, f32[512,512]{1,0:T(8,128)}, u32[]{:S(2)}, u32[]{:S(2)}) collective-permute-start(f32[512,512]{1,0:T(8,128)} %get-tuple-element.72), channel_id=1, source_target_pairs={{0,4},{4,0},{8,12},{12,8},{16,20},{20,16},{24,28},{28,24},{1,5},{5... | collective-permute-start | bytes 3145736 | tf_op jit(solution)/shard_map/ppermute | solution.py:44
  76.9 13.7 %collective-permute-start.18 = (f32[512,512]{1,0:T(8,128)}, f32[512,512]{1,0:T(8,128)}, u32[]{:S(2)}, u32[]{:S(2)}) collective-permute-start(f32[512,512]{1,0:T(8,128)} %get-tuple-element.75), channel_id=1, source_target_pairs={{0,4},{4,0},{8,12},{12,8},{16,20},{20,16},{24,28},{28,24},{1,5},{5... | collective-permute-start | bytes 3145736 | tf_op jit(solution)/shard_map/ppermute | solution.py:44
  77.0 15.0 %collective-permute-start.19 = (f32[512,512]{1,0:T(8,128)}, f32[512,512]{1,0:T(8,128)S(1)}, u32[]{:S(2)}, u32[]{:S(2)}) collective-permute-start(f32[512,512]{1,0:T(8,128)} %get-tuple-element.78), channel_id=1, source_target_pairs={{0,4},{4,0},{8,12},{12,8},{16,20},{20,16},{24,28},{28,24},{1,5},{5... | collective-permute-start | bytes 3145736 | tf_op jit(solution)/shard_map/ppermute | solution.py:44
  77.4 14.8 %collective-permute-start.20 = (f32[512,512]{1,0:T(8,128)}, f32[512,512]{1,0:T(8,128)S(1)}, u32[]{:S(2)}, u32[]{:S(2)}) collective-permute-start(f32[512,512]{1,0:T(8,128)} %get-tuple-element.81), channel_id=1, source_target_pairs={{0,4},{4,0},{8,12},{12,8},{16,20},{20,16},{24,28},{28,24},{1,5},{5... | collective-permute-start | bytes 3145736 | tf_op jit(solution)/shard_map/ppermute | solution.py:44
  78.7 9.3 %collective-permute-start.15 = (f32[128,768]{1,0:T(8,128)S(1)}, f32[128,768]{1,0:T(8,128)S(1)}, u32[]{:S(2)}, u32[]{:S(2)}) collective-permute-start(f32[128,768]{1,0:T(8,128)S(1)} %dynamic-slice_add_fusion.refs_0_), channel_id=1, source_target_pairs={{0,8},{4,20},{8,0},{12,28},{16,24},{20,4},{24,16},{28,12},{1,9},{5... | collective-permute-start | bytes 1179656 | tf_op jit(solution)/shard_map/ppermute | solution.py:44
  96.7 13.7 %collective-permute-start.25 = (f32[512,256]{1,0:T(8,128)S(1)}, f32[512,256]{1,0:T(8,128)S(1)}, u32[]{:S(2)}, u32[]{:S(2)}) collective-permute-start(f32[512,256]{1,0:T(8,128)S(1)} %get-tuple-element.90), channel_id=1, source_target_pairs={{0,8},{4,20},{8,0},{12,28},{16,24},{20,4},{24,16},{28,12},{1,9},{5... | collective-permute-start | bytes 1572872 | tf_op jit(solution)/shard_map/ppermute | solution.py:44
  97.6 18.8 %collective-permute-start.26 = (f32[512,256]{1,0:T(8,128)S(1)}, f32[512,256]{1,0:T(8,128)S(1)}, u32[]{:S(2)}, u32[]{:S(2)}) collective-permute-start(f32[512,256]{1,0:T(8,128)S(1)} %get-tuple-element.92), channel_id=1, source_target_pairs={{0,8},{4,20},{8,0},{12,28},{16,24},{20,4},{24,16},{28,12},{1,9},{5... | collective-permute-start | bytes 1572872 | tf_op jit(solution)/shard_map/ppermute | solution.py:44
  98.1 25.9 %collective-permute-start.27 = (f32[512,256]{1,0:T(8,128)S(1)}, f32[512,256]{1,0:T(8,128)S(1)}, u32[]{:S(2)}, u32[]{:S(2)}) collective-permute-start(f32[512,256]{1,0:T(8,128)S(1)} %get-tuple-element.94), channel_id=1, source_target_pairs={{0,8},{4,20},{8,0},{12,28},{16,24},{20,4},{24,16},{28,12},{1,9},{5... | collective-permute-start | bytes 1572872 | tf_op jit(solution)/shard_map/ppermute | solution.py:44
  99.0 28.9 %collective-permute-start.22 = (f32[512,256]{1,0:T(8,128)S(1)}, f32[512,256]{1,0:T(8,128)S(1)}, u32[]{:S(2)}, u32[]{:S(2)}) collective-permute-start(f32[512,256]{1,0:T(8,128)S(1)} %get-tuple-element.87), channel_id=1, source_target_pairs={{0,8},{4,20},{8,0},{12,28},{16,24},{20,4},{24,16},{28,12},{1,9},{5... | collective-permute-start | bytes 1572872 | tf_op jit(solution)/shard_map/ppermute | solution.py:44
  116.5 15.3 %collective-permute-start.29 = (f32[512,128]{1,0:T(8,128)S(1)}, f32[512,128]{1,0:T(8,128)S(1)}, u32[]{:S(2)}, u32[]{:S(2)}) collective-permute-start(f32[512,128]{1,0:T(8,128)S(1)} %get-tuple-element.96), channel_id=1, source_target_pairs={{0,16},{4,12},{8,24},{12,4},{16,0},{20,28},{24,8},{28,20},{1,17},{... | collective-permute-start | bytes 786440 | tf_op jit(solution)/shard_map/ppermute | solution.py:44
  118.9 11.6 %collective-permute-start.34 = (f32[512,128]{1,0:T(8,128)S(1)}, f32[512,128]{1,0:T(8,128)S(1)}, u32[]{:S(2)}, u32[]{:S(2)}) collective-permute-start(f32[512,128]{1,0:T(8,128)S(1)} %add.28.refs_0_), channel_id=1, source_target_pairs={{0,16},{4,12},{8,24},{12,4},{16,0},{20,28},{24,8},{28,20},{1,17},{... | collective-permute-start | bytes 786440 | tf_op jit(solution)/shard_map/ppermute | solution.py:44
  137.7 9.7 %collective-permute-start.31 = (f32[1024,128]{1,0:T(8,128)S(1)}, f32[1024,128]{1,0:T(8,128)S(1)}, u32[]{:S(2)}, u32[]{:S(2)}) collective-permute-start(f32[1024,128]{1,0:T(8,128)S(1)} %join_pieces.7), channel_id=1, source_target_pairs={{0,8},{4,20},{8,0},{12,28},{16,24},{20,4},{24,16},{28,12},{1,9},{5... | collective-permute-start | bytes 1572872 | tf_op jit(solution)/shard_map/ppermute | solution.py:44
  140.8 33.0 %collective-permute-start.36 = (f32[2048,128]{1,0:T(8,128)}, f32[2048,128]{1,0:T(8,128)}, u32[]{:S(2)}, u32[]{:S(2)}) collective-permute-start(f32[2048,128]{1,0:T(8,128)} %pad_maximum_fusion.1.rest_0_.rest_1_), channel_id=1, source_target_pairs={{0,4},{4,0},{8,12},{12,8},{16,20},{20,16},{24,28},{28,24},{1,5},{5... | collective-permute-start | bytes 3145736 | tf_op jit(solution)/shard_map/ppermute | solution.py:44
  146.4 10.8 %collective-permute-start.38 = (f32[512,128]{1,0:T(8,128)S(1)}, f32[512,128]{1,0:T(8,128)S(1)}, u32[]{:S(2)}, u32[]{:S(2)}) collective-permute-start(f32[512,128]{1,0:T(8,128)S(1)} %get-tuple-element.102), channel_id=1, source_target_pairs={{0,16},{4,12},{8,24},{12,4},{16,0},{20,28},{24,8},{28,20},{1,17},{... | collective-permute-start | bytes 786440 | tf_op jit(solution)/shard_map/ppermute | solution.py:44
  147.5 38.4 %collective-permute-start.32 = (f32[2048,128]{1,0:T(8,128)S(1)}, f32[2048,128]{1,0:T(8,128)}, u32[]{:S(2)}, u32[]{:S(2)}) collective-permute-start(f32[2048,128]{1,0:T(8,128)S(1)} %pad_maximum_fusion.rest_0_.rest_1_), channel_id=1, source_target_pairs={{0,4},{4,0},{8,12},{12,8},{16,20},{20,16},{24,28},{28,24},{1,5},{5... | collective-permute-start | bytes 3145736 | tf_op jit(solution)/shard_map/ppermute | solution.py:44
  164.9 16.1 %collective-permute-start.40 = (f32[1024,128]{1,0:T(8,128)}, f32[1024,128]{1,0:T(8,128)}, u32[]{:S(2)}, u32[]{:S(2)}) collective-permute-start(f32[1024,128]{1,0:T(8,128)} %join_pieces.10.refs_0_), channel_id=1, source_target_pairs={{0,8},{4,20},{8,0},{12,28},{16,24},{20,4},{24,16},{28,12},{1,9},{5... | collective-permute-start | bytes 1572872 | tf_op jit(solution)/shard_map/ppermute | solution.py:44
  172.6 20.2 %collective-permute-start.28 = (f32[1024,128]{1,0:T(8,128)S(1)}, f32[1024,128]{1,0:T(8,128)S(1)}, u32[]{:S(2)}, u32[]{:S(2)}) collective-permute-start(f32[1024,128]{1,0:T(8,128)S(1)} %join_pieces.6.refs_0_), channel_id=1, source_target_pairs={{0,8},{4,20},{8,0},{12,28},{16,24},{20,4},{24,16},{28,12},{1,9},{5... | collective-permute-start | bytes 1572872 | tf_op jit(solution)/shard_map/ppermute | solution.py:44
  182.2 10.7 %collective-permute-start.41 = (f32[2048,128]{1,0:T(8,128)S(1)}, f32[2048,128]{1,0:T(8,128)S(1)}, u32[]{:S(2)}, u32[]{:S(2)}) collective-permute-start(f32[2048,128]{1,0:T(8,128)S(1)} %join_pieces.11.rest_0_.rest_1_), channel_id=1, source_target_pairs={{0,4},{4,0},{8,12},{12,8},{16,20},{20,16},{24,28},{28,24},{1,5},{5... | collective-permute-start | bytes 3145736 | tf_op jit(solution)/shard_map/ppermute | solution.py:44
  (49 other events, 438.3 us)

commit v9 on v8

--- a/solution.py
+++ b/solution.py
@@ -13,7 +13,6 @@
 PANELS = 4
 LEAD = PB * PANELS
 HALF = LEAD // 2
-BLOCK = 256
 LAG = 2
 WIDE = 512
 VMEM_BYTES = 48 * 1024 * 1024
@@ -498,16 +497,13 @@
 
 def project_kernel(blocks, places_ref, top_ref, bottom_ref, basis_ref, *rest):
     del places_ref
-    near_even, near_odd, far_even, far_odd, front_ref = rest[:5]
+    each = WIDE // PB
+    near_refs, far_refs, front_ref = rest[:each], rest[each : 2 * each], rest[2 * each]
     upper_ref, out_ref, done_ref = rest[-3:]
     done_ref[...] = jnp.zeros_like(done_ref)
     near = pl.program_id(0) < blocks
     sums = jnp.concatenate(
-        [
-            jnp.where(near, near_even[...], far_even[...]),
-            jnp.where(near, near_odd[...], far_odd[...]),
-        ],
-        axis=1,
+        [jnp.where(near, a[...], b[...]) for a, b in zip(near_refs, far_refs)], axis=1
     )
     hi, lo = parts2(sums)
     upper_ref[:HALF, :] = jnp.dot(
@@ -526,33 +522,32 @@
 def project(places, c, chunks, factor, near, far, front, upper):
     top, bottom, basis = factor
     rows, columns = front.shape
-    blocks = near.shape[0] // LEAD // 2
+    each = WIDE // PB
+    blocks = near.shape[0] // LEAD // each
     begin = c * 2 * blocks
     near_at = chunks * 2 * blocks
-    far_at = near_at + 2 * blocks
-
-    def near_piece(odd):
-        return lambda i, p: (p[near_at + 2 * jnp.minimum(i, blocks - 1) + odd], 0)
-
-    def far_piece(odd):
-        return lambda i, p: (p[far_at + 2 * jnp.maximum(i - blocks, 0) + odd], 0)
+    far_at = near_at + each * blocks
+
+    def near_piece(j):
+        return lambda i, p: (p[near_at + each * jnp.minimum(i, blocks - 1) + j], 0)
+
+    def far_piece(j):
+        return lambda i, p: (p[far_at + each * jnp.maximum(i - blocks, 0) + j], 0)
 
     in_specs = [
         pl.BlockSpec(top.shape, lambda i, p: (0, 0)),
         pl.BlockSpec(bottom.shape, lambda i, p: (0, 0)),
         pl.BlockSpec(basis.shape, lambda i, p: (0, 0)),
-        pl.BlockSpec((LEAD, PB), near_piece(0)),
-        pl.BlockSpec((LEAD, PB), near_piece(1)),
-        pl.BlockSpec((LEAD, PB), far_piece(0)),
-        pl.BlockSpec((LEAD, PB), far_piece(1)),
-        pl.BlockSpec((rows, BLOCK), lambda i, p: (0, p[begin + i])),
+        *[pl.BlockSpec((LEAD, PB), near_piece(j)) for j in range(each)],
+        *[pl.BlockSpec((LEAD, PB), far_piece(j)) for j in range(each)],
+        pl.BlockSpec((rows, WIDE), lambda i, p: (0, p[begin + i])),
     ]
-    operands = [places, top, bottom, basis, near, near, far, far, front]
-    aliases = {8: 1}
+    operands = [places, top, bottom, basis] + [near] * each + [far] * each + [front]
+    aliases = {4 + 2 * each: 1}
     if upper is not None:
         in_specs.append(pl.BlockSpec(memory_space=pl.ANY))
         operands.append(upper)
-        aliases[9] = 0
+        aliases[5 + 2 * each] = 0
     return pl.pallas_call(
         functools.partial(project_kernel, blocks),
         grid_spec=pltpu.PrefetchScalarGridSpec(
@@ -560,8 +555,8 @@
             grid=(2 * blocks,),
             in_specs=in_specs,
             out_specs=(
-                pl.BlockSpec((LEAD, BLOCK), lambda i, p: (0, p[begin + i])),
-                pl.BlockSpec((rows, BLOCK), lambda i, p: (0, p[begin + i])),
+                pl.BlockSpec((LEAD, WIDE), lambda i, p: (0, p[begin + i])),
+                pl.BlockSpec((rows, WIDE), lambda i, p: (0, p[begin + i])),
                 pl.BlockSpec((8, PB), lambda i, p: (0, 0)),
             ),
         ),
@@ -621,7 +616,7 @@
 
     chunks = max(1, min(4, local_cols // (PB * row_count)))
     width = local_cols // 2 // chunks
-    blocks = width // BLOCK
+    blocks = width // WIDE
     core = upper_side(0, row_count)
     *send, front = product(1 - core, left, place, front_matrix, child, None, chunks)
     *keep, front = product(core, left, place, front_matrix, child, front, chunks)

time: 208 us -> 207 us (level)
  Pallas kernels: 79.4 us -> 75.5 us
  local copies, waits for them, and re-layouts: 19.9 us -> 23.3 us
    pallas_call x4, Pallas kernels: 27.3 us -> 23.3 us  [project(): pl.pallas_call(functools.partial(project_kernel, blocks), grid_spec=pltpu...]
    unnamed x60 -> x70, local copies, waits for them, and re-layouts: 16.3 us -> 19.7 us
  transfers between devices with their start and end apart: 43 -> 43, of which waited for: 19 -> 18; matrix products, arithmetic and copies ran while one was open for 3% -> 2% of each run, Pallas kernels for 33% -> 32%
where the time goes in v9:
time: 207 us; the launch traced here: 206 us
  Pallas kernels  75.5 us (36%)
  starting transfers between devices  58.6 us (28%)
  waiting for transfers between devices  45 us (22%)
  local copies, waits for them, and re-layouts  23.3 us (11%)
  other arithmetic  2.13 us (1%)
    ppermute x28, starting transfers between devices, swap(): return lax.ppermute(value, 'row', pairs)  34.8 us
    pallas_call x4, Pallas kernels, project(): pl.pallas_call(functools.partial(project_kernel, blocks), grid_spec=pltpu...  23.3 us
    ppermute x28, waiting for transfers between devices, swap(): return lax.ppermute(value, 'row', pairs)  23.1 us
    pallas_call x4, Pallas kernels, eliminate(): pl.pallas_call(functools.partial(eliminate_kernel, k), out_shape=jax.Shap...  20.1 us
    unnamed x70, local copies, waits for them, and re-layouts  19.7 us
    pallas_call x2, Pallas kernels, product(): pl.pallas_call(functools.partial(product_kernel, blocks, chunks), grid_sp...  16.4 us
    ppermute x3, waiting for transfers between devices, first_hop(): return lax.ppermute(value, 'col', [(0, count // 2)])  14.5 us
    ppermute x7, starting transfers between devices, on_device(): pieces[mask] = lax.ppermute(pieces[mask], 'row', pairs)  9.48 us
  transfers between devices with their start and end apart: 43, of which 18 were waited for; matrix products, arithmetic and copies ran while one was open for 2% of the time, Pallas kernels for 32%

profile of v9, /device:TPU:21, one launch (start us, length us, event | category | flops | bytes accessed | tf_op | source)
XLA Modules:
  0.0 205.6 jit_solution(16152628794019074231)
XLA Ops:
  5.3 4.5 %all-to-all-start = ((f32[8,16,4096]{2,1,0:T(8,128)}), f32[8,16,4096]{2,1,0:T(8,128)S(1)}, u32[]{:S(2)}, u32[]{:S(2)}) async-start(f32[8,16,4096]{2,1,0:T(8,128)} %bitcast.11), calls=%async_computation | async-start | bytes 4194304 | tf_op jit(solution)/shard_map/all_to_all | solution.py:578
  13.2 5.0 %collective-permute-done.refs_1_ = f32[64,512]{1,0:T(8,128)S(1)} collective-permute-done((f32[64,512]{1,0:T(8,128)S(1)}, f32[64,512]{1,0:T(8,128)S(1)}, u32[]{:S(2)}, u32[]{:S(2)}) %collective-permute-start) | collective-permute-done | bytes 131104 | tf_op jit(solution)/shard_map/ppermute | solution.py:168
  27.3 3.2 %collective-permute-done.1.refs_1_ = f32[192,512]{1,0:T(8,128)S(1)} collective-permute-done((f32[192,512]{1,0:T(8,128)S(1)}, f32[192,512]{1,0:T(8,128)S(1)}, u32[]{:S(2)}, u32[]{:S(2)}) %collective-permute-start.1) | collective-permute-done | bytes 393248 | tf_op jit(solution)/shard_map/ppermute | solution.py:168
  32.6 6.3 %collective-permute-done.3.refs_1_ = f32[192,512]{1,0:T(8,128)S(1)} collective-permute-done((f32[192,512]{1,0:T(8,128)S(1)}, f32[192,512]{1,0:T(8,128)S(1)}, u32[]{:S(2)}, u32[]{:S(2)}) %collective-permute-start.3) | collective-permute-done | bytes 393248 | tf_op jit(solution)/shard_map/ppermute | solution.py:168
  43.1 3.8 %collective-permute-start.7 = (f32[16,640]{1,0:T(8,128)S(1)}, f32[16,640]{1,0:T(8,128)S(1)}, u32[]{:S(2)}, u32[]{:S(2)}) collective-permute-start(f32[16,640]{1,0:T(8,128)S(1)} %get-tuple-element.60), channel_id=1, source_target_pairs={{0,4},{4,0},{8,12},{12,8},{16,20},{20,16},{24,28},{28,24},{1,5},{5... | collective-permute-start | bytes 122888 | tf_op jit(solution)/shard_map/ppermute | solution.py:610
  61.9 3.1 %lead_setup.1 = (f32[384,512]{1,0:T(8,128)S(1)}, bf16[512,1152]{1,0:T(8,128)(2,1)S(1)}, bf16[384,384]{1,0:T(8,128)(2,1)S(1)}, f32[256,768]{1,0:T(8,128)S(1)}) custom-call(f32[192,512]{1,0:T(8,128)S(1)} %copy-done.18, f32[192,512]{1,0:T(8,128)} %collective-permute-done.2.refs_1_, f32[192,512]{1,0:T(8,128)S(1)} %copy-done.16, f32[192,512]{1,0:T(8,128)S(1)} %copy-done.26, ...), custom_call_target="tpu_custom_call" | custom-call | tf_op jit(solution)/shard_map/lead_setup/pallas_call | solution.py:293
  67.6 8.9 %lead_product.2 = (f32[512,512]{1,0:T(8,128)}, f32[512,512]{1,0:T(8,128)}, f32[512,512]{1,0:T(8,128)}, f32[512,512]{1,0:T(8,128)}, f32[384,4096]{1,0:T(8,128)}) custom-call(s32[1]{0:T(128)} %bitcast.6.base_ref, bf16[512,1152]{1,0:T(8,128)(2,1)S(1)} %get-tuple-element.68.left_ref, bf16[384,384]{1,0:T(8,128)(2,1)S(1)} %get-tuple-element.69.place_ref, ...), custom_call_target="tpu_custom_call" | custom-call | tf_op jit(solution)/shard_map/lead_product/pallas_call | solution.py:343
  80.6 7.5 %lead_product.3 = (f32[512,512]{1,0:T(8,128)S(1)}, f32[512,512]{1,0:T(8,128)S(1)}, f32[512,512]{1,0:T(8,128)S(1)}, f32[512,512]{1,0:T(8,128)S(1)}, f32[384,4096]{1,0:T(8,128)}) custom-call(s32[1]{0:T(128)} %bitcast.5.base_ref, bf16[512,1152]{1,0:T(8,128)(2,1)S(1)} %get-tuple-element.68.left_ref, ...), custom_call_target="tpu_custom_call", output_to_operand_aliasing={{4}: (5, {})} | custom-call | tf_op jit(solution)/shard_map/lead_product/pallas_call | solution.py:343
  92.4 2.7 %collective-permute-done.16.refs_1_ = f32[128,768]{1,0:T(8,128)S(1)} collective-permute-done((f32[128,768]{1,0:T(8,128)S(1)}, f32[128,768]{1,0:T(8,128)S(1)}, u32[]{:S(2)}, u32[]{:S(2)}) %collective-permute-start.16) | collective-permute-done | bytes 393248 | tf_op jit(solution)/shard_map/ppermute | solution.py:43
  99.7 5.5 %eliminate_panel.4.refs_0_.refs_2_ = f32[512,512]{1,0:T(8,128)S(1)} custom-call(f32[128,768]{1,0:T(8,128)S(1)} %add_gram.3.refs_0_, f32[128,768]{1,0:T(8,128)S(1)} %collective-permute-done.21.refs_1_), custom_call_target="tpu_custom_call" | custom-call | flops 6000000000 | bytes 1048576 | tf_op jit(solution)/shard_map/eliminate_panel/pallas_call | solution.py:458
  105.2 5.2 %eliminate_panel.5.refs_0_.refs_2_ = f32[512,512]{1,0:T(8,128)S(1)} custom-call(f32[512,512]{1,0:T(8,128)S(1)} %eliminate_panel.4.refs_0_.refs_2_), custom_call_target="tpu_custom_call" | custom-call | flops 6000000000 | bytes 1048576 | tf_op jit(solution)/shard_map/eliminate_panel/pallas_call | solution.py:458
  111.3 5.1 %eliminate_panel.6.refs_0_.refs_2_ = f32[512,512]{1,0:T(8,128)S(1)} custom-call(f32[512,512]{1,0:T(8,128)S(1)} %eliminate_panel.5.refs_0_.refs_2_), custom_call_target="tpu_custom_call" | custom-call | flops 6000000000 | bytes 1048576 | tf_op jit(solution)/shard_map/eliminate_panel/pallas_call | solution.py:458
  119.8 4.3 %eliminate_panel.7.matrix_ref.refs_2_ = f32[512,512]{1,0:T(8,128)S(1)} custom-call(f32[512,512]{1,0:T(8,128)S(1)} %eliminate_panel.6.refs_0_.refs_2_), custom_call_target="tpu_custom_call" | custom-call | flops 6000000000 | bytes 1048576 | tf_op jit(solution)/shard_map/eliminate_panel/pallas_call | solution.py:458
  124.2 3.7 %collective-permute-done.22.refs_1_ = f32[512,256]{1,0:T(8,128)S(1)} collective-permute-done((f32[512,256]{1,0:T(8,128)S(1)}, f32[512,256]{1,0:T(8,128)S(1)}, u32[]{:S(2)}, u32[]{:S(2)}) %collective-permute-start.22) | collective-permute-done | bytes 524320 | tf_op jit(solution)/shard_map/ppermute | solution.py:43
  128.1 2.4 %finish_factor.1 = (bf16[256,768]{1,0:T(8,128)(2,1)S(1)}, bf16[256,1536]{1,0:T(8,128)(2,1)S(1)}, bf16[384,1536]{1,0:T(8,128)(2,1)S(1)}, f32[384,512]{1,0:T(8,128)}) custom-call(f32[512,512]{1,0:T(8,128)S(1)} %eliminate_panel.7.matrix_ref.refs_2_, f32[384,512]{1,0:T(8,128)S(1)} %copy-done.31), custom_call_target="tpu_custom_call" | custom-call | flops 2000000000 | bytes 1048576 | tf_op jit(solution)/shard_map/finish_factor/pallas_call | solution.py:482
  132.8 5.8 %collective-permute-done.30.refs_1_ = f32[512,128]{1,0:T(8,128)S(1)} collective-permute-done((f32[512,128]{1,0:T(8,128)S(1)}, f32[512,128]{1,0:T(8,128)S(1)}, u32[]{:S(2)}, u32[]{:S(2)}) %collective-permute-start.30) | collective-permute-done | bytes 262176 | tf_op jit(solution)/shard_map/ppermute | solution.py:43
  140.6 5.8 %collective-permute-start.36 = (f32[2048,128]{1,0:T(8,128)S(1)}, f32[2048,128]{1,0:T(8,128)}, u32[]{:S(2)}, u32[]{:S(2)}) collective-permute-start(f32[2048,128]{1,0:T(8,128)S(1)} %pad_maximum_fusion.1.rest_0_.rest_1_.rest_2_.rest_3_), channel_id=1, source_target_pairs={{0,4},{4,0},{8,12},{12,8},{16,20},{20,16},{24,28},{28,24},{1,5},{5... | collective-permute-start | bytes 3145736 | tf_op jit(solution)/shard_map/ppermute | solution.py:43
  148.3 8.1 %collective-permute-start.32 = (f32[2048,128]{1,0:T(8,128)S(1)}, f32[2048,128]{1,0:T(8,128)S(1)}, u32[]{:S(2)}, u32[]{:S(2)}) collective-permute-start(f32[2048,128]{1,0:T(8,128)S(1)} %pad_maximum_fusion.rest_0_.rest_1_.rest_2_.rest_3_), channel_id=1, source_target_pairs={{0,4},{4,0},{8,12},{12,8},{16,20},{20,16},{24,28},{28,24},{1,5},{5... | collective-permute-start | bytes 3145736 | tf_op jit(solution)/shard_map/ppermute | solution.py:43
  158.2 3.9 %collective-permute-done.23 = f32[512,128]{1,0:T(8,128)S(1)} collective-permute-done((f32[512,128]{1,0:T(8,128)S(1)}, f32[512,128]{1,0:T(8,128)S(1)}, u32[]{:S(2)}, u32[]{:S(2)}) %collective-permute-start.23) | collective-permute-done | bytes 262176 | tf_op jit(solution)/shard_map/ppermute | solution.py:43
  177.2 6.1 %project_columns.4 = (f32[512,4096]{1,0:T(8,128)}, f32[384,4096]{1,0:T(8,128)}, f32[8,128]{1,0:T(8,128)S(1)}) custom-call(s32[16]{0:T(128)S(1)} %fusion.places_ref, bf16[256,768]{1,0:T(8,128)(2,1)S(1)} %get-tuple-element.84.refs_6_.top_ref, bf16[256,1536]{1,0:T(8,128)(2,1)S(1)} %copy-done.4, ...), custom_call_target="tpu_custom_call", output_to_operand_aliasing={{1}: (12, {})} | custom-call | flops 3000000000 | bytes 1048576 | tf_op jit(solution)/shard_map/project_columns/pallas_call | solution.py:551
  184.6 3.7 %collective-permute-start.41 = (f32[2048,128]{1,0:T(8,128)S(1)}, f32[2048,128]{1,0:T(8,128)S(1)}, u32[]{:S(2)}, u32[]{:S(2)}) collective-permute-start(f32[2048,128]{1,0:T(8,128)S(1)} %join_pieces.11.rest_0_.rest_1_.rest_2_.rest_3_), channel_id=1, source_target_pairs={{0,4},{4,0},{8,12},{12,8},{16,20},{20,16},{24,28},{28,24},{1,5},{5... | collective-permute-start | bytes 3145736 | tf_op jit(solution)/shard_map/ppermute | solution.py:43
  188.2 5.7 %project_columns.5 = (f32[512,4096]{1,0:T(8,128)}, f32[384,4096]{1,0:T(8,128)}, f32[8,128]{1,0:T(8,128)S(1)}) custom-call(s32[16]{0:T(128)S(1)} %fusion.places_ref, bf16[256,768]{1,0:T(8,128)(2,1)S(1)} %get-tuple-element.84.refs_6_.top_ref, bf16[256,1536]{1,0:T(8,128)(2,1)S(1)} %copy-done.5, ...), custom_call_target="tpu_custom_call", output_to_operand_aliasing={{1}: (12, {}), {0}: (13, {})} | custom-call | flops 3000000000 | bytes 1048576 | tf_op jit(solution)/shard_map/project_columns/pallas_call | solution.py:551
  194.2 5.7 %project_columns.6 = (f32[512,4096]{1,0:T(8,128)}, f32[384,4096]{1,0:T(8,128)}, f32[8,128]{1,0:T(8,128)}) custom-call(s32[16]{0:T(128)S(1)} %fusion.places_ref, bf16[256,768]{1,0:T(8,128)(2,1)S(1)} %get-tuple-element.84.refs_6_.top_ref, bf16[256,1536]{1,0:T(8,128)(2,1)S(1)} %copy-done.5, ...), custom_call_target="tpu_custom_call", output_to_operand_aliasing={{1}: (12, {}), {0}: (13, {})} | custom-call | flops 3000000000 | bytes 1048576 | tf_op jit(solution)/shard_map/project_columns/pallas_call | solution.py:551
  199.9 5.7 %project_columns.7 = (f32[512,4096]{1,0:T(8,128)}, f32[384,4096]{1,0:T(8,128)}, f32[8,128]{1,0:T(8,128)}) custom-call(s32[16]{0:T(128)S(1)} %fusion.places_ref, bf16[256,768]{1,0:T(8,128)(2,1)S(1)} %get-tuple-element.84.refs_6_.top_ref, bf16[256,1536]{1,0:T(8,128)(2,1)S(1)} %copy-done.5, ...), custom_call_target="tpu_custom_call", output_to_operand_aliasing={{1}: (12, {}), {0}: (13, {})} | custom-call | flops 3000000000 | bytes 1048576 | tf_op jit(solution)/shard_map/project_columns/pallas_call | solution.py:551
  (177 shorter events, 82.6 us)
Async XLA Ops:
  5.3 34.5 %all-to-all-start = ((f32[8,16,4096]{2,1,0:T(8,128)}), f32[8,16,4096]{2,1,0:T(8,128)S(1)}, u32[]{:S(2)}, u32[]{:S(2)}) async-start(f32[8,16,4096]{2,1,0:T(8,128)} %bitcast.11), calls=%async_computation | async-start | bytes 4194304 | tf_op jit(solution)/shard_map/all_to_all | solution.py:578
  18.3 12.2 %collective-permute-start.1 = (f32[192,512]{1,0:T(8,128)S(1)}, f32[192,512]{1,0:T(8,128)S(1)}, u32[]{:S(2)}, u32[]{:S(2)}) collective-permute-start(f32[192,512]{1,0:T(8,128)S(1)} %get-tuple-element.57.refs_0_), channel_id=1, source_target_pairs={{0,2},{4,6},{8,10},{12,14},{16,18},{20,22},{24,26},{28,30}} | collective-permute-start | bytes 1179656 | tf_op jit(solution)/shard_map/ppermute | solution.py:168
  19.6 19.3 %collective-permute-start.3 = (f32[192,512]{1,0:T(8,128)S(1)}, f32[192,512]{1,0:T(8,128)S(1)}, u32[]{:S(2)}, u32[]{:S(2)}) collective-permute-start(f32[192,512]{1,0:T(8,128)S(1)} %get-tuple-element.58.refs_0_), channel_id=1, source_target_pairs={{0,2},{4,6},{8,10},{12,14},{16,18},{20,22},{24,26},{28,30}} | collective-permute-start | bytes 1179656 | tf_op jit(solution)/shard_map/ppermute | solution.py:168
  30.6 27.5 %collective-permute-start.2 = (f32[192,512]{1,0:T(8,128)S(1)}, f32[192,512]{1,0:T(8,128)}, u32[]{:S(2)}, u32[]{:S(2)}) collective-permute-start(f32[192,512]{1,0:T(8,128)S(1)} %relay.4.refs_0_), channel_id=1, source_target_pairs={{0,1},{2,3},{4,5},{6,7},{8,9},{10,11},{12,13},{14,15},{16,17},{18,... | collective-permute-start | bytes 1179656 | tf_op jit(solution)/shard_map/ppermute | solution.py:154
  41.1 17.0 %collective-permute-start.6 = (f32[192,512]{1,0:T(8,128)S(1)}, f32[192,512]{1,0:T(8,128)S(1)}, u32[]{:S(2)}, u32[]{:S(2)}) collective-permute-start(f32[192,512]{1,0:T(8,128)S(1)} %relay.5.refs_2_), channel_id=1, source_target_pairs={{0,1},{2,3},{4,5},{6,7},{8,9},{10,11},{12,13},{14,15},{16,17},{18,... | collective-permute-start | bytes 1179656 | tf_op jit(solution)/shard_map/ppermute | solution.py:154
  67.6 10.0 %collective-permute-start.14 = (f32[128,768]{1,0:T(8,128)}, f32[128,768]{1,0:T(8,128)}, u32[]{:S(2)}, u32[]{:S(2)}) collective-permute-start(f32[128,768]{1,0:T(8,128)} %constant_dynamic-slice_fusion), channel_id=1, source_target_pairs={{0,4},{4,0},{8,12},{12,8},{16,20},{20,16},{24,28},{28,24},{1,5},{5... | collective-permute-start | bytes 1179656 | tf_op jit(solution)/shard_map/ppermute | solution.py:43
  76.5 12.9 %collective-permute-start.17 = (f32[512,512]{1,0:T(8,128)}, f32[512,512]{1,0:T(8,128)}, u32[]{:S(2)}, u32[]{:S(2)}) collective-permute-start(f32[512,512]{1,0:T(8,128)} %get-tuple-element.72), channel_id=1, source_target_pairs={{0,4},{4,0},{8,12},{12,8},{16,20},{20,16},{24,28},{28,24},{1,5},{5... | collective-permute-start | bytes 3145736 | tf_op jit(solution)/shard_map/ppermute | solution.py:43
  77.0 13.7 %collective-permute-start.18 = (f32[512,512]{1,0:T(8,128)}, f32[512,512]{1,0:T(8,128)}, u32[]{:S(2)}, u32[]{:S(2)}) collective-permute-start(f32[512,512]{1,0:T(8,128)} %get-tuple-element.75), channel_id=1, source_target_pairs={{0,4},{4,0},{8,12},{12,8},{16,20},{20,16},{24,28},{28,24},{1,5},{5... | collective-permute-start | bytes 3145736 | tf_op jit(solution)/shard_map/ppermute | solution.py:43
  77.1 15.0 %collective-permute-start.19 = (f32[512,512]{1,0:T(8,128)}, f32[512,512]{1,0:T(8,128)S(1)}, u32[]{:S(2)}, u32[]{:S(2)}) collective-permute-start(f32[512,512]{1,0:T(8,128)} %get-tuple-element.78), channel_id=1, source_target_pairs={{0,4},{4,0},{8,12},{12,8},{16,20},{20,16},{24,28},{28,24},{1,5},{5... | collective-permute-start | bytes 3145736 | tf_op jit(solution)/shard_map/ppermute | solution.py:43
  77.5 14.8 %collective-permute-start.20 = (f32[512,512]{1,0:T(8,128)}, f32[512,512]{1,0:T(8,128)S(1)}, u32[]{:S(2)}, u32[]{:S(2)}) collective-permute-start(f32[512,512]{1,0:T(8,128)} %get-tuple-element.81), channel_id=1, source_target_pairs={{0,4},{4,0},{8,12},{12,8},{16,20},{20,16},{24,28},{28,24},{1,5},{5... | collective-permute-start | bytes 3145736 | tf_op jit(solution)/shard_map/ppermute | solution.py:43
  78.8 9.4 %collective-permute-start.15 = (f32[128,768]{1,0:T(8,128)S(1)}, f32[128,768]{1,0:T(8,128)S(1)}, u32[]{:S(2)}, u32[]{:S(2)}) collective-permute-start(f32[128,768]{1,0:T(8,128)S(1)} %dynamic-slice_add_fusion.refs_0_), channel_id=1, source_target_pairs={{0,8},{4,20},{8,0},{12,28},{16,24},{20,4},{24,16},{28,12},{1,9},{5... | collective-permute-start | bytes 1179656 | tf_op jit(solution)/shard_map/ppermute | solution.py:43
  96.8 13.7 %collective-permute-start.25 = (f32[512,256]{1,0:T(8,128)S(1)}, f32[512,256]{1,0:T(8,128)S(1)}, u32[]{:S(2)}, u32[]{:S(2)}) collective-permute-start(f32[512,256]{1,0:T(8,128)S(1)} %get-tuple-element.90), channel_id=1, source_target_pairs={{0,8},{4,20},{8,0},{12,28},{16,24},{20,4},{24,16},{28,12},{1,9},{5... | collective-permute-start | bytes 1572872 | tf_op jit(solution)/shard_map/ppermute | solution.py:43
  97.6 18.8 %collective-permute-start.26 = (f32[512,256]{1,0:T(8,128)S(1)}, f32[512,256]{1,0:T(8,128)S(1)}, u32[]{:S(2)}, u32[]{:S(2)}) collective-permute-start(f32[512,256]{1,0:T(8,128)S(1)} %get-tuple-element.92), channel_id=1, source_target_pairs={{0,8},{4,20},{8,0},{12,28},{16,24},{20,4},{24,16},{28,12},{1,9},{5... | collective-permute-start | bytes 1572872 | tf_op jit(solution)/shard_map/ppermute | solution.py:43
  98.2 25.9 %collective-permute-start.27 = (f32[512,256]{1,0:T(8,128)S(1)}, f32[512,256]{1,0:T(8,128)S(1)}, u32[]{:S(2)}, u32[]{:S(2)}) collective-permute-start(f32[512,256]{1,0:T(8,128)S(1)} %get-tuple-element.94), channel_id=1, source_target_pairs={{0,8},{4,20},{8,0},{12,28},{16,24},{20,4},{24,16},{28,12},{1,9},{5... | collective-permute-start | bytes 1572872 | tf_op jit(solution)/shard_map/ppermute | solution.py:43
  99.1 28.9 %collective-permute-start.22 = (f32[512,256]{1,0:T(8,128)S(1)}, f32[512,256]{1,0:T(8,128)S(1)}, u32[]{:S(2)}, u32[]{:S(2)}) collective-permute-start(f32[512,256]{1,0:T(8,128)S(1)} %get-tuple-element.87), channel_id=1, source_target_pairs={{0,8},{4,20},{8,0},{12,28},{16,24},{20,4},{24,16},{28,12},{1,9},{5... | collective-permute-start | bytes 1572872 | tf_op jit(solution)/shard_map/ppermute | solution.py:43
  116.5 16.2 %collective-permute-start.29 = (f32[512,128]{1,0:T(8,128)S(1)}, f32[512,128]{1,0:T(8,128)S(1)}, u32[]{:S(2)}, u32[]{:S(2)}) collective-permute-start(f32[512,128]{1,0:T(8,128)S(1)} %get-tuple-element.96), channel_id=1, source_target_pairs={{0,16},{4,12},{8,24},{12,4},{16,0},{20,28},{24,8},{28,20},{1,17},{... | collective-permute-start | bytes 786440 | tf_op jit(solution)/shard_map/ppermute | solution.py:43
  119.0 12.3 %collective-permute-start.34 = (f32[512,128]{1,0:T(8,128)S(1)}, f32[512,128]{1,0:T(8,128)S(1)}, u32[]{:S(2)}, u32[]{:S(2)}) collective-permute-start(f32[512,128]{1,0:T(8,128)S(1)} %add.28.refs_0_), channel_id=1, source_target_pairs={{0,16},{4,12},{8,24},{12,4},{16,0},{20,28},{24,8},{28,20},{1,17},{... | collective-permute-start | bytes 786440 | tf_op jit(solution)/shard_map/ppermute | solution.py:43
  138.6 9.6 %collective-permute-start.31 = (f32[1024,128]{1,0:T(8,128)S(1)}, f32[1024,128]{1,0:T(8,128)S(1)}, u32[]{:S(2)}, u32[]{:S(2)}) collective-permute-start(f32[1024,128]{1,0:T(8,128)S(1)} %join_pieces.7), channel_id=1, source_target_pairs={{0,8},{4,20},{8,0},{12,28},{16,24},{20,4},{24,16},{28,12},{1,9},{5... | collective-permute-start | bytes 1572872 | tf_op jit(solution)/shard_map/ppermute | solution.py:43
  140.6 34.2 %collective-permute-start.36 = (f32[2048,128]{1,0:T(8,128)S(1)}, f32[2048,128]{1,0:T(8,128)}, u32[]{:S(2)}, u32[]{:S(2)}) collective-permute-start(f32[2048,128]{1,0:T(8,128)S(1)} %pad_maximum_fusion.1.rest_0_.rest_1_.rest_2_.rest_3_), channel_id=1, source_target_pairs={{0,4},{4,0},{8,12},{12,8},{16,20},{20,16},{24,28},{28,24},{1,5},{5... | collective-permute-start | bytes 3145736 | tf_op jit(solution)/shard_map/ppermute | solution.py:43
  146.4 11.7 %collective-permute-start.38 = (f32[512,128]{1,0:T(8,128)S(1)}, f32[512,128]{1,0:T(8,128)S(1)}, u32[]{:S(2)}, u32[]{:S(2)}) collective-permute-start(f32[512,128]{1,0:T(8,128)S(1)} %get-tuple-element.102), channel_id=1, source_target_pairs={{0,16},{4,12},{8,24},{12,4},{16,0},{20,28},{24,8},{28,20},{1,17},{... | collective-permute-start | bytes 786440 | tf_op jit(solution)/shard_map/ppermute | solution.py:43
  148.3 39.9 %collective-permute-start.32 = (f32[2048,128]{1,0:T(8,128)S(1)}, f32[2048,128]{1,0:T(8,128)S(1)}, u32[]{:S(2)}, u32[]{:S(2)}) collective-permute-start(f32[2048,128]{1,0:T(8,128)S(1)} %pad_maximum_fusion.rest_0_.rest_1_.rest_2_.rest_3_), channel_id=1, source_target_pairs={{0,4},{4,0},{8,12},{12,8},{16,20},{20,16},{24,28},{28,24},{1,5},{5... | collective-permute-start | bytes 3145736 | tf_op jit(solution)/shard_map/ppermute | solution.py:43
  165.8 17.5 %collective-permute-start.40 = (f32[1024,128]{1,0:T(8,128)}, f32[1024,128]{1,0:T(8,128)}, u32[]{:S(2)}, u32[]{:S(2)}) collective-permute-start(f32[1024,128]{1,0:T(8,128)} %join_pieces.10.refs_0_), channel_id=1, source_target_pairs={{0,8},{4,20},{8,0},{12,28},{16,24},{20,4},{24,16},{28,12},{1,9},{5... | collective-permute-start | bytes 1572872 | tf_op jit(solution)/shard_map/ppermute | solution.py:43
  173.6 20.4 %collective-permute-start.28 = (f32[1024,128]{1,0:T(8,128)S(1)}, f32[1024,128]{1,0:T(8,128)S(1)}, u32[]{:S(2)}, u32[]{:S(2)}) collective-permute-start(f32[1024,128]{1,0:T(8,128)S(1)} %join_pieces.6.refs_0_), channel_id=1, source_target_pairs={{0,8},{4,20},{8,0},{12,28},{16,24},{20,4},{24,16},{28,12},{1,9},{5... | collective-permute-start | bytes 1572872 | tf_op jit(solution)/shard_map/ppermute | solution.py:43
  184.6 9.6 %collective-permute-start.41 = (f32[2048,128]{1,0:T(8,128)S(1)}, f32[2048,128]{1,0:T(8,128)S(1)}, u32[]{:S(2)}, u32[]{:S(2)}) collective-permute-start(f32[2048,128]{1,0:T(8,128)S(1)} %join_pieces.11.rest_0_.rest_1_.rest_2_.rest_3_), channel_id=1, source_target_pairs={{0,4},{4,0},{8,12},{12,8},{16,20},{20,16},{24,28},{28,24},{1,5},{5... | collective-permute-start | bytes 3145736 | tf_op jit(solution)/shard_map/ppermute | solution.py:43
  (54 other events, 489.8 us)

commit v10 on v9

--- a/solution.py
+++ b/solution.py
@@ -15,7 +15,7 @@
 HALF = LEAD // 2
 LAG = 2
 WIDE = 512
-VMEM_BYTES = 48 * 1024 * 1024
+VMEM_BYTES = 40 * 1024 * 1024
 HIGHEST = lax.Precision.HIGHEST
 F32 = jnp.float32
 BF16 = jnp.bfloat16

time: 207 us -> 210 us (1.014)
  local copies, waits for them, and re-layouts: 23.3 us -> 27.9 us
  waiting for transfers between devices: 45 us -> 42.8 us
    unnamed x70 -> x74, local copies, waits for them, and re-layouts: 19.7 us -> 24.3 us
    pallas_call x20, Pallas kernels: 6.92 us -> 9.34 us  [ordered(): pl.pallas_call(kernel, out_shape=tuple(outs), in_specs=in_vmem(count) + [...]
    ppermute x28, waiting for transfers between devices: 23.1 us -> 20.9 us  [swap(): return lax.ppermute(value, 'row', pairs)]
    pallas_call x2, Pallas kernels: 16.4 us -> 14.3 us  [product(): pl.pallas_call(functools.partial(product_kernel, blocks, chunks), grid_sp...]
where the time goes in v10:
time: 210 us; the launch traced here: 208 us
  Pallas kernels  75.8 us (36%)
  starting transfers between devices  58.3 us (28%)
  waiting for transfers between devices  42.8 us (20%)
  local copies, waits for them, and re-layouts  27.9 us (13%)
  other arithmetic  2.11 us (1%)
    ppermute x28, starting transfers between devices, swap(): return lax.ppermute(value, 'row', pairs)  34.5 us
    unnamed x74, local copies, waits for them, and re-layouts  24.3 us
    pallas_call x4, Pallas kernels, project(): pl.pallas_call(functools.partial(project_kernel, blocks), grid_spec=pltpu...  23.3 us
    ppermute x28, waiting for transfers between devices, swap(): return lax.ppermute(value, 'row', pairs)  20.9 us
    pallas_call x4, Pallas kernels, eliminate(): pl.pallas_call(functools.partial(eliminate_kernel, k), out_shape=jax.Shap...  20.1 us
    ppermute x3, waiting for transfers between devices, first_hop(): return lax.ppermute(value, 'col', [(0, count // 2)])  14.5 us
    pallas_call x2, Pallas kernels, product(): pl.pallas_call(functools.partial(product_kernel, blocks, chunks), grid_sp...  14.3 us
    ppermute x7, starting transfers between devices, on_device(): pieces[mask] = lax.ppermute(pieces[mask], 'row', pairs)  9.48 us
  transfers between devices with their start and end apart: 43, of which 18 were waited for; matrix products, arithmetic and copies ran while one was open for 2% of the time, Pallas kernels for 32%

profile of v10, /device:TPU:21, one launch (start us, length us, event | category | flops | bytes accessed | tf_op | source)
XLA Modules:
  0.0 208.0 jit_solution(2695409648609020097)
XLA Ops:
  5.3 4.5 %all-to-all-start = ((f32[8,16,4096]{2,1,0:T(8,128)}), f32[8,16,4096]{2,1,0:T(8,128)S(1)}, u32[]{:S(2)}, u32[]{:S(2)}) async-start(f32[8,16,4096]{2,1,0:T(8,128)} %bitcast.11), calls=%async_computation | async-start | bytes 4194304 | tf_op jit(solution)/shard_map/all_to_all | solution.py:578
  13.2 5.0 %collective-permute-done.refs_1_ = f32[64,512]{1,0:T(8,128)S(1)} collective-permute-done((f32[64,512]{1,0:T(8,128)S(1)}, f32[64,512]{1,0:T(8,128)S(1)}, u32[]{:S(2)}, u32[]{:S(2)}) %collective-permute-start) | collective-permute-done | bytes 131104 | tf_op jit(solution)/shard_map/ppermute | solution.py:168
  27.3 3.2 %collective-permute-done.1.refs_1_ = f32[192,512]{1,0:T(8,128)S(1)} collective-permute-done((f32[192,512]{1,0:T(8,128)S(1)}, f32[192,512]{1,0:T(8,128)S(1)}, u32[]{:S(2)}, u32[]{:S(2)}) %collective-permute-start.1) | collective-permute-done | bytes 393248 | tf_op jit(solution)/shard_map/ppermute | solution.py:168
  32.7 6.3 %collective-permute-done.3.refs_1_ = f32[192,512]{1,0:T(8,128)S(1)} collective-permute-done((f32[192,512]{1,0:T(8,128)S(1)}, f32[192,512]{1,0:T(8,128)S(1)}, u32[]{:S(2)}, u32[]{:S(2)}) %collective-permute-start.3) | collective-permute-done | bytes 393248 | tf_op jit(solution)/shard_map/ppermute | solution.py:168
  42.8 3.8 %collective-permute-start.7 = (f32[16,640]{1,0:T(8,128)S(1)}, f32[16,640]{1,0:T(8,128)S(1)}, u32[]{:S(2)}, u32[]{:S(2)}) collective-permute-start(f32[16,640]{1,0:T(8,128)S(1)} %get-tuple-element.60), channel_id=1, source_target_pairs={{0,4},{4,0},{8,12},{12,8},{16,20},{20,16},{24,28},{28,24},{1,5},{5... | collective-permute-start | bytes 122888 | tf_op jit(solution)/shard_map/ppermute | solution.py:610
  61.5 3.1 %lead_setup.1 = (f32[384,512]{1,0:T(8,128)S(1)}, bf16[512,1152]{1,0:T(8,128)(2,1)S(1)}, bf16[384,384]{1,0:T(8,128)(2,1)S(1)}, f32[256,768]{1,0:T(8,128)S(1)}) custom-call(f32[192,512]{1,0:T(8,128)S(1)} %copy-done.20, f32[192,512]{1,0:T(8,128)} %collective-permute-done.2.refs_1_, f32[192,512]{1,0:T(8,128)S(1)} %copy-done.18, f32[192,512]{1,0:T(8,128)S(1)} %copy-done.28, ...), custom_call_target="tpu_custom_call" | custom-call | tf_op jit(solution)/shard_map/lead_setup/pallas_call | solution.py:293
  66.5 2.8 %copy-done = f32[384,4096]{1,0:T(8,128)S(1)} copy-done((f32[384,4096]{1,0:T(8,128)S(1)}, f32[384,4096]{1,0:T(8,128)}, u32[]{:S(2)}) %copy-start) | copy-done | bytes 6291480
  69.3 7.8 %lead_product.2 = (f32[512,512]{1,0:T(8,128)}, f32[512,512]{1,0:T(8,128)}, f32[512,512]{1,0:T(8,128)}, f32[512,512]{1,0:T(8,128)}, f32[384,4096]{1,0:T(8,128)}) custom-call(s32[1]{0:T(128)} %bitcast.6.base_ref, bf16[512,1152]{1,0:T(8,128)(2,1)S(1)} %get-tuple-element.68.left_ref, bf16[384,384]{1,0:T(8,128)(2,1)S(1)} %get-tuple-element.69.place_ref, ...), custom_call_target="tpu_custom_call" | custom-call | tf_op jit(solution)/shard_map/lead_product/pallas_call | solution.py:343
  80.2 2.8 %copy-done.1 = f32[384,4096]{1,0:T(8,128)S(1)} copy-done((f32[384,4096]{1,0:T(8,128)S(1)}, f32[384,4096]{1,0:T(8,128)}, u32[]{:S(2)}) %copy-start.1) | copy-done | bytes 6291480
  83.9 6.4 %lead_product.3 = (f32[512,512]{1,0:T(8,128)S(1)}, f32[512,512]{1,0:T(8,128)S(1)}, f32[512,512]{1,0:T(8,128)S(1)}, f32[512,512]{1,0:T(8,128)S(1)}, f32[384,4096]{1,0:T(8,128)}) custom-call(s32[1]{0:T(128)} %bitcast.5.base_ref, bf16[512,1152]{1,0:T(8,128)(2,1)S(1)} %get-tuple-element.68.left_ref, ...), custom_call_target="tpu_custom_call", output_to_operand_aliasing={{4}: (5, {})} | custom-call | tf_op jit(solution)/shard_map/lead_product/pallas_call | solution.py:343
  102.0 5.5 %eliminate_panel.4.refs_0_.refs_2_ = f32[512,512]{1,0:T(8,128)S(1)} custom-call(f32[128,768]{1,0:T(8,128)S(1)} %add_gram.3.refs_0_, f32[128,768]{1,0:T(8,128)S(1)} %collective-permute-done.21.refs_1_), custom_call_target="tpu_custom_call" | custom-call | flops 6000000000 | bytes 1048576 | tf_op jit(solution)/shard_map/eliminate_panel/pallas_call | solution.py:458
  107.5 5.2 %eliminate_panel.5.refs_0_.refs_2_ = f32[512,512]{1,0:T(8,128)S(1)} custom-call(f32[512,512]{1,0:T(8,128)S(1)} %eliminate_panel.4.refs_0_.refs_2_), custom_call_target="tpu_custom_call" | custom-call | flops 6000000000 | bytes 1048576 | tf_op jit(solution)/shard_map/eliminate_panel/pallas_call | solution.py:458
  113.5 5.1 %eliminate_panel.6.refs_0_.refs_2_ = f32[512,512]{1,0:T(8,128)S(1)} custom-call(f32[512,512]{1,0:T(8,128)S(1)} %eliminate_panel.5.refs_0_.refs_2_), custom_call_target="tpu_custom_call" | custom-call | flops 6000000000 | bytes 1048576 | tf_op jit(solution)/shard_map/eliminate_panel/pallas_call | solution.py:458
  122.0 4.3 %eliminate_panel.7.matrix_ref.refs_2_ = f32[512,512]{1,0:T(8,128)S(1)} custom-call(f32[512,512]{1,0:T(8,128)S(1)} %eliminate_panel.6.refs_0_.refs_2_), custom_call_target="tpu_custom_call" | custom-call | flops 6000000000 | bytes 1048576 | tf_op jit(solution)/shard_map/eliminate_panel/pallas_call | solution.py:458
  126.5 3.8 %collective-permute-done.22.refs_1_ = f32[512,256]{1,0:T(8,128)S(1)} collective-permute-done((f32[512,256]{1,0:T(8,128)S(1)}, f32[512,256]{1,0:T(8,128)S(1)}, u32[]{:S(2)}, u32[]{:S(2)}) %collective-permute-start.22) | collective-permute-done | bytes 524320 | tf_op jit(solution)/shard_map/ppermute | solution.py:43
  135.2 5.8 %collective-permute-done.30.refs_1_ = f32[512,128]{1,0:T(8,128)S(1)} collective-permute-done((f32[512,128]{1,0:T(8,128)S(1)}, f32[512,128]{1,0:T(8,128)S(1)}, u32[]{:S(2)}, u32[]{:S(2)}) %collective-permute-start.30) | collective-permute-done | bytes 262176 | tf_op jit(solution)/shard_map/ppermute | solution.py:43
  143.0 5.8 %collective-permute-start.36 = (f32[2048,128]{1,0:T(8,128)S(1)}, f32[2048,128]{1,0:T(8,128)}, u32[]{:S(2)}, u32[]{:S(2)}) collective-permute-start(f32[2048,128]{1,0:T(8,128)S(1)} %pad_maximum_fusion.1.rest_0_.rest_1_.rest_2_.rest_3_), channel_id=1, source_target_pairs={{0,4},{4,0},{8,12},{12,8},{16,20},{20,16},{24,28},{28,24},{1,5},{5... | collective-permute-start | bytes 3145736 | tf_op jit(solution)/shard_map/ppermute | solution.py:43
  150.7 8.1 %collective-permute-start.32 = (f32[2048,128]{1,0:T(8,128)S(1)}, f32[2048,128]{1,0:T(8,128)S(1)}, u32[]{:S(2)}, u32[]{:S(2)}) collective-permute-start(f32[2048,128]{1,0:T(8,128)S(1)} %pad_maximum_fusion.rest_0_.rest_1_.rest_2_.rest_3_), channel_id=1, source_target_pairs={{0,4},{4,0},{8,12},{12,8},{16,20},{20,16},{24,28},{28,24},{1,5},{5... | collective-permute-start | bytes 3145736 | tf_op jit(solution)/shard_map/ppermute | solution.py:43
  160.6 3.9 %collective-permute-done.23 = f32[512,128]{1,0:T(8,128)S(1)} collective-permute-done((f32[512,128]{1,0:T(8,128)S(1)}, f32[512,128]{1,0:T(8,128)S(1)}, u32[]{:S(2)}, u32[]{:S(2)}) %collective-permute-start.23) | collective-permute-done | bytes 262176 | tf_op jit(solution)/shard_map/ppermute | solution.py:43
  179.5 6.1 %project_columns.4 = (f32[512,4096]{1,0:T(8,128)}, f32[384,4096]{1,0:T(8,128)}, f32[8,128]{1,0:T(8,128)S(1)}) custom-call(s32[16]{0:T(128)S(1)} %fusion.places_ref, bf16[256,768]{1,0:T(8,128)(2,1)S(1)} %get-tuple-element.84.refs_6_.top_ref, bf16[256,1536]{1,0:T(8,128)(2,1)S(1)} %copy-done.6, ...), custom_call_target="tpu_custom_call", output_to_operand_aliasing={{1}: (12, {})} | custom-call | flops 3000000000 | bytes 1048576 | tf_op jit(solution)/shard_map/project_columns/pallas_call | solution.py:551
  186.9 3.7 %collective-permute-start.41 = (f32[2048,128]{1,0:T(8,128)S(1)}, f32[2048,128]{1,0:T(8,128)S(1)}, u32[]{:S(2)}, u32[]{:S(2)}) collective-permute-start(f32[2048,128]{1,0:T(8,128)S(1)} %join_pieces.11.rest_0_.rest_1_.rest_2_.rest_3_), channel_id=1, source_target_pairs={{0,4},{4,0},{8,12},{12,8},{16,20},{20,16},{24,28},{28,24},{1,5},{5... | collective-permute-start | bytes 3145736 | tf_op jit(solution)/shard_map/ppermute | solution.py:43
  190.6 5.8 %project_columns.5 = (f32[512,4096]{1,0:T(8,128)}, f32[384,4096]{1,0:T(8,128)}, f32[8,128]{1,0:T(8,128)S(1)}) custom-call(s32[16]{0:T(128)S(1)} %fusion.places_ref, bf16[256,768]{1,0:T(8,128)(2,1)S(1)} %get-tuple-element.84.refs_6_.top_ref, bf16[256,1536]{1,0:T(8,128)(2,1)S(1)} %copy-done.7, ...), custom_call_target="tpu_custom_call", output_to_operand_aliasing={{1}: (12, {}), {0}: (13, {})} | custom-call | flops 3000000000 | bytes 1048576 | tf_op jit(solution)/shard_map/project_columns/pallas_call | solution.py:551
  196.6 5.7 %project_columns.6 = (f32[512,4096]{1,0:T(8,128)}, f32[384,4096]{1,0:T(8,128)}, f32[8,128]{1,0:T(8,128)}) custom-call(s32[16]{0:T(128)S(1)} %fusion.places_ref, bf16[256,768]{1,0:T(8,128)(2,1)S(1)} %get-tuple-element.84.refs_6_.top_ref, bf16[256,1536]{1,0:T(8,128)(2,1)S(1)} %copy-done.7, ...), custom_call_target="tpu_custom_call", output_to_operand_aliasing={{1}: (12, {}), {0}: (13, {})} | custom-call | flops 3000000000 | bytes 1048576 | tf_op jit(solution)/shard_map/project_columns/pallas_call | solution.py:551
  202.3 5.7 %project_columns.7 = (f32[512,4096]{1,0:T(8,128)}, f32[384,4096]{1,0:T(8,128)}, f32[8,128]{1,0:T(8,128)}) custom-call(s32[16]{0:T(128)S(1)} %fusion.places_ref, bf16[256,768]{1,0:T(8,128)(2,1)S(1)} %get-tuple-element.84.refs_6_.top_ref, bf16[256,1536]{1,0:T(8,128)(2,1)S(1)} %copy-done.7, ...), custom_call_target="tpu_custom_call", output_to_operand_aliasing={{1}: (12, {}), {0}: (13, {})} | custom-call | flops 3000000000 | bytes 1048576 | tf_op jit(solution)/shard_map/project_columns/pallas_call | solution.py:551
  (181 shorter events, 86.6 us)
Async XLA Ops:
  5.3 34.4 %all-to-all-start = ((f32[8,16,4096]{2,1,0:T(8,128)}), f32[8,16,4096]{2,1,0:T(8,128)S(1)}, u32[]{:S(2)}, u32[]{:S(2)}) async-start(f32[8,16,4096]{2,1,0:T(8,128)} %bitcast.11), calls=%async_computation | async-start | bytes 4194304 | tf_op jit(solution)/shard_map/all_to_all | solution.py:578
  18.3 12.2 %collective-permute-start.1 = (f32[192,512]{1,0:T(8,128)S(1)}, f32[192,512]{1,0:T(8,128)S(1)}, u32[]{:S(2)}, u32[]{:S(2)}) collective-permute-start(f32[192,512]{1,0:T(8,128)S(1)} %get-tuple-element.57.refs_0_), channel_id=1, source_target_pairs={{0,2},{4,6},{8,10},{12,14},{16,18},{20,22},{24,26},{28,30}} | collective-permute-start | bytes 1179656 | tf_op jit(solution)/shard_map/ppermute | solution.py:168
  19.6 19.3 %collective-permute-start.3 = (f32[192,512]{1,0:T(8,128)S(1)}, f32[192,512]{1,0:T(8,128)S(1)}, u32[]{:S(2)}, u32[]{:S(2)}) collective-permute-start(f32[192,512]{1,0:T(8,128)S(1)} %get-tuple-element.58.refs_0_), channel_id=1, source_target_pairs={{0,2},{4,6},{8,10},{12,14},{16,18},{20,22},{24,26},{28,30}} | collective-permute-start | bytes 1179656 | tf_op jit(solution)/shard_map/ppermute | solution.py:168
  30.6 27.2 %collective-permute-start.2 = (f32[192,512]{1,0:T(8,128)S(1)}, f32[192,512]{1,0:T(8,128)}, u32[]{:S(2)}, u32[]{:S(2)}) collective-permute-start(f32[192,512]{1,0:T(8,128)S(1)} %relay.4.refs_0_), channel_id=1, source_target_pairs={{0,1},{2,3},{4,5},{6,7},{8,9},{10,11},{12,13},{14,15},{16,17},{18,... | collective-permute-start | bytes 1179656 | tf_op jit(solution)/shard_map/ppermute | solution.py:154
  40.8 17.0 %collective-permute-start.6 = (f32[192,512]{1,0:T(8,128)S(1)}, f32[192,512]{1,0:T(8,128)S(1)}, u32[]{:S(2)}, u32[]{:S(2)}) collective-permute-start(f32[192,512]{1,0:T(8,128)S(1)} %relay.5.refs_2_), channel_id=1, source_target_pairs={{0,1},{2,3},{4,5},{6,7},{8,9},{10,11},{12,13},{14,15},{16,17},{18,... | collective-permute-start | bytes 1179656 | tf_op jit(solution)/shard_map/ppermute | solution.py:154
  66.4 11.8 %collective-permute-start.14 = (f32[128,768]{1,0:T(8,128)}, f32[128,768]{1,0:T(8,128)}, u32[]{:S(2)}, u32[]{:S(2)}) collective-permute-start(f32[128,768]{1,0:T(8,128)} %constant_dynamic-slice_fusion), channel_id=1, source_target_pairs={{0,4},{4,0},{8,12},{12,8},{16,20},{20,16},{24,28},{28,24},{1,5},{5... | collective-permute-start | bytes 1179656 | tf_op jit(solution)/shard_map/ppermute | solution.py:43
  77.2 14.4 %collective-permute-start.17 = (f32[512,512]{1,0:T(8,128)}, f32[512,512]{1,0:T(8,128)}, u32[]{:S(2)}, u32[]{:S(2)}) collective-permute-start(f32[512,512]{1,0:T(8,128)} %get-tuple-element.72), channel_id=1, source_target_pairs={{0,4},{4,0},{8,12},{12,8},{16,20},{20,16},{24,28},{28,24},{1,5},{5... | collective-permute-start | bytes 3145736 | tf_op jit(solution)/shard_map/ppermute | solution.py:43
  77.5 15.5 %collective-permute-start.18 = (f32[512,512]{1,0:T(8,128)}, f32[512,512]{1,0:T(8,128)}, u32[]{:S(2)}, u32[]{:S(2)}) collective-permute-start(f32[512,512]{1,0:T(8,128)} %get-tuple-element.75), channel_id=1, source_target_pairs={{0,4},{4,0},{8,12},{12,8},{16,20},{20,16},{24,28},{28,24},{1,5},{5... | collective-permute-start | bytes 3145736 | tf_op jit(solution)/shard_map/ppermute | solution.py:43
  77.7 16.7 %collective-permute-start.19 = (f32[512,512]{1,0:T(8,128)}, f32[512,512]{1,0:T(8,128)}, u32[]{:S(2)}, u32[]{:S(2)}) collective-permute-start(f32[512,512]{1,0:T(8,128)} %get-tuple-element.78), channel_id=1, source_target_pairs={{0,4},{4,0},{8,12},{12,8},{16,20},{20,16},{24,28},{28,24},{1,5},{5... | collective-permute-start | bytes 3145736 | tf_op jit(solution)/shard_map/ppermute | solution.py:43
  78.0 17.7 %collective-permute-start.20 = (f32[512,512]{1,0:T(8,128)}, f32[512,512]{1,0:T(8,128)}, u32[]{:S(2)}, u32[]{:S(2)}) collective-permute-start(f32[512,512]{1,0:T(8,128)} %get-tuple-element.81), channel_id=1, source_target_pairs={{0,4},{4,0},{8,12},{12,8},{16,20},{20,16},{24,28},{28,24},{1,5},{5... | collective-permute-start | bytes 3145736 | tf_op jit(solution)/shard_map/ppermute | solution.py:43
  79.4 11.0 %collective-permute-start.15 = (f32[128,768]{1,0:T(8,128)S(1)}, f32[128,768]{1,0:T(8,128)S(1)}, u32[]{:S(2)}, u32[]{:S(2)}) collective-permute-start(f32[128,768]{1,0:T(8,128)S(1)} %dynamic-slice_add_fusion.refs_0_), channel_id=1, source_target_pairs={{0,8},{4,20},{8,0},{12,28},{16,24},{20,4},{24,16},{28,12},{1,9},{5... | collective-permute-start | bytes 1179656 | tf_op jit(solution)/shard_map/ppermute | solution.py:43
  99.0 13.7 %collective-permute-start.25 = (f32[512,256]{1,0:T(8,128)S(1)}, f32[512,256]{1,0:T(8,128)S(1)}, u32[]{:S(2)}, u32[]{:S(2)}) collective-permute-start(f32[512,256]{1,0:T(8,128)S(1)} %get-tuple-element.90), channel_id=1, source_target_pairs={{0,8},{4,20},{8,0},{12,28},{16,24},{20,4},{24,16},{28,12},{1,9},{5... | collective-permute-start | bytes 1572872 | tf_op jit(solution)/shard_map/ppermute | solution.py:43
  99.9 18.7 %collective-permute-start.26 = (f32[512,256]{1,0:T(8,128)S(1)}, f32[512,256]{1,0:T(8,128)S(1)}, u32[]{:S(2)}, u32[]{:S(2)}) collective-permute-start(f32[512,256]{1,0:T(8,128)S(1)} %get-tuple-element.92), channel_id=1, source_target_pairs={{0,8},{4,20},{8,0},{12,28},{16,24},{20,4},{24,16},{28,12},{1,9},{5... | collective-permute-start | bytes 1572872 | tf_op jit(solution)/shard_map/ppermute | solution.py:43
  100.5 25.9 %collective-permute-start.27 = (f32[512,256]{1,0:T(8,128)S(1)}, f32[512,256]{1,0:T(8,128)S(1)}, u32[]{:S(2)}, u32[]{:S(2)}) collective-permute-start(f32[512,256]{1,0:T(8,128)S(1)} %get-tuple-element.94), channel_id=1, source_target_pairs={{0,8},{4,20},{8,0},{12,28},{16,24},{20,4},{24,16},{28,12},{1,9},{5... | collective-permute-start | bytes 1572872 | tf_op jit(solution)/shard_map/ppermute | solution.py:43
  101.4 28.9 %collective-permute-start.22 = (f32[512,256]{1,0:T(8,128)S(1)}, f32[512,256]{1,0:T(8,128)S(1)}, u32[]{:S(2)}, u32[]{:S(2)}) collective-permute-start(f32[512,256]{1,0:T(8,128)S(1)} %get-tuple-element.87), channel_id=1, source_target_pairs={{0,8},{4,20},{8,0},{12,28},{16,24},{20,4},{24,16},{28,12},{1,9},{5... | collective-permute-start | bytes 1572872 | tf_op jit(solution)/shard_map/ppermute | solution.py:43
  118.8 16.4 %collective-permute-start.29 = (f32[512,128]{1,0:T(8,128)S(1)}, f32[512,128]{1,0:T(8,128)S(1)}, u32[]{:S(2)}, u32[]{:S(2)}) collective-permute-start(f32[512,128]{1,0:T(8,128)S(1)} %get-tuple-element.96), channel_id=1, source_target_pairs={{0,16},{4,12},{8,24},{12,4},{16,0},{20,28},{24,8},{28,20},{1,17},{... | collective-permute-start | bytes 786440 | tf_op jit(solution)/shard_map/ppermute | solution.py:43
  121.3 12.5 %collective-permute-start.34 = (f32[512,128]{1,0:T(8,128)S(1)}, f32[512,128]{1,0:T(8,128)S(1)}, u32[]{:S(2)}, u32[]{:S(2)}) collective-permute-start(f32[512,128]{1,0:T(8,128)S(1)} %add.28.refs_0_), channel_id=1, source_target_pairs={{0,16},{4,12},{8,24},{12,4},{16,0},{20,28},{24,8},{28,20},{1,17},{... | collective-permute-start | bytes 786440 | tf_op jit(solution)/shard_map/ppermute | solution.py:43
  141.1 9.6 %collective-permute-start.31 = (f32[1024,128]{1,0:T(8,128)S(1)}, f32[1024,128]{1,0:T(8,128)S(1)}, u32[]{:S(2)}, u32[]{:S(2)}) collective-permute-start(f32[1024,128]{1,0:T(8,128)S(1)} %join_pieces.7), channel_id=1, source_target_pairs={{0,8},{4,20},{8,0},{12,28},{16,24},{20,4},{24,16},{28,12},{1,9},{5... | collective-permute-start | bytes 1572872 | tf_op jit(solution)/shard_map/ppermute | solution.py:43
  143.0 34.1 %collective-permute-start.36 = (f32[2048,128]{1,0:T(8,128)S(1)}, f32[2048,128]{1,0:T(8,128)}, u32[]{:S(2)}, u32[]{:S(2)}) collective-permute-start(f32[2048,128]{1,0:T(8,128)S(1)} %pad_maximum_fusion.1.rest_0_.rest_1_.rest_2_.rest_3_), channel_id=1, source_target_pairs={{0,4},{4,0},{8,12},{12,8},{16,20},{20,16},{24,28},{28,24},{1,5},{5... | collective-permute-start | bytes 3145736 | tf_op jit(solution)/shard_map/ppermute | solution.py:43
  148.8 11.7 %collective-permute-start.38 = (f32[512,128]{1,0:T(8,128)S(1)}, f32[512,128]{1,0:T(8,128)S(1)}, u32[]{:S(2)}, u32[]{:S(2)}) collective-permute-start(f32[512,128]{1,0:T(8,128)S(1)} %get-tuple-element.102), channel_id=1, source_target_pairs={{0,16},{4,12},{8,24},{12,4},{16,0},{20,28},{24,8},{28,20},{1,17},{... | collective-permute-start | bytes 786440 | tf_op jit(solution)/shard_map/ppermute | solution.py:43
  150.7 39.9 %collective-permute-start.32 = (f32[2048,128]{1,0:T(8,128)S(1)}, f32[2048,128]{1,0:T(8,128)S(1)}, u32[]{:S(2)}, u32[]{:S(2)}) collective-permute-start(f32[2048,128]{1,0:T(8,128)S(1)} %pad_maximum_fusion.rest_0_.rest_1_.rest_2_.rest_3_), channel_id=1, source_target_pairs={{0,4},{4,0},{8,12},{12,8},{16,20},{20,16},{24,28},{28,24},{1,5},{5... | collective-permute-start | bytes 3145736 | tf_op jit(solution)/shard_map/ppermute | solution.py:43
  168.2 17.4 %collective-permute-start.40 = (f32[1024,128]{1,0:T(8,128)}, f32[1024,128]{1,0:T(8,128)}, u32[]{:S(2)}, u32[]{:S(2)}) collective-permute-start(f32[1024,128]{1,0:T(8,128)} %join_pieces.10.refs_0_), channel_id=1, source_target_pairs={{0,8},{4,20},{8,0},{12,28},{16,24},{20,4},{24,16},{28,12},{1,9},{5... | collective-permute-start | bytes 1572872 | tf_op jit(solution)/shard_map/ppermute | solution.py:43
  176.0 20.4 %collective-permute-start.28 = (f32[1024,128]{1,0:T(8,128)S(1)}, f32[1024,128]{1,0:T(8,128)S(1)}, u32[]{:S(2)}, u32[]{:S(2)}) collective-permute-start(f32[1024,128]{1,0:T(8,128)S(1)} %join_pieces.6.refs_0_), channel_id=1, source_target_pairs={{0,8},{4,20},{8,0},{12,28},{16,24},{20,4},{24,16},{28,12},{1,9},{5... | collective-permute-start | bytes 1572872 | tf_op jit(solution)/shard_map/ppermute | solution.py:43
  186.9 9.7 %collective-permute-start.41 = (f32[2048,128]{1,0:T(8,128)S(1)}, f32[2048,128]{1,0:T(8,128)S(1)}, u32[]{:S(2)}, u32[]{:S(2)}) collective-permute-start(f32[2048,128]{1,0:T(8,128)S(1)} %join_pieces.11.rest_0_.rest_1_.rest_2_.rest_3_), channel_id=1, source_target_pairs={{0,4},{4,0},{8,12},{12,8},{16,20},{20,16},{24,28},{28,24},{1,5},{5... | collective-permute-start | bytes 3145736 | tf_op jit(solution)/shard_map/ppermute | solution.py:43
  (56 other events, 480.2 us)
